TPU v7x, 32 devices: a whole 2x2x4 slice. The times are simulated.
32 devices in a mesh: groups: 2 (over x), tensor: 16 (over z, y, core).
Axes of the slice: x: 2, y: 2, z: 4, core: 2. Of those that a mesh axis runs over, the one named last changes fastest.
Arguments:
- activations: bfloat16 [256, 26624], P('groups', 'tensor'), parts along dimension 0, may hold values from -6 to 6
- rotation_small: float32 [52, 52], replicated, may hold values from -0.875 to 0.875
- down_weight: bfloat16 [26624, 8192], P('tensor'), may hold values from -0.0546875 to 0.0546875
Outputs:
- projected: bfloat16 [256, 8192], P('groups', 'tensor'), parts along dimension 0
There are 2 independent parts, one for each index of `groups`. A program takes and returns all parts, laid end to end along the dimension named above; an argument that names none is the same for every part. Nothing has to cross between parts.
All inputs are finite; a program needn't handle non-finite values.
Results may differ from a plain program's by a relative error of at most 0.005.
Values sent between devices are 32-bit elements; how exact they have to be, the bound alone decides.
No kernel may reach another device: no remote copies, remote signals or barrier semaphores. Data moves between devices by JAX's collectives and lax.ppermute only.
A program may use at most 128 MiB of HBM per device.

v0:
```python
import jax
import jax.numpy as jnp
from jax import lax
from jax.sharding import PartitionSpec as P

BLOCK = 52


def sylvester(order):
    index = jnp.arange(order, dtype=jnp.int32)
    common = jnp.zeros((order, order), jnp.int32)
    for place in range(max(order.bit_length(), 1)):
        common = common + (index[:, None] >> place & 1) * (index[None, :] >> place & 1)
    return (1 - 2 * (common % 2)).astype(jnp.float32)


def body(activations, rotation_small, down_weight):
    tokens, local = activations.shape
    shards = lax.axis_size("tensor")
    span = local // BLOCK
    kronecker = jnp.kron(sylvester(span), rotation_small)
    factor = (span * shards) ** (-0.5)
    values = activations.astype(jnp.float32)
    gathered = lax.all_to_all(values, "tensor", split_axis=0, concat_axis=1, tiled=True)
    gathered = gathered.reshape(-1, shards, local)
    gathered = jnp.einsum(
        "rsl,su->rul", gathered, sylvester(shards), precision=lax.Precision.HIGHEST
    )
    gathered = jnp.dot(gathered.reshape(-1, local), kronecker, precision=lax.Precision.HIGHEST)
    gathered = gathered.reshape(-1, shards * local)
    returned = lax.all_to_all(gathered, "tensor", split_axis=1, concat_axis=0, tiled=True)
    rotated = (returned * factor).astype(jnp.bfloat16)
    summed = lax.psum_scatter(
        lax.dot_general(
            down_weight, rotated, (((0,), (1,)), ((), ())), preferred_element_type=jnp.float32
        ),
        "tensor",
        scatter_dimension=0,
        tiled=True,
    )
    return summed.T.astype(jnp.bfloat16)


def solution(mesh):
    placed = (P("groups", "tensor"), P(), P("tensor", None))
    return jax.shard_map(
        body, mesh=mesh, in_specs=placed, out_specs=P("groups", "tensor"), check_vma=False
    )
```

profile of v0, /device:TPU:0, one launch (start us, length us, event | category | flops | bytes accessed | tf_op | source)
XLA Modules:
  0.0 189.5 jit_solution(4873965791969258324)
XLA Ops:
  6.5 2.0 %bitcast_convert_fusion = f32[16,8,1664]{2,1,0:T(8,128)} fusion(bf16[128,1664]{1,0:T(8,128)(2,1)} %param.3), kind=kLoop, calls=%fused_computation.9 | loop fusion | flops 212992 | bytes 1277952 | tf_op jit(solution)/shard_map/all_to_all | solution.py:24
  8.5 7.4 %all-to-all-start = ((f32[16,8,1664]{2,1,0:T(8,128)}), f32[16,8,1664]{2,1,0:T(8,128)S(1)}, u32[]{:S(2)}, u32[]{:S(2)}) async-start(f32[16,8,1664]{2,1,0:T(8,128)} %bitcast_convert_fusion), calls=%async_computation | async-start | bytes 1703936 | tf_op jit(solution)/shard_map/all_to_all | solution.py:24
  15.9 0.0 reduce-scatter.2.cloned.1.call-start
  16.0 0.1 fusion.10
  16.1 13.3 %broadcast_multiply_fusion = f32[32,52,32,52]{3,2,1,0:T(8,128)} fusion(f32[52,52]{1,0:T(8,128)} %param.4, f32[32,32]{1,0:T(8,128)S(1)} %fusion.10), kind=kLoop, calls=%fused_computation | loop fusion | flops 2768896 | bytes 11090496 | tf_op jit(solution)/shard_map/jit(kron)/mul | solution.py:21
  29.5 25.8 %reshape.360 = f32[1664,1664,1]{1,0,2:T(8,128)} reshape(f32[32,52,32,52]{3,2,1,0:T(8,128)} %broadcast_multiply_fusion) | data formatting | bytes 22151168 | tf_op jit(solution)/shard_map/jit(kron)/mul | solution.py:21
  55.3 0.0 all-to-all-done
  55.3 0.9 convolution_bitcast_fusion.1
  56.2 10.5 %fusion.1 = f32[8,16,1664]{2,0,1:T(8,128)S(1)} fusion(f32[1664,1664,1]{1,0,2:T(8,128)} %reshape.360, f32[8,16,1664]{2,1,0:T(8,128)S(1)} %convolution_bitcast_fusion.1), kind=kOutput, calls=%fused_computation.4 | convolution fusion | flops 4253024256 | bytes 12779520 | tf_op jit(solution)/shard_map/dot_general | solution.py:29
  66.7 27.2 %all_to_all.30 = f32[8,16,1664]{2,0,1:T(8,128)S(1)} all-to-all(f32[8,16,1664]{2,0,1:T(8,128)S(1)} %fusion.1), channel_id=1, replica_groups=mesh['groups'=2,'tensor'=16] {'tensor'}, dimensions={1} | all-to-all | bytes 1703936 | tf_op jit(solution)/shard_map/all_to_all | solution.py:31
  94.0 14.7 %convolution_bitcast_fusion = f32[8192,128]{0,1:T(8,128)} fusion(bf16[1664,8192]{1,0:T(8,128)(2,1)} %param.5, f32[8,16,1664]{2,0,1:T(8,128)S(1)} %all_to_all.30), kind=kOutput, calls=%fused_computation.1 | convolution fusion | flops 3490086912 | bytes 32309248 | tf_op jit(solution)/shard_map/dot_general | solution.py:34
  108.6 0.0 reduce-scatter.2.cloned.1.call-update
  108.6 72.4 %reduce-scatter.2.cloned.1.call-done = f32[512,128]{0,1:T(8,128)} async-done(((f32[8192,128]{0,1:T(8,128)}), f32[512,128]{0,1:T(8,128)}) %reduce-scatter.2.cloned.1.call-update) | async-done | bytes 262160 | tf_op jit(solution)/shard_map/reduce_scatter | solution.py:33
  181.0 1.6 convert_bitcast_fusion
  (6 shorter events, 0.0 us)
Async XLA Ops:
  8.5 46.8 %all-to-all-start = ((f32[16,8,1664]{2,1,0:T(8,128)}), f32[16,8,1664]{2,1,0:T(8,128)S(1)}, u32[]{:S(2)}, u32[]{:S(2)}) async-start(f32[16,8,1664]{2,1,0:T(8,128)} %bitcast_convert_fusion), calls=%async_computation | async-start | bytes 1703936 | tf_op jit(solution)/shard_map/all_to_all | solution.py:24
  15.9 165.1 %reduce-scatter.2.cloned.1.call-start = ((), (), s32[]{:S(2)}) async-start(), calls=%async_computation.3 | async-start | bytes 4456448 | tf_op jit(solution)/shard_map/reduce_scatter | solution.py:33
Sparse Core Ops, SparseCore 0:
  108.8 72.2 reduce-scatter.1
where the time goes:
time: 190 us; the launch traced here: 189 us
  waiting for transfers between devices  72.4 us (38%)
  blocking collectives  27.2 us (14%)
  matrix products  26.1 us (14%)
  local copies, waits for them, and re-layouts  25.8 us (14%)
  other arithmetic  17.1 us (9%)
  between operations  13.5 us (7%)
  starting transfers between devices  7.43 us (4%)
    reduce_scatter x1, waiting for transfers between devices, body(): lax.psum_scatter(lax.dot_general(down_weight, rotated, (((0,), (1,)), (()...  72.4 us
    all_to_all x1, blocking collectives, body(): lax.all_to_all(gathered, 'tensor', split_axis=1, concat_axis=0, tiled=True)  27.2 us
    mul x1, local copies, waits for them, and re-layouts, body(): kronecker = jnp.kron(sylvester(span), rotation_small)  25.8 us
    dot_general x1, matrix products, body(): lax.dot_general(down_weight, rotated, (((0,), (1,)), ((), ())), preferred...  14.7 us
    mul x1, other arithmetic, body(): kronecker = jnp.kron(sylvester(span), rotation_small)  13.3 us
    dot_general x1, matrix products, body(): jnp.dot(gathered.reshape(-1, local), kronecker, precision=lax.Precision.H...  10.5 us
    all_to_all x1, starting transfers between devices, body(): lax.all_to_all(values, 'tensor', split_axis=0, concat_axis=1, tiled=True)  7.39 us
  transfers between devices with their start and end apart: 2, of which 1 were waited for; matrix products, arithmetic and copies ran while one was open for 21% of the time, Pallas kernels for 0%

commit v1 on v0

v1 whole, which is shorter than its diff:
```python
import functools

import jax
import jax.numpy as jnp
import numpy as np
from jax import lax
from jax.experimental import pallas as pl
from jax.experimental.pallas import tpu as pltpu
from jax.sharding import PartitionSpec as P

LANES = 128
F32 = jnp.float32
BF16 = jnp.bfloat16


def quotient(index, divisor, limit):
    shift = 16
    scale = -(-(1 << shift) // divisor)
    numbers = np.arange(limit, dtype=np.int64)
    assert np.array_equal((numbers * scale) >> shift, numbers // divisor)
    assert limit * scale < 2**31
    return (index * scale) >> shift


def sign_of(common, count):
    parity = common
    for place in range(1, count):
        parity = parity ^ (common >> place)
    return (1 - 2 * (parity & 1)).astype(F32)


def mix_kernel(start, group, activations, small, out):
    tokens, local = activations.shape
    block = small.shape[0]
    cols = out.shape[1]
    rows = group * block
    span = local // block
    low = group.bit_length() - 1
    high = span.bit_length() - 1 - low
    full = small[...]
    head = full.astype(BF16)
    tail = (full - head.astype(F32)).astype(BF16)

    row = lax.broadcasted_iota(jnp.int32, (rows, block), 0)
    unit = lax.broadcasted_iota(jnp.int32, (rows, block), 1)
    spread_rows = (row - quotient(row, block, rows) * block == unit).astype(F32).astype(BF16)
    col = lax.broadcasted_iota(jnp.int32, (block, cols), 1) + start
    unit = lax.broadcasted_iota(jnp.int32, (block, cols), 0)
    spread_cols = (col - quotient(col, block, local) * block == unit).astype(F32).astype(BF16)
    at_row = quotient(lax.broadcasted_iota(jnp.int32, (rows, cols), 0), block, rows)
    at_col = quotient(lax.broadcasted_iota(jnp.int32, (rows, cols), 1) + start, block, local)
    sign = sign_of(at_row & at_col, max(low, 1))

    def tiled(part):
        tall = jnp.dot(spread_rows, part, preferred_element_type=F32).astype(BF16)
        return (jnp.dot(tall, spread_cols, preferred_element_type=F32) * sign).astype(BF16)

    head, tail = tiled(head), tiled(tail)
    owner = quotient(lax.broadcasted_iota(jnp.int32, (8, cols), 1) + start, block, local) >> low
    total = jnp.zeros((tokens, cols), F32)
    for piece in range(span // group):
        values = activations[:, piece * rows:(piece + 1) * rows]
        term = jnp.dot(values, head, preferred_element_type=F32)
        term = term + jnp.dot(values, tail, preferred_element_type=F32)
        total = total + term * sign_of(owner & piece, max(high, 1))[0:1]
    out[...] = total


def mix(activations, small, start, cols):
    tokens, local = activations.shape
    block = small.shape[0]
    span = local // block
    group = min(4, span)
    return pl.pallas_call(
        functools.partial(mix_kernel, start, group),
        out_shape=jax.ShapeDtypeStruct((tokens, cols), F32),
        in_specs=[pl.BlockSpec(memory_space=pltpu.VMEM)] * 2,
        out_specs=pl.BlockSpec(memory_space=pltpu.VMEM),
        cost_estimate=pl.CostEstimate(
            flops=4 * tokens * local * cols, bytes_accessed=tokens * (2 * local + 4 * cols), transcendentals=0
        ),
        compiler_params=pltpu.CompilerParams(vmem_limit_bytes=24 * 2**20),
        name="mix",
    )(activations, small)


def product_kernel(edges, order, *refs):
    chunks, weight, out = refs[:-2], refs[-2], refs[-1]
    total = None
    for chunk, begin, end in zip(chunks, edges[:-1], edges[1:]):
        term = jnp.dot(chunk[...], weight[begin:end, :], preferred_element_type=F32)
        total = term if total is None else total + term
    out[0] = total


def product(chunks, weight, me, edges, order, width, part, parts):
    tokens = chunks[0].shape[0]
    local = weight.shape[0]
    blocks = len(order)
    table = jnp.asarray(np.array(order, np.int32)) ^ me

    def kernel(table_ref, *refs):
        product_kernel(edges, order, *refs)

    return pl.pallas_call(
        kernel,
        grid_spec=pltpu.PrefetchScalarGridSpec(
            num_scalar_prefetch=1,
            grid=(blocks,),
            in_specs=[pl.BlockSpec(chunk.shape, lambda i, t: (0, 0)) for chunk in chunks]
            + [pl.BlockSpec((local, width), lambda i, t: (0, t[i] * parts + part))],
            out_specs=pl.BlockSpec((1, tokens, width), lambda i, t: (i, 0, 0)),
        ),
        out_shape=jax.ShapeDtypeStruct((blocks, tokens, width), F32),
        cost_estimate=pl.CostEstimate(
            flops=2 * tokens * local * width * blocks,
            bytes_accessed=blocks * width * (2 * local + 4 * tokens),
            transcendentals=0,
        ),
        compiler_params=pltpu.CompilerParams(vmem_limit_bytes=24 * 2**20),
        name="product",
    )(table, *chunks, weight)


def relative_owners(bits):
    found = [0]
    for bit in bits:
        found = [value | extra for value in found for extra in (0, bit)]
    return found


def body(activations, rotation_small, down_weight):
    shards = lax.axis_size("tensor")
    me = lax.axis_index("tensor")
    tokens, local = activations.shape
    block = rotation_small.shape[0]
    features = down_weight.shape[1]
    factor = (local // block * shards) ** (-0.5)
    bits = [1 << place for place in range(shards.bit_length() - 1)]

    def swap(x, bit):
        return lax.ppermute(x, "tensor", [(d, d ^ bit) for d in range(shards)])

    tiles = -(-local // LANES)
    count = max(1, min(len(bits), tiles))
    edges = [min(local, (tiles * c // count) * LANES) for c in range(count)] + [local]
    chunks = [mix(activations, rotation_small, a, b - a) for a, b in zip(edges[:-1], edges[1:])]
    cycle = bits[::-1][:1] + bits[1:-1] + bits[:1] if len(bits) > 1 else bits
    for phase in range(len(bits)):
        for c in range(count):
            bit = cycle[(phase - c) % len(bits)]
            sign = jnp.where(me & bit, -1.0, 1.0).astype(F32)
            chunks[c] = swap(chunks[c], bit) + sign * chunks[c]
    chunks = [(chunk * factor).astype(BF16) for chunk in chunks]

    share = features // shards
    parts = 2 if share % (2 * LANES) == 0 else 1
    width = share // parts
    results = []
    for part in range(parts):
        order = list(bits)
        if part and len(bits) > 2:
            order[1], order[2] = order[2], order[1]
        owners = relative_owners(order)
        half = len(owners) // 2
        send = product(chunks, down_weight, me, edges, owners[half:], width, part, parts)
        keep = product(chunks, down_weight, me, edges, owners[:half], width, part, parts)
        for bit in order:
            keep = keep + swap(send, bit)
            half = keep.shape[0] // 2
            if half:
                keep, send = keep[:half], keep[half:]
        results.append(keep[0])
    return jnp.concatenate(results, axis=1).astype(BF16)


def solution(mesh):
    placed = (P("groups", "tensor"), P(), P("tensor", None))
    return jax.shard_map(
        body, mesh=mesh, in_specs=placed, out_specs=P("groups", "tensor"), check_vma=False
    )
```

time: 190 us -> 131 us (0.69)
  blocking collectives: 27.2 us -> 0 us
  matrix products: 26.1 us -> 0 us
  Pallas kernels: 0 us -> 20.7 us
  starting transfers between devices: 7.43 us -> 25.1 us
  other arithmetic: 17.1 us -> 2.3 us
  between operations: 13.5 us -> 0.36 us
  waiting for transfers between devices: 72.4 us -> 62.6 us
  local copies, waits for them, and re-layouts: 25.8 us -> 19.4 us
    reduce_scatter x1 -> x0, waiting for transfers between devices: 72.4 us -> none  [body(): lax.psum_scatter(lax.dot_general(down_weight, rotated, (((0,), (1,)), (()...]
    ppermute x0 -> x24, waiting for transfers between devices: none -> 62.6 us  [swap(): return lax.ppermute(x, 'tensor', [(d, d ^ bit) for d in range(shards)])]
    all_to_all x1 -> x0, blocking collectives: 27.2 us -> none  [body(): lax.all_to_all(gathered, 'tensor', split_axis=1, concat_axis=0, tiled=True)]
    dot_general x3 -> x0, matrix products: 26.1 us -> none  [the longest x1 14.7 us: body(): lax.dot_general(down_weight, rotated, (((0,), (1,)), ((), ())), preferred...]
    mul x1 -> x0, local copies, waits for them, and re-layouts: 25.8 us -> none  [body(): kronecker = jnp.kron(sylvester(span), rotation_small)]
    ppermute x0 -> x24, starting transfers between devices: none -> 25.1 us  [swap(): return lax.ppermute(x, 'tensor', [(d, d ^ bit) for d in range(shards)])]
    pallas_call x0 -> x8, Pallas kernels: none -> 20.7 us  [the longest x4 15.9 us: product(): pl.pallas_call(kernel, grid_spec=pltpu.PrefetchScalarGridSpec(num_scalar_...]
    unnamed x0 -> x14, local copies, waits for them, and re-layouts: none -> 19.3 us
  transfers between devices with their start and end apart: 2 -> 24, of which waited for: 1 -> 14; matrix products, arithmetic and copies ran while one was open for 21% -> 1% of each run, Pallas kernels for 0% -> 12%
where the time goes in v1:
time: 131 us; the launch traced here: 130 us
  waiting for transfers between devices  62.6 us (48%)
  starting transfers between devices  25.1 us (19%)
  Pallas kernels  20.7 us (16%)
  local copies, waits for them, and re-layouts  19.4 us (15%)
  other arithmetic  2.3 us (2%)
    ppermute x24, waiting for transfers between devices, swap(): return lax.ppermute(x, 'tensor', [(d, d ^ bit) for d in range(shards)])  62.6 us
    ppermute x24, starting transfers between devices, swap(): return lax.ppermute(x, 'tensor', [(d, d ^ bit) for d in range(shards)])  25.1 us
    unnamed x14, local copies, waits for them, and re-layouts  19.3 us
    pallas_call x4, Pallas kernels, product(): pl.pallas_call(kernel, grid_spec=pltpu.PrefetchScalarGridSpec(num_scalar_...  15.9 us
    pallas_call x4, Pallas kernels, mix(): pl.pallas_call(functools.partial(mix_kernel, start, group), out_shape=jax...  4.73 us
  transfers between devices with their start and end apart: 24, of which 14 were waited for; matrix products, arithmetic and copies ran while one was open for 1% of the time, Pallas kernels for 12%

profile of v1, /device:TPU:0, one launch (start us, length us, event | category | flops | bytes accessed | tf_op | source)
XLA Modules:
  0.0 130.5 jit_solution(8667498143595930159)
XLA Ops:
  0.0 1.0 copy-done.2
  1.0 0.7 copy-done.3
  1.8 1.2 mix.7
  3.0 3.0 %collective-permute-start.12 = (f32[128,512]{1,0:T(8,128)S(1)}, f32[128,512]{1,0:T(8,128)S(1)}, u32[]{:S(2)}, u32[]{:S(2)}) collective-permute-start(f32[128,512]{1,0:T(8,128)S(1)} %mix.7), channel_id=1, source_target_pairs={{0,2},{1,3},{2,0},{3,1},{4,6},{5,7},{6,4},{7,5},{8,10},{9,11},{10,... | collective-permute-start | bytes 786440 | tf_op jit(solution)/shard_map/ppermute | solution.py:142
  6.0 1.2 mix.6
  7.2 1.6 %collective-permute-start.8 = (f32[128,384]{1,0:T(8,128)S(1)}, f32[128,384]{1,0:T(8,128)S(1)}, u32[]{:S(2)}, u32[]{:S(2)}) collective-permute-start(f32[128,384]{1,0:T(8,128)S(1)} %mix.6), channel_id=1, source_target_pairs={{0,4},{1,5},{2,6},{3,7},{4,0},{5,1},{6,2},{7,3},{8,12},{9,13},{10,... | collective-permute-start | bytes 589832 | tf_op jit(solution)/shard_map/ppermute | solution.py:142
  8.8 1.2 mix.5
  10.0 0.1 collective-permute-start.4
  10.1 1.2 mix.4
  11.3 2.7 %collective-permute-start = (f32[128,384]{1,0:T(8,128)S(1)}, f32[128,384]{1,0:T(8,128)S(1)}, u32[]{:S(2)}, u32[]{:S(2)}) collective-permute-start(f32[128,384]{1,0:T(8,128)S(1)} %mix.4), channel_id=1, source_target_pairs={{0,8},{1,9},{2,10},{3,11},{4,12},{5,13},{6,14},{7,15},{8,0},{9,1},... | collective-permute-start | bytes 589832 | tf_op jit(solution)/shard_map/ppermute | solution.py:142
  13.9 0.7 broadcast_xor_fusion.2.table_ref
  14.6 0.0 collective-permute-done.8
  14.6 0.3 collective-permute-start.9
  14.9 0.0 collective-permute-done.4
  14.9 1.8 %collective-permute-start.5 = (f32[128,384]{1,0:T(8,128)S(1)}, f32[128,384]{1,0:T(8,128)S(1)}, u32[]{:S(2)}, u32[]{:S(2)}) collective-permute-start(f32[128,384]{1,0:T(8,128)S(1)} %multiply_add_fusion.8), channel_id=1, source_target_pairs={{0,8},{1,9},{2,10},{3,11},{4,12},{5,13},{6,14},{7,15},{8,0},{9,1},... | collective-permute-start | bytes 589832 | tf_op jit(solution)/shard_map/ppermute | solution.py:142
  16.7 11.4 %collective-permute-done = f32[128,384]{1,0:T(8,128)S(1)} collective-permute-done((f32[128,384]{1,0:T(8,128)S(1)}, f32[128,384]{1,0:T(8,128)S(1)}, u32[]{:S(2)}, u32[]{:S(2)}) %collective-permute-start) | collective-permute-done | bytes 196640 | tf_op jit(solution)/shard_map/ppermute | solution.py:142
  28.2 0.5 collective-permute-start.1
  28.8 0.0 collective-permute-done.12
  28.8 0.1 collective-permute-start.13
  28.9 3.3 %collective-permute-start.10 = (f32[128,384]{1,0:T(8,128)S(1)}, f32[128,384]{1,0:T(8,128)S(1)}, u32[]{:S(2)}, u32[]{:S(2)}) collective-permute-start(f32[128,384]{1,0:T(8,128)S(1)} %multiply_add_fusion.4), channel_id=1, source_target_pairs={{0,8},{1,9},{2,10},{3,11},{4,12},{5,13},{6,14},{7,15},{8,0},{9,1},... | collective-permute-start | bytes 589832 | tf_op jit(solution)/shard_map/ppermute | solution.py:142
  32.2 0.3 collective-permute-done.5
  32.5 1.3 collective-permute-start.6
  33.8 0.9 collective-permute-done.1
  34.8 0.1 collective-permute-start.2
  34.8 7.3 %collective-permute-done.13 = f32[128,512]{1,0:T(8,128)S(1)} collective-permute-done((f32[128,512]{1,0:T(8,128)S(1)}, f32[128,512]{1,0:T(8,128)S(1)}, u32[]{:S(2)}, u32[]{:S(2)}) %collective-permute-start.13) | collective-permute-done | bytes 262176 | tf_op jit(solution)/shard_map/ppermute | solution.py:142
  42.1 0.1 collective-permute-start.14
  42.2 0.0 collective-permute-done.10
  42.3 1.4 %collective-permute-start.11 = (f32[128,384]{1,0:T(8,128)S(1)}, f32[128,384]{1,0:T(8,128)S(1)}, u32[]{:S(2)}, u32[]{:S(2)}) collective-permute-start(f32[128,384]{1,0:T(8,128)S(1)} %multiply_add_fusion.3), channel_id=1, source_target_pairs={{0,2},{1,3},{2,0},{3,1},{4,6},{5,7},{6,4},{7,5},{8,10},{9,11},{10,... | collective-permute-start | bytes 589832 | tf_op jit(solution)/shard_map/ppermute | solution.py:142
  43.6 0.0 collective-permute-done.6
  43.6 1.6 %collective-permute-start.7 = (f32[128,384]{1,0:T(8,128)S(1)}, f32[128,384]{1,0:T(8,128)S(1)}, u32[]{:S(2)}, u32[]{:S(2)}) collective-permute-start(f32[128,384]{1,0:T(8,128)S(1)} %multiply_add_fusion.6), channel_id=1, source_target_pairs={{0,4},{1,5},{2,6},{3,7},{4,0},{5,1},{6,2},{7,3},{8,12},{9,13},{10,... | collective-permute-start | bytes 589832 | tf_op jit(solution)/shard_map/ppermute | solution.py:142
  45.3 1.0 collective-permute-done.2
  46.2 0.1 collective-permute-start.3
  46.3 0.0 collective-permute-done.14
  46.4 0.6 collective-permute-start.15
  47.0 2.6 %collective-permute-done.11 = f32[128,384]{1,0:T(8,128)S(1)} collective-permute-done((f32[128,384]{1,0:T(8,128)S(1)}, f32[128,384]{1,0:T(8,128)S(1)}, u32[]{:S(2)}, u32[]{:S(2)}) %collective-permute-start.11) | collective-permute-done | bytes 196640 | tf_op jit(solution)/shard_map/ppermute | solution.py:142
  49.6 1.5 %collective-permute-done.7 = f32[128,384]{1,0:T(8,128)S(1)} collective-permute-done((f32[128,384]{1,0:T(8,128)S(1)}, f32[128,384]{1,0:T(8,128)S(1)}, u32[]{:S(2)}, u32[]{:S(2)}) %collective-permute-start.7) | collective-permute-done | bytes 196640 | tf_op jit(solution)/shard_map/ppermute | solution.py:142
  51.2 10.5 %collective-permute-done.15 = f32[128,512]{1,0:T(8,128)S(1)} collective-permute-done((f32[128,512]{1,0:T(8,128)S(1)}, f32[128,512]{1,0:T(8,128)S(1)}, u32[]{:S(2)}, u32[]{:S(2)}) %collective-permute-start.15) | collective-permute-done | bytes 262176 | tf_op jit(solution)/shard_map/ppermute | solution.py:142
  61.7 0.0 copy-start
  61.7 8.7 %copy-done = bf16[1664,8192]{1,0:T(8,128)(2,1)S(1)} copy-done((bf16[1664,8192]{1,0:T(8,128)(2,1)S(1)}, bf16[1664,8192]{1,0:T(8,128)(2,1)}, u32[]{:S(2)}) %copy-start) | copy-done | bytes 27263000
  70.5 4.0 %product.5 = f32[8,128,256]{2,1,0:T(8,128)S(1)} custom-call(s32[8]{0:T(128)S(1)} %broadcast_xor_fusion.2.table_ref, bf16[128,384]{1,0:T(8,128)(2,1)S(1)} %multiply_convert_fusion.3.refs_0_, bf16[128,384]{1,0:T(8,128)(2,1)S(1)} %multiply_convert_fusion.2.refs_1_, bf16[128,384]{1,0:T(8,128)(2,1)S(1)} %multiply_convert_fusion.1.refs_2_, ...), custom_call_target="tpu_custom_call" | custom-call | flops 872415232 | bytes 7864320 | tf_op jit(solution)/shard_map/product/pallas_call | solution.py:105
  74.4 0.1 collective-permute-start.16
  74.5 4.0 %product.7 = f32[8,128,256]{2,1,0:T(8,128)S(1)} custom-call(s32[8]{0:T(128)S(1)} %broadcast_xor_fusion.table_ref, bf16[128,384]{1,0:T(8,128)(2,1)S(1)} %multiply_convert_fusion.3.refs_0_, bf16[128,384]{1,0:T(8,128)(2,1)S(1)} %multiply_convert_fusion.2.refs_1_, bf16[128,384]{1,0:T(8,128)(2,1)S(1)} %multiply_convert_fusion.1.refs_2_, ...), custom_call_target="tpu_custom_call" | custom-call | flops 872415232 | bytes 7864320 | tf_op jit(solution)/shard_map/product/pallas_call | solution.py:105
  78.5 0.5 collective-permute-start.20
  79.1 4.0 %product.4 = f32[8,128,256]{2,1,0:T(8,128)S(1)} custom-call(s32[8]{0:T(128)S(1)} %get-tuple-element.6.table_ref, bf16[128,384]{1,0:T(8,128)(2,1)S(1)} %multiply_convert_fusion.3.refs_0_, bf16[128,384]{1,0:T(8,128)(2,1)S(1)} %multiply_convert_fusion.2.refs_1_, bf16[128,384]{1,0:T(8,128)(2,1)S(1)} %multiply_convert_fusion.1.refs_2_, ...), custom_call_target="tpu_custom_call" | custom-call | flops 872415232 | bytes 7864320 | tf_op jit(solution)/shard_map/product/pallas_call | solution.py:105
  83.1 0.1 add.88
  83.3 0.5 collective-permute-start.17
  83.9 8.8 %copy-done.1 = bf16[1664,8192]{1,0:T(8,128)(2,1)S(1)} copy-done((bf16[1664,8192]{1,0:T(8,128)(2,1)S(1)}, bf16[1664,8192]{1,0:T(8,128)(2,1)}, u32[]{:S(2)}) %copy-start.1) | copy-done | bytes 27263000
  92.6 4.0 %product.6 = f32[8,128,256]{2,1,0:T(8,128)S(1)} custom-call(s32[8]{0:T(128)S(1)} %get-tuple-element.5.table_ref, bf16[128,384]{1,0:T(8,128)(2,1)S(1)} %multiply_convert_fusion.3.refs_0_, bf16[128,384]{1,0:T(8,128)(2,1)S(1)} %multiply_convert_fusion.2.refs_1_, bf16[128,384]{1,0:T(8,128)(2,1)S(1)} %multiply_convert_fusion.1.refs_2_, ...), custom_call_target="tpu_custom_call" | custom-call | flops 872415232 | bytes 7864320 | tf_op jit(solution)/shard_map/product/pallas_call | solution.py:105
  96.6 0.0 collective-permute-done.20
  96.6 0.1 add.92
  96.8 0.1 collective-permute-start.21
  96.9 0.4 collective-permute-done.17
  97.2 0.1 slice_add_fusion.1
  97.3 1.7 %collective-permute-start.18 = (f32[2,128,256]{2,1,0:T(8,128)S(1)}, f32[2,128,256]{2,1,0:T(8,128)S(1)}, u32[]{:S(2)}, u32[]{:S(2)}) collective-permute-start(f32[2,128,256]{2,1,0:T(8,128)S(1)} %slice.51), channel_id=1, source_target_pairs={{0,4},{1,5},{2,6},{3,7},{4,0},{5,1},{6,2},{7,3},{8,12},{9,13},{10,... | collective-permute-start | bytes 786440 | tf_op jit(solution)/shard_map/ppermute | solution.py:142
  99.1 12.6 %collective-permute-done.21 = f32[4,128,256]{2,1,0:T(8,128)S(1)} collective-permute-done((f32[4,128,256]{2,1,0:T(8,128)S(1)}, f32[4,128,256]{2,1,0:T(8,128)S(1)}, u32[]{:S(2)}, u32[]{:S(2)}) %collective-permute-start.21) | collective-permute-done | bytes 524320 | tf_op jit(solution)/shard_map/ppermute | solution.py:142
  111.7 0.1 slice_add_fusion
  111.8 1.6 %collective-permute-start.22 = (f32[2,128,256]{2,1,0:T(8,128)S(1)}, f32[2,128,256]{2,1,0:T(8,128)S(1)}, u32[]{:S(2)}, u32[]{:S(2)}) collective-permute-start(f32[2,128,256]{2,1,0:T(8,128)S(1)} %slice.57), channel_id=1, source_target_pairs={{0,2},{1,3},{2,0},{3,1},{4,6},{5,7},{6,4},{7,5},{8,10},{9,11},{10,... | collective-permute-start | bytes 786440 | tf_op jit(solution)/shard_map/ppermute | solution.py:142
  113.4 2.7 %collective-permute-done.18 = f32[2,128,256]{2,1,0:T(8,128)S(1)} collective-permute-done((f32[2,128,256]{2,1,0:T(8,128)S(1)}, f32[2,128,256]{2,1,0:T(8,128)S(1)}, u32[]{:S(2)}, u32[]{:S(2)}) %collective-permute-start.18) | collective-permute-done | bytes 262176 | tf_op jit(solution)/shard_map/ppermute | solution.py:142
  116.1 1.1 collective-permute-start.19
  117.2 1.0 collective-permute-done.22
  118.3 1.0 collective-permute-start.23
  119.2 8.2 %collective-permute-done.19 = f32[1,128,256]{2,1,0:T(8,128)S(1)} collective-permute-done((f32[1,128,256]{2,1,0:T(8,128)S(1)}, f32[1,128,256]{2,1,0:T(8,128)S(1)}, u32[]{:S(2)}, u32[]{:S(2)}) %collective-permute-start.19) | collective-permute-done | bytes 131104 | tf_op jit(solution)/shard_map/ppermute | solution.py:142
  127.5 2.3 %collective-permute-done.23 = f32[1,128,256]{2,1,0:T(8,128)S(1)} collective-permute-done((f32[1,128,256]{2,1,0:T(8,128)S(1)}, f32[1,128,256]{2,1,0:T(8,128)S(1)}, u32[]{:S(2)}, u32[]{:S(2)}) %collective-permute-start.23) | collective-permute-done | bytes 131104 | tf_op jit(solution)/shard_map/ppermute | solution.py:142
  129.8 0.7 pad_maximum_fusion
  (40 shorter events, 0.7 us)
Async XLA Ops:
  0.0 74.5 %copy-start.6 = (s32[8]{0:T(128)S(1)}, s32[8]{0:T(128)}, u32[]{:S(2)}) copy-start(s32[8]{0:T(128)} %constant.47.clone) | copy-start | bytes 100
  0.0 1.0 copy-start.2
  1.0 0.7 copy-start.3
  3.0 25.8 %collective-permute-start.12 = (f32[128,512]{1,0:T(8,128)S(1)}, f32[128,512]{1,0:T(8,128)S(1)}, u32[]{:S(2)}, u32[]{:S(2)}) collective-permute-start(f32[128,512]{1,0:T(8,128)S(1)} %mix.7), channel_id=1, source_target_pairs={{0,2},{1,3},{2,0},{3,1},{4,6},{5,7},{6,4},{7,5},{8,10},{9,11},{10,... | collective-permute-start | bytes 786440 | tf_op jit(solution)/shard_map/ppermute | solution.py:142
  7.2 7.4 %collective-permute-start.8 = (f32[128,384]{1,0:T(8,128)S(1)}, f32[128,384]{1,0:T(8,128)S(1)}, u32[]{:S(2)}, u32[]{:S(2)}) collective-permute-start(f32[128,384]{1,0:T(8,128)S(1)} %mix.6), channel_id=1, source_target_pairs={{0,4},{1,5},{2,6},{3,7},{4,0},{5,1},{6,2},{7,3},{8,12},{9,13},{10,... | collective-permute-start | bytes 589832 | tf_op jit(solution)/shard_map/ppermute | solution.py:142
  10.0 4.9 %collective-permute-start.4 = (f32[128,384]{1,0:T(8,128)S(1)}, f32[128,384]{1,0:T(8,128)S(1)}, u32[]{:S(2)}, u32[]{:S(2)}) collective-permute-start(f32[128,384]{1,0:T(8,128)S(1)} %mix.5), channel_id=1, source_target_pairs={{0,1},{1,0},{2,3},{3,2},{4,5},{5,4},{6,7},{7,6},{8,9},{9,8},{10,11... | collective-permute-start | bytes 589832 | tf_op jit(solution)/shard_map/ppermute | solution.py:142
  11.3 16.9 %collective-permute-start = (f32[128,384]{1,0:T(8,128)S(1)}, f32[128,384]{1,0:T(8,128)S(1)}, u32[]{:S(2)}, u32[]{:S(2)}) collective-permute-start(f32[128,384]{1,0:T(8,128)S(1)} %mix.4), channel_id=1, source_target_pairs={{0,8},{1,9},{2,10},{3,11},{4,12},{5,13},{6,14},{7,15},{8,0},{9,1},... | collective-permute-start | bytes 589832 | tf_op jit(solution)/shard_map/ppermute | solution.py:142
  14.6 14.3 %collective-permute-start.9 = (f32[128,384]{1,0:T(8,128)S(1)}, f32[128,384]{1,0:T(8,128)S(1)}, u32[]{:S(2)}, u32[]{:S(2)}) collective-permute-start(f32[128,384]{1,0:T(8,128)S(1)} %multiply_add_fusion.5), channel_id=1, source_target_pairs={{0,1},{1,0},{2,3},{3,2},{4,5},{5,4},{6,7},{7,6},{8,9},{9,8},{10,11... | collective-permute-start | bytes 589832 | tf_op jit(solution)/shard_map/ppermute | solution.py:142
  14.9 17.6 %collective-permute-start.5 = (f32[128,384]{1,0:T(8,128)S(1)}, f32[128,384]{1,0:T(8,128)S(1)}, u32[]{:S(2)}, u32[]{:S(2)}) collective-permute-start(f32[128,384]{1,0:T(8,128)S(1)} %multiply_add_fusion.8), channel_id=1, source_target_pairs={{0,8},{1,9},{2,10},{3,11},{4,12},{5,13},{6,14},{7,15},{8,0},{9,1},... | collective-permute-start | bytes 589832 | tf_op jit(solution)/shard_map/ppermute | solution.py:142
  28.2 6.5 %collective-permute-start.1 = (f32[128,384]{1,0:T(8,128)S(1)}, f32[128,384]{1,0:T(8,128)S(1)}, u32[]{:S(2)}, u32[]{:S(2)}) collective-permute-start(f32[128,384]{1,0:T(8,128)S(1)} %multiply_add_fusion.11), channel_id=1, source_target_pairs={{0,2},{1,3},{2,0},{3,1},{4,6},{5,7},{6,4},{7,5},{8,10},{9,11},{10,... | collective-permute-start | bytes 589832 | tf_op jit(solution)/shard_map/ppermute | solution.py:142
  28.8 13.3 %collective-permute-start.13 = (f32[128,512]{1,0:T(8,128)S(1)}, f32[128,512]{1,0:T(8,128)S(1)}, u32[]{:S(2)}, u32[]{:S(2)}) collective-permute-start(f32[128,512]{1,0:T(8,128)S(1)} %multiply_add_fusion.2), channel_id=1, source_target_pairs={{0,4},{1,5},{2,6},{3,7},{4,0},{5,1},{6,2},{7,3},{8,12},{9,13},{10,... | collective-permute-start | bytes 786440 | tf_op jit(solution)/shard_map/ppermute | solution.py:142
  28.9 13.3 %collective-permute-start.10 = (f32[128,384]{1,0:T(8,128)S(1)}, f32[128,384]{1,0:T(8,128)S(1)}, u32[]{:S(2)}, u32[]{:S(2)}) collective-permute-start(f32[128,384]{1,0:T(8,128)S(1)} %multiply_add_fusion.4), channel_id=1, source_target_pairs={{0,8},{1,9},{2,10},{3,11},{4,12},{5,13},{6,14},{7,15},{8,0},{9,1},... | collective-permute-start | bytes 589832 | tf_op jit(solution)/shard_map/ppermute | solution.py:142
  32.5 11.1 %collective-permute-start.6 = (f32[128,384]{1,0:T(8,128)S(1)}, f32[128,384]{1,0:T(8,128)S(1)}, u32[]{:S(2)}, u32[]{:S(2)}) collective-permute-start(f32[128,384]{1,0:T(8,128)S(1)} %multiply_add_fusion.7), channel_id=1, source_target_pairs={{0,2},{1,3},{2,0},{3,1},{4,6},{5,7},{6,4},{7,5},{8,10},{9,11},{10,... | collective-permute-start | bytes 589832 | tf_op jit(solution)/shard_map/ppermute | solution.py:142
  34.8 11.5 %collective-permute-start.2 = (f32[128,384]{1,0:T(8,128)S(1)}, f32[128,384]{1,0:T(8,128)S(1)}, u32[]{:S(2)}, u32[]{:S(2)}) collective-permute-start(f32[128,384]{1,0:T(8,128)S(1)} %multiply_add_fusion.10), channel_id=1, source_target_pairs={{0,4},{1,5},{2,6},{3,7},{4,0},{5,1},{6,2},{7,3},{8,12},{9,13},{10,... | collective-permute-start | bytes 589832 | tf_op jit(solution)/shard_map/ppermute | solution.py:142
  42.1 4.2 %collective-permute-start.14 = (f32[128,512]{1,0:T(8,128)S(1)}, f32[128,512]{1,0:T(8,128)S(1)}, u32[]{:S(2)}, u32[]{:S(2)}) collective-permute-start(f32[128,512]{1,0:T(8,128)S(1)} %multiply_add_fusion.1), channel_id=1, source_target_pairs={{0,1},{1,0},{2,3},{3,2},{4,5},{5,4},{6,7},{7,6},{8,9},{9,8},{10,11... | collective-permute-start | bytes 786440 | tf_op jit(solution)/shard_map/ppermute | solution.py:142
  42.3 7.4 %collective-permute-start.11 = (f32[128,384]{1,0:T(8,128)S(1)}, f32[128,384]{1,0:T(8,128)S(1)}, u32[]{:S(2)}, u32[]{:S(2)}) collective-permute-start(f32[128,384]{1,0:T(8,128)S(1)} %multiply_add_fusion.3), channel_id=1, source_target_pairs={{0,2},{1,3},{2,0},{3,1},{4,6},{5,7},{6,4},{7,5},{8,10},{9,11},{10,... | collective-permute-start | bytes 589832 | tf_op jit(solution)/shard_map/ppermute | solution.py:142
  43.6 7.5 %collective-permute-start.7 = (f32[128,384]{1,0:T(8,128)S(1)}, f32[128,384]{1,0:T(8,128)S(1)}, u32[]{:S(2)}, u32[]{:S(2)}) collective-permute-start(f32[128,384]{1,0:T(8,128)S(1)} %multiply_add_fusion.6), channel_id=1, source_target_pairs={{0,4},{1,5},{2,6},{3,7},{4,0},{5,1},{6,2},{7,3},{8,12},{9,13},{10,... | collective-permute-start | bytes 589832 | tf_op jit(solution)/shard_map/ppermute | solution.py:142
  46.2 4.9 %collective-permute-start.3 = (f32[128,384]{1,0:T(8,128)S(1)}, f32[128,384]{1,0:T(8,128)S(1)}, u32[]{:S(2)}, u32[]{:S(2)}) collective-permute-start(f32[128,384]{1,0:T(8,128)S(1)} %multiply_add_fusion.9), channel_id=1, source_target_pairs={{0,1},{1,0},{2,3},{3,2},{4,5},{5,4},{6,7},{7,6},{8,9},{9,8},{10,11... | collective-permute-start | bytes 589832 | tf_op jit(solution)/shard_map/ppermute | solution.py:142
  46.4 15.3 %collective-permute-start.15 = (f32[128,512]{1,0:T(8,128)S(1)}, f32[128,512]{1,0:T(8,128)S(1)}, u32[]{:S(2)}, u32[]{:S(2)}) collective-permute-start(f32[128,512]{1,0:T(8,128)S(1)} %multiply_add_fusion), channel_id=1, source_target_pairs={{0,8},{1,9},{2,10},{3,11},{4,12},{5,13},{6,14},{7,15},{8,0},{9,1},... | collective-permute-start | bytes 786440 | tf_op jit(solution)/shard_map/ppermute | solution.py:142
  61.7 8.8 %copy-start = (bf16[1664,8192]{1,0:T(8,128)(2,1)S(1)}, bf16[1664,8192]{1,0:T(8,128)(2,1)}, u32[]{:S(2)}) copy-start(bf16[1664,8192]{1,0:T(8,128)(2,1)} %refs_4_.7) | copy-start | bytes 81788928
  70.5 8.6 %copy-start.4 = (s32[8]{0:T(128)S(1)}, s32[8]{0:T(128)}, u32[]{:S(2)}) copy-start(s32[8]{0:T(128)} %constant.46.clone) | copy-start | bytes 100
  70.5 8.6 %copy-start.5 = (s32[8]{0:T(128)S(1)}, s32[8]{0:T(128)}, u32[]{:S(2)}) copy-start(s32[8]{0:T(128)} %constant.48.clone) | copy-start | bytes 100
  74.4 8.7 %collective-permute-start.16 = (f32[8,128,256]{2,1,0:T(8,128)S(1)}, f32[8,128,256]{2,1,0:T(8,128)S(1)}, u32[]{:S(2)}, u32[]{:S(2)}) collective-permute-start(f32[8,128,256]{2,1,0:T(8,128)S(1)} %product.5), channel_id=1, source_target_pairs={{0,1},{1,0},{2,3},{3,2},{4,5},{5,4},{6,7},{7,6},{8,9},{9,8},{10,11... | collective-permute-start | bytes 3145736 | tf_op jit(solution)/shard_map/ppermute | solution.py:142
  78.5 18.1 %collective-permute-start.20 = (f32[8,128,256]{2,1,0:T(8,128)S(1)}, f32[8,128,256]{2,1,0:T(8,128)S(1)}, u32[]{:S(2)}, u32[]{:S(2)}) collective-permute-start(f32[8,128,256]{2,1,0:T(8,128)S(1)} %product.7), channel_id=1, source_target_pairs={{0,1},{1,0},{2,3},{3,2},{4,5},{5,4},{6,7},{7,6},{8,9},{9,8},{10,11... | collective-permute-start | bytes 3145736 | tf_op jit(solution)/shard_map/ppermute | solution.py:142
  83.3 13.9 %collective-permute-start.17 = (f32[4,128,256]{2,1,0:T(8,128)S(1)}, f32[4,128,256]{2,1,0:T(8,128)S(1)}, u32[]{:S(2)}, u32[]{:S(2)}) collective-permute-start(f32[4,128,256]{2,1,0:T(8,128)S(1)} %slice.49), channel_id=1, source_target_pairs={{0,2},{1,3},{2,0},{3,1},{4,6},{5,7},{6,4},{7,5},{8,10},{9,11},{10,... | collective-permute-start | bytes 1572872 | tf_op jit(solution)/shard_map/ppermute | solution.py:142
  83.8 8.8 %copy-start.1 = (bf16[1664,8192]{1,0:T(8,128)(2,1)S(1)}, bf16[1664,8192]{1,0:T(8,128)(2,1)}, u32[]{:S(2)}) copy-start(bf16[1664,8192]{1,0:T(8,128)(2,1)} %refs_4_.7) | copy-start | bytes 81788928
  96.8 14.9 %collective-permute-start.21 = (f32[4,128,256]{2,1,0:T(8,128)S(1)}, f32[4,128,256]{2,1,0:T(8,128)S(1)}, u32[]{:S(2)}, u32[]{:S(2)}) collective-permute-start(f32[4,128,256]{2,1,0:T(8,128)S(1)} %slice.55), channel_id=1, source_target_pairs={{0,4},{1,5},{2,6},{3,7},{4,0},{5,1},{6,2},{7,3},{8,12},{9,13},{10,... | collective-permute-start | bytes 1572872 | tf_op jit(solution)/shard_map/ppermute | solution.py:142
  97.3 18.7 %collective-permute-start.18 = (f32[2,128,256]{2,1,0:T(8,128)S(1)}, f32[2,128,256]{2,1,0:T(8,128)S(1)}, u32[]{:S(2)}, u32[]{:S(2)}) collective-permute-start(f32[2,128,256]{2,1,0:T(8,128)S(1)} %slice.51), channel_id=1, source_target_pairs={{0,4},{1,5},{2,6},{3,7},{4,0},{5,1},{6,2},{7,3},{8,12},{9,13},{10,... | collective-permute-start | bytes 786440 | tf_op jit(solution)/shard_map/ppermute | solution.py:142
  111.8 6.4 %collective-permute-start.22 = (f32[2,128,256]{2,1,0:T(8,128)S(1)}, f32[2,128,256]{2,1,0:T(8,128)S(1)}, u32[]{:S(2)}, u32[]{:S(2)}) collective-permute-start(f32[2,128,256]{2,1,0:T(8,128)S(1)} %slice.57), channel_id=1, source_target_pairs={{0,2},{1,3},{2,0},{3,1},{4,6},{5,7},{6,4},{7,5},{8,10},{9,11},{10,... | collective-permute-start | bytes 786440 | tf_op jit(solution)/shard_map/ppermute | solution.py:142
  116.1 11.3 %collective-permute-start.19 = (f32[1,128,256]{2,1,0:T(8,128)S(1)}, f32[1,128,256]{2,1,0:T(8,128)S(1)}, u32[]{:S(2)}, u32[]{:S(2)}) collective-permute-start(f32[1,128,256]{2,1,0:T(8,128)S(1)} %slice.53), channel_id=1, source_target_pairs={{0,8},{1,9},{2,10},{3,11},{4,12},{5,13},{6,14},{7,15},{8,0},{9,1},... | collective-permute-start | bytes 393224 | tf_op jit(solution)/shard_map/ppermute | solution.py:142
  118.3 11.5 %collective-permute-start.23 = (f32[1,128,256]{2,1,0:T(8,128)S(1)}, f32[1,128,256]{2,1,0:T(8,128)S(1)}, u32[]{:S(2)}, u32[]{:S(2)}) collective-permute-start(f32[1,128,256]{2,1,0:T(8,128)S(1)} %slice.59), channel_id=1, source_target_pairs={{0,8},{1,9},{2,10},{3,11},{4,12},{5,13},{6,14},{7,15},{8,0},{9,1},... | collective-permute-start | bytes 393224 | tf_op jit(solution)/shard_map/ppermute | solution.py:142

commit v2 on v1

v2 whole, which is shorter than its diff:
```python
import functools

import jax
import jax.numpy as jnp
import numpy as np
from jax import lax
from jax.experimental import pallas as pl
from jax.experimental.pallas import tpu as pltpu
from jax.sharding import PartitionSpec as P

LANES = 128
F32 = jnp.float32
BF16 = jnp.bfloat16


def quotient(index, divisor, limit):
    shift = 16
    scale = -(-(1 << shift) // divisor)
    numbers = np.arange(limit, dtype=np.int64)
    assert np.array_equal((numbers * scale) >> shift, numbers // divisor)
    assert limit * scale < 2**31
    return (index * scale) >> shift


def sign_of(common, count):
    parity = common
    for place in range(1, count):
        parity = parity ^ (common >> place)
    return (1 - 2 * (parity & 1)).astype(F32)


def mix_kernel(start, group, activations, small, *refs):
    out = refs[-1]
    tokens, local = activations.shape
    block = small.shape[0]
    cols = out.shape[1]
    rows = group * block
    span = local // block
    low = group.bit_length() - 1
    high = span.bit_length() - 1 - low
    full = small[...]
    head = full.astype(BF16)
    tail = (full - head.astype(F32)).astype(BF16)

    row = lax.broadcasted_iota(jnp.int32, (rows, block), 0)
    unit = lax.broadcasted_iota(jnp.int32, (rows, block), 1)
    spread_rows = (row - quotient(row, block, rows) * block == unit).astype(F32).astype(BF16)
    col = lax.broadcasted_iota(jnp.int32, (block, cols), 1) + start
    unit = lax.broadcasted_iota(jnp.int32, (block, cols), 0)
    spread_cols = (col - quotient(col, block, local) * block == unit).astype(F32).astype(BF16)
    at_row = quotient(lax.broadcasted_iota(jnp.int32, (rows, cols), 0), block, rows)
    at_col = quotient(lax.broadcasted_iota(jnp.int32, (rows, cols), 1) + start, block, local)
    sign = sign_of(at_row & at_col, max(low, 1))

    def tiled(part):
        tall = jnp.dot(spread_rows, part, preferred_element_type=F32).astype(BF16)
        return (jnp.dot(tall, spread_cols, preferred_element_type=F32) * sign).astype(BF16)

    head, tail = tiled(head), tiled(tail)
    owner = quotient(lax.broadcasted_iota(jnp.int32, (8, cols), 1) + start, block, local) >> low
    total = jnp.zeros((tokens, cols), F32)
    for piece in range(span // group):
        values = activations[:, piece * rows:(piece + 1) * rows]
        term = jnp.dot(values, head, preferred_element_type=F32)
        term = term + jnp.dot(values, tail, preferred_element_type=F32)
        total = total + term * sign_of(owner & piece, max(high, 1))[0:1]
    out[...] = total


VMEM = pl.BlockSpec(memory_space=pltpu.VMEM)
SMEM = pl.BlockSpec(memory_space=pltpu.SMEM)
UNREAD = pl.BlockSpec(memory_space=pl.ANY)
PARAMS = pltpu.CompilerParams(vmem_limit_bytes=24 * 2**20)


def mix(activations, small, start, cols, after):
    tokens, local = activations.shape
    block = small.shape[0]
    group = min(4, local // block)
    return pl.pallas_call(
        functools.partial(mix_kernel, start, group),
        out_shape=jax.ShapeDtypeStruct((tokens, cols), F32),
        in_specs=[VMEM] * 2 + [UNREAD] * len(after),
        out_specs=VMEM,
        cost_estimate=pl.CostEstimate(
            flops=4 * tokens * local * cols, bytes_accessed=tokens * (2 * local + 4 * cols), transcendentals=0
        ),
        compiler_params=PARAMS,
        name="mix",
    )(activations, small, *after)


def fold(me, own, got, bit, after, factor=None):
    sign = jnp.where((me[0] & bit) != 0, -1.0, 1.0).astype(F32)
    if after:
        own, *_ = lax.optimization_barrier((own, *after))
    total = got + sign * own
    return total if factor is None else (total * factor).astype(BF16)


def product(chunks, weight, me, edges, distances, width, part, parts, after):
    tokens = chunks[0].shape[0]
    local = weight.shape[0]
    blocks = len(distances)
    count = len(chunks)
    slots = min(3, blocks)

    def kernel(me_ref, *refs):
        chunk_refs, weight_ref = refs[:count], refs[count]
        out, left, held, sems = refs[-4:]

        def fetch(i):
            column = pl.multiple_of(((distances[i] ^ me_ref[0]) * parts + part) * width, LANES)
            return pltpu.make_async_copy(
                weight_ref.at[:, pl.ds(column, width)], held.at[i % slots], sems.at[i % slots]
            )

        for i in range(slots):
            fetch(i).start()
        for ref, begin, end in zip(chunk_refs, edges[:-1], edges[1:]):
            left[:, begin:end] = ref[...]
        for i in range(blocks):
            fetch(i).wait()
            out[i] = jnp.dot(left[...], held[i % slots], preferred_element_type=F32)
            if i + slots < blocks:
                fetch(i + slots).start()

    return pl.pallas_call(
        kernel,
        out_shape=jax.ShapeDtypeStruct((blocks, tokens, width), F32),
        in_specs=[SMEM] + [VMEM] * count + [pl.BlockSpec(memory_space=pltpu.HBM)] + [UNREAD] * len(after),
        out_specs=VMEM,
        scratch_shapes=[
            pltpu.VMEM((tokens, local), BF16),
            pltpu.VMEM((slots, local, width), BF16),
            pltpu.SemaphoreType.DMA((slots,)),
        ],
        cost_estimate=pl.CostEstimate(
            flops=2 * tokens * local * width * blocks,
            bytes_accessed=blocks * width * (2 * local + 4 * tokens),
            transcendentals=0,
        ),
        compiler_params=pltpu.CompilerParams(vmem_limit_bytes=44 * 2**20),
        name="product",
    )(me, *chunks, weight, *after)


def halve(own, got, distances, plans, after):
    width = own.shape[2]
    shapes = []
    for rows, bit in plans:
        shapes += [jax.ShapeDtypeStruct((len(distances) // 2, rows[1] - rows[0], width), F32)] * 2

    def kernel(own_ref, got_ref, *refs):
        outs = refs[-len(shapes):]
        for at, ((begin, end), bit) in enumerate(plans):
            kept = [d for d in distances if not d & bit]
            for place, d in enumerate(kept):
                for out, source in ((outs[2 * at], d), (outs[2 * at + 1], d | bit)):
                    i = distances.index(source)
                    out[place] = own_ref[i, begin:end, :] + got_ref[i, begin:end, :]

    return pl.pallas_call(
        kernel,
        out_shape=shapes,
        in_specs=[VMEM] * 2 + [UNREAD] * len(after),
        out_specs=[VMEM] * len(shapes),
        cost_estimate=pl.CostEstimate(flops=own.size, bytes_accessed=12 * own.size, transcendentals=0),
        compiler_params=PARAMS,
        name="halve",
    )(own, got, *after)


def finish(pieces, tokens, width, parts):
    flat = [x for _, _, own, got in pieces for x in (own, got)]

    def kernel(*refs):
        out = refs[-1]
        for at, (part, (begin, end), _, _) in enumerate(pieces):
            total = refs[2 * at][0] + refs[2 * at + 1][0]
            out[begin:end, part * width:(part + 1) * width] = total.astype(BF16)

    return pl.pallas_call(
        kernel,
        out_shape=jax.ShapeDtypeStruct((tokens, width * parts), BF16),
        in_specs=[VMEM] * len(flat),
        out_specs=VMEM,
        compiler_params=PARAMS,
        name="finish",
    )(*flat)


def body(activations, rotation_small, down_weight):
    shards = lax.axis_size("tensor")
    me = lax.axis_index("tensor").astype(jnp.int32).reshape(1)
    tokens, local = activations.shape
    block = rotation_small.shape[0]
    features = down_weight.shape[1]
    factor = (local // block * shards) ** (-0.5)
    bits = [1 << place for place in range(shards.bit_length() - 1)]
    assert len(bits) >= 2 and shards == 1 << len(bits)

    def swap(x, bit):
        return lax.ppermute(x, "tensor", [(d, d ^ bit) for d in range(shards)])

    tiles = -(-local // LANES)
    count = max(1, min(len(bits), tiles))
    edges = [min(local, (tiles * c // count) * LANES) for c in range(count)] + [local]
    chunks = []
    for begin, end in zip(edges[:-1], edges[1:]):
        chunks.append(mix(activations, rotation_small, begin, end - begin, chunks[-1:]))
    cycle = bits[-1:] + bits[1:-1] + bits[:1]
    events = []
    for phase in range(len(bits)):
        for c in range(count):
            bit = cycle[(phase - c) % len(bits)]
            events.append((phase, bit, c))
    after = []
    for phase, bit, c in sorted(events):
        got = swap(chunks[c], bit)
        chunks[c] = fold(me, chunks[c], got, bit, after, factor if phase == len(bits) - 1 else None)
        after = [chunks[c]]

    share = features // shards
    parts = 2 if share % (2 * LANES) == 0 else 1
    width = share // parts
    order = list(bits)
    twisted = list(bits)
    if len(bits) > 2:
        twisted[1], twisted[2] = twisted[2], twisted[1]
    near = [d for d in range(shards) if not d & bits[0]]
    sends, keeps = [], []
    after = []
    for part in range(parts):
        for found, distances in ((sends, [d | bits[0] for d in near]), (keeps, near)):
            found.append(product(chunks, down_weight, me, edges, distances, width, part, parts, after))
            after = [found[-1]]
    half = tokens // 2
    whole = (0, tokens)
    routes = [[(whole, order)], [((0, half), order), ((half, tokens), twisted)]][-parts:]
    live = []
    for part in range(parts):
        got = swap(sends[part], bits[0])
        plans = [(rows, route[1]) for rows, route in routes[part]]
        outs = halve(keeps[part], got, near, plans, after)
        after = outs[-1:]
        for at, (rows, route) in enumerate(routes[part]):
            live.append((part, rows, route, [d for d in near if not d & route[1]], outs[2 * at], outs[2 * at + 1]))
    live = live[:1] + live[:0:-1]
    for step in range(1, len(bits) - 1):
        later = []
        for part, rows, route, distances, keep, send in live:
            got = swap(send, route[step])
            bit = route[step + 1]
            outs = halve(keep, got, distances, [((0, rows[1] - rows[0]), bit)], after)
            after = outs[-1:]
            later.append((part, rows, route, [d for d in distances if not d & bit], outs[0], outs[1]))
        live = later
    pieces = [(part, rows, keep, swap(send, route[-1])) for part, rows, route, _, keep, send in live]
    return finish(pieces, tokens, width, parts)


def solution(mesh):
    placed = (P("groups", "tensor"), P(), P("tensor", None))
    return jax.shard_map(
        body, mesh=mesh, in_specs=placed, out_specs=P("groups", "tensor"), check_vma=False
    )
```

time: 131 us -> 119 us (0.908)
  local copies, waits for them, and re-layouts: 19.4 us -> 1.75 us
  Pallas kernels: 20.7 us -> 25.2 us
  starting transfers between devices: 25.1 us -> 28.8 us
  other arithmetic: 2.3 us -> 0.44 us
    unnamed x14 -> x4, local copies, waits for them, and re-layouts: 19.3 us -> 1.75 us
    pallas_call x4 -> x13, Pallas kernels: 15.9 us -> 20.4 us  [the longest x4 19.3 us: product(): pl.pallas_call(kernel, out_shape=jax.ShapeDtypeStruct((blocks, tokens, wi...]
    ppermute x24 -> x27, starting transfers between devices: 25.1 us -> 28.8 us  [swap(): return lax.ppermute(x, 'tensor', [(d, d ^ bit) for d in range(shards)])]
    ppermute x24 -> x27, waiting for transfers between devices: 62.6 us -> 62.2 us  [swap(): return lax.ppermute(x, 'tensor', [(d, d ^ bit) for d in range(shards)])]
  transfers between devices with their start and end apart: 24 -> 27, of which waited for: 14 -> 17; matrix products, arithmetic and copies ran while one was open for 1% -> 0% of each run, Pallas kernels for 12% -> 15%
where the time goes in v2:
time: 119 us
  waiting for transfers between devices  62.2 us (52%)
  starting transfers between devices  28.8 us (24%)
  Pallas kernels  25.2 us (21%)
  local copies, waits for them, and re-layouts  1.75 us (1%)
    ppermute x27, waiting for transfers between devices, swap(): return lax.ppermute(x, 'tensor', [(d, d ^ bit) for d in range(shards)])  62.2 us
    ppermute x27, starting transfers between devices, swap(): return lax.ppermute(x, 'tensor', [(d, d ^ bit) for d in range(shards)])  28.8 us
    pallas_call x4, Pallas kernels, product(): pl.pallas_call(kernel, out_shape=jax.ShapeDtypeStruct((blocks, tokens, wi...  19.3 us
    pallas_call x4, Pallas kernels, mix(): pl.pallas_call(functools.partial(mix_kernel, start, group), out_shape=jax...  4.73 us
  transfers between devices with their start and end apart: 27, of which 17 were waited for; matrix products, arithmetic and copies ran while one was open for 0% of the time, Pallas kernels for 15%

profile of v2, /device:TPU:0, one launch (start us, length us, event | category | flops | bytes accessed | tf_op | source)
XLA Modules:
  0.0 118.6 jit_solution(12573780645659631020)
XLA Ops:
  0.0 1.0 copy-done
  1.0 0.7 copy-done.1
  1.8 1.2 mix.4.refs_0_
  2.9 1.2 mix.5.refs_0_
  4.1 0.5 collective-permute-start.3
  4.7 1.2 mix.6.refs_0_
  5.9 1.2 mix.7
  7.0 2.6 %collective-permute-start.2 = (f32[128,512]{1,0:T(8,128)S(1)}, f32[128,512]{1,0:T(8,128)S(1)}, u32[]{:S(2)}, u32[]{:S(2)}) collective-permute-start(f32[128,512]{1,0:T(8,128)S(1)} %mix.7), channel_id=1, source_target_pairs={{0,2},{1,3},{2,0},{3,1},{4,6},{5,7},{6,4},{7,5},{8,10},{9,11},{10,... | collective-permute-start | bytes 786440 | tf_op jit(solution)/shard_map/ppermute | solution.py:204
  9.6 2.6 %collective-permute-start = (f32[128,384]{1,0:T(8,128)S(1)}, f32[128,384]{1,0:T(8,128)S(1)}, u32[]{:S(2)}, u32[]{:S(2)}) collective-permute-start(f32[128,384]{1,0:T(8,128)S(1)} %mix.4.refs_0_), channel_id=1, source_target_pairs={{0,8},{1,9},{2,10},{3,11},{4,12},{5,13},{6,14},{7,15},{8,0},{9,1},... | collective-permute-start | bytes 589832 | tf_op jit(solution)/shard_map/ppermute | solution.py:204
  12.2 1.6 %collective-permute-start.1 = (f32[128,384]{1,0:T(8,128)S(1)}, f32[128,384]{1,0:T(8,128)S(1)}, u32[]{:S(2)}, u32[]{:S(2)}) collective-permute-start(f32[128,384]{1,0:T(8,128)S(1)} %mix.6.refs_0_), channel_id=1, source_target_pairs={{0,4},{1,5},{2,6},{3,7},{4,0},{5,1},{6,2},{7,3},{8,12},{9,13},{10,... | collective-permute-start | bytes 589832 | tf_op jit(solution)/shard_map/ppermute | solution.py:204
  13.8 0.0 collective-permute-done.3
  13.8 0.4 collective-permute-start.7
  14.2 2.4 %collective-permute-done.2 = f32[128,512]{1,0:T(8,128)S(1)} collective-permute-done((f32[128,512]{1,0:T(8,128)S(1)}, f32[128,512]{1,0:T(8,128)S(1)}, u32[]{:S(2)}, u32[]{:S(2)}) %collective-permute-start.2) | collective-permute-done | bytes 262176 | tf_op jit(solution)/shard_map/ppermute | solution.py:204
  16.6 6.0 %collective-permute-done.1 = f32[128,384]{1,0:T(8,128)S(1)} collective-permute-done((f32[128,384]{1,0:T(8,128)S(1)}, f32[128,384]{1,0:T(8,128)S(1)}, u32[]{:S(2)}, u32[]{:S(2)}) %collective-permute-start.1) | collective-permute-done | bytes 196640 | tf_op jit(solution)/shard_map/ppermute | solution.py:204
  22.6 0.1 collective-permute-start.5
  22.7 0.2 collective-permute-done
  23.0 0.4 collective-permute-start.4
  23.3 1.6 %collective-permute-start.8 = (f32[128,512]{1,0:T(8,128)S(1)}, f32[128,512]{1,0:T(8,128)S(1)}, u32[]{:S(2)}, u32[]{:S(2)}) collective-permute-start(f32[128,512]{1,0:T(8,128)S(1)} %multiply_add_fusion.2), channel_id=1, source_target_pairs={{0,4},{1,5},{2,6},{3,7},{4,0},{5,1},{6,2},{7,3},{8,12},{9,13},{10,... | collective-permute-start | bytes 786440 | tf_op jit(solution)/shard_map/ppermute | solution.py:204
  24.9 0.0 collective-permute-done.5
  25.0 5.1 %collective-permute-done.4 = f32[128,384]{1,0:T(8,128)S(1)} collective-permute-done((f32[128,384]{1,0:T(8,128)S(1)}, f32[128,384]{1,0:T(8,128)S(1)}, u32[]{:S(2)}, u32[]{:S(2)}) %collective-permute-start.4) | collective-permute-done | bytes 196640 | tf_op jit(solution)/shard_map/ppermute | solution.py:204
  30.1 4.7 %collective-permute-done.8 = f32[128,512]{1,0:T(8,128)S(1)} collective-permute-done((f32[128,512]{1,0:T(8,128)S(1)}, f32[128,512]{1,0:T(8,128)S(1)}, u32[]{:S(2)}, u32[]{:S(2)}) %collective-permute-start.8) | collective-permute-done | bytes 262176 | tf_op jit(solution)/shard_map/ppermute | solution.py:204
  34.9 0.1 collective-permute-start.10
  35.0 0.1 collective-permute-start.6
  35.0 4.2 %collective-permute-start.12 = (f32[128,384]{1,0:T(8,128)S(1)}, f32[128,384]{1,0:T(8,128)S(1)}, u32[]{:S(2)}, u32[]{:S(2)}) collective-permute-start(f32[128,384]{1,0:T(8,128)S(1)} %multiply_add_fusion.8), channel_id=1, source_target_pairs={{0,8},{1,9},{2,10},{3,11},{4,12},{5,13},{6,14},{7,15},{8,0},{9,1},... | collective-permute-start | bytes 589832 | tf_op jit(solution)/shard_map/ppermute | solution.py:204
  39.3 1.4 %collective-permute-start.9 = (f32[128,384]{1,0:T(8,128)S(1)}, f32[128,384]{1,0:T(8,128)S(1)}, u32[]{:S(2)}, u32[]{:S(2)}) collective-permute-start(f32[128,384]{1,0:T(8,128)S(1)} %multiply_add_fusion.6), channel_id=1, source_target_pairs={{0,2},{1,3},{2,0},{3,1},{4,6},{5,7},{6,4},{7,5},{8,10},{9,11},{10,... | collective-permute-start | bytes 589832 | tf_op jit(solution)/shard_map/ppermute | solution.py:204
  40.7 5.3 %collective-permute-done.9 = f32[128,384]{1,0:T(8,128)S(1)} collective-permute-done((f32[128,384]{1,0:T(8,128)S(1)}, f32[128,384]{1,0:T(8,128)S(1)}, u32[]{:S(2)}, u32[]{:S(2)}) %collective-permute-start.9) | collective-permute-done | bytes 196640 | tf_op jit(solution)/shard_map/ppermute | solution.py:204
  46.1 0.2 collective-permute-done.6
  46.3 0.1 collective-permute-start.11
  46.4 0.2 collective-permute-start.13
  46.5 2.2 %collective-permute-done.12 = f32[128,384]{1,0:T(8,128)S(1)} collective-permute-done((f32[128,384]{1,0:T(8,128)S(1)}, f32[128,384]{1,0:T(8,128)S(1)}, u32[]{:S(2)}, u32[]{:S(2)}) %collective-permute-start.12) | collective-permute-done | bytes 196640 | tf_op jit(solution)/shard_map/ppermute | solution.py:204
  48.8 1.4 %collective-permute-start.14 = (f32[128,384]{1,0:T(8,128)S(1)}, f32[128,384]{1,0:T(8,128)S(1)}, u32[]{:S(2)}, u32[]{:S(2)}) collective-permute-start(f32[128,384]{1,0:T(8,128)S(1)} %multiply_add_fusion.3), channel_id=1, source_target_pairs={{0,2},{1,3},{2,0},{3,1},{4,6},{5,7},{6,4},{7,5},{8,10},{9,11},{10,... | collective-permute-start | bytes 589832 | tf_op jit(solution)/shard_map/ppermute | solution.py:204
  50.1 0.0 collective-permute-done.11
  50.2 4.3 %collective-permute-done.14 = f32[128,384]{1,0:T(8,128)S(1)} collective-permute-done((f32[128,384]{1,0:T(8,128)S(1)}, f32[128,384]{1,0:T(8,128)S(1)}, u32[]{:S(2)}, u32[]{:S(2)}) %collective-permute-start.14) | collective-permute-done | bytes 196640 | tf_op jit(solution)/shard_map/ppermute | solution.py:204
  54.5 1.0 collective-permute-done.13
  55.5 7.4 %collective-permute-done.15 = f32[128,512]{1,0:T(8,128)S(1)} collective-permute-done((f32[128,512]{1,0:T(8,128)S(1)}, f32[128,512]{1,0:T(8,128)S(1)}, u32[]{:S(2)}, u32[]{:S(2)}) %collective-permute-start.15) | collective-permute-done | bytes 262176 | tf_op jit(solution)/shard_map/ppermute | solution.py:204
  62.9 4.8 %product.4.refs_5_ = f32[8,128,256]{2,1,0:T(8,128)S(1)} custom-call(s32[1]{0:T(128)} %bitcast.me_ref, bf16[128,384]{1,0:T(8,128)(2,1)S(1)} %multiply_convert_fusion.3.refs_0_, bf16[128,384]{1,0:T(8,128)(2,1)S(1)} %multiply_convert_fusion.1.refs_1_, bf16[128,384]{1,0:T(8,128)(2,1)S(1)} %multiply_convert_fusion.2.refs_2_, ...), custom_call_target="tpu_custom_call" | custom-call | flops 872415232 | bytes 7864320 | tf_op jit(solution)/shard_map/product/pallas_call | solution.py:128
  67.8 0.1 collective-permute-start.16
  67.9 4.8 %product.5.refs_5_.own_ref = f32[8,128,256]{2,1,0:T(8,128)S(1)} custom-call(s32[1]{0:T(128)} %bitcast.me_ref, bf16[128,384]{1,0:T(8,128)(2,1)S(1)} %multiply_convert_fusion.3.refs_0_, bf16[128,384]{1,0:T(8,128)(2,1)S(1)} %multiply_convert_fusion.1.refs_1_, bf16[128,384]{1,0:T(8,128)(2,1)S(1)} %multiply_convert_fusion.2.refs_2_, ...), custom_call_target="tpu_custom_call" | custom-call | flops 872415232 | bytes 7864320 | tf_op jit(solution)/shard_map/product/pallas_call | solution.py:128
  72.7 4.8 %product.6.refs_5_ = f32[8,128,256]{2,1,0:T(8,128)S(1)} custom-call(s32[1]{0:T(128)} %bitcast.me_ref, bf16[128,384]{1,0:T(8,128)(2,1)S(1)} %multiply_convert_fusion.3.refs_0_, bf16[128,384]{1,0:T(8,128)(2,1)S(1)} %multiply_convert_fusion.1.refs_1_, bf16[128,384]{1,0:T(8,128)(2,1)S(1)} %multiply_convert_fusion.2.refs_2_, ...), custom_call_target="tpu_custom_call" | custom-call | flops 872415232 | bytes 7864320 | tf_op jit(solution)/shard_map/product/pallas_call | solution.py:128
  77.6 0.6 collective-permute-start.18
  78.1 4.8 %product.7.refs_0_.own_ref = f32[8,128,256]{2,1,0:T(8,128)S(1)} custom-call(s32[1]{0:T(128)} %bitcast.me_ref, bf16[128,384]{1,0:T(8,128)(2,1)S(1)} %multiply_convert_fusion.3.refs_0_, bf16[128,384]{1,0:T(8,128)(2,1)S(1)} %multiply_convert_fusion.1.refs_1_, bf16[128,384]{1,0:T(8,128)(2,1)S(1)} %multiply_convert_fusion.2.refs_2_, ...), custom_call_target="tpu_custom_call" | custom-call | flops 872415232 | bytes 7864320 | tf_op jit(solution)/shard_map/product/pallas_call | solution.py:128
  83.0 0.0 collective-permute-done.16.got_ref
  83.0 0.1 halve.8
  83.1 0.6 collective-permute-start.17
  83.7 0.0 collective-permute-done.18.got_ref
  83.7 0.1 halve.9
  83.8 1.0 collective-permute-start.21
  84.8 1.3 %collective-permute-start.20 = (f32[4,64,256]{2,1,0:T(8,128)S(1)}, f32[4,64,256]{2,1,0:T(8,128)S(1)}, u32[]{:S(2)}, u32[]{:S(2)}) collective-permute-start(f32[4,64,256]{2,1,0:T(8,128)S(1)} %get-tuple-element.59), channel_id=1, source_target_pairs={{0,2},{1,3},{2,0},{3,1},{4,6},{5,7},{6,4},{7,5},{8,10},{9,11},{10,... | collective-permute-start | bytes 786440 | tf_op jit(solution)/shard_map/ppermute | solution.py:204
  86.1 11.8 %collective-permute-done.17.got_ref = f32[4,128,256]{2,1,0:T(8,128)S(1)} collective-permute-done((f32[4,128,256]{2,1,0:T(8,128)S(1)}, f32[4,128,256]{2,1,0:T(8,128)S(1)}, u32[]{:S(2)}, u32[]{:S(2)}) %collective-permute-start.17) | collective-permute-done | bytes 524320 | tf_op jit(solution)/shard_map/ppermute | solution.py:204
  97.9 0.1 halve.10
  98.0 0.8 collective-permute-start.19
  98.9 0.8 collective-permute-start.23
  99.7 3.9 %collective-permute-done.20.got_ref = f32[4,64,256]{2,1,0:T(8,128)S(1)} collective-permute-done((f32[4,64,256]{2,1,0:T(8,128)S(1)}, f32[4,64,256]{2,1,0:T(8,128)S(1)}, u32[]{:S(2)}, u32[]{:S(2)}) %collective-permute-start.20) | collective-permute-done | bytes 262176 | tf_op jit(solution)/shard_map/ppermute | solution.py:204
  103.6 0.8 collective-permute-start.25
  104.4 0.1 collective-permute-done.19.got_ref
  104.6 3.3 %collective-permute-start.22 = (f32[1,128,256]{2,1,0:T(8,128)S(1)}, f32[1,128,256]{2,1,0:T(8,128)S(1)}, u32[]{:S(2)}, u32[]{:S(2)}) collective-permute-start(f32[1,128,256]{2,1,0:T(8,128)S(1)} %get-tuple-element.64.refs_0_), channel_id=1, source_target_pairs={{0,8},{1,9},{2,10},{3,11},{4,12},{5,13},{6,14},{7,15},{8,0},{9,1},... | collective-permute-start | bytes 393224 | tf_op jit(solution)/shard_map/ppermute | solution.py:204
  107.9 0.0 collective-permute-done.23.got_ref
  107.9 0.1 collective-permute-start.24
  108.0 1.6 %collective-permute-done.25.got_ref = f32[2,64,256]{2,1,0:T(8,128)S(1)} collective-permute-done((f32[2,64,256]{2,1,0:T(8,128)S(1)}, f32[2,64,256]{2,1,0:T(8,128)S(1)}, u32[]{:S(2)}, u32[]{:S(2)}) %collective-permute-start.25) | collective-permute-done | bytes 131104 | tf_op jit(solution)/shard_map/ppermute | solution.py:204
  109.6 2.4 %collective-permute-start.26 = (f32[1,64,256]{2,1,0:T(8,128)S(1)}, f32[1,64,256]{2,1,0:T(8,128)S(1)}, u32[]{:S(2)}, u32[]{:S(2)}) collective-permute-start(f32[1,64,256]{2,1,0:T(8,128)S(1)} %get-tuple-element.70), channel_id=1, source_target_pairs={{0,8},{1,9},{2,10},{3,11},{4,12},{5,13},{6,14},{7,15},{8,0},{9,1},... | collective-permute-start | bytes 196616 | tf_op jit(solution)/shard_map/ppermute | solution.py:204
  112.0 5.3 %collective-permute-done.24.refs_3_ = f32[1,64,256]{2,1,0:T(8,128)S(1)} collective-permute-done((f32[1,64,256]{2,1,0:T(8,128)S(1)}, f32[1,64,256]{2,1,0:T(8,128)S(1)}, u32[]{:S(2)}, u32[]{:S(2)}) %collective-permute-start.24) | collective-permute-done | bytes 65568 | tf_op jit(solution)/shard_map/ppermute | solution.py:204
  117.2 0.7 collective-permute-done.26.refs_5_
  117.9 0.0 collective-permute-done.22.refs_1_
  117.9 0.7 finish.1
  (27 shorter events, 0.6 us)
Async XLA Ops:
  0.0 1.0 copy-start
  1.0 0.7 copy-start.1
  4.1 9.7 %collective-permute-start.3 = (f32[128,384]{1,0:T(8,128)S(1)}, f32[128,384]{1,0:T(8,128)S(1)}, u32[]{:S(2)}, u32[]{:S(2)}) collective-permute-start(f32[128,384]{1,0:T(8,128)S(1)} %mix.5.refs_0_), channel_id=1, source_target_pairs={{0,1},{1,0},{2,3},{3,2},{4,5},{5,4},{6,7},{7,6},{8,9},{9,8},{10,11... | collective-permute-start | bytes 589832 | tf_op jit(solution)/shard_map/ppermute | solution.py:204
  7.0 9.6 %collective-permute-start.2 = (f32[128,512]{1,0:T(8,128)S(1)}, f32[128,512]{1,0:T(8,128)S(1)}, u32[]{:S(2)}, u32[]{:S(2)}) collective-permute-start(f32[128,512]{1,0:T(8,128)S(1)} %mix.7), channel_id=1, source_target_pairs={{0,2},{1,3},{2,0},{3,1},{4,6},{5,7},{6,4},{7,5},{8,10},{9,11},{10,... | collective-permute-start | bytes 786440 | tf_op jit(solution)/shard_map/ppermute | solution.py:204
  9.6 13.3 %collective-permute-start = (f32[128,384]{1,0:T(8,128)S(1)}, f32[128,384]{1,0:T(8,128)S(1)}, u32[]{:S(2)}, u32[]{:S(2)}) collective-permute-start(f32[128,384]{1,0:T(8,128)S(1)} %mix.4.refs_0_), channel_id=1, source_target_pairs={{0,8},{1,9},{2,10},{3,11},{4,12},{5,13},{6,14},{7,15},{8,0},{9,1},... | collective-permute-start | bytes 589832 | tf_op jit(solution)/shard_map/ppermute | solution.py:204
  12.2 10.4 %collective-permute-start.1 = (f32[128,384]{1,0:T(8,128)S(1)}, f32[128,384]{1,0:T(8,128)S(1)}, u32[]{:S(2)}, u32[]{:S(2)}) collective-permute-start(f32[128,384]{1,0:T(8,128)S(1)} %mix.6.refs_0_), channel_id=1, source_target_pairs={{0,4},{1,5},{2,6},{3,7},{4,0},{5,1},{6,2},{7,3},{8,12},{9,13},{10,... | collective-permute-start | bytes 589832 | tf_op jit(solution)/shard_map/ppermute | solution.py:204
  13.8 25.4 %collective-permute-start.7 = (f32[128,384]{1,0:T(8,128)S(1)}, f32[128,384]{1,0:T(8,128)S(1)}, u32[]{:S(2)}, u32[]{:S(2)}) collective-permute-start(f32[128,384]{1,0:T(8,128)S(1)} %multiply_add_fusion.11), channel_id=1, source_target_pairs={{0,8},{1,9},{2,10},{3,11},{4,12},{5,13},{6,14},{7,15},{8,0},{9,1},... | collective-permute-start | bytes 589832 | tf_op jit(solution)/shard_map/ppermute | solution.py:204
  22.6 2.3 %collective-permute-start.5 = (f32[128,384]{1,0:T(8,128)S(1)}, f32[128,384]{1,0:T(8,128)S(1)}, u32[]{:S(2)}, u32[]{:S(2)}) collective-permute-start(f32[128,384]{1,0:T(8,128)S(1)} %multiply_add_fusion.10), channel_id=1, source_target_pairs={{0,1},{1,0},{2,3},{3,2},{4,5},{5,4},{6,7},{7,6},{8,9},{9,8},{10,11... | collective-permute-start | bytes 589832 | tf_op jit(solution)/shard_map/ppermute | solution.py:204
  23.0 7.1 %collective-permute-start.4 = (f32[128,384]{1,0:T(8,128)S(1)}, f32[128,384]{1,0:T(8,128)S(1)}, u32[]{:S(2)}, u32[]{:S(2)}) collective-permute-start(f32[128,384]{1,0:T(8,128)S(1)} %multiply_add_fusion.9), channel_id=1, source_target_pairs={{0,2},{1,3},{2,0},{3,1},{4,6},{5,7},{6,4},{7,5},{8,10},{9,11},{10,... | collective-permute-start | bytes 589832 | tf_op jit(solution)/shard_map/ppermute | solution.py:204
  23.3 11.5 %collective-permute-start.8 = (f32[128,512]{1,0:T(8,128)S(1)}, f32[128,512]{1,0:T(8,128)S(1)}, u32[]{:S(2)}, u32[]{:S(2)}) collective-permute-start(f32[128,512]{1,0:T(8,128)S(1)} %multiply_add_fusion.2), channel_id=1, source_target_pairs={{0,4},{1,5},{2,6},{3,7},{4,0},{5,1},{6,2},{7,3},{8,12},{9,13},{10,... | collective-permute-start | bytes 786440 | tf_op jit(solution)/shard_map/ppermute | solution.py:204
  34.9 5.8 %collective-permute-start.10 = (f32[128,512]{1,0:T(8,128)S(1)}, f32[128,512]{1,0:T(8,128)S(1)}, u32[]{:S(2)}, u32[]{:S(2)}) collective-permute-start(f32[128,512]{1,0:T(8,128)S(1)} %multiply_add_fusion.1), channel_id=1, source_target_pairs={{0,1},{1,0},{2,3},{3,2},{4,5},{5,4},{6,7},{7,6},{8,9},{9,8},{10,11... | collective-permute-start | bytes 786440 | tf_op jit(solution)/shard_map/ppermute | solution.py:204
  35.0 11.3 %collective-permute-start.6 = (f32[128,384]{1,0:T(8,128)S(1)}, f32[128,384]{1,0:T(8,128)S(1)}, u32[]{:S(2)}, u32[]{:S(2)}) collective-permute-start(f32[128,384]{1,0:T(8,128)S(1)} %multiply_add_fusion.7), channel_id=1, source_target_pairs={{0,4},{1,5},{2,6},{3,7},{4,0},{5,1},{6,2},{7,3},{8,12},{9,13},{10,... | collective-permute-start | bytes 589832 | tf_op jit(solution)/shard_map/ppermute | solution.py:204
  35.0 13.7 %collective-permute-start.12 = (f32[128,384]{1,0:T(8,128)S(1)}, f32[128,384]{1,0:T(8,128)S(1)}, u32[]{:S(2)}, u32[]{:S(2)}) collective-permute-start(f32[128,384]{1,0:T(8,128)S(1)} %multiply_add_fusion.8), channel_id=1, source_target_pairs={{0,8},{1,9},{2,10},{3,11},{4,12},{5,13},{6,14},{7,15},{8,0},{9,1},... | collective-permute-start | bytes 589832 | tf_op jit(solution)/shard_map/ppermute | solution.py:204
  39.3 6.8 %collective-permute-start.9 = (f32[128,384]{1,0:T(8,128)S(1)}, f32[128,384]{1,0:T(8,128)S(1)}, u32[]{:S(2)}, u32[]{:S(2)}) collective-permute-start(f32[128,384]{1,0:T(8,128)S(1)} %multiply_add_fusion.6), channel_id=1, source_target_pairs={{0,2},{1,3},{2,0},{3,1},{4,6},{5,7},{6,4},{7,5},{8,10},{9,11},{10,... | collective-permute-start | bytes 589832 | tf_op jit(solution)/shard_map/ppermute | solution.py:204
  46.3 3.9 %collective-permute-start.11 = (f32[128,384]{1,0:T(8,128)S(1)}, f32[128,384]{1,0:T(8,128)S(1)}, u32[]{:S(2)}, u32[]{:S(2)}) collective-permute-start(f32[128,384]{1,0:T(8,128)S(1)} %multiply_add_fusion.4), channel_id=1, source_target_pairs={{0,1},{1,0},{2,3},{3,2},{4,5},{5,4},{6,7},{7,6},{8,9},{9,8},{10,11... | collective-permute-start | bytes 589832 | tf_op jit(solution)/shard_map/ppermute | solution.py:204
  46.4 9.2 %collective-permute-start.13 = (f32[128,384]{1,0:T(8,128)S(1)}, f32[128,384]{1,0:T(8,128)S(1)}, u32[]{:S(2)}, u32[]{:S(2)}) collective-permute-start(f32[128,384]{1,0:T(8,128)S(1)} %multiply_add_fusion.5), channel_id=1, source_target_pairs={{0,4},{1,5},{2,6},{3,7},{4,0},{5,1},{6,2},{7,3},{8,12},{9,13},{10,... | collective-permute-start | bytes 589832 | tf_op jit(solution)/shard_map/ppermute | solution.py:204
  48.8 5.7 %collective-permute-start.14 = (f32[128,384]{1,0:T(8,128)S(1)}, f32[128,384]{1,0:T(8,128)S(1)}, u32[]{:S(2)}, u32[]{:S(2)}) collective-permute-start(f32[128,384]{1,0:T(8,128)S(1)} %multiply_add_fusion.3), channel_id=1, source_target_pairs={{0,2},{1,3},{2,0},{3,1},{4,6},{5,7},{6,4},{7,5},{8,10},{9,11},{10,... | collective-permute-start | bytes 589832 | tf_op jit(solution)/shard_map/ppermute | solution.py:204
  50.1 12.8 %collective-permute-start.15 = (f32[128,512]{1,0:T(8,128)S(1)}, f32[128,512]{1,0:T(8,128)S(1)}, u32[]{:S(2)}, u32[]{:S(2)}) collective-permute-start(f32[128,512]{1,0:T(8,128)S(1)} %multiply_add_fusion), channel_id=1, source_target_pairs={{0,8},{1,9},{2,10},{3,11},{4,12},{5,13},{6,14},{7,15},{8,0},{9,1},... | collective-permute-start | bytes 786440 | tf_op jit(solution)/shard_map/ppermute | solution.py:204
  67.8 15.2 %collective-permute-start.16 = (f32[8,128,256]{2,1,0:T(8,128)S(1)}, f32[8,128,256]{2,1,0:T(8,128)S(1)}, u32[]{:S(2)}, u32[]{:S(2)}) collective-permute-start(f32[8,128,256]{2,1,0:T(8,128)S(1)} %product.4.refs_5_), channel_id=1, source_target_pairs={{0,1},{1,0},{2,3},{3,2},{4,5},{5,4},{6,7},{7,6},{8,9},{9,8},{10,11... | collective-permute-start | bytes 3145736 | tf_op jit(solution)/shard_map/ppermute | solution.py:204
  77.6 6.2 %collective-permute-start.18 = (f32[8,128,256]{2,1,0:T(8,128)S(1)}, f32[8,128,256]{2,1,0:T(8,128)S(1)}, u32[]{:S(2)}, u32[]{:S(2)}) collective-permute-start(f32[8,128,256]{2,1,0:T(8,128)S(1)} %product.6.refs_5_), channel_id=1, source_target_pairs={{0,1},{1,0},{2,3},{3,2},{4,5},{5,4},{6,7},{7,6},{8,9},{9,8},{10,11... | collective-permute-start | bytes 3145736 | tf_op jit(solution)/shard_map/ppermute | solution.py:204
  83.1 14.9 %collective-permute-start.17 = (f32[4,128,256]{2,1,0:T(8,128)S(1)}, f32[4,128,256]{2,1,0:T(8,128)S(1)}, u32[]{:S(2)}, u32[]{:S(2)}) collective-permute-start(f32[4,128,256]{2,1,0:T(8,128)S(1)} %get-tuple-element.54.refs_0_), channel_id=1, source_target_pairs={{0,2},{1,3},{2,0},{3,1},{4,6},{5,7},{6,4},{7,5},{8,10},{9,11},{10,... | collective-permute-start | bytes 1572872 | tf_op jit(solution)/shard_map/ppermute | solution.py:204
  83.8 15.0 %collective-permute-start.21 = (f32[4,64,256]{2,1,0:T(8,128)S(1)}, f32[4,64,256]{2,1,0:T(8,128)S(1)}, u32[]{:S(2)}, u32[]{:S(2)}) collective-permute-start(f32[4,64,256]{2,1,0:T(8,128)S(1)} %get-tuple-element.55.refs_0_), channel_id=1, source_target_pairs={{0,4},{1,5},{2,6},{3,7},{4,0},{5,1},{6,2},{7,3},{8,12},{9,13},{10,... | collective-permute-start | bytes 786440 | tf_op jit(solution)/shard_map/ppermute | solution.py:204
  84.8 18.7 %collective-permute-start.20 = (f32[4,64,256]{2,1,0:T(8,128)S(1)}, f32[4,64,256]{2,1,0:T(8,128)S(1)}, u32[]{:S(2)}, u32[]{:S(2)}) collective-permute-start(f32[4,64,256]{2,1,0:T(8,128)S(1)} %get-tuple-element.59), channel_id=1, source_target_pairs={{0,2},{1,3},{2,0},{3,1},{4,6},{5,7},{6,4},{7,5},{8,10},{9,11},{10,... | collective-permute-start | bytes 786440 | tf_op jit(solution)/shard_map/ppermute | solution.py:204
  98.0 6.5 %collective-permute-start.19 = (f32[2,128,256]{2,1,0:T(8,128)S(1)}, f32[2,128,256]{2,1,0:T(8,128)S(1)}, u32[]{:S(2)}, u32[]{:S(2)}) collective-permute-start(f32[2,128,256]{2,1,0:T(8,128)S(1)} %get-tuple-element.57.refs_0_), channel_id=1, source_target_pairs={{0,4},{1,5},{2,6},{3,7},{4,0},{5,1},{6,2},{7,3},{8,12},{9,13},{10,... | collective-permute-start | bytes 786440 | tf_op jit(solution)/shard_map/ppermute | solution.py:204
  98.9 9.0 %collective-permute-start.23 = (f32[2,64,256]{2,1,0:T(8,128)S(1)}, f32[2,64,256]{2,1,0:T(8,128)S(1)}, u32[]{:S(2)}, u32[]{:S(2)}) collective-permute-start(f32[2,64,256]{2,1,0:T(8,128)S(1)} %get-tuple-element.61.refs_0_), channel_id=1, source_target_pairs={{0,2},{1,3},{2,0},{3,1},{4,6},{5,7},{6,4},{7,5},{8,10},{9,11},{10,... | collective-permute-start | bytes 393224 | tf_op jit(solution)/shard_map/ppermute | solution.py:204
  103.6 6.0 %collective-permute-start.25 = (f32[2,64,256]{2,1,0:T(8,128)S(1)}, f32[2,64,256]{2,1,0:T(8,128)S(1)}, u32[]{:S(2)}, u32[]{:S(2)}) collective-permute-start(f32[2,64,256]{2,1,0:T(8,128)S(1)} %get-tuple-element.62.refs_0_), channel_id=1, source_target_pairs={{0,4},{1,5},{2,6},{3,7},{4,0},{5,1},{6,2},{7,3},{8,12},{9,13},{10,... | collective-permute-start | bytes 393224 | tf_op jit(solution)/shard_map/ppermute | solution.py:204
  104.6 13.4 %collective-permute-start.22 = (f32[1,128,256]{2,1,0:T(8,128)S(1)}, f32[1,128,256]{2,1,0:T(8,128)S(1)}, u32[]{:S(2)}, u32[]{:S(2)}) collective-permute-start(f32[1,128,256]{2,1,0:T(8,128)S(1)} %get-tuple-element.64.refs_0_), channel_id=1, source_target_pairs={{0,8},{1,9},{2,10},{3,11},{4,12},{5,13},{6,14},{7,15},{8,0},{9,1},... | collective-permute-start | bytes 393224 | tf_op jit(solution)/shard_map/ppermute | solution.py:204
  107.9 9.3 %collective-permute-start.24 = (f32[1,64,256]{2,1,0:T(8,128)S(1)}, f32[1,64,256]{2,1,0:T(8,128)S(1)}, u32[]{:S(2)}, u32[]{:S(2)}) collective-permute-start(f32[1,64,256]{2,1,0:T(8,128)S(1)} %get-tuple-element.67.refs_0_), channel_id=1, source_target_pairs={{0,8},{1,9},{2,10},{3,11},{4,12},{5,13},{6,14},{7,15},{8,0},{9,1},... | collective-permute-start | bytes 196616 | tf_op jit(solution)/shard_map/ppermute | solution.py:204
  109.6 8.3 %collective-permute-start.26 = (f32[1,64,256]{2,1,0:T(8,128)S(1)}, f32[1,64,256]{2,1,0:T(8,128)S(1)}, u32[]{:S(2)}, u32[]{:S(2)}) collective-permute-start(f32[1,64,256]{2,1,0:T(8,128)S(1)} %get-tuple-element.70), channel_id=1, source_target_pairs={{0,8},{1,9},{2,10},{3,11},{4,12},{5,13},{6,14},{7,15},{8,0},{9,1},... | collective-permute-start | bytes 196616 | tf_op jit(solution)/shard_map/ppermute | solution.py:204

commit v3 on v0

v3 whole, which is shorter than its diff:
```python
import functools

import jax
import jax.numpy as jnp
import numpy as np
from jax import lax
from jax.experimental import pallas as pl
from jax.experimental.pallas import tpu as pltpu
from jax.sharding import PartitionSpec as P

LANES = 128
F32 = jnp.float32
BF16 = jnp.bfloat16


def quotient(index, divisor, limit):
    shift = 16
    scale = -(-(1 << shift) // divisor)
    numbers = np.arange(limit, dtype=np.int64)
    assert np.array_equal((numbers * scale) >> shift, numbers // divisor)
    assert limit * scale < 2**31
    return (index * scale) >> shift


def sign_of(common, count):
    parity = common
    for place in range(1, count):
        parity = parity ^ (common >> place)
    return (1 - 2 * (parity & 1)).astype(F32)


def mix_kernel(rows, start, group, activations, small, *refs):
    out = refs[-1]
    local = activations.shape[1]
    block = small.shape[0]
    tokens, cols = out.shape
    tall = group * block
    span = local // block
    low = group.bit_length() - 1
    high = span.bit_length() - 1 - low
    full = small[...]
    head = full.astype(BF16)
    tail = (full - head.astype(F32)).astype(BF16)

    row = lax.broadcasted_iota(jnp.int32, (tall, block), 0)
    unit = lax.broadcasted_iota(jnp.int32, (tall, block), 1)
    spread_rows = (row - quotient(row, block, tall) * block == unit).astype(F32).astype(BF16)
    col = lax.broadcasted_iota(jnp.int32, (block, cols), 1) + start
    unit = lax.broadcasted_iota(jnp.int32, (block, cols), 0)
    spread_cols = (col - quotient(col, block, local) * block == unit).astype(F32).astype(BF16)
    at_row = quotient(lax.broadcasted_iota(jnp.int32, (tall, cols), 0), block, tall)
    at_col = quotient(lax.broadcasted_iota(jnp.int32, (tall, cols), 1) + start, block, local)
    sign = sign_of(at_row & at_col, max(low, 1))

    def tiled(part):
        rolled = jnp.dot(spread_rows, part, preferred_element_type=F32).astype(BF16)
        return (jnp.dot(rolled, spread_cols, preferred_element_type=F32) * sign).astype(BF16)

    head, tail = tiled(head), tiled(tail)
    owner = quotient(lax.broadcasted_iota(jnp.int32, (8, cols), 1) + start, block, local) >> low
    total = jnp.zeros((tokens, cols), F32)
    for piece in range(span // group):
        values = activations[rows[0]:rows[1], piece * tall:(piece + 1) * tall]
        term = jnp.dot(values, head, preferred_element_type=F32)
        term = term + jnp.dot(values, tail, preferred_element_type=F32)
        total = total + term * sign_of(owner & piece, max(high, 1))[0:1]
    out[...] = total


VMEM = pl.BlockSpec(memory_space=pltpu.VMEM)
SMEM = pl.BlockSpec(memory_space=pltpu.SMEM)
UNREAD = pl.BlockSpec(memory_space=pl.ANY)
COST = pl.CostEstimate(flops=10**10, bytes_accessed=10**8, transcendentals=0)


def call(name, kernel, operands, specs, shapes, after, scratch=(), limit=16):
    return pl.pallas_call(
        kernel,
        out_shape=shapes,
        in_specs=list(specs) + [UNREAD] * len(after),
        out_specs=jax.tree.map(lambda _: VMEM, shapes),
        scratch_shapes=list(scratch),
        cost_estimate=COST,
        compiler_params=pltpu.CompilerParams(vmem_limit_bytes=limit * 2**20),
        name=name,
    )(*operands, *after)


def mix(activations, small, rows, cols, after):
    block = small.shape[0]
    group = min(4, activations.shape[1] // block)
    kernel = functools.partial(mix_kernel, rows, cols[0], group)
    shape = jax.ShapeDtypeStruct((rows[1] - rows[0], cols[1] - cols[0]), F32)
    return call("mix", kernel, (activations, small), (VMEM, VMEM), shape, after)


def fold(me, own, got, bit, after, factor=None):
    def kernel(me_ref, own_ref, got_ref, *refs):
        sign = jnp.where((me_ref[0] & bit) != 0, -1.0, 1.0).astype(F32)
        total = got_ref[...] + own_ref[...] * sign
        if factor is not None:
            total = total * factor
        refs[-1][...] = total.astype(refs[-1].dtype)

    shape = jax.ShapeDtypeStruct(own.shape, F32 if factor is None else BF16)
    return call("fold", kernel, (me, own, got), (SMEM, VMEM, VMEM), shape, after)


def gather(me, weight, rows, distances, width, columns, sems):
    parts = 1 + max(part for _, part in distances)
    copies = []
    for i, (distance, part) in enumerate(distances):
        column = pl.multiple_of(((distance ^ me) * parts + part) * width, LANES)
        copies.append(
            pltpu.make_async_copy(
                weight.at[rows[0]:rows[1], pl.ds(column, width)], columns.at[:, pl.ds(i * width, width)], sems.at[i]
            )
        )
    return copies


def step(me, chunk, columns, total, weight, rows, distances, width, after):
    blocks = len(distances)
    values = [] if chunk is None else [chunk, columns] + ([] if total is None else [total])
    wide = max(width, min(1024, blocks * width))

    def kernel(me_ref, weight_ref, *refs):
        refs, sems = refs[:-1], refs[-1]
        loaded = refs[-1]
        copies = gather(me_ref[0], weight_ref, rows, distances, width, loaded, sems)
        for copy in copies:
            copy.start()
        if chunk is not None:
            out = refs[-2]
            for at in range(0, blocks * width, wide):
                sums = jnp.dot(refs[0][...], refs[1][:, at:at + wide], preferred_element_type=F32)
                for i in range(wide // width):
                    term = sums[:, i * width:(i + 1) * width]
                    out[at // width + i] = term if total is None else refs[2][at // width + i] + term
        for copy in copies:
            copy.wait()

    shapes = [jax.ShapeDtypeStruct((rows[1] - rows[0], blocks * width), BF16)]
    if chunk is not None:
        shapes.insert(0, jax.ShapeDtypeStruct((blocks, chunk.shape[0], width), F32))
    outs = call(
        "step",
        kernel,
        (me, weight, *values),
        [SMEM, pl.BlockSpec(memory_space=pltpu.HBM)] + [VMEM] * len(values),
        shapes,
        after,
        [pltpu.SemaphoreType.DMA((blocks,))],
        40 if chunk is None else 28,
    )
    return (None, *outs) if chunk is None else outs


def product(chunk, columns, total, begin, end, after):
    width = total.shape[2]
    wide = max(width, min(1024, (end - begin) * width))

    def kernel(chunk_ref, columns_ref, total_ref, *refs):
        out = refs[-1]
        for at in range(begin * width, end * width, wide):
            sums = jnp.dot(chunk_ref[...], columns_ref[:, at:at + wide], preferred_element_type=F32)
            for i in range(wide // width):
                block = at // width + i
                out[block - begin] = total_ref[block] + sums[:, i * width:(i + 1) * width]

    shape = jax.ShapeDtypeStruct((end - begin, chunk.shape[0], width), F32)
    return call("product", kernel, (chunk, columns, total), [VMEM] * 3, shape, after)


def halve(own, got, distances, plans, after):
    shapes = []
    for rows, _ in plans:
        shapes += [jax.ShapeDtypeStruct((len(distances) // 2, rows[1] - rows[0], own.shape[2]), F32)] * 2

    def kernel(own_ref, got_ref, *refs):
        outs = refs[-len(shapes):]
        for at, ((begin, end), bit) in enumerate(plans):
            for place, d in enumerate(d for d in distances if not d & bit):
                for out, source in ((outs[2 * at], d), (outs[2 * at + 1], d | bit)):
                    i = distances.index(source)
                    out[place] = own_ref[i, begin:end, :] + got_ref[i, begin:end, :]

    return call("halve", kernel, (own, got), (VMEM, VMEM), shapes, after)


def tick(after):
    def kernel(*refs):
        refs[-1][...] = jnp.zeros_like(refs[-1])

    return call("tick", kernel, (), (), jax.ShapeDtypeStruct((8, LANES), F32), after)


def finish(pieces, own, got, tokens, width, parts, after):
    held = [x for _, _, x in pieces[:-1]] if len(pieces) > 1 else []

    def kernel(own_ref, got_ref, *refs):
        out = refs[-1]
        value = (own_ref[0] + got_ref[0]).astype(BF16)
        if not pieces:
            out[...] = value
            return
        for ((begin, end), part, _), ref in zip(pieces, [*refs[:len(held)], None]):
            out[begin:end, part * width:(part + 1) * width] = value if ref is None else ref[...]

    shape = (tokens, width * parts) if pieces else own.shape[1:]
    operands = (own, got, *held)
    return call("finish", kernel, operands, [VMEM] * len(operands), jax.ShapeDtypeStruct(shape, BF16), after)


def body(activations, rotation_small, down_weight):
    shards = lax.axis_size("tensor")
    me = lax.axis_index("tensor").astype(jnp.int32).reshape(1)
    tokens, local = activations.shape
    block = rotation_small.shape[0]
    share = down_weight.shape[1] // shards
    factor = (local // block * shards) ** (-0.5)
    bits = [1 << place for place in range(shards.bit_length() - 1)]
    assert len(bits) >= 3 and shards == 1 << len(bits)
    after = []

    def swap(x, bit):
        return lax.ppermute(x, "tensor", [(d, d ^ bit) for d in range(shards)])

    def ran(outs, link=-1):
        after[:] = [jax.tree.leaves(outs)[link]]
        return outs

    parts = 2 if share % (2 * LANES) == 0 else 1
    width = share // parts
    near = [d for d in range(shards) if not d & bits[0]]
    groups = [(part, kept) for part in range(parts) for kept in (False, True)]
    distances = [(d | (0 if kept else bits[0]), part) for part, kept in groups for d in near]

    tiles = -(-local // LANES)
    count = max(1, min(len(bits), tiles))
    edges = [min(local, (tiles * c // count) * LANES) for c in range(count)] + [local]
    spans = list(zip(edges[:-1], edges[1:]))
    chunks = []
    for span in spans:
        chunks.append(ran(mix(activations, rotation_small, (0, tokens), span, after)))
    cycle = bits[-1:] + bits[1:-1] + bits[:1]
    events = []
    for phase in range(len(bits)):
        for c in range(count):
            events.append((phase, cycle[(phase - c) % len(bits)], c))
    events.sort()
    final = [c for phase, _, c in events if phase == len(bits) - 1]
    total = None
    for number, (phase, bit, c) in enumerate(events):
        got = swap(chunks[c], bit)
        last = phase == len(bits) - 1
        chunks[c] = ran(fold(me, chunks[c], got, bit, after, factor if last else None))
        if number == len(events) - count - 2:
            _, columns = ran(step(me, None, None, None, down_weight, spans[final[0]], distances, width, after))
        if last and c != final[-1]:
            rows = spans[final[final.index(c) + 1]]
            total, columns = ran(step(me, chunks[c], columns, total, down_weight, rows, distances, width, after))

    inner = bits[1:]
    late = inner[-1:] + inner[:-1]
    swapped = [inner[1], inner[0]] + inner[2:]
    half = tokens // 2
    routes = [
        [((0, half), inner), ((half, tokens), late)],
        [((0, half), swapped), ((half, tokens), inner)],
    ][:parts]
    free = dict.fromkeys(bits, 0.0)
    clock = 0.0
    kernels = 0
    pieces = []
    queue = []

    def send(x, bit, use):
        nonlocal clock
        clock += 0.7
        micros = x.size * 4e-6 * (2 if bit == bits[0] else 40 if bit == bits[-1] else 20)
        free[bit] = max(clock + 1.0, free[bit]) + micros
        queue.append((free[bit] + 0.3, kernels, swap(x, bit), use))

    def split(part, stage, pieces_of, left, keep, got):
        base = pieces_of[0][0][0]
        plans = [((begin - base, end - base), route[stage]) for (begin, end), route in pieces_of]
        outs = ran(halve(keep, got, left, plans, after))
        for i, (rows, route) in enumerate(pieces_of):
            rest = [d for d in left if not d & route[stage]]
            if stage + 1 < len(inner):
                use = functools.partial(split, part, stage + 1, [(rows, route)], rest, outs[2 * i])
            else:
                use = functools.partial(close, part, rows, outs[2 * i])
            send(outs[2 * i + 1], route[stage], use)

    def close(part, rows, keep, got):
        last = len(pieces) + 1 == parts * len(routes[0])
        held = pieces + [(rows, part, None)] if last else []
        pieces.append((rows, part, ran(finish(held, keep, got, tokens, width, parts, after))))

    for at, (part, kept) in enumerate(groups):
        begin, end = at * len(near), (at + 1) * len(near)
        x = ran(product(chunks[final[-1]], columns, total, begin, end, after))
        clock += 0.6
        kernels += 1
        if not kept:
            send(x, bits[0], None)
        else:
            when, _, got, _ = queue.pop()
            queue.append((when, kernels - 1, got, functools.partial(split, part, 0, routes[part], near, x)))
    while queue:
        item = min(queue, key=lambda item: item[0])
        queue.remove(item)
        when, at, got, use = item
        if at == kernels:
            ran(tick(after))
            kernels += 1
            clock += 0.1
        clock = max(clock, when) + 0.15
        kernels += 1
        use(got)
    return pieces[-1][2]


def solution(mesh):
    placed = (P("groups", "tensor"), P(), P("tensor", None))
    return jax.shard_map(
        body, mesh=mesh, in_specs=placed, out_specs=P("groups", "tensor"), check_vma=False
    )
```

time: 190 us -> 102 us (0.54)
  blocking collectives: 27.2 us -> 0 us
  matrix products: 26.1 us -> 0 us
  Pallas kernels: 0 us -> 24.8 us
  local copies, waits for them, and re-layouts: 25.8 us -> 1.75 us
  waiting for transfers between devices: 72.4 us -> 49.5 us
  starting transfers between devices: 7.43 us -> 25.8 us
  other arithmetic: 17.1 us -> 0 us
  between operations: 13.5 us -> 0.41 us
    reduce_scatter x1 -> x0, waiting for transfers between devices: 72.4 us -> none  [body(): lax.psum_scatter(lax.dot_general(down_weight, rotated, (((0,), (1,)), (()...]
    ppermute x0 -> x30, waiting for transfers between devices: none -> 49.5 us  [swap(): return lax.ppermute(x, 'tensor', [(d, d ^ bit) for d in range(shards)])]
    all_to_all x1 -> x0, blocking collectives: 27.2 us -> none  [body(): lax.all_to_all(gathered, 'tensor', split_axis=1, concat_axis=0, tiled=True)]
    dot_general x3 -> x0, matrix products: 26.1 us -> none  [the longest x1 14.7 us: body(): lax.dot_general(down_weight, rotated, (((0,), (1,)), ((), ())), preferred...]
    mul x1 -> x0, local copies, waits for them, and re-layouts: 25.8 us -> none  [body(): kronecker = jnp.kron(sylvester(span), rotation_small)]
    ppermute x0 -> x30, starting transfers between devices: none -> 25.8 us  [swap(): return lax.ppermute(x, 'tensor', [(d, d ^ bit) for d in range(shards)])]
    pallas_call x0 -> x42, Pallas kernels: none -> 24.8 us  [call(): pl.pallas_call(kernel, out_shape=shapes, in_specs=list(specs) + [UNREAD]...]
    mul x1 -> x0, other arithmetic: 13.3 us -> none  [body(): kronecker = jnp.kron(sylvester(span), rotation_small)]
  transfers between devices with their start and end apart: 2 -> 30, of which waited for: 1 -> 14; matrix products, arithmetic and copies ran while one was open for 21% -> 0% of each run, Pallas kernels for 0% -> 22%
where the time goes in v3:
time: 102 us
  waiting for transfers between devices  49.5 us (49%)
  starting transfers between devices  25.8 us (25%)
  Pallas kernels  24.8 us (24%)
  local copies, waits for them, and re-layouts  1.75 us (2%)
    ppermute x30, waiting for transfers between devices, swap(): return lax.ppermute(x, 'tensor', [(d, d ^ bit) for d in range(shards)])  49.5 us
    ppermute x30, starting transfers between devices, swap(): return lax.ppermute(x, 'tensor', [(d, d ^ bit) for d in range(shards)])  25.8 us
    pallas_call x42, Pallas kernels, call(): pl.pallas_call(kernel, out_shape=shapes, in_specs=list(specs) + [UNREAD]...  24.8 us
  transfers between devices with their start and end apart: 30, of which 14 were waited for; matrix products, arithmetic and copies ran while one was open for 0% of the time, Pallas kernels for 22%

profile of v3, /device:TPU:0, one launch (start us, length us, event | category | flops | bytes accessed | tf_op | source)
XLA Modules:
  0.0 102.2 jit_solution(1143318345381610191)
XLA Ops:
  0.0 1.0 copy-done
  1.0 0.7 copy-done.1
  1.8 1.2 %mix.4.refs_0_.own_ref = f32[128,384]{1,0:T(8,128)S(1)} custom-call(bf16[128,1664]{1,0:T(8,128)(2,1)S(1)} %copy-done, f32[52,52]{1,0:T(8,128)S(1)} %copy-done.1), custom_call_target="tpu_custom_call" | custom-call | flops 10000000000 | bytes 100000000 | tf_op jit(solution)/shard_map/mix/pallas_call | solution.py:77
  2.9 4.1 %collective-permute-start.3 = (f32[128,384]{1,0:T(8,128)S(1)}, f32[128,384]{1,0:T(8,128)S(1)}, u32[]{:S(2)}, u32[]{:S(2)}) collective-permute-start(f32[128,384]{1,0:T(8,128)S(1)} %mix.4.refs_0_.own_ref), channel_id=1, source_target_pairs={{0,8},{1,9},{2,10},{3,11},{4,12},{5,13},{6,14},{7,15},{8,0},{9,1},... | collective-permute-start | bytes 589832 | tf_op jit(solution)/shard_map/ppermute | solution.py:227
  7.0 1.2 %mix.5.refs_0_.own_ref = f32[128,384]{1,0:T(8,128)S(1)} custom-call(bf16[128,1664]{1,0:T(8,128)(2,1)S(1)} %copy-done, f32[52,52]{1,0:T(8,128)S(1)} %copy-done.1, f32[128,384]{1,0:T(8,128)S(1)} %mix.4.refs_0_.own_ref), custom_call_target="tpu_custom_call" | custom-call | flops 10000000000 | bytes 100000000 | tf_op jit(solution)/shard_map/mix/pallas_call | solution.py:77
  8.2 0.1 collective-permute-start.1
  8.3 1.2 %mix.6.refs_0_.own_ref = f32[128,384]{1,0:T(8,128)S(1)} custom-call(bf16[128,1664]{1,0:T(8,128)(2,1)S(1)} %copy-done, f32[52,52]{1,0:T(8,128)S(1)} %copy-done.1, f32[128,384]{1,0:T(8,128)S(1)} %mix.5.refs_0_.own_ref), custom_call_target="tpu_custom_call" | custom-call | flops 10000000000 | bytes 100000000 | tf_op jit(solution)/shard_map/mix/pallas_call | solution.py:77
  9.5 1.6 %collective-permute-start.4 = (f32[128,384]{1,0:T(8,128)S(1)}, f32[128,384]{1,0:T(8,128)S(1)}, u32[]{:S(2)}, u32[]{:S(2)}) collective-permute-start(f32[128,384]{1,0:T(8,128)S(1)} %mix.6.refs_0_.own_ref), channel_id=1, source_target_pairs={{0,4},{1,5},{2,6},{3,7},{4,0},{5,1},{6,2},{7,3},{8,12},{9,13},{10,... | collective-permute-start | bytes 589832 | tf_op jit(solution)/shard_map/ppermute | solution.py:227
  11.2 1.2 %mix.7.refs_0_.own_ref = f32[128,512]{1,0:T(8,128)S(1)} custom-call(bf16[128,1664]{1,0:T(8,128)(2,1)S(1)} %copy-done, f32[52,52]{1,0:T(8,128)S(1)} %copy-done.1, f32[128,384]{1,0:T(8,128)S(1)} %mix.6.refs_0_.own_ref), custom_call_target="tpu_custom_call" | custom-call | flops 10000000000 | bytes 100000000 | tf_op jit(solution)/shard_map/mix/pallas_call | solution.py:77
  12.3 1.6 %collective-permute-start = (f32[128,512]{1,0:T(8,128)S(1)}, f32[128,512]{1,0:T(8,128)S(1)}, u32[]{:S(2)}, u32[]{:S(2)}) collective-permute-start(f32[128,512]{1,0:T(8,128)S(1)} %mix.7.refs_0_.own_ref), channel_id=1, source_target_pairs={{0,2},{1,3},{2,0},{3,1},{4,6},{5,7},{6,4},{7,5},{8,10},{9,11},{10,... | collective-permute-start | bytes 786440 | tf_op jit(solution)/shard_map/ppermute | solution.py:227
  13.9 0.0 collective-permute-done.1.got_ref
  14.0 0.4 collective-permute-start.8
  14.4 6.5 %collective-permute-done.got_ref = f32[128,512]{1,0:T(8,128)S(1)} collective-permute-done((f32[128,512]{1,0:T(8,128)S(1)}, f32[128,512]{1,0:T(8,128)S(1)}, u32[]{:S(2)}, u32[]{:S(2)}) %collective-permute-start) | collective-permute-done | bytes 262176 | tf_op jit(solution)/shard_map/ppermute | solution.py:227
  20.9 0.5 collective-permute-start.2
  21.4 0.0 collective-permute-done.4.got_ref
  21.4 0.1 collective-permute-start.6
  21.5 0.0 collective-permute-done.3.got_ref
  21.5 1.6 %collective-permute-start.5 = (f32[128,384]{1,0:T(8,128)S(1)}, f32[128,384]{1,0:T(8,128)S(1)}, u32[]{:S(2)}, u32[]{:S(2)}) collective-permute-start(f32[128,384]{1,0:T(8,128)S(1)} %fold.19.refs_0_.own_ref), channel_id=1, source_target_pairs={{0,2},{1,3},{2,0},{3,1},{4,6},{5,7},{6,4},{7,5},{8,10},{9,11},{10,... | collective-permute-start | bytes 589832 | tf_op jit(solution)/shard_map/ppermute | solution.py:227
  23.2 0.4 collective-permute-start.12
  23.6 5.3 %collective-permute-done.5.got_ref = f32[128,384]{1,0:T(8,128)S(1)} collective-permute-done((f32[128,384]{1,0:T(8,128)S(1)}, f32[128,384]{1,0:T(8,128)S(1)}, u32[]{:S(2)}, u32[]{:S(2)}) %collective-permute-start.5) | collective-permute-done | bytes 196640 | tf_op jit(solution)/shard_map/ppermute | solution.py:227
  28.9 1.6 %collective-permute-start.13 = (f32[128,384]{1,0:T(8,128)S(1)}, f32[128,384]{1,0:T(8,128)S(1)}, u32[]{:S(2)}, u32[]{:S(2)}) collective-permute-start(f32[128,384]{1,0:T(8,128)S(1)} %fold.21.refs_0_.own_ref), channel_id=1, source_target_pairs={{0,4},{1,5},{2,6},{3,7},{4,0},{5,1},{6,2},{7,3},{8,12},{9,13},{10,... | collective-permute-start | bytes 589832 | tf_op jit(solution)/shard_map/ppermute | solution.py:227
  30.6 5.1 %collective-permute-done.2.got_ref = f32[128,512]{1,0:T(8,128)S(1)} collective-permute-done((f32[128,512]{1,0:T(8,128)S(1)}, f32[128,512]{1,0:T(8,128)S(1)}, u32[]{:S(2)}, u32[]{:S(2)}) %collective-permute-start.2) | collective-permute-done | bytes 262176 | tf_op jit(solution)/shard_map/ppermute | solution.py:227
  35.7 0.1 collective-permute-start.7
  35.8 0.1 collective-permute-start.10
  35.9 1.4 %collective-permute-done.7.got_ref = f32[128,512]{1,0:T(8,128)S(1)} collective-permute-done((f32[128,512]{1,0:T(8,128)S(1)}, f32[128,512]{1,0:T(8,128)S(1)}, u32[]{:S(2)}, u32[]{:S(2)}) %collective-permute-start.7) | collective-permute-done | bytes 262176 | tf_op jit(solution)/shard_map/ppermute | solution.py:227
  37.4 0.7 collective-permute-start.9
  38.1 5.1 %collective-permute-done.10.got_ref = f32[128,384]{1,0:T(8,128)S(1)} collective-permute-done((f32[128,384]{1,0:T(8,128)S(1)}, f32[128,384]{1,0:T(8,128)S(1)}, u32[]{:S(2)}, u32[]{:S(2)}) %collective-permute-start.10) | collective-permute-done | bytes 196640 | tf_op jit(solution)/shard_map/ppermute | solution.py:227
  43.2 0.1 collective-permute-start.11
  43.4 0.1 collective-permute-start.15
  43.4 3.3 %step.4.refs_0_.refs_1_ = bf16[384,8192]{1,0:T(8,128)(2,1)S(1)} custom-call(s32[1]{0:T(128)} %bitcast.me_ref, bf16[1664,8192]{1,0:T(8,128)(2,1)} %weight_ref.7, f32[128,384]{1,0:T(8,128)S(1)} %fold.26.refs_0_.own_ref), custom_call_target="tpu_custom_call" | custom-call | flops 10000000000 | bytes 100000000 | tf_op jit(solution)/shard_map/step/pallas_call | solution.py:77
  46.7 0.4 collective-permute-start.14
  47.1 4.2 %step.5 = (f32[32,128,256]{2,1,0:T(8,128)S(1)}, bf16[384,8192]{1,0:T(8,128)(2,1)S(1)}) custom-call(s32[1]{0:T(128)} %bitcast.me_ref, bf16[1664,8192]{1,0:T(8,128)(2,1)} %weight_ref.7, bf16[128,384]{1,0:T(8,128)(2,1)S(1)} %fold.28.refs_0_.refs_2_, bf16[384,8192]{1,0:T(8,128)(2,1)S(1)} %step.4.refs_0_.refs_1_, bf16[128,384]{1,0:T(8,128)(2,1)S(1)} %fold.28.refs_0_.refs_2_), custom_call_target="tpu_custom_call" | custom-call | flops 10000000000 | bytes 100000000 | tf_op jit(solution)/shard_map/step/pallas_call | solution.py:77
  51.4 2.7 %collective-permute-done.14.got_ref = f32[128,384]{1,0:T(8,128)S(1)} collective-permute-done((f32[128,384]{1,0:T(8,128)S(1)}, f32[128,384]{1,0:T(8,128)S(1)}, u32[]{:S(2)}, u32[]{:S(2)}) %collective-permute-start.14) | collective-permute-done | bytes 196640 | tf_op jit(solution)/shard_map/ppermute | solution.py:227
  54.1 4.4 %step.6 = (f32[32,128,256]{2,1,0:T(8,128)S(1)}, bf16[384,8192]{1,0:T(8,128)(2,1)S(1)}) custom-call(s32[1]{0:T(128)} %bitcast.me_ref, bf16[1664,8192]{1,0:T(8,128)(2,1)} %weight_ref.7, bf16[128,384]{1,0:T(8,128)(2,1)S(1)} %fold.29.refs_0_.refs_3_, bf16[384,8192]{1,0:T(8,128)(2,1)S(1)} %get-tuple-element.35.refs_0_.refs_1_, ...), custom_call_target="tpu_custom_call" | custom-call | flops 10000000000 | bytes 100000000 | tf_op jit(solution)/shard_map/step/pallas_call | solution.py:77
  58.6 4.9 %step.7 = (f32[32,128,256]{2,1,0:T(8,128)S(1)}, bf16[512,8192]{1,0:T(8,128)(2,1)S(1)}) custom-call(s32[1]{0:T(128)} %bitcast.me_ref, bf16[1664,8192]{1,0:T(8,128)(2,1)} %weight_ref.7, bf16[128,384]{1,0:T(8,128)(2,1)S(1)} %fold.30.refs_0_.refs_3_, bf16[384,8192]{1,0:T(8,128)(2,1)S(1)} %get-tuple-element.37.refs_0_.refs_1_, ...), custom_call_target="tpu_custom_call" | custom-call | flops 10000000000 | bytes 100000000 | tf_op jit(solution)/shard_map/step/pallas_call | solution.py:77
  63.5 0.5 product.4.refs_0_
  63.9 0.5 product.5.refs_0_.own_ref
  64.4 0.1 collective-permute-start.17
  64.5 0.5 product.6.refs_0_
  64.9 0.6 collective-permute-start.16
  65.5 0.4 product.7.refs_0_.own_ref
  66.0 1.2 %collective-permute-done.17.got_ref = f32[8,128,256]{2,1,0:T(8,128)S(1)} collective-permute-done((f32[8,128,256]{2,1,0:T(8,128)S(1)}, f32[8,128,256]{2,1,0:T(8,128)S(1)}, u32[]{:S(2)}, u32[]{:S(2)}) %collective-permute-start.17) | collective-permute-done | bytes 1048608 | tf_op jit(solution)/shard_map/ppermute | solution.py:227
  67.1 0.1 halve.10
  67.2 0.3 collective-permute-start.19
  67.6 4.2 %collective-permute-start.25 = (f32[4,64,256]{2,1,0:T(8,128)S(1)}, f32[4,64,256]{2,1,0:T(8,128)S(1)}, u32[]{:S(2)}, u32[]{:S(2)}) collective-permute-start(f32[4,64,256]{2,1,0:T(8,128)S(1)} %get-tuple-element.41.refs_0_), channel_id=1, source_target_pairs={{0,8},{1,9},{2,10},{3,11},{4,12},{5,13},{6,14},{7,15},{8,0},{9,1},... | collective-permute-start | bytes 786440 | tf_op jit(solution)/shard_map/ppermute | solution.py:227
  71.8 0.2 halve.11
  72.0 0.1 collective-permute-start.21
  72.1 0.4 collective-permute-start.18
  72.5 3.9 %collective-permute-done.19.got_ref = f32[4,64,256]{2,1,0:T(8,128)S(1)} collective-permute-done((f32[4,64,256]{2,1,0:T(8,128)S(1)}, f32[4,64,256]{2,1,0:T(8,128)S(1)}, u32[]{:S(2)}, u32[]{:S(2)}) %collective-permute-start.19) | collective-permute-done | bytes 262176 | tf_op jit(solution)/shard_map/ppermute | solution.py:227
  76.5 2.1 %collective-permute-start.20 = (f32[2,64,256]{2,1,0:T(8,128)S(1)}, f32[2,64,256]{2,1,0:T(8,128)S(1)}, u32[]{:S(2)}, u32[]{:S(2)}) collective-permute-start(f32[2,64,256]{2,1,0:T(8,128)S(1)} %get-tuple-element.47.refs_0_), channel_id=1, source_target_pairs={{0,4},{1,5},{2,6},{3,7},{4,0},{5,1},{6,2},{7,3},{8,12},{9,13},{10,... | collective-permute-start | bytes 393224 | tf_op jit(solution)/shard_map/ppermute | solution.py:227
  78.6 8.2 %collective-permute-done.21.got_ref = f32[4,64,256]{2,1,0:T(8,128)S(1)} collective-permute-done((f32[4,64,256]{2,1,0:T(8,128)S(1)}, f32[4,64,256]{2,1,0:T(8,128)S(1)}, u32[]{:S(2)}, u32[]{:S(2)}) %collective-permute-start.21) | collective-permute-done | bytes 262176 | tf_op jit(solution)/shard_map/ppermute | solution.py:227
  86.8 0.1 collective-permute-start.24
  86.9 1.3 %collective-permute-done.20.got_ref = f32[2,64,256]{2,1,0:T(8,128)S(1)} collective-permute-done((f32[2,64,256]{2,1,0:T(8,128)S(1)}, f32[2,64,256]{2,1,0:T(8,128)S(1)}, u32[]{:S(2)}, u32[]{:S(2)}) %collective-permute-start.20) | collective-permute-done | bytes 131104 | tf_op jit(solution)/shard_map/ppermute | solution.py:227
  88.2 0.1 collective-permute-start.23
  88.3 0.9 collective-permute-start.22
  89.2 0.7 collective-permute-start.28
  89.9 2.7 %collective-permute-done.24.got_ref = f32[2,64,256]{2,1,0:T(8,128)S(1)} collective-permute-done((f32[2,64,256]{2,1,0:T(8,128)S(1)}, f32[2,64,256]{2,1,0:T(8,128)S(1)}, u32[]{:S(2)}, u32[]{:S(2)}) %collective-permute-start.24) | collective-permute-done | bytes 131104 | tf_op jit(solution)/shard_map/ppermute | solution.py:227
  92.6 0.1 collective-permute-start.27
  92.7 2.3 %collective-permute-done.23.got_ref = f32[1,64,256]{2,1,0:T(8,128)S(1)} collective-permute-done((f32[1,64,256]{2,1,0:T(8,128)S(1)}, f32[1,64,256]{2,1,0:T(8,128)S(1)}, u32[]{:S(2)}, u32[]{:S(2)}) %collective-permute-start.23) | collective-permute-done | bytes 65568 | tf_op jit(solution)/shard_map/ppermute | solution.py:227
  95.1 1.5 %collective-permute-start.26 = (f32[1,64,256]{2,1,0:T(8,128)S(1)}, f32[1,64,256]{2,1,0:T(8,128)S(1)}, u32[]{:S(2)}, u32[]{:S(2)}) collective-permute-start(f32[1,64,256]{2,1,0:T(8,128)S(1)} %get-tuple-element.60.refs_0_), channel_id=1, source_target_pairs={{0,8},{1,9},{2,10},{3,11},{4,12},{5,13},{6,14},{7,15},{8,0},{9,1},... | collective-permute-start | bytes 196616 | tf_op jit(solution)/shard_map/ppermute | solution.py:227
  96.6 1.3 %collective-permute-start.29 = (f32[1,64,256]{2,1,0:T(8,128)S(1)}, f32[1,64,256]{2,1,0:T(8,128)S(1)}, u32[]{:S(2)}, u32[]{:S(2)}) collective-permute-start(f32[1,64,256]{2,1,0:T(8,128)S(1)} %get-tuple-element.63.refs_0_), channel_id=1, source_target_pairs={{0,4},{1,5},{2,6},{3,7},{4,0},{5,1},{6,2},{7,3},{8,12},{9,13},{10,... | collective-permute-start | bytes 196616 | tf_op jit(solution)/shard_map/ppermute | solution.py:227
  97.9 0.8 collective-permute-done.27.got_ref
  98.7 2.9 %collective-permute-done.29.got_ref = f32[1,64,256]{2,1,0:T(8,128)S(1)} collective-permute-done((f32[1,64,256]{2,1,0:T(8,128)S(1)}, f32[1,64,256]{2,1,0:T(8,128)S(1)}, u32[]{:S(2)}, u32[]{:S(2)}) %collective-permute-start.29) | collective-permute-done | bytes 65568 | tf_op jit(solution)/shard_map/ppermute | solution.py:227
  101.6 0.7 finish.7
  (42 shorter events, 0.7 us)
Async XLA Ops:
  0.0 1.0 copy-start
  1.0 0.7 copy-start.1
  2.9 18.5 %collective-permute-start.3 = (f32[128,384]{1,0:T(8,128)S(1)}, f32[128,384]{1,0:T(8,128)S(1)}, u32[]{:S(2)}, u32[]{:S(2)}) collective-permute-start(f32[128,384]{1,0:T(8,128)S(1)} %mix.4.refs_0_.own_ref), channel_id=1, source_target_pairs={{0,8},{1,9},{2,10},{3,11},{4,12},{5,13},{6,14},{7,15},{8,0},{9,1},... | collective-permute-start | bytes 589832 | tf_op jit(solution)/shard_map/ppermute | solution.py:227
  8.2 5.7 %collective-permute-start.1 = (f32[128,384]{1,0:T(8,128)S(1)}, f32[128,384]{1,0:T(8,128)S(1)}, u32[]{:S(2)}, u32[]{:S(2)}) collective-permute-start(f32[128,384]{1,0:T(8,128)S(1)} %mix.5.refs_0_.own_ref), channel_id=1, source_target_pairs={{0,1},{1,0},{2,3},{3,2},{4,5},{5,4},{6,7},{7,6},{8,9},{9,8},{10,11... | collective-permute-start | bytes 589832 | tf_op jit(solution)/shard_map/ppermute | solution.py:227
  9.5 11.9 %collective-permute-start.4 = (f32[128,384]{1,0:T(8,128)S(1)}, f32[128,384]{1,0:T(8,128)S(1)}, u32[]{:S(2)}, u32[]{:S(2)}) collective-permute-start(f32[128,384]{1,0:T(8,128)S(1)} %mix.6.refs_0_.own_ref), channel_id=1, source_target_pairs={{0,4},{1,5},{2,6},{3,7},{4,0},{5,1},{6,2},{7,3},{8,12},{9,13},{10,... | collective-permute-start | bytes 589832 | tf_op jit(solution)/shard_map/ppermute | solution.py:227
  12.3 8.5 %collective-permute-start = (f32[128,512]{1,0:T(8,128)S(1)}, f32[128,512]{1,0:T(8,128)S(1)}, u32[]{:S(2)}, u32[]{:S(2)}) collective-permute-start(f32[128,512]{1,0:T(8,128)S(1)} %mix.7.refs_0_.own_ref), channel_id=1, source_target_pairs={{0,2},{1,3},{2,0},{3,1},{4,6},{5,7},{6,4},{7,5},{8,10},{9,11},{10,... | collective-permute-start | bytes 786440 | tf_op jit(solution)/shard_map/ppermute | solution.py:227
  14.0 21.9 %collective-permute-start.8 = (f32[128,384]{1,0:T(8,128)S(1)}, f32[128,384]{1,0:T(8,128)S(1)}, u32[]{:S(2)}, u32[]{:S(2)}) collective-permute-start(f32[128,384]{1,0:T(8,128)S(1)} %fold.16.refs_0_.own_ref), channel_id=1, source_target_pairs={{0,8},{1,9},{2,10},{3,11},{4,12},{5,13},{6,14},{7,15},{8,0},{9,1},... | collective-permute-start | bytes 589832 | tf_op jit(solution)/shard_map/ppermute | solution.py:227
  20.9 14.8 %collective-permute-start.2 = (f32[128,512]{1,0:T(8,128)S(1)}, f32[128,512]{1,0:T(8,128)S(1)}, u32[]{:S(2)}, u32[]{:S(2)}) collective-permute-start(f32[128,512]{1,0:T(8,128)S(1)} %fold.17.refs_0_.own_ref), channel_id=1, source_target_pairs={{0,4},{1,5},{2,6},{3,7},{4,0},{5,1},{6,2},{7,3},{8,12},{9,13},{10,... | collective-permute-start | bytes 786440 | tf_op jit(solution)/shard_map/ppermute | solution.py:227
  21.4 1.7 %collective-permute-start.6 = (f32[128,384]{1,0:T(8,128)S(1)}, f32[128,384]{1,0:T(8,128)S(1)}, u32[]{:S(2)}, u32[]{:S(2)}) collective-permute-start(f32[128,384]{1,0:T(8,128)S(1)} %fold.18.refs_0_.own_ref), channel_id=1, source_target_pairs={{0,1},{1,0},{2,3},{3,2},{4,5},{5,4},{6,7},{7,6},{8,9},{9,8},{10,11... | collective-permute-start | bytes 589832 | tf_op jit(solution)/shard_map/ppermute | solution.py:227
  21.5 7.4 %collective-permute-start.5 = (f32[128,384]{1,0:T(8,128)S(1)}, f32[128,384]{1,0:T(8,128)S(1)}, u32[]{:S(2)}, u32[]{:S(2)}) collective-permute-start(f32[128,384]{1,0:T(8,128)S(1)} %fold.19.refs_0_.own_ref), channel_id=1, source_target_pairs={{0,2},{1,3},{2,0},{3,1},{4,6},{5,7},{6,4},{7,5},{8,10},{9,11},{10,... | collective-permute-start | bytes 589832 | tf_op jit(solution)/shard_map/ppermute | solution.py:227
  23.2 23.6 %collective-permute-start.12 = (f32[128,384]{1,0:T(8,128)S(1)}, f32[128,384]{1,0:T(8,128)S(1)}, u32[]{:S(2)}, u32[]{:S(2)}) collective-permute-start(f32[128,384]{1,0:T(8,128)S(1)} %fold.20.refs_0_.own_ref), channel_id=1, source_target_pairs={{0,8},{1,9},{2,10},{3,11},{4,12},{5,13},{6,14},{7,15},{8,0},{9,1},... | collective-permute-start | bytes 589832 | tf_op jit(solution)/shard_map/ppermute | solution.py:227
  28.9 14.4 %collective-permute-start.13 = (f32[128,384]{1,0:T(8,128)S(1)}, f32[128,384]{1,0:T(8,128)S(1)}, u32[]{:S(2)}, u32[]{:S(2)}) collective-permute-start(f32[128,384]{1,0:T(8,128)S(1)} %fold.21.refs_0_.own_ref), channel_id=1, source_target_pairs={{0,4},{1,5},{2,6},{3,7},{4,0},{5,1},{6,2},{7,3},{8,12},{9,13},{10,... | collective-permute-start | bytes 589832 | tf_op jit(solution)/shard_map/ppermute | solution.py:227
  35.7 1.6 %collective-permute-start.7 = (f32[128,512]{1,0:T(8,128)S(1)}, f32[128,512]{1,0:T(8,128)S(1)}, u32[]{:S(2)}, u32[]{:S(2)}) collective-permute-start(f32[128,512]{1,0:T(8,128)S(1)} %fold.22.refs_0_.own_ref), channel_id=1, source_target_pairs={{0,1},{1,0},{2,3},{3,2},{4,5},{5,4},{6,7},{7,6},{8,9},{9,8},{10,11... | collective-permute-start | bytes 786440 | tf_op jit(solution)/shard_map/ppermute | solution.py:227
  35.8 7.4 %collective-permute-start.10 = (f32[128,384]{1,0:T(8,128)S(1)}, f32[128,384]{1,0:T(8,128)S(1)}, u32[]{:S(2)}, u32[]{:S(2)}) collective-permute-start(f32[128,384]{1,0:T(8,128)S(1)} %fold.23.refs_0_.own_ref), channel_id=1, source_target_pairs={{0,2},{1,3},{2,0},{3,1},{4,6},{5,7},{6,4},{7,5},{8,10},{9,11},{10,... | collective-permute-start | bytes 589832 | tf_op jit(solution)/shard_map/ppermute | solution.py:227
  37.4 26.1 %collective-permute-start.9 = (f32[128,512]{1,0:T(8,128)S(1)}, f32[128,512]{1,0:T(8,128)S(1)}, u32[]{:S(2)}, u32[]{:S(2)}) collective-permute-start(f32[128,512]{1,0:T(8,128)S(1)} %fold.24.refs_0_.own_ref), channel_id=1, source_target_pairs={{0,8},{1,9},{2,10},{3,11},{4,12},{5,13},{6,14},{7,15},{8,0},{9,1},... | collective-permute-start | bytes 786440 | tf_op jit(solution)/shard_map/ppermute | solution.py:227
  43.2 15.3 %collective-permute-start.11 = (f32[128,384]{1,0:T(8,128)S(1)}, f32[128,384]{1,0:T(8,128)S(1)}, u32[]{:S(2)}, u32[]{:S(2)}) collective-permute-start(f32[128,384]{1,0:T(8,128)S(1)} %fold.25.refs_0_.own_ref), channel_id=1, source_target_pairs={{0,4},{1,5},{2,6},{3,7},{4,0},{5,1},{6,2},{7,3},{8,12},{9,13},{10,... | collective-permute-start | bytes 589832 | tf_op jit(solution)/shard_map/ppermute | solution.py:227
  43.4 3.8 %collective-permute-start.15 = (f32[128,384]{1,0:T(8,128)S(1)}, f32[128,384]{1,0:T(8,128)S(1)}, u32[]{:S(2)}, u32[]{:S(2)}) collective-permute-start(f32[128,384]{1,0:T(8,128)S(1)} %fold.26.refs_0_.own_ref), channel_id=1, source_target_pairs={{0,1},{1,0},{2,3},{3,2},{4,5},{5,4},{6,7},{7,6},{8,9},{9,8},{10,11... | collective-permute-start | bytes 589832 | tf_op jit(solution)/shard_map/ppermute | solution.py:227
  46.7 7.4 %collective-permute-start.14 = (f32[128,384]{1,0:T(8,128)S(1)}, f32[128,384]{1,0:T(8,128)S(1)}, u32[]{:S(2)}, u32[]{:S(2)}) collective-permute-start(f32[128,384]{1,0:T(8,128)S(1)} %fold.27.refs_0_.own_ref), channel_id=1, source_target_pairs={{0,2},{1,3},{2,0},{3,1},{4,6},{5,7},{6,4},{7,5},{8,10},{9,11},{10,... | collective-permute-start | bytes 589832 | tf_op jit(solution)/shard_map/ppermute | solution.py:227
  64.4 2.7 %collective-permute-start.17 = (f32[8,128,256]{2,1,0:T(8,128)S(1)}, f32[8,128,256]{2,1,0:T(8,128)S(1)}, u32[]{:S(2)}, u32[]{:S(2)}) collective-permute-start(f32[8,128,256]{2,1,0:T(8,128)S(1)} %product.4.refs_0_), channel_id=1, source_target_pairs={{0,1},{1,0},{2,3},{3,2},{4,5},{5,4},{6,7},{7,6},{8,9},{9,8},{10,11... | collective-permute-start | bytes 3145736 | tf_op jit(solution)/shard_map/ppermute | solution.py:227
  64.9 6.9 %collective-permute-start.16 = (f32[8,128,256]{2,1,0:T(8,128)S(1)}, f32[8,128,256]{2,1,0:T(8,128)S(1)}, u32[]{:S(2)}, u32[]{:S(2)}) collective-permute-start(f32[8,128,256]{2,1,0:T(8,128)S(1)} %product.6.refs_0_), channel_id=1, source_target_pairs={{0,1},{1,0},{2,3},{3,2},{4,5},{5,4},{6,7},{7,6},{8,9},{9,8},{10,11... | collective-permute-start | bytes 3145736 | tf_op jit(solution)/shard_map/ppermute | solution.py:227
  67.2 9.2 %collective-permute-start.19 = (f32[4,64,256]{2,1,0:T(8,128)S(1)}, f32[4,64,256]{2,1,0:T(8,128)S(1)}, u32[]{:S(2)}, u32[]{:S(2)}) collective-permute-start(f32[4,64,256]{2,1,0:T(8,128)S(1)} %get-tuple-element.45), channel_id=1, source_target_pairs={{0,2},{1,3},{2,0},{3,1},{4,6},{5,7},{6,4},{7,5},{8,10},{9,11},{10,... | collective-permute-start | bytes 786440 | tf_op jit(solution)/shard_map/ppermute | solution.py:227
  67.6 21.6 %collective-permute-start.25 = (f32[4,64,256]{2,1,0:T(8,128)S(1)}, f32[4,64,256]{2,1,0:T(8,128)S(1)}, u32[]{:S(2)}, u32[]{:S(2)}) collective-permute-start(f32[4,64,256]{2,1,0:T(8,128)S(1)} %get-tuple-element.41.refs_0_), channel_id=1, source_target_pairs={{0,8},{1,9},{2,10},{3,11},{4,12},{5,13},{6,14},{7,15},{8,0},{9,1},... | collective-permute-start | bytes 786440 | tf_op jit(solution)/shard_map/ppermute | solution.py:227
  72.0 14.8 %collective-permute-start.21 = (f32[4,64,256]{2,1,0:T(8,128)S(1)}, f32[4,64,256]{2,1,0:T(8,128)S(1)}, u32[]{:S(2)}, u32[]{:S(2)}) collective-permute-start(f32[4,64,256]{2,1,0:T(8,128)S(1)} %get-tuple-element.49), channel_id=1, source_target_pairs={{0,4},{1,5},{2,6},{3,7},{4,0},{5,1},{6,2},{7,3},{8,12},{9,13},{10,... | collective-permute-start | bytes 786440 | tf_op jit(solution)/shard_map/ppermute | solution.py:227
  72.1 16.2 %collective-permute-start.18 = (f32[4,64,256]{2,1,0:T(8,128)S(1)}, f32[4,64,256]{2,1,0:T(8,128)S(1)}, u32[]{:S(2)}, u32[]{:S(2)}) collective-permute-start(f32[4,64,256]{2,1,0:T(8,128)S(1)} %get-tuple-element.43.refs_0_), channel_id=1, source_target_pairs={{0,2},{1,3},{2,0},{3,1},{4,6},{5,7},{6,4},{7,5},{8,10},{9,11},{10,... | collective-permute-start | bytes 786440 | tf_op jit(solution)/shard_map/ppermute | solution.py:227
  76.5 11.7 %collective-permute-start.20 = (f32[2,64,256]{2,1,0:T(8,128)S(1)}, f32[2,64,256]{2,1,0:T(8,128)S(1)}, u32[]{:S(2)}, u32[]{:S(2)}) collective-permute-start(f32[2,64,256]{2,1,0:T(8,128)S(1)} %get-tuple-element.47.refs_0_), channel_id=1, source_target_pairs={{0,4},{1,5},{2,6},{3,7},{4,0},{5,1},{6,2},{7,3},{8,12},{9,13},{10,... | collective-permute-start | bytes 393224 | tf_op jit(solution)/shard_map/ppermute | solution.py:227
  86.8 5.8 %collective-permute-start.24 = (f32[2,64,256]{2,1,0:T(8,128)S(1)}, f32[2,64,256]{2,1,0:T(8,128)S(1)}, u32[]{:S(2)}, u32[]{:S(2)}) collective-permute-start(f32[2,64,256]{2,1,0:T(8,128)S(1)} %get-tuple-element.50.refs_0_), channel_id=1, source_target_pairs={{0,2},{1,3},{2,0},{3,1},{4,6},{5,7},{6,4},{7,5},{8,10},{9,11},{10,... | collective-permute-start | bytes 393224 | tf_op jit(solution)/shard_map/ppermute | solution.py:227
  88.2 6.8 %collective-permute-start.23 = (f32[1,64,256]{2,1,0:T(8,128)S(1)}, f32[1,64,256]{2,1,0:T(8,128)S(1)}, u32[]{:S(2)}, u32[]{:S(2)}) collective-permute-start(f32[1,64,256]{2,1,0:T(8,128)S(1)} %get-tuple-element.51.refs_0_), channel_id=1, source_target_pairs={{0,8},{1,9},{2,10},{3,11},{4,12},{5,13},{6,14},{7,15},{8,0},{9,1},... | collective-permute-start | bytes 196616 | tf_op jit(solution)/shard_map/ppermute | solution.py:227
  88.3 6.7 %collective-permute-start.22 = (f32[2,64,256]{2,1,0:T(8,128)S(1)}, f32[2,64,256]{2,1,0:T(8,128)S(1)}, u32[]{:S(2)}, u32[]{:S(2)}) collective-permute-start(f32[2,64,256]{2,1,0:T(8,128)S(1)} %get-tuple-element.53.refs_0_), channel_id=1, source_target_pairs={{0,4},{1,5},{2,6},{3,7},{4,0},{5,1},{6,2},{7,3},{8,12},{9,13},{10,... | collective-permute-start | bytes 393224 | tf_op jit(solution)/shard_map/ppermute | solution.py:227
  89.2 7.3 %collective-permute-start.28 = (f32[2,64,256]{2,1,0:T(8,128)S(1)}, f32[2,64,256]{2,1,0:T(8,128)S(1)}, u32[]{:S(2)}, u32[]{:S(2)}) collective-permute-start(f32[2,64,256]{2,1,0:T(8,128)S(1)} %get-tuple-element.57.refs_0_), channel_id=1, source_target_pairs={{0,2},{1,3},{2,0},{3,1},{4,6},{5,7},{6,4},{7,5},{8,10},{9,11},{10,... | collective-permute-start | bytes 393224 | tf_op jit(solution)/shard_map/ppermute | solution.py:227
  92.6 6.0 %collective-permute-start.27 = (f32[1,64,256]{2,1,0:T(8,128)S(1)}, f32[1,64,256]{2,1,0:T(8,128)S(1)}, u32[]{:S(2)}, u32[]{:S(2)}) collective-permute-start(f32[1,64,256]{2,1,0:T(8,128)S(1)} %get-tuple-element.58.refs_0_), channel_id=1, source_target_pairs={{0,8},{1,9},{2,10},{3,11},{4,12},{5,13},{6,14},{7,15},{8,0},{9,1},... | collective-permute-start | bytes 196616 | tf_op jit(solution)/shard_map/ppermute | solution.py:227
  95.1 6.5 %collective-permute-start.26 = (f32[1,64,256]{2,1,0:T(8,128)S(1)}, f32[1,64,256]{2,1,0:T(8,128)S(1)}, u32[]{:S(2)}, u32[]{:S(2)}) collective-permute-start(f32[1,64,256]{2,1,0:T(8,128)S(1)} %get-tuple-element.60.refs_0_), channel_id=1, source_target_pairs={{0,8},{1,9},{2,10},{3,11},{4,12},{5,13},{6,14},{7,15},{8,0},{9,1},... | collective-permute-start | bytes 196616 | tf_op jit(solution)/shard_map/ppermute | solution.py:227
  96.6 5.0 %collective-permute-start.29 = (f32[1,64,256]{2,1,0:T(8,128)S(1)}, f32[1,64,256]{2,1,0:T(8,128)S(1)}, u32[]{:S(2)}, u32[]{:S(2)}) collective-permute-start(f32[1,64,256]{2,1,0:T(8,128)S(1)} %get-tuple-element.63.refs_0_), channel_id=1, source_target_pairs={{0,4},{1,5},{2,6},{3,7},{4,0},{5,1},{6,2},{7,3},{8,12},{9,13},{10,... | collective-permute-start | bytes 196616 | tf_op jit(solution)/shard_map/ppermute | solution.py:227

commit v4 on v3

--- a/solution.py
+++ b/solution.py
@@ -106,70 +106,80 @@
     return call("fold", kernel, (me, own, got), (SMEM, VMEM, VMEM), shape, after)
 
 
-def gather(me, weight, rows, distances, width, columns, sems):
-    parts = 1 + max(part for _, part in distances)
-    copies = []
-    for i, (distance, part) in enumerate(distances):
-        column = pl.multiple_of(((distance ^ me) * parts + part) * width, LANES)
-        copies.append(
-            pltpu.make_async_copy(
-                weight.at[rows[0]:rows[1], pl.ds(column, width)], columns.at[:, pl.ds(i * width, width)], sems.at[i]
+def load(me, weight, rows, after, limit, distances=(), share=0):
+    begin, end = rows
+
+    def kernel(me_ref, weight_ref, *refs):
+        out, mark, sems = refs[-3:]
+        copies = []
+        if not distances:
+            copies.append(pltpu.make_async_copy(weight_ref.at[begin:end, :], out, sems.at[0]))
+        for i, distance in enumerate(distances):
+            column = pl.multiple_of((distance ^ me_ref[0]) * share, LANES)
+            copies.append(
+                pltpu.make_async_copy(
+                    weight_ref.at[begin:end, pl.ds(column, share)], out.at[:, pl.ds(i * share, share)], sems.at[i]
+                )
             )
-        )
-    return copies
-
-
-def step(me, chunk, columns, total, weight, rows, distances, width, after):
-    blocks = len(distances)
-    values = [] if chunk is None else [chunk, columns] + ([] if total is None else [total])
-    wide = max(width, min(1024, blocks * width))
-
-    def kernel(me_ref, weight_ref, *refs):
-        refs, sems = refs[:-1], refs[-1]
-        loaded = refs[-1]
-        copies = gather(me_ref[0], weight_ref, rows, distances, width, loaded, sems)
         for copy in copies:
             copy.start()
-        if chunk is not None:
-            out = refs[-2]
-            for at in range(0, blocks * width, wide):
-                sums = jnp.dot(refs[0][...], refs[1][:, at:at + wide], preferred_element_type=F32)
-                for i in range(wide // width):
-                    term = sums[:, i * width:(i + 1) * width]
-                    out[at // width + i] = term if total is None else refs[2][at // width + i] + term
+        mark[...] = jnp.zeros_like(mark)
         for copy in copies:
             copy.wait()
 
-    shapes = [jax.ShapeDtypeStruct((rows[1] - rows[0], blocks * width), BF16)]
-    if chunk is not None:
-        shapes.insert(0, jax.ShapeDtypeStruct((blocks, chunk.shape[0], width), F32))
-    outs = call(
-        "step",
+    shapes = [
+        jax.ShapeDtypeStruct((end - begin, weight.shape[1]), BF16),
+        jax.ShapeDtypeStruct((8, LANES), F32),
+    ]
+    return call(
+        "load",
         kernel,
-        (me, weight, *values),
-        [SMEM, pl.BlockSpec(memory_space=pltpu.HBM)] + [VMEM] * len(values),
+        (me, weight),
+        (SMEM, pl.BlockSpec(memory_space=pltpu.HBM)),
         shapes,
         after,
-        [pltpu.SemaphoreType.DMA((blocks,))],
-        40 if chunk is None else 28,
+        [pltpu.SemaphoreType.DMA((max(1, len(distances)),))],
+        limit,
     )
-    return (None, *outs) if chunk is None else outs
-
-
-def product(chunk, columns, total, begin, end, after):
-    width = total.shape[2]
-    wide = max(width, min(1024, (end - begin) * width))
-
-    def kernel(chunk_ref, columns_ref, total_ref, *refs):
+
+
+def step(chunk, columns, total, shards, after):
+    tokens = chunk.shape[0]
+    share = columns.shape[1] // shards
+    group = max(1, 1024 // share)
+    values = [chunk, columns] + ([] if total is None else [total])
+
+    def kernel(*refs):
         out = refs[-1]
-        for at in range(begin * width, end * width, wide):
-            sums = jnp.dot(chunk_ref[...], columns_ref[:, at:at + wide], preferred_element_type=F32)
-            for i in range(wide // width):
-                block = at // width + i
-                out[block - begin] = total_ref[block] + sums[:, i * width:(i + 1) * width]
-
-    shape = jax.ShapeDtypeStruct((end - begin, chunk.shape[0], width), F32)
-    return call("product", kernel, (chunk, columns, total), [VMEM] * 3, shape, after)
+        for at in range(0, shards, group):
+            sums = jnp.dot(refs[0][...], refs[1][:, at * share:(at + group) * share], preferred_element_type=F32)
+            for i in range(group):
+                term = sums[:, i * share:(i + 1) * share]
+                out[at + i] = term if total is None else refs[2][at + i] + term
+
+    shape = jax.ShapeDtypeStruct((shards, tokens, share), F32)
+    return call("step", kernel, values, [VMEM] * len(values), shape, after)
+
+
+def product(me, chunk, columns, total, begin, distances, parts, after):
+    share = total.shape[2]
+    width = share // parts
+    group = max(1, min(len(distances), 1024 // share))
+
+    def kernel(me_ref, chunk_ref, columns_ref, total_ref, *refs):
+        outs = refs[-parts:]
+        for at in range(0, len(distances), group):
+            start = (begin + at) * share
+            sums = jnp.dot(
+                chunk_ref[...], columns_ref[:, start:start + group * share], preferred_element_type=F32
+            )
+            for i in range(group):
+                value = total_ref[distances[at + i] ^ me_ref[0]] + sums[:, i * share:(i + 1) * share]
+                for part in range(parts):
+                    outs[part][at + i] = value[:, part * width:(part + 1) * width]
+
+    shapes = [jax.ShapeDtypeStruct((len(distances), chunk.shape[0], width), F32)] * parts
+    return call("product", kernel, (me, chunk, columns, total), [SMEM] + [VMEM] * 3, shapes, after)
 
 
 def halve(own, got, distances, plans, after):
@@ -233,8 +243,7 @@
     parts = 2 if share % (2 * LANES) == 0 else 1
     width = share // parts
     near = [d for d in range(shards) if not d & bits[0]]
-    groups = [(part, kept) for part in range(parts) for kept in (False, True)]
-    distances = [(d | (0 if kept else bits[0]), part) for part, kept in groups for d in near]
+    distances = [d | bits[0] for d in near] + near
 
     tiles = -(-local // LANES)
     count = max(1, min(len(bits), tiles))
@@ -251,15 +260,20 @@
     events.sort()
     final = [c for phase, _, c in events if phase == len(bits) - 1]
     total = None
+    loaded = []
+    room = 40 * 2**20
+    places = [0] * (count - count // 2) + [len(events) - count] * (count // 2)
     for number, (phase, bit, c) in enumerate(events):
         got = swap(chunks[c], bit)
         last = phase == len(bits) - 1
         chunks[c] = ran(fold(me, chunks[c], got, bit, after, factor if last else None))
-        if number == len(events) - count - 2:
-            _, columns = ran(step(me, None, None, None, down_weight, spans[final[0]], distances, width, after))
         if last and c != final[-1]:
-            rows = spans[final[final.index(c) + 1]]
-            total, columns = ran(step(me, chunks[c], columns, total, down_weight, rows, distances, width, after))
+            total = ran(step(chunks[c], loaded[final.index(c)], total, shards, after))
+        while len(loaded) < count and number == places[len(loaded)]:
+            rows = spans[final[len(loaded)]]
+            wanted = (distances, share) if len(loaded) == count - 1 else ()
+            loaded.append(ran(load(me, down_weight, rows, after, room // 2**20, *wanted))[0])
+            room -= loaded[-1].size * 2
 
     inner = bits[1:]
     late = inner[-1:] + inner[:-1]
@@ -299,16 +313,19 @@
         held = pieces + [(rows, part, None)] if last else []
         pieces.append((rows, part, ran(finish(held, keep, got, tokens, width, parts, after))))
 
-    for at, (part, kept) in enumerate(groups):
-        begin, end = at * len(near), (at + 1) * len(near)
-        x = ran(product(chunks[final[-1]], columns, total, begin, end, after))
-        clock += 0.6
-        kernels += 1
-        if not kept:
-            send(x, bits[0], None)
-        else:
-            when, _, got, _ = queue.pop()
-            queue.append((when, kernels - 1, got, functools.partial(split, part, 0, routes[part], near, x)))
+    last_chunk = chunks[final[-1]]
+    sends = ran(product(me, last_chunk, loaded[-1], total, 0, distances[:len(near)], parts, after))
+    clock += 0.9
+    kernels += 1
+    for x in sends:
+        send(x, bits[0], None)
+    keeps = ran(product(me, last_chunk, loaded[-1], total, len(near), near, parts, after))
+    clock += 0.9
+    kernels += 1
+    queue[:] = [
+        (when, at, got, functools.partial(split, part, 0, routes[part], near, keeps[part]))
+        for part, (when, at, got, _) in enumerate(queue)
+    ]
     while queue:
         item = min(queue, key=lambda item: item[0])
         queue.remove(item)

time: 102 us -> 93.8 us (0.920)
  waiting for transfers between devices: 49.5 us -> 37.4 us
  starting transfers between devices: 25.8 us -> 30.2 us
  Pallas kernels: 24.8 us -> 23.7 us
    ppermute x30, waiting for transfers between devices: 49.5 us -> 37.4 us  [swap(): return lax.ppermute(x, 'tensor', [(d, d ^ bit) for d in range(shards)])]
    ppermute x30, starting transfers between devices: 25.8 us -> 30.2 us  [swap(): return lax.ppermute(x, 'tensor', [(d, d ^ bit) for d in range(shards)])]
    pallas_call x42 -> x43, Pallas kernels: 24.8 us -> 23.7 us  [call(): pl.pallas_call(kernel, out_shape=shapes, in_specs=list(specs) + [UNREAD]...]
  transfers between devices with their start and end apart: 30 -> 30, of which waited for: 14 -> 15; matrix products, arithmetic and copies ran while one was open for 0% -> 0% of each run, Pallas kernels for 22% -> 23%
where the time goes in v4:
time: 93.8 us; the launch traced here: 93.5 us
  waiting for transfers between devices  37.4 us (40%)
  starting transfers between devices  30.2 us (32%)
  Pallas kernels  23.7 us (25%)
  local copies, waits for them, and re-layouts  1.75 us (2%)
    ppermute x30, waiting for transfers between devices, swap(): return lax.ppermute(x, 'tensor', [(d, d ^ bit) for d in range(shards)])  37.4 us
    ppermute x30, starting transfers between devices, swap(): return lax.ppermute(x, 'tensor', [(d, d ^ bit) for d in range(shards)])  30.2 us
    pallas_call x43, Pallas kernels, call(): pl.pallas_call(kernel, out_shape=shapes, in_specs=list(specs) + [UNREAD]...  23.7 us
  transfers between devices with their start and end apart: 30, of which 15 were waited for; matrix products, arithmetic and copies ran while one was open for 0% of the time, Pallas kernels for 23%

profile of v4, /device:TPU:0, one launch (start us, length us, event | category | flops | bytes accessed | tf_op | source)
XLA Modules:
  0.0 93.5 jit_solution(7918615891524949726)
XLA Ops:
  0.0 1.0 %copy-done = bf16[128,1664]{1,0:T(8,128)(2,1)S(1)} copy-done((bf16[128,1664]{1,0:T(8,128)(2,1)S(1)}, bf16[128,1664]{1,0:T(8,128)(2,1)}, u32[]{:S(2)}) %copy-start) | copy-done | bytes 426008
  1.0 0.7 copy-done.1
  1.8 1.2 %mix.4.refs_0_.own_ref = f32[128,384]{1,0:T(8,128)S(1)} custom-call(bf16[128,1664]{1,0:T(8,128)(2,1)S(1)} %copy-done, f32[52,52]{1,0:T(8,128)S(1)} %copy-done.1), custom_call_target="tpu_custom_call" | custom-call | flops 10000000000 | bytes 100000000 | tf_op jit(solution)/shard_map/mix/pallas_call | solution.py:77
  2.9 4.1 %collective-permute-start.3 = (f32[128,384]{1,0:T(8,128)S(1)}, f32[128,384]{1,0:T(8,128)S(1)}, u32[]{:S(2)}, u32[]{:S(2)}) collective-permute-start(f32[128,384]{1,0:T(8,128)S(1)} %mix.4.refs_0_.own_ref), channel_id=1, source_target_pairs={{0,8},{1,9},{2,10},{3,11},{4,12},{5,13},{6,14},{7,15},{8,0},{9,1},... | collective-permute-start | bytes 589832 | tf_op jit(solution)/shard_map/ppermute | solution.py:237
  7.0 1.2 %mix.5.refs_0_.own_ref = f32[128,384]{1,0:T(8,128)S(1)} custom-call(bf16[128,1664]{1,0:T(8,128)(2,1)S(1)} %copy-done, f32[52,52]{1,0:T(8,128)S(1)} %copy-done.1, f32[128,384]{1,0:T(8,128)S(1)} %mix.4.refs_0_.own_ref), custom_call_target="tpu_custom_call" | custom-call | flops 10000000000 | bytes 100000000 | tf_op jit(solution)/shard_map/mix/pallas_call | solution.py:77
  8.2 0.1 collective-permute-start.1
  8.3 1.2 %mix.6.refs_0_.own_ref = f32[128,384]{1,0:T(8,128)S(1)} custom-call(bf16[128,1664]{1,0:T(8,128)(2,1)S(1)} %copy-done, f32[52,52]{1,0:T(8,128)S(1)} %copy-done.1, f32[128,384]{1,0:T(8,128)S(1)} %mix.5.refs_0_.own_ref), custom_call_target="tpu_custom_call" | custom-call | flops 10000000000 | bytes 100000000 | tf_op jit(solution)/shard_map/mix/pallas_call | solution.py:77
  9.5 1.6 %collective-permute-start.4 = (f32[128,384]{1,0:T(8,128)S(1)}, f32[128,384]{1,0:T(8,128)S(1)}, u32[]{:S(2)}, u32[]{:S(2)}) collective-permute-start(f32[128,384]{1,0:T(8,128)S(1)} %mix.6.refs_0_.own_ref), channel_id=1, source_target_pairs={{0,4},{1,5},{2,6},{3,7},{4,0},{5,1},{6,2},{7,3},{8,12},{9,13},{10,... | collective-permute-start | bytes 589832 | tf_op jit(solution)/shard_map/ppermute | solution.py:237
  11.2 1.2 %mix.7.refs_0_.own_ref = f32[128,512]{1,0:T(8,128)S(1)} custom-call(bf16[128,1664]{1,0:T(8,128)(2,1)S(1)} %copy-done, f32[52,52]{1,0:T(8,128)S(1)} %copy-done.1, f32[128,384]{1,0:T(8,128)S(1)} %mix.6.refs_0_.own_ref), custom_call_target="tpu_custom_call" | custom-call | flops 10000000000 | bytes 100000000 | tf_op jit(solution)/shard_map/mix/pallas_call | solution.py:77
  12.3 1.6 %collective-permute-start = (f32[128,512]{1,0:T(8,128)S(1)}, f32[128,512]{1,0:T(8,128)S(1)}, u32[]{:S(2)}, u32[]{:S(2)}) collective-permute-start(f32[128,512]{1,0:T(8,128)S(1)} %mix.7.refs_0_.own_ref), channel_id=1, source_target_pairs={{0,2},{1,3},{2,0},{3,1},{4,6},{5,7},{6,4},{7,5},{8,10},{9,11},{10,... | collective-permute-start | bytes 786440 | tf_op jit(solution)/shard_map/ppermute | solution.py:237
  13.9 0.0 collective-permute-done.1.got_ref
  14.0 0.4 collective-permute-start.8
  14.4 2.8 %load.4 = (bf16[384,8192]{1,0:T(8,128)(2,1)S(1)}, f32[8,128]{1,0:T(8,128)S(1)}) custom-call(s32[1]{0:T(128)} %bitcast.me_ref, bf16[1664,8192]{1,0:T(8,128)(2,1)} %weight_ref.7, f32[128,384]{1,0:T(8,128)S(1)} %fold.16.refs_0_.own_ref), custom_call_target="tpu_custom_call" | custom-call | flops 10000000000 | bytes 100000000 | tf_op jit(solution)/shard_map/load/pallas_call | solution.py:77
  17.2 2.8 %load.5 = (bf16[384,8192]{1,0:T(8,128)(2,1)S(1)}, f32[8,128]{1,0:T(8,128)S(1)}) custom-call(s32[1]{0:T(128)} %bitcast.me_ref, bf16[1664,8192]{1,0:T(8,128)(2,1)} %weight_ref.7, f32[8,128]{1,0:T(8,128)S(1)} %get-tuple-element.41.refs_0_), custom_call_target="tpu_custom_call" | custom-call | flops 10000000000 | bytes 100000000 | tf_op jit(solution)/shard_map/load/pallas_call | solution.py:77
  20.0 0.9 collective-permute-done.got_ref
  20.9 0.5 collective-permute-start.2
  21.4 0.1 collective-permute-start.6
  21.5 1.6 %collective-permute-start.5 = (f32[128,384]{1,0:T(8,128)S(1)}, f32[128,384]{1,0:T(8,128)S(1)}, u32[]{:S(2)}, u32[]{:S(2)}) collective-permute-start(f32[128,384]{1,0:T(8,128)S(1)} %fold.19.refs_0_.own_ref), channel_id=1, source_target_pairs={{0,2},{1,3},{2,0},{3,1},{4,6},{5,7},{6,4},{7,5},{8,10},{9,11},{10,... | collective-permute-start | bytes 589832 | tf_op jit(solution)/shard_map/ppermute | solution.py:237
  23.2 1.6 %collective-permute-start.12 = (f32[128,384]{1,0:T(8,128)S(1)}, f32[128,384]{1,0:T(8,128)S(1)}, u32[]{:S(2)}, u32[]{:S(2)}) collective-permute-start(f32[128,384]{1,0:T(8,128)S(1)} %fold.20.refs_0_.own_ref), channel_id=1, source_target_pairs={{0,8},{1,9},{2,10},{3,11},{4,12},{5,13},{6,14},{7,15},{8,0},{9,1},... | collective-permute-start | bytes 589832 | tf_op jit(solution)/shard_map/ppermute | solution.py:237
  24.8 4.1 %collective-permute-done.5.got_ref = f32[128,384]{1,0:T(8,128)S(1)} collective-permute-done((f32[128,384]{1,0:T(8,128)S(1)}, f32[128,384]{1,0:T(8,128)S(1)}, u32[]{:S(2)}, u32[]{:S(2)}) %collective-permute-start.5) | collective-permute-done | bytes 196640 | tf_op jit(solution)/shard_map/ppermute | solution.py:237
  28.9 1.6 %collective-permute-start.13 = (f32[128,384]{1,0:T(8,128)S(1)}, f32[128,384]{1,0:T(8,128)S(1)}, u32[]{:S(2)}, u32[]{:S(2)}) collective-permute-start(f32[128,384]{1,0:T(8,128)S(1)} %fold.21.refs_0_.own_ref), channel_id=1, source_target_pairs={{0,4},{1,5},{2,6},{3,7},{4,0},{5,1},{6,2},{7,3},{8,12},{9,13},{10,... | collective-permute-start | bytes 589832 | tf_op jit(solution)/shard_map/ppermute | solution.py:237
  30.6 5.1 %collective-permute-done.2.got_ref = f32[128,512]{1,0:T(8,128)S(1)} collective-permute-done((f32[128,512]{1,0:T(8,128)S(1)}, f32[128,512]{1,0:T(8,128)S(1)}, u32[]{:S(2)}, u32[]{:S(2)}) %collective-permute-start.2) | collective-permute-done | bytes 262176 | tf_op jit(solution)/shard_map/ppermute | solution.py:237
  35.7 0.1 collective-permute-start.7
  35.8 0.1 collective-permute-start.10
  35.9 1.4 %collective-permute-done.7.got_ref = f32[128,512]{1,0:T(8,128)S(1)} collective-permute-done((f32[128,512]{1,0:T(8,128)S(1)}, f32[128,512]{1,0:T(8,128)S(1)}, u32[]{:S(2)}, u32[]{:S(2)}) %collective-permute-start.7) | collective-permute-done | bytes 262176 | tf_op jit(solution)/shard_map/ppermute | solution.py:237
  37.4 0.7 collective-permute-start.9
  38.1 5.1 %collective-permute-done.10.got_ref = f32[128,384]{1,0:T(8,128)S(1)} collective-permute-done((f32[128,384]{1,0:T(8,128)S(1)}, f32[128,384]{1,0:T(8,128)S(1)}, u32[]{:S(2)}, u32[]{:S(2)}) %collective-permute-start.10) | collective-permute-done | bytes 196640 | tf_op jit(solution)/shard_map/ppermute | solution.py:237
  43.2 0.1 collective-permute-start.11
  43.4 0.1 collective-permute-start.15
  43.5 0.4 collective-permute-start.14
  43.8 1.0 %collective-permute-done.15.got_ref = f32[128,384]{1,0:T(8,128)S(1)} collective-permute-done((f32[128,384]{1,0:T(8,128)S(1)}, f32[128,384]{1,0:T(8,128)S(1)}, u32[]{:S(2)}, u32[]{:S(2)}) %collective-permute-start.15) | collective-permute-done | bytes 196640 | tf_op jit(solution)/shard_map/ppermute | solution.py:237
  44.9 1.3 %step.3.refs_0_.refs_2_ = f32[16,128,512]{2,1,0:T(8,128)S(1)} custom-call(bf16[128,384]{1,0:T(8,128)(2,1)S(1)} %fold.28.refs_0_.refs_2_, bf16[384,8192]{1,0:T(8,128)(2,1)S(1)} %get-tuple-element.43.refs_1_, bf16[128,384]{1,0:T(8,128)(2,1)S(1)} %fold.28.refs_0_.refs_2_), custom_call_target="tpu_custom_call" | custom-call | flops 10000000000 | bytes 100000000 | tf_op jit(solution)/shard_map/step/pallas_call | solution.py:77
  46.2 2.8 %load.6 = (bf16[384,8192]{1,0:T(8,128)(2,1)S(1)}, f32[8,128]{1,0:T(8,128)S(1)}) custom-call(s32[1]{0:T(128)} %bitcast.me_ref, bf16[1664,8192]{1,0:T(8,128)(2,1)} %weight_ref.7, f32[16,128,512]{2,1,0:T(8,128)S(1)} %step.3.refs_0_.refs_2_), custom_call_target="tpu_custom_call" | custom-call | flops 10000000000 | bytes 100000000 | tf_op jit(solution)/shard_map/load/pallas_call | solution.py:77
  49.0 3.6 %load.7 = (bf16[512,8192]{1,0:T(8,128)(2,1)S(1)}, f32[8,128]{1,0:T(8,128)S(1)}) custom-call(s32[1]{0:T(128)} %bitcast.me_ref, bf16[1664,8192]{1,0:T(8,128)(2,1)} %weight_ref.7, f32[8,128]{1,0:T(8,128)S(1)} %get-tuple-element.44.refs_0_), custom_call_target="tpu_custom_call" | custom-call | flops 10000000000 | bytes 100000000 | tf_op jit(solution)/shard_map/load/pallas_call | solution.py:77
  52.6 1.3 %step.4.refs_0_.refs_2_ = f32[16,128,512]{2,1,0:T(8,128)S(1)} custom-call(bf16[128,384]{1,0:T(8,128)(2,1)S(1)} %fold.29.refs_0_.refs_3_, bf16[384,8192]{1,0:T(8,128)(2,1)S(1)} %get-tuple-element.46.refs_1_, f32[16,128,512]{2,1,0:T(8,128)S(1)} %step.3.refs_0_.refs_2_, bf16[128,384]{1,0:T(8,128)(2,1)S(1)} %fold.29.refs_0_.refs_3_), custom_call_target="tpu_custom_call" | custom-call | flops 10000000000 | bytes 100000000 | tf_op jit(solution)/shard_map/step/pallas_call | solution.py:77
  53.9 1.4 %collective-permute-done.11.got_ref = f32[128,384]{1,0:T(8,128)S(1)} collective-permute-done((f32[128,384]{1,0:T(8,128)S(1)}, f32[128,384]{1,0:T(8,128)S(1)}, u32[]{:S(2)}, u32[]{:S(2)}) %collective-permute-start.11) | collective-permute-done | bytes 196640 | tf_op jit(solution)/shard_map/ppermute | solution.py:237
  55.3 1.3 %step.5.refs_0_.total_ref = f32[16,128,512]{2,1,0:T(8,128)S(1)} custom-call(bf16[128,384]{1,0:T(8,128)(2,1)S(1)} %fold.30.refs_0_.refs_3_, bf16[384,8192]{1,0:T(8,128)(2,1)S(1)} %get-tuple-element.47.refs_1_, f32[16,128,512]{2,1,0:T(8,128)S(1)} %step.4.refs_0_.refs_2_, bf16[128,384]{1,0:T(8,128)(2,1)S(1)} %fold.30.refs_0_.refs_3_), custom_call_target="tpu_custom_call" | custom-call | flops 10000000000 | bytes 100000000 | tf_op jit(solution)/shard_map/step/pallas_call | solution.py:77
  56.8 0.8 product.2
  57.6 0.1 collective-permute-start.17
  57.6 0.5 collective-permute-start.16
  58.1 0.8 product.3
  58.9 1.3 %collective-permute-done.17.got_ref = f32[8,128,256]{2,1,0:T(8,128)S(1)} collective-permute-done((f32[8,128,256]{2,1,0:T(8,128)S(1)}, f32[8,128,256]{2,1,0:T(8,128)S(1)}, u32[]{:S(2)}, u32[]{:S(2)}) %collective-permute-start.17) | collective-permute-done | bytes 1048608 | tf_op jit(solution)/shard_map/ppermute | solution.py:237
  60.3 0.1 halve.10
  60.4 0.1 collective-permute-start.19
  60.5 3.1 %collective-permute-start.25 = (f32[4,64,256]{2,1,0:T(8,128)S(1)}, f32[4,64,256]{2,1,0:T(8,128)S(1)}, u32[]{:S(2)}, u32[]{:S(2)}) collective-permute-start(f32[4,64,256]{2,1,0:T(8,128)S(1)} %get-tuple-element.53.refs_0_), channel_id=1, source_target_pairs={{0,8},{1,9},{2,10},{3,11},{4,12},{5,13},{6,14},{7,15},{8,0},{9,1},... | collective-permute-start | bytes 786440 | tf_op jit(solution)/shard_map/ppermute | solution.py:237
  63.6 0.1 halve.11
  63.7 1.2 %collective-permute-start.21 = (f32[4,64,256]{2,1,0:T(8,128)S(1)}, f32[4,64,256]{2,1,0:T(8,128)S(1)}, u32[]{:S(2)}, u32[]{:S(2)}) collective-permute-start(f32[4,64,256]{2,1,0:T(8,128)S(1)} %get-tuple-element.61), channel_id=1, source_target_pairs={{0,4},{1,5},{2,6},{3,7},{4,0},{5,1},{6,2},{7,3},{8,12},{9,13},{10,... | collective-permute-start | bytes 786440 | tf_op jit(solution)/shard_map/ppermute | solution.py:237
  64.9 0.7 collective-permute-start.18
  65.6 4.0 %collective-permute-done.19.got_ref = f32[4,64,256]{2,1,0:T(8,128)S(1)} collective-permute-done((f32[4,64,256]{2,1,0:T(8,128)S(1)}, f32[4,64,256]{2,1,0:T(8,128)S(1)}, u32[]{:S(2)}, u32[]{:S(2)}) %collective-permute-start.19) | collective-permute-done | bytes 262176 | tf_op jit(solution)/shard_map/ppermute | solution.py:237
  69.6 0.7 collective-permute-start.20
  70.3 7.4 %collective-permute-done.21.got_ref = f32[4,64,256]{2,1,0:T(8,128)S(1)} collective-permute-done((f32[4,64,256]{2,1,0:T(8,128)S(1)}, f32[4,64,256]{2,1,0:T(8,128)S(1)}, u32[]{:S(2)}, u32[]{:S(2)}) %collective-permute-start.21) | collective-permute-done | bytes 262176 | tf_op jit(solution)/shard_map/ppermute | solution.py:237
  77.7 1.4 %collective-permute-start.24 = (f32[2,64,256]{2,1,0:T(8,128)S(1)}, f32[2,64,256]{2,1,0:T(8,128)S(1)}, u32[]{:S(2)}, u32[]{:S(2)}) collective-permute-start(f32[2,64,256]{2,1,0:T(8,128)S(1)} %get-tuple-element.62.refs_0_), channel_id=1, source_target_pairs={{0,2},{1,3},{2,0},{3,1},{4,6},{5,7},{6,4},{7,5},{8,10},{9,11},{10,... | collective-permute-start | bytes 393224 | tf_op jit(solution)/shard_map/ppermute | solution.py:237
  79.2 0.2 collective-permute-done.20.got_ref
  79.4 0.2 collective-permute-start.23
  79.6 2.2 %collective-permute-start.22 = (f32[2,64,256]{2,1,0:T(8,128)S(1)}, f32[2,64,256]{2,1,0:T(8,128)S(1)}, u32[]{:S(2)}, u32[]{:S(2)}) collective-permute-start(f32[2,64,256]{2,1,0:T(8,128)S(1)} %get-tuple-element.65.refs_0_), channel_id=1, source_target_pairs={{0,4},{1,5},{2,6},{3,7},{4,0},{5,1},{6,2},{7,3},{8,12},{9,13},{10,... | collective-permute-start | bytes 393224 | tf_op jit(solution)/shard_map/ppermute | solution.py:237
  81.9 1.2 %collective-permute-start.28 = (f32[2,64,256]{2,1,0:T(8,128)S(1)}, f32[2,64,256]{2,1,0:T(8,128)S(1)}, u32[]{:S(2)}, u32[]{:S(2)}) collective-permute-start(f32[2,64,256]{2,1,0:T(8,128)S(1)} %get-tuple-element.69.refs_0_), channel_id=1, source_target_pairs={{0,2},{1,3},{2,0},{3,1},{4,6},{5,7},{6,4},{7,5},{8,10},{9,11},{10,... | collective-permute-start | bytes 393224 | tf_op jit(solution)/shard_map/ppermute | solution.py:237
  83.1 1.1 %collective-permute-start.27 = (f32[1,64,256]{2,1,0:T(8,128)S(1)}, f32[1,64,256]{2,1,0:T(8,128)S(1)}, u32[]{:S(2)}, u32[]{:S(2)}) collective-permute-start(f32[1,64,256]{2,1,0:T(8,128)S(1)} %get-tuple-element.70.refs_0_), channel_id=1, source_target_pairs={{0,8},{1,9},{2,10},{3,11},{4,12},{5,13},{6,14},{7,15},{8,0},{9,1},... | collective-permute-start | bytes 196616 | tf_op jit(solution)/shard_map/ppermute | solution.py:237
  84.2 1.1 %collective-permute-done.23.got_ref = f32[1,64,256]{2,1,0:T(8,128)S(1)} collective-permute-done((f32[1,64,256]{2,1,0:T(8,128)S(1)}, f32[1,64,256]{2,1,0:T(8,128)S(1)}, u32[]{:S(2)}, u32[]{:S(2)}) %collective-permute-start.23) | collective-permute-done | bytes 65568 | tf_op jit(solution)/shard_map/ppermute | solution.py:237
  85.3 1.2 %collective-permute-done.22.got_ref = f32[2,64,256]{2,1,0:T(8,128)S(1)} collective-permute-done((f32[2,64,256]{2,1,0:T(8,128)S(1)}, f32[2,64,256]{2,1,0:T(8,128)S(1)}, u32[]{:S(2)}, u32[]{:S(2)}) %collective-permute-start.22) | collective-permute-done | bytes 131104 | tf_op jit(solution)/shard_map/ppermute | solution.py:237
  86.5 1.5 %collective-permute-start.26 = (f32[1,64,256]{2,1,0:T(8,128)S(1)}, f32[1,64,256]{2,1,0:T(8,128)S(1)}, u32[]{:S(2)}, u32[]{:S(2)}) collective-permute-start(f32[1,64,256]{2,1,0:T(8,128)S(1)} %get-tuple-element.72.refs_0_), channel_id=1, source_target_pairs={{0,8},{1,9},{2,10},{3,11},{4,12},{5,13},{6,14},{7,15},{8,0},{9,1},... | collective-permute-start | bytes 196616 | tf_op jit(solution)/shard_map/ppermute | solution.py:237
  88.1 1.6 %collective-permute-start.29 = (f32[1,64,256]{2,1,0:T(8,128)S(1)}, f32[1,64,256]{2,1,0:T(8,128)S(1)}, u32[]{:S(2)}, u32[]{:S(2)}) collective-permute-start(f32[1,64,256]{2,1,0:T(8,128)S(1)} %get-tuple-element.75.refs_0_), channel_id=1, source_target_pairs={{0,4},{1,5},{2,6},{3,7},{4,0},{5,1},{6,2},{7,3},{8,12},{9,13},{10,... | collective-permute-start | bytes 196616 | tf_op jit(solution)/shard_map/ppermute | solution.py:237
  89.7 0.4 collective-permute-done.27.got_ref
  90.1 2.6 %collective-permute-done.29.got_ref = f32[1,64,256]{2,1,0:T(8,128)S(1)} collective-permute-done((f32[1,64,256]{2,1,0:T(8,128)S(1)}, f32[1,64,256]{2,1,0:T(8,128)S(1)}, u32[]{:S(2)}, u32[]{:S(2)}) %collective-permute-start.29) | collective-permute-done | bytes 65568 | tf_op jit(solution)/shard_map/ppermute | solution.py:237
  92.8 0.7 finish.7
  (43 shorter events, 0.7 us)
Async XLA Ops:
  0.0 1.0 %copy-start = (bf16[128,1664]{1,0:T(8,128)(2,1)S(1)}, bf16[128,1664]{1,0:T(8,128)(2,1)}, u32[]{:S(2)}) copy-start(bf16[128,1664]{1,0:T(8,128)(2,1)} %activations.7) | copy-start | bytes 1277956
  1.0 0.7 copy-start.1
  2.9 18.5 %collective-permute-start.3 = (f32[128,384]{1,0:T(8,128)S(1)}, f32[128,384]{1,0:T(8,128)S(1)}, u32[]{:S(2)}, u32[]{:S(2)}) collective-permute-start(f32[128,384]{1,0:T(8,128)S(1)} %mix.4.refs_0_.own_ref), channel_id=1, source_target_pairs={{0,8},{1,9},{2,10},{3,11},{4,12},{5,13},{6,14},{7,15},{8,0},{9,1},... | collective-permute-start | bytes 589832 | tf_op jit(solution)/shard_map/ppermute | solution.py:237
  8.2 5.7 %collective-permute-start.1 = (f32[128,384]{1,0:T(8,128)S(1)}, f32[128,384]{1,0:T(8,128)S(1)}, u32[]{:S(2)}, u32[]{:S(2)}) collective-permute-start(f32[128,384]{1,0:T(8,128)S(1)} %mix.5.refs_0_.own_ref), channel_id=1, source_target_pairs={{0,1},{1,0},{2,3},{3,2},{4,5},{5,4},{6,7},{7,6},{8,9},{9,8},{10,11... | collective-permute-start | bytes 589832 | tf_op jit(solution)/shard_map/ppermute | solution.py:237
  9.5 11.9 %collective-permute-start.4 = (f32[128,384]{1,0:T(8,128)S(1)}, f32[128,384]{1,0:T(8,128)S(1)}, u32[]{:S(2)}, u32[]{:S(2)}) collective-permute-start(f32[128,384]{1,0:T(8,128)S(1)} %mix.6.refs_0_.own_ref), channel_id=1, source_target_pairs={{0,4},{1,5},{2,6},{3,7},{4,0},{5,1},{6,2},{7,3},{8,12},{9,13},{10,... | collective-permute-start | bytes 589832 | tf_op jit(solution)/shard_map/ppermute | solution.py:237
  12.3 8.5 %collective-permute-start = (f32[128,512]{1,0:T(8,128)S(1)}, f32[128,512]{1,0:T(8,128)S(1)}, u32[]{:S(2)}, u32[]{:S(2)}) collective-permute-start(f32[128,512]{1,0:T(8,128)S(1)} %mix.7.refs_0_.own_ref), channel_id=1, source_target_pairs={{0,2},{1,3},{2,0},{3,1},{4,6},{5,7},{6,4},{7,5},{8,10},{9,11},{10,... | collective-permute-start | bytes 786440 | tf_op jit(solution)/shard_map/ppermute | solution.py:237
  14.0 21.9 %collective-permute-start.8 = (f32[128,384]{1,0:T(8,128)S(1)}, f32[128,384]{1,0:T(8,128)S(1)}, u32[]{:S(2)}, u32[]{:S(2)}) collective-permute-start(f32[128,384]{1,0:T(8,128)S(1)} %fold.16.refs_0_.own_ref), channel_id=1, source_target_pairs={{0,8},{1,9},{2,10},{3,11},{4,12},{5,13},{6,14},{7,15},{8,0},{9,1},... | collective-permute-start | bytes 589832 | tf_op jit(solution)/shard_map/ppermute | solution.py:237
  20.9 14.8 %collective-permute-start.2 = (f32[128,512]{1,0:T(8,128)S(1)}, f32[128,512]{1,0:T(8,128)S(1)}, u32[]{:S(2)}, u32[]{:S(2)}) collective-permute-start(f32[128,512]{1,0:T(8,128)S(1)} %fold.17.refs_0_.own_ref), channel_id=1, source_target_pairs={{0,4},{1,5},{2,6},{3,7},{4,0},{5,1},{6,2},{7,3},{8,12},{9,13},{10,... | collective-permute-start | bytes 786440 | tf_op jit(solution)/shard_map/ppermute | solution.py:237
  21.4 1.7 %collective-permute-start.6 = (f32[128,384]{1,0:T(8,128)S(1)}, f32[128,384]{1,0:T(8,128)S(1)}, u32[]{:S(2)}, u32[]{:S(2)}) collective-permute-start(f32[128,384]{1,0:T(8,128)S(1)} %fold.18.refs_0_.own_ref), channel_id=1, source_target_pairs={{0,1},{1,0},{2,3},{3,2},{4,5},{5,4},{6,7},{7,6},{8,9},{9,8},{10,11... | collective-permute-start | bytes 589832 | tf_op jit(solution)/shard_map/ppermute | solution.py:237
  21.5 7.4 %collective-permute-start.5 = (f32[128,384]{1,0:T(8,128)S(1)}, f32[128,384]{1,0:T(8,128)S(1)}, u32[]{:S(2)}, u32[]{:S(2)}) collective-permute-start(f32[128,384]{1,0:T(8,128)S(1)} %fold.19.refs_0_.own_ref), channel_id=1, source_target_pairs={{0,2},{1,3},{2,0},{3,1},{4,6},{5,7},{6,4},{7,5},{8,10},{9,11},{10,... | collective-permute-start | bytes 589832 | tf_op jit(solution)/shard_map/ppermute | solution.py:237
  23.2 20.3 %collective-permute-start.12 = (f32[128,384]{1,0:T(8,128)S(1)}, f32[128,384]{1,0:T(8,128)S(1)}, u32[]{:S(2)}, u32[]{:S(2)}) collective-permute-start(f32[128,384]{1,0:T(8,128)S(1)} %fold.20.refs_0_.own_ref), channel_id=1, source_target_pairs={{0,8},{1,9},{2,10},{3,11},{4,12},{5,13},{6,14},{7,15},{8,0},{9,1},... | collective-permute-start | bytes 589832 | tf_op jit(solution)/shard_map/ppermute | solution.py:237
  28.9 14.4 %collective-permute-start.13 = (f32[128,384]{1,0:T(8,128)S(1)}, f32[128,384]{1,0:T(8,128)S(1)}, u32[]{:S(2)}, u32[]{:S(2)}) collective-permute-start(f32[128,384]{1,0:T(8,128)S(1)} %fold.21.refs_0_.own_ref), channel_id=1, source_target_pairs={{0,4},{1,5},{2,6},{3,7},{4,0},{5,1},{6,2},{7,3},{8,12},{9,13},{10,... | collective-permute-start | bytes 589832 | tf_op jit(solution)/shard_map/ppermute | solution.py:237
  35.7 1.6 %collective-permute-start.7 = (f32[128,512]{1,0:T(8,128)S(1)}, f32[128,512]{1,0:T(8,128)S(1)}, u32[]{:S(2)}, u32[]{:S(2)}) collective-permute-start(f32[128,512]{1,0:T(8,128)S(1)} %fold.22.refs_0_.own_ref), channel_id=1, source_target_pairs={{0,1},{1,0},{2,3},{3,2},{4,5},{5,4},{6,7},{7,6},{8,9},{9,8},{10,11... | collective-permute-start | bytes 786440 | tf_op jit(solution)/shard_map/ppermute | solution.py:237
  35.8 7.4 %collective-permute-start.10 = (f32[128,384]{1,0:T(8,128)S(1)}, f32[128,384]{1,0:T(8,128)S(1)}, u32[]{:S(2)}, u32[]{:S(2)}) collective-permute-start(f32[128,384]{1,0:T(8,128)S(1)} %fold.23.refs_0_.own_ref), channel_id=1, source_target_pairs={{0,2},{1,3},{2,0},{3,1},{4,6},{5,7},{6,4},{7,5},{8,10},{9,11},{10,... | collective-permute-start | bytes 589832 | tf_op jit(solution)/shard_map/ppermute | solution.py:237
  37.4 19.3 %collective-permute-start.9 = (f32[128,512]{1,0:T(8,128)S(1)}, f32[128,512]{1,0:T(8,128)S(1)}, u32[]{:S(2)}, u32[]{:S(2)}) collective-permute-start(f32[128,512]{1,0:T(8,128)S(1)} %fold.24.refs_0_.own_ref), channel_id=1, source_target_pairs={{0,8},{1,9},{2,10},{3,11},{4,12},{5,13},{6,14},{7,15},{8,0},{9,1},... | collective-permute-start | bytes 786440 | tf_op jit(solution)/shard_map/ppermute | solution.py:237
  43.2 12.1 %collective-permute-start.11 = (f32[128,384]{1,0:T(8,128)S(1)}, f32[128,384]{1,0:T(8,128)S(1)}, u32[]{:S(2)}, u32[]{:S(2)}) collective-permute-start(f32[128,384]{1,0:T(8,128)S(1)} %fold.25.refs_0_.own_ref), channel_id=1, source_target_pairs={{0,4},{1,5},{2,6},{3,7},{4,0},{5,1},{6,2},{7,3},{8,12},{9,13},{10,... | collective-permute-start | bytes 589832 | tf_op jit(solution)/shard_map/ppermute | solution.py:237
  43.4 1.5 %collective-permute-start.15 = (f32[128,384]{1,0:T(8,128)S(1)}, f32[128,384]{1,0:T(8,128)S(1)}, u32[]{:S(2)}, u32[]{:S(2)}) collective-permute-start(f32[128,384]{1,0:T(8,128)S(1)} %fold.26.refs_0_.own_ref), channel_id=1, source_target_pairs={{0,1},{1,0},{2,3},{3,2},{4,5},{5,4},{6,7},{7,6},{8,9},{9,8},{10,11... | collective-permute-start | bytes 589832 | tf_op jit(solution)/shard_map/ppermute | solution.py:237
  43.5 9.1 %collective-permute-start.14 = (f32[128,384]{1,0:T(8,128)S(1)}, f32[128,384]{1,0:T(8,128)S(1)}, u32[]{:S(2)}, u32[]{:S(2)}) collective-permute-start(f32[128,384]{1,0:T(8,128)S(1)} %fold.27.refs_0_.own_ref), channel_id=1, source_target_pairs={{0,2},{1,3},{2,0},{3,1},{4,6},{5,7},{6,4},{7,5},{8,10},{9,11},{10,... | collective-permute-start | bytes 589832 | tf_op jit(solution)/shard_map/ppermute | solution.py:237
  57.6 2.7 %collective-permute-start.17 = (f32[8,128,256]{2,1,0:T(8,128)S(1)}, f32[8,128,256]{2,1,0:T(8,128)S(1)}, u32[]{:S(2)}, u32[]{:S(2)}) collective-permute-start(f32[8,128,256]{2,1,0:T(8,128)S(1)} %get-tuple-element.52), channel_id=1, source_target_pairs={{0,1},{1,0},{2,3},{3,2},{4,5},{5,4},{6,7},{7,6},{8,9},{9,8},{10,11... | collective-permute-start | bytes 3145736 | tf_op jit(solution)/shard_map/ppermute | solution.py:237
  57.6 6.0 %collective-permute-start.16 = (f32[8,128,256]{2,1,0:T(8,128)S(1)}, f32[8,128,256]{2,1,0:T(8,128)S(1)}, u32[]{:S(2)}, u32[]{:S(2)}) collective-permute-start(f32[8,128,256]{2,1,0:T(8,128)S(1)} %get-tuple-element.49.refs_0_), channel_id=1, source_target_pairs={{0,1},{1,0},{2,3},{3,2},{4,5},{5,4},{6,7},{7,6},{8,9},{9,8},{10,11... | collective-permute-start | bytes 3145736 | tf_op jit(solution)/shard_map/ppermute | solution.py:237
  60.4 9.2 %collective-permute-start.19 = (f32[4,64,256]{2,1,0:T(8,128)S(1)}, f32[4,64,256]{2,1,0:T(8,128)S(1)}, u32[]{:S(2)}, u32[]{:S(2)}) collective-permute-start(f32[4,64,256]{2,1,0:T(8,128)S(1)} %get-tuple-element.57), channel_id=1, source_target_pairs={{0,2},{1,3},{2,0},{3,1},{4,6},{5,7},{6,4},{7,5},{8,10},{9,11},{10,... | collective-permute-start | bytes 786440 | tf_op jit(solution)/shard_map/ppermute | solution.py:237
  60.5 21.3 %collective-permute-start.25 = (f32[4,64,256]{2,1,0:T(8,128)S(1)}, f32[4,64,256]{2,1,0:T(8,128)S(1)}, u32[]{:S(2)}, u32[]{:S(2)}) collective-permute-start(f32[4,64,256]{2,1,0:T(8,128)S(1)} %get-tuple-element.53.refs_0_), channel_id=1, source_target_pairs={{0,8},{1,9},{2,10},{3,11},{4,12},{5,13},{6,14},{7,15},{8,0},{9,1},... | collective-permute-start | bytes 786440 | tf_op jit(solution)/shard_map/ppermute | solution.py:237
  63.7 14.0 %collective-permute-start.21 = (f32[4,64,256]{2,1,0:T(8,128)S(1)}, f32[4,64,256]{2,1,0:T(8,128)S(1)}, u32[]{:S(2)}, u32[]{:S(2)}) collective-permute-start(f32[4,64,256]{2,1,0:T(8,128)S(1)} %get-tuple-element.61), channel_id=1, source_target_pairs={{0,4},{1,5},{2,6},{3,7},{4,0},{5,1},{6,2},{7,3},{8,12},{9,13},{10,... | collective-permute-start | bytes 786440 | tf_op jit(solution)/shard_map/ppermute | solution.py:237
  64.9 14.7 %collective-permute-start.18 = (f32[4,64,256]{2,1,0:T(8,128)S(1)}, f32[4,64,256]{2,1,0:T(8,128)S(1)}, u32[]{:S(2)}, u32[]{:S(2)}) collective-permute-start(f32[4,64,256]{2,1,0:T(8,128)S(1)} %get-tuple-element.55.refs_0_), channel_id=1, source_target_pairs={{0,2},{1,3},{2,0},{3,1},{4,6},{5,7},{6,4},{7,5},{8,10},{9,11},{10,... | collective-permute-start | bytes 786440 | tf_op jit(solution)/shard_map/ppermute | solution.py:237
  69.6 9.7 %collective-permute-start.20 = (f32[2,64,256]{2,1,0:T(8,128)S(1)}, f32[2,64,256]{2,1,0:T(8,128)S(1)}, u32[]{:S(2)}, u32[]{:S(2)}) collective-permute-start(f32[2,64,256]{2,1,0:T(8,128)S(1)} %get-tuple-element.59.refs_0_), channel_id=1, source_target_pairs={{0,4},{1,5},{2,6},{3,7},{4,0},{5,1},{6,2},{7,3},{8,12},{9,13},{10,... | collective-permute-start | bytes 393224 | tf_op jit(solution)/shard_map/ppermute | solution.py:237
  77.7 5.3 %collective-permute-start.24 = (f32[2,64,256]{2,1,0:T(8,128)S(1)}, f32[2,64,256]{2,1,0:T(8,128)S(1)}, u32[]{:S(2)}, u32[]{:S(2)}) collective-permute-start(f32[2,64,256]{2,1,0:T(8,128)S(1)} %get-tuple-element.62.refs_0_), channel_id=1, source_target_pairs={{0,2},{1,3},{2,0},{3,1},{4,6},{5,7},{6,4},{7,5},{8,10},{9,11},{10,... | collective-permute-start | bytes 393224 | tf_op jit(solution)/shard_map/ppermute | solution.py:237
  79.4 5.9 %collective-permute-start.23 = (f32[1,64,256]{2,1,0:T(8,128)S(1)}, f32[1,64,256]{2,1,0:T(8,128)S(1)}, u32[]{:S(2)}, u32[]{:S(2)}) collective-permute-start(f32[1,64,256]{2,1,0:T(8,128)S(1)} %get-tuple-element.63.refs_0_), channel_id=1, source_target_pairs={{0,8},{1,9},{2,10},{3,11},{4,12},{5,13},{6,14},{7,15},{8,0},{9,1},... | collective-permute-start | bytes 196616 | tf_op jit(solution)/shard_map/ppermute | solution.py:237
  79.6 6.9 %collective-permute-start.22 = (f32[2,64,256]{2,1,0:T(8,128)S(1)}, f32[2,64,256]{2,1,0:T(8,128)S(1)}, u32[]{:S(2)}, u32[]{:S(2)}) collective-permute-start(f32[2,64,256]{2,1,0:T(8,128)S(1)} %get-tuple-element.65.refs_0_), channel_id=1, source_target_pairs={{0,4},{1,5},{2,6},{3,7},{4,0},{5,1},{6,2},{7,3},{8,12},{9,13},{10,... | collective-permute-start | bytes 393224 | tf_op jit(solution)/shard_map/ppermute | solution.py:237
  81.9 6.2 %collective-permute-start.28 = (f32[2,64,256]{2,1,0:T(8,128)S(1)}, f32[2,64,256]{2,1,0:T(8,128)S(1)}, u32[]{:S(2)}, u32[]{:S(2)}) collective-permute-start(f32[2,64,256]{2,1,0:T(8,128)S(1)} %get-tuple-element.69.refs_0_), channel_id=1, source_target_pairs={{0,2},{1,3},{2,0},{3,1},{4,6},{5,7},{6,4},{7,5},{8,10},{9,11},{10,... | collective-permute-start | bytes 393224 | tf_op jit(solution)/shard_map/ppermute | solution.py:237
  83.1 7.0 %collective-permute-start.27 = (f32[1,64,256]{2,1,0:T(8,128)S(1)}, f32[1,64,256]{2,1,0:T(8,128)S(1)}, u32[]{:S(2)}, u32[]{:S(2)}) collective-permute-start(f32[1,64,256]{2,1,0:T(8,128)S(1)} %get-tuple-element.70.refs_0_), channel_id=1, source_target_pairs={{0,8},{1,9},{2,10},{3,11},{4,12},{5,13},{6,14},{7,15},{8,0},{9,1},... | collective-permute-start | bytes 196616 | tf_op jit(solution)/shard_map/ppermute | solution.py:237
  86.5 6.2 %collective-permute-start.26 = (f32[1,64,256]{2,1,0:T(8,128)S(1)}, f32[1,64,256]{2,1,0:T(8,128)S(1)}, u32[]{:S(2)}, u32[]{:S(2)}) collective-permute-start(f32[1,64,256]{2,1,0:T(8,128)S(1)} %get-tuple-element.72.refs_0_), channel_id=1, source_target_pairs={{0,8},{1,9},{2,10},{3,11},{4,12},{5,13},{6,14},{7,15},{8,0},{9,1},... | collective-permute-start | bytes 196616 | tf_op jit(solution)/shard_map/ppermute | solution.py:237
  88.1 4.6 %collective-permute-start.29 = (f32[1,64,256]{2,1,0:T(8,128)S(1)}, f32[1,64,256]{2,1,0:T(8,128)S(1)}, u32[]{:S(2)}, u32[]{:S(2)}) collective-permute-start(f32[1,64,256]{2,1,0:T(8,128)S(1)} %get-tuple-element.75.refs_0_), channel_id=1, source_target_pairs={{0,4},{1,5},{2,6},{3,7},{4,0},{5,1},{6,2},{7,3},{8,12},{9,13},{10,... | collective-permute-start | bytes 196616 | tf_op jit(solution)/shard_map/ppermute | solution.py:237

commit v5 on v4

--- a/solution.py
+++ b/solution.py
@@ -11,6 +11,13 @@
 LANES = 128
 F32 = jnp.float32
 BF16 = jnp.bfloat16
+
+
+TILES = (3, 3, 3, 4)
+ORDERS = ((3, 1, 2, 0), (0, 3, 1, 2), (2, 0, 3, 1), (1, 2, 0, 3))
+FIRST = (0, 2, 3, 1)
+PATIENCE = 1.8
+RULE = 1
 
 
 def quotient(index, divisor, limit):
@@ -222,6 +229,92 @@
     return call("finish", kernel, operands, [VMEM] * len(operands), jax.ShapeDtypeStruct(shape, BF16), after)
 
 
+class Links:
+    def __init__(self, bits):
+        self.bits = bits
+        self.taken = {bit: [] for bit in bits}
+
+    def needs(self, bit, size):
+        if bit == self.bits[0]:
+            return {bit: size * 8e-6}
+        if bit != self.bits[-1]:
+            return {bit: size * 80e-6}
+        return {bit: size * 160e-6, self.bits[-2]: size * 80e-6}
+
+    def free(self, bit, now):
+        share, until = 1.0, float("inf")
+        for begin, end, used in self.taken[bit]:
+            if begin <= now < end:
+                share -= used
+            if begin <= now < end or begin > now:
+                until = min(until, end if begin <= now else begin)
+        return max(share, 0.0), until
+
+    def send(self, bit, size, now):
+        needs = self.needs(bit, size)
+        now += 1.0
+        left = 1.0
+        spans = []
+        while left > 1e-6:
+            shares = [(self.free(link, now), need) for link, need in needs.items()]
+            rate = min(share / need for (share, _), need in shares)
+            until = min(until for (_, until), _ in shares)
+            if rate > 1e-6:
+                until = min(until, now + left / rate)
+                spans.append((now, until, rate))
+                left -= rate * (until - now)
+            now = until
+        for begin, end, rate in spans:
+            for link, need in needs.items():
+                self.taken[link].append((begin, end, rate * need))
+        return now + 0.3
+
+
+def plan(bits, tokens, sizes, orders, first, loads):
+    links = Links(bits)
+    clock = 1.8
+    flights = []
+    done = []
+    wait = list(first)
+    loads = list(loads)
+    missing = list(loads)
+
+    def start(c, stage):
+        nonlocal clock
+        clock += 0.9
+        flights.append((links.send(orders[c][stage], tokens * sizes[c], clock), len(done), c, stage))
+
+    while wait or flights:
+        flights.sort(key=lambda flight: (flight[3] if RULE else 0, flight))
+        arrival = flights[0][0] if flights else float("inf")
+        if wait and arrival > clock:
+            done.append(("mix", wait[0]))
+            clock += 1.2
+            start(wait.pop(0), 0)
+        elif loads and arrival - clock > PATIENCE:
+            done.append(("load", loads.pop(0)))
+            clock += 2.8
+        else:
+            _, began, c, stage = flights.pop(0)
+            if began == len(done):
+                done.append(("tick", c))
+            clock = max(clock, arrival) + 0.1
+            done.append(("fold", c))
+            if stage + 1 < len(bits):
+                start(c, stage + 1)
+            elif flights or wait:
+                if c in loads:
+                    loads.remove(c)
+                    done.append(("load", c))
+                    clock += 2.8
+                done.append(("step", c))
+                clock += 1.3
+            else:
+                done += [("load", c) for c in loads]
+                done.append(("last", c))
+    return done
+
+
 def body(activations, rotation_small, down_weight):
     shards = lax.axis_size("tensor")
     me = lax.axis_index("tensor").astype(jnp.int32).reshape(1)
@@ -246,34 +339,37 @@
     distances = [d | bits[0] for d in near] + near
 
     tiles = -(-local // LANES)
-    count = max(1, min(len(bits), tiles))
-    edges = [min(local, (tiles * c // count) * LANES) for c in range(count)] + [local]
+    ends = [round(tiles * sum(TILES[:c]) / sum(TILES)) for c in range(len(TILES) + 1)]
+    edges = [min(local, end * LANES) for end in ends]
+    assert all(begin < end for begin, end in zip(edges[:-1], edges[1:]))
     spans = list(zip(edges[:-1], edges[1:]))
-    chunks = []
-    for span in spans:
-        chunks.append(ran(mix(activations, rotation_small, (0, tokens), span, after)))
-    cycle = bits[-1:] + bits[1:-1] + bits[:1]
-    events = []
-    for phase in range(len(bits)):
-        for c in range(count):
-            events.append((phase, cycle[(phase - c) % len(bits)], c))
-    events.sort()
-    final = [c for phase, _, c in events if phase == len(bits) - 1]
+    sizes = [end - begin for begin, end in spans]
+    roles = [bits[:1], bits[1:-2], bits[-2:-1], bits[-1:]]
+    orders = [sum((roles[role] for role in order), []) for order in ORDERS]
+    first = FIRST
+    loads = [c for what, c in plan(bits, tokens, sizes, orders, first, ()) if what in ("step", "last")]
     total = None
-    loaded = []
+    loaded = {}
+    chunks = {}
+    stages = [0] * len(spans)
     room = 40 * 2**20
-    places = [0] * (count - count // 2) + [len(events) - count] * (count // 2)
-    for number, (phase, bit, c) in enumerate(events):
-        got = swap(chunks[c], bit)
-        last = phase == len(bits) - 1
-        chunks[c] = ran(fold(me, chunks[c], got, bit, after, factor if last else None))
-        if last and c != final[-1]:
-            total = ran(step(chunks[c], loaded[final.index(c)], total, shards, after))
-        while len(loaded) < count and number == places[len(loaded)]:
-            rows = spans[final[len(loaded)]]
-            wanted = (distances, share) if len(loaded) == count - 1 else ()
-            loaded.append(ran(load(me, down_weight, rows, after, room // 2**20, *wanted))[0])
-            room -= loaded[-1].size * 2
+    for what, c in plan(bits, tokens, sizes, orders, first, loads):
+        if what == "mix":
+            chunks[c] = ran(mix(activations, rotation_small, (0, tokens), spans[c], after))
+        elif what == "load":
+            wanted = (distances, share) if c == loads[-1] else ()
+            loaded[c] = ran(load(me, down_weight, spans[c], after, room // 2**20, *wanted))[0]
+            room -= loaded[c].size * 2
+        elif what == "fold":
+            bit = orders[c][stages[c]]
+            stages[c] += 1
+            got = swap(chunks[c], bit)
+            end = stages[c] == len(bits)
+            chunks[c] = ran(fold(me, chunks[c], got, bit, after, factor if end else None))
+        elif what == "tick":
+            ran(tick(after))
+        elif what == "step":
+            total = ran(step(chunks[c], loaded[c], total, shards, after))
 
     inner = bits[1:]
     late = inner[-1:] + inner[:-1]
@@ -283,7 +379,7 @@
         [((0, half), inner), ((half, tokens), late)],
         [((0, half), swapped), ((half, tokens), inner)],
     ][:parts]
-    free = dict.fromkeys(bits, 0.0)
+    links = Links(bits)
     clock = 0.0
     kernels = 0
     pieces = []
@@ -291,10 +387,8 @@
 
     def send(x, bit, use):
         nonlocal clock
-        clock += 0.7
-        micros = x.size * 4e-6 * (2 if bit == bits[0] else 40 if bit == bits[-1] else 20)
-        free[bit] = max(clock + 1.0, free[bit]) + micros
-        queue.append((free[bit] + 0.3, kernels, swap(x, bit), use))
+        clock += 0.9
+        queue.append((links.send(bit, x.size, clock), kernels, swap(x, bit), use))
 
     def split(part, stage, pieces_of, left, keep, got):
         base = pieces_of[0][0][0]
@@ -313,13 +407,13 @@
         held = pieces + [(rows, part, None)] if last else []
         pieces.append((rows, part, ran(finish(held, keep, got, tokens, width, parts, after))))
 
-    last_chunk = chunks[final[-1]]
-    sends = ran(product(me, last_chunk, loaded[-1], total, 0, distances[:len(near)], parts, after))
+    last_chunk, last_columns = chunks[loads[-1]], loaded[loads[-1]]
+    sends = ran(product(me, last_chunk, last_columns, total, 0, distances[:len(near)], parts, after))
     clock += 0.9
     kernels += 1
     for x in sends:
         send(x, bits[0], None)
-    keeps = ran(product(me, last_chunk, loaded[-1], total, len(near), near, parts, after))
+    keeps = ran(product(me, last_chunk, last_columns, total, len(near), near, parts, after))
     clock += 0.9
     kernels += 1
     queue[:] = [

time: 93.8 us -> 91.6 us (0.977)
  starting transfers between devices: 30.2 us -> 28.5 us
    ppermute x30, starting transfers between devices: 30.2 us -> 28.5 us  [swap(): return lax.ppermute(x, 'tensor', [(d, d ^ bit) for d in range(shards)])]
    pallas_call x43 -> x44, Pallas kernels: 23.7 us -> 23.7 us  [call(): pl.pallas_call(kernel, out_shape=shapes, in_specs=list(specs) + [UNREAD]...]
  transfers between devices with their start and end apart: 30 -> 30, of which waited for: 15 -> 21; matrix products, arithmetic and copies ran while one was open for 0% -> 0% of each run, Pallas kernels for 23% -> 23%
where the time goes in v5:
time: 91.6 us; the launch traced here: 91.3 us
  waiting for transfers between devices  37 us (40%)
  starting transfers between devices  28.5 us (31%)
  Pallas kernels  23.7 us (26%)
  local copies, waits for them, and re-layouts  1.75 us (2%)
    ppermute x30, waiting for transfers between devices, swap(): return lax.ppermute(x, 'tensor', [(d, d ^ bit) for d in range(shards)])  37 us
    ppermute x30, starting transfers between devices, swap(): return lax.ppermute(x, 'tensor', [(d, d ^ bit) for d in range(shards)])  28.5 us
    pallas_call x44, Pallas kernels, call(): pl.pallas_call(kernel, out_shape=shapes, in_specs=list(specs) + [UNREAD]...  23.7 us
  transfers between devices with their start and end apart: 30, of which 21 were waited for; matrix products, arithmetic and copies ran while one was open for 0% of the time, Pallas kernels for 23%

profile of v5, /device:TPU:0, one launch (start us, length us, event | category | flops | bytes accessed | tf_op | source)
XLA Modules:
  0.0 91.3 jit_solution(8154539074695549558)
XLA Ops:
  0.0 1.0 %copy-done = bf16[128,1664]{1,0:T(8,128)(2,1)S(1)} copy-done((bf16[128,1664]{1,0:T(8,128)(2,1)S(1)}, bf16[128,1664]{1,0:T(8,128)(2,1)}, u32[]{:S(2)}) %copy-start) | copy-done | bytes 426008
  1.0 0.7 copy-done.1
  1.8 1.2 %mix.4.refs_0_.own_ref = f32[128,384]{1,0:T(8,128)S(1)} custom-call(bf16[128,1664]{1,0:T(8,128)(2,1)S(1)} %copy-done, f32[52,52]{1,0:T(8,128)S(1)} %copy-done.1), custom_call_target="tpu_custom_call" | custom-call | flops 10000000000 | bytes 100000000 | tf_op jit(solution)/shard_map/mix/pallas_call | solution.py:84
  2.9 4.1 %collective-permute-start.2 = (f32[128,384]{1,0:T(8,128)S(1)}, f32[128,384]{1,0:T(8,128)S(1)}, u32[]{:S(2)}, u32[]{:S(2)}) collective-permute-start(f32[128,384]{1,0:T(8,128)S(1)} %mix.4.refs_0_.own_ref), channel_id=1, source_target_pairs={{0,8},{1,9},{2,10},{3,11},{4,12},{5,13},{6,14},{7,15},{8,0},{9,1},... | collective-permute-start | bytes 589832 | tf_op jit(solution)/shard_map/ppermute | solution.py:330
  7.0 1.2 %mix.5.refs_0_.own_ref = f32[128,384]{1,0:T(8,128)S(1)} custom-call(bf16[128,1664]{1,0:T(8,128)(2,1)S(1)} %copy-done, f32[52,52]{1,0:T(8,128)S(1)} %copy-done.1, f32[128,384]{1,0:T(8,128)S(1)} %mix.4.refs_0_.own_ref), custom_call_target="tpu_custom_call" | custom-call | flops 10000000000 | bytes 100000000 | tf_op jit(solution)/shard_map/mix/pallas_call | solution.py:84
  8.2 1.6 %collective-permute-start.1 = (f32[128,384]{1,0:T(8,128)S(1)}, f32[128,384]{1,0:T(8,128)S(1)}, u32[]{:S(2)}, u32[]{:S(2)}) collective-permute-start(f32[128,384]{1,0:T(8,128)S(1)} %mix.5.refs_0_.own_ref), channel_id=1, source_target_pairs={{0,4},{1,5},{2,6},{3,7},{4,0},{5,1},{6,2},{7,3},{8,12},{9,13},{10,... | collective-permute-start | bytes 589832 | tf_op jit(solution)/shard_map/ppermute | solution.py:330
  9.9 1.2 %mix.6.refs_0_.own_ref = f32[128,512]{1,0:T(8,128)S(1)} custom-call(bf16[128,1664]{1,0:T(8,128)(2,1)S(1)} %copy-done, f32[52,52]{1,0:T(8,128)S(1)} %copy-done.1, f32[128,384]{1,0:T(8,128)S(1)} %mix.5.refs_0_.own_ref), custom_call_target="tpu_custom_call" | custom-call | flops 10000000000 | bytes 100000000 | tf_op jit(solution)/shard_map/mix/pallas_call | solution.py:84
  11.1 1.6 %collective-permute-start = (f32[128,512]{1,0:T(8,128)S(1)}, f32[128,512]{1,0:T(8,128)S(1)}, u32[]{:S(2)}, u32[]{:S(2)}) collective-permute-start(f32[128,512]{1,0:T(8,128)S(1)} %mix.6.refs_0_.own_ref), channel_id=1, source_target_pairs={{0,2},{1,3},{2,0},{3,1},{4,6},{5,7},{6,4},{7,5},{8,10},{9,11},{10,... | collective-permute-start | bytes 786440 | tf_op jit(solution)/shard_map/ppermute | solution.py:330
  12.7 1.2 %mix.7.refs_0_.own_ref = f32[128,384]{1,0:T(8,128)S(1)} custom-call(bf16[128,1664]{1,0:T(8,128)(2,1)S(1)} %copy-done, f32[52,52]{1,0:T(8,128)S(1)} %copy-done.1, f32[128,512]{1,0:T(8,128)S(1)} %mix.6.refs_0_.own_ref), custom_call_target="tpu_custom_call" | custom-call | flops 10000000000 | bytes 100000000 | tf_op jit(solution)/shard_map/mix/pallas_call | solution.py:84
  13.9 0.1 collective-permute-start.3
  13.9 1.4 %collective-permute-done.3.got_ref = f32[128,384]{1,0:T(8,128)S(1)} collective-permute-done((f32[128,384]{1,0:T(8,128)S(1)}, f32[128,384]{1,0:T(8,128)S(1)}, u32[]{:S(2)}, u32[]{:S(2)}) %collective-permute-start.3) | collective-permute-done | bytes 196640 | tf_op jit(solution)/shard_map/ppermute | solution.py:330
  15.4 0.4 collective-permute-start.5
  15.8 0.5 collective-permute-done.2.got_ref
  16.3 1.6 %collective-permute-start.6 = (f32[128,384]{1,0:T(8,128)S(1)}, f32[128,384]{1,0:T(8,128)S(1)}, u32[]{:S(2)}, u32[]{:S(2)}) collective-permute-start(f32[128,384]{1,0:T(8,128)S(1)} %fold.17.refs_0_.own_ref), channel_id=1, source_target_pairs={{0,2},{1,3},{2,0},{3,1},{4,6},{5,7},{6,4},{7,5},{8,10},{9,11},{10,... | collective-permute-start | bytes 589832 | tf_op jit(solution)/shard_map/ppermute | solution.py:330
  18.0 0.1 collective-permute-start.7
  18.0 0.8 collective-permute-done.got_ref
  18.9 0.3 collective-permute-start.4
  19.2 0.3 collective-permute-done.7.got_ref
  19.5 3.2 %collective-permute-start.11 = (f32[128,384]{1,0:T(8,128)S(1)}, f32[128,384]{1,0:T(8,128)S(1)}, u32[]{:S(2)}, u32[]{:S(2)}) collective-permute-start(f32[128,384]{1,0:T(8,128)S(1)} %fold.20.refs_0_.own_ref), channel_id=1, source_target_pairs={{0,8},{1,9},{2,10},{3,11},{4,12},{5,13},{6,14},{7,15},{8,0},{9,1},... | collective-permute-start | bytes 589832 | tf_op jit(solution)/shard_map/ppermute | solution.py:330
  22.7 0.1 collective-permute-done.6.got_ref
  22.9 1.3 %collective-permute-start.13 = (f32[128,384]{1,0:T(8,128)S(1)}, f32[128,384]{1,0:T(8,128)S(1)}, u32[]{:S(2)}, u32[]{:S(2)}) collective-permute-start(f32[128,384]{1,0:T(8,128)S(1)} %fold.21.refs_0_.own_ref), channel_id=1, source_target_pairs={{0,4},{1,5},{2,6},{3,7},{4,0},{5,1},{6,2},{7,3},{8,12},{9,13},{10,... | collective-permute-start | bytes 589832 | tf_op jit(solution)/shard_map/ppermute | solution.py:330
  24.1 3.4 %collective-permute-done.5.got_ref = f32[128,384]{1,0:T(8,128)S(1)} collective-permute-done((f32[128,384]{1,0:T(8,128)S(1)}, f32[128,384]{1,0:T(8,128)S(1)}, u32[]{:S(2)}, u32[]{:S(2)}) %collective-permute-start.5) | collective-permute-done | bytes 196640 | tf_op jit(solution)/shard_map/ppermute | solution.py:330
  27.6 0.6 collective-permute-start.9
  28.2 2.8 %load.4 = (bf16[384,8192]{1,0:T(8,128)(2,1)S(1)}, f32[8,128]{1,0:T(8,128)S(1)}) custom-call(s32[1]{0:T(128)} %bitcast.me_ref, bf16[1664,8192]{1,0:T(8,128)(2,1)} %weight_ref.7, f32[128,384]{1,0:T(8,128)S(1)} %fold.22.refs_0_.own_ref), custom_call_target="tpu_custom_call" | custom-call | flops 10000000000 | bytes 100000000 | tf_op jit(solution)/shard_map/load/pallas_call | solution.py:84
  31.0 5.5 %collective-permute-done.4.got_ref = f32[128,512]{1,0:T(8,128)S(1)} collective-permute-done((f32[128,512]{1,0:T(8,128)S(1)}, f32[128,512]{1,0:T(8,128)S(1)}, u32[]{:S(2)}, u32[]{:S(2)}) %collective-permute-start.4) | collective-permute-done | bytes 262176 | tf_op jit(solution)/shard_map/ppermute | solution.py:330
  36.5 0.1 collective-permute-start.8
  36.7 1.4 %collective-permute-done.8.got_ref = f32[128,512]{1,0:T(8,128)S(1)} collective-permute-done((f32[128,512]{1,0:T(8,128)S(1)}, f32[128,512]{1,0:T(8,128)S(1)}, u32[]{:S(2)}, u32[]{:S(2)}) %collective-permute-start.8) | collective-permute-done | bytes 262176 | tf_op jit(solution)/shard_map/ppermute | solution.py:330
  38.2 2.8 %load.5 = (bf16[384,8192]{1,0:T(8,128)(2,1)S(1)}, f32[8,128]{1,0:T(8,128)S(1)}) custom-call(s32[1]{0:T(128)} %bitcast.me_ref, bf16[1664,8192]{1,0:T(8,128)(2,1)} %weight_ref.7, f32[128,512]{1,0:T(8,128)S(1)} %fold.25.refs_0_.own_ref), custom_call_target="tpu_custom_call" | custom-call | flops 10000000000 | bytes 100000000 | tf_op jit(solution)/shard_map/load/pallas_call | solution.py:84
  41.0 0.8 collective-permute-start.10
  41.8 1.4 %collective-permute-start.12 = (f32[128,384]{1,0:T(8,128)S(1)}, f32[128,384]{1,0:T(8,128)S(1)}, u32[]{:S(2)}, u32[]{:S(2)}) collective-permute-start(f32[128,384]{1,0:T(8,128)S(1)} %fold.26.refs_0_.own_ref), channel_id=1, source_target_pairs={{0,2},{1,3},{2,0},{3,1},{4,6},{5,7},{6,4},{7,5},{8,10},{9,11},{10,... | collective-permute-start | bytes 589832 | tf_op jit(solution)/shard_map/ppermute | solution.py:330
  43.3 0.1 collective-permute-start.14
  43.4 0.6 collective-permute-done.15.got_ref
  44.0 2.8 %load.6 = (bf16[384,8192]{1,0:T(8,128)(2,1)S(1)}, f32[8,128]{1,0:T(8,128)S(1)}) custom-call(s32[1]{0:T(128)} %bitcast.me_ref, bf16[1664,8192]{1,0:T(8,128)(2,1)} %weight_ref.7, bf16[128,384]{1,0:T(8,128)(2,1)S(1)} %fold.28.refs_0_), custom_call_target="tpu_custom_call" | custom-call | flops 10000000000 | bytes 100000000 | tf_op jit(solution)/shard_map/load/pallas_call | solution.py:84
  46.9 1.3 %step.3.refs_0_.refs_2_ = f32[16,128,512]{2,1,0:T(8,128)S(1)} custom-call(bf16[128,384]{1,0:T(8,128)(2,1)S(1)} %fold.28.refs_0_, bf16[384,8192]{1,0:T(8,128)(2,1)S(1)} %get-tuple-element.43.refs_1_, f32[8,128]{1,0:T(8,128)S(1)} %get-tuple-element.44.refs_2_), custom_call_target="tpu_custom_call" | custom-call | flops 10000000000 | bytes 100000000 | tf_op jit(solution)/shard_map/step/pallas_call | solution.py:84
  48.2 1.3 %step.4.refs_0_.refs_2_ = f32[16,128,512]{2,1,0:T(8,128)S(1)} custom-call(bf16[128,384]{1,0:T(8,128)(2,1)S(1)} %fold.29.refs_0_.refs_3_, bf16[384,8192]{1,0:T(8,128)(2,1)S(1)} %get-tuple-element.45.refs_1_, f32[16,128,512]{2,1,0:T(8,128)S(1)} %step.3.refs_0_.refs_2_, bf16[128,384]{1,0:T(8,128)(2,1)S(1)} %fold.29.refs_0_.refs_3_), custom_call_target="tpu_custom_call" | custom-call | flops 10000000000 | bytes 100000000 | tf_op jit(solution)/shard_map/step/pallas_call | solution.py:84
  49.5 1.3 %step.5.refs_0_.total_ref = f32[16,128,512]{2,1,0:T(8,128)S(1)} custom-call(bf16[128,384]{1,0:T(8,128)(2,1)S(1)} %fold.30.refs_0_.refs_3_, bf16[384,8192]{1,0:T(8,128)(2,1)S(1)} %get-tuple-element.46.refs_1_, f32[16,128,512]{2,1,0:T(8,128)S(1)} %step.4.refs_0_.refs_2_, bf16[128,384]{1,0:T(8,128)(2,1)S(1)} %fold.30.refs_0_.refs_3_), custom_call_target="tpu_custom_call" | custom-call | flops 10000000000 | bytes 100000000 | tf_op jit(solution)/shard_map/step/pallas_call | solution.py:84
  50.8 3.6 %load.7 = (bf16[512,8192]{1,0:T(8,128)(2,1)S(1)}, f32[8,128]{1,0:T(8,128)S(1)}) custom-call(s32[1]{0:T(128)} %bitcast.me_ref, bf16[1664,8192]{1,0:T(8,128)(2,1)} %weight_ref.7, f32[16,128,512]{2,1,0:T(8,128)S(1)} %step.5.refs_0_.total_ref), custom_call_target="tpu_custom_call" | custom-call | flops 10000000000 | bytes 100000000 | tf_op jit(solution)/shard_map/load/pallas_call | solution.py:84
  54.4 1.5 %collective-permute-done.10.got_ref = f32[128,512]{1,0:T(8,128)S(1)} collective-permute-done((f32[128,512]{1,0:T(8,128)S(1)}, f32[128,512]{1,0:T(8,128)S(1)}, u32[]{:S(2)}, u32[]{:S(2)}) %collective-permute-start.10) | collective-permute-done | bytes 262176 | tf_op jit(solution)/shard_map/ppermute | solution.py:330
  55.9 0.8 product.2
  56.8 0.5 collective-permute-start.16
  57.3 0.8 product.3
  58.1 1.4 %collective-permute-done.17.got_ref = f32[8,128,256]{2,1,0:T(8,128)S(1)} collective-permute-done((f32[8,128,256]{2,1,0:T(8,128)S(1)}, f32[8,128,256]{2,1,0:T(8,128)S(1)}, u32[]{:S(2)}, u32[]{:S(2)}) %collective-permute-start.17) | collective-permute-done | bytes 1048608 | tf_op jit(solution)/shard_map/ppermute | solution.py:330
  59.5 0.1 halve.10
  59.6 1.5 %collective-permute-start.21 = (f32[4,64,256]{2,1,0:T(8,128)S(1)}, f32[4,64,256]{2,1,0:T(8,128)S(1)}, u32[]{:S(2)}, u32[]{:S(2)}) collective-permute-start(f32[4,64,256]{2,1,0:T(8,128)S(1)} %get-tuple-element.60), channel_id=1, source_target_pairs={{0,2},{1,3},{2,0},{3,1},{4,6},{5,7},{6,4},{7,5},{8,10},{9,11},{10,... | collective-permute-start | bytes 786440 | tf_op jit(solution)/shard_map/ppermute | solution.py:330
  61.0 0.1 halve.11
  61.2 1.4 %collective-permute-start.20 = (f32[4,64,256]{2,1,0:T(8,128)S(1)}, f32[4,64,256]{2,1,0:T(8,128)S(1)}, u32[]{:S(2)}, u32[]{:S(2)}) collective-permute-start(f32[4,64,256]{2,1,0:T(8,128)S(1)} %get-tuple-element.58.refs_0_), channel_id=1, source_target_pairs={{0,2},{1,3},{2,0},{3,1},{4,6},{5,7},{6,4},{7,5},{8,10},{9,11},{10,... | collective-permute-start | bytes 786440 | tf_op jit(solution)/shard_map/ppermute | solution.py:330
  62.5 1.5 %collective-permute-start.18 = (f32[4,64,256]{2,1,0:T(8,128)S(1)}, f32[4,64,256]{2,1,0:T(8,128)S(1)}, u32[]{:S(2)}, u32[]{:S(2)}) collective-permute-start(f32[4,64,256]{2,1,0:T(8,128)S(1)} %get-tuple-element.55), channel_id=1, source_target_pairs={{0,4},{1,5},{2,6},{3,7},{4,0},{5,1},{6,2},{7,3},{8,12},{9,13},{10,... | collective-permute-start | bytes 786440 | tf_op jit(solution)/shard_map/ppermute | solution.py:330
  64.0 4.8 %collective-permute-done.21.got_ref = f32[4,64,256]{2,1,0:T(8,128)S(1)} collective-permute-done((f32[4,64,256]{2,1,0:T(8,128)S(1)}, f32[4,64,256]{2,1,0:T(8,128)S(1)}, u32[]{:S(2)}, u32[]{:S(2)}) %collective-permute-start.21) | collective-permute-done | bytes 262176 | tf_op jit(solution)/shard_map/ppermute | solution.py:330
  68.8 0.1 collective-permute-start.25
  68.9 4.7 %collective-permute-done.20.got_ref = f32[4,64,256]{2,1,0:T(8,128)S(1)} collective-permute-done((f32[4,64,256]{2,1,0:T(8,128)S(1)}, f32[4,64,256]{2,1,0:T(8,128)S(1)}, u32[]{:S(2)}, u32[]{:S(2)}) %collective-permute-start.20) | collective-permute-done | bytes 262176 | tf_op jit(solution)/shard_map/ppermute | solution.py:330
  73.7 1.0 %collective-permute-done.19.got_ref = f32[4,64,256]{2,1,0:T(8,128)S(1)} collective-permute-done((f32[4,64,256]{2,1,0:T(8,128)S(1)}, f32[4,64,256]{2,1,0:T(8,128)S(1)}, u32[]{:S(2)}, u32[]{:S(2)}) %collective-permute-start.19) | collective-permute-done | bytes 262176 | tf_op jit(solution)/shard_map/ppermute | solution.py:330
  74.7 0.8 collective-permute-start.24
  75.5 1.7 %collective-permute-done.18.got_ref = f32[4,64,256]{2,1,0:T(8,128)S(1)} collective-permute-done((f32[4,64,256]{2,1,0:T(8,128)S(1)}, f32[4,64,256]{2,1,0:T(8,128)S(1)}, u32[]{:S(2)}, u32[]{:S(2)}) %collective-permute-start.18) | collective-permute-done | bytes 262176 | tf_op jit(solution)/shard_map/ppermute | solution.py:330
  77.3 0.9 %collective-permute-start.22 = (f32[2,64,256]{2,1,0:T(8,128)S(1)}, f32[2,64,256]{2,1,0:T(8,128)S(1)}, u32[]{:S(2)}, u32[]{:S(2)}) collective-permute-start(f32[2,64,256]{2,1,0:T(8,128)S(1)} %get-tuple-element.65.refs_0_), channel_id=1, source_target_pairs={{0,2},{1,3},{2,0},{3,1},{4,6},{5,7},{6,4},{7,5},{8,10},{9,11},{10,... | collective-permute-start | bytes 393224 | tf_op jit(solution)/shard_map/ppermute | solution.py:330
  78.2 1.8 %collective-permute-done.25.got_ref = f32[2,64,256]{2,1,0:T(8,128)S(1)} collective-permute-done((f32[2,64,256]{2,1,0:T(8,128)S(1)}, f32[2,64,256]{2,1,0:T(8,128)S(1)}, u32[]{:S(2)}, u32[]{:S(2)}) %collective-permute-start.25) | collective-permute-done | bytes 131104 | tf_op jit(solution)/shard_map/ppermute | solution.py:330
  80.2 1.0 %collective-permute-done.24.got_ref = f32[2,64,256]{2,1,0:T(8,128)S(1)} collective-permute-done((f32[2,64,256]{2,1,0:T(8,128)S(1)}, f32[2,64,256]{2,1,0:T(8,128)S(1)}, u32[]{:S(2)}, u32[]{:S(2)}) %collective-permute-start.24) | collective-permute-done | bytes 131104 | tf_op jit(solution)/shard_map/ppermute | solution.py:330
  81.2 1.2 %collective-permute-start.28 = (f32[1,64,256]{2,1,0:T(8,128)S(1)}, f32[1,64,256]{2,1,0:T(8,128)S(1)}, u32[]{:S(2)}, u32[]{:S(2)}) collective-permute-start(f32[1,64,256]{2,1,0:T(8,128)S(1)} %get-tuple-element.70.refs_0_), channel_id=1, source_target_pairs={{0,4},{1,5},{2,6},{3,7},{4,0},{5,1},{6,2},{7,3},{8,12},{9,13},{10,... | collective-permute-start | bytes 196616 | tf_op jit(solution)/shard_map/ppermute | solution.py:330
  82.4 0.1 collective-permute-done.23.got_ref
  82.5 1.6 %collective-permute-start.29 = (f32[1,64,256]{2,1,0:T(8,128)S(1)}, f32[1,64,256]{2,1,0:T(8,128)S(1)}, u32[]{:S(2)}, u32[]{:S(2)}) collective-permute-start(f32[1,64,256]{2,1,0:T(8,128)S(1)} %get-tuple-element.71.refs_0_), channel_id=1, source_target_pairs={{0,8},{1,9},{2,10},{3,11},{4,12},{5,13},{6,14},{7,15},{8,0},{9,1},... | collective-permute-start | bytes 196616 | tf_op jit(solution)/shard_map/ppermute | solution.py:330
  84.1 1.5 %collective-permute-start.26 = (f32[1,64,256]{2,1,0:T(8,128)S(1)}, f32[1,64,256]{2,1,0:T(8,128)S(1)}, u32[]{:S(2)}, u32[]{:S(2)}) collective-permute-start(f32[1,64,256]{2,1,0:T(8,128)S(1)} %get-tuple-element.73.refs_0_), channel_id=1, source_target_pairs={{0,8},{1,9},{2,10},{3,11},{4,12},{5,13},{6,14},{7,15},{8,0},{9,1},... | collective-permute-start | bytes 196616 | tf_op jit(solution)/shard_map/ppermute | solution.py:330
  85.6 1.5 %collective-permute-done.27.got_ref = f32[1,64,256]{2,1,0:T(8,128)S(1)} collective-permute-done((f32[1,64,256]{2,1,0:T(8,128)S(1)}, f32[1,64,256]{2,1,0:T(8,128)S(1)}, u32[]{:S(2)}, u32[]{:S(2)}) %collective-permute-start.27) | collective-permute-done | bytes 65568 | tf_op jit(solution)/shard_map/ppermute | solution.py:330
  87.1 2.1 %collective-permute-done.29.got_ref = f32[1,64,256]{2,1,0:T(8,128)S(1)} collective-permute-done((f32[1,64,256]{2,1,0:T(8,128)S(1)}, f32[1,64,256]{2,1,0:T(8,128)S(1)}, u32[]{:S(2)}, u32[]{:S(2)}) %collective-permute-start.29) | collective-permute-done | bytes 65568 | tf_op jit(solution)/shard_map/ppermute | solution.py:330
  89.2 1.4 %collective-permute-done.26.got_ref = f32[1,64,256]{2,1,0:T(8,128)S(1)} collective-permute-done((f32[1,64,256]{2,1,0:T(8,128)S(1)}, f32[1,64,256]{2,1,0:T(8,128)S(1)}, u32[]{:S(2)}, u32[]{:S(2)}) %collective-permute-start.26) | collective-permute-done | bytes 65568 | tf_op jit(solution)/shard_map/ppermute | solution.py:330
  90.6 0.7 finish.7
  (44 shorter events, 1.0 us)
Async XLA Ops:
  0.0 1.0 %copy-start = (bf16[128,1664]{1,0:T(8,128)(2,1)S(1)}, bf16[128,1664]{1,0:T(8,128)(2,1)}, u32[]{:S(2)}) copy-start(bf16[128,1664]{1,0:T(8,128)(2,1)} %activations.7) | copy-start | bytes 1277956
  1.0 0.7 copy-start.1
  2.9 13.3 %collective-permute-start.2 = (f32[128,384]{1,0:T(8,128)S(1)}, f32[128,384]{1,0:T(8,128)S(1)}, u32[]{:S(2)}, u32[]{:S(2)}) collective-permute-start(f32[128,384]{1,0:T(8,128)S(1)} %mix.4.refs_0_.own_ref), channel_id=1, source_target_pairs={{0,8},{1,9},{2,10},{3,11},{4,12},{5,13},{6,14},{7,15},{8,0},{9,1},... | collective-permute-start | bytes 589832 | tf_op jit(solution)/shard_map/ppermute | solution.py:330
  8.2 9.7 %collective-permute-start.1 = (f32[128,384]{1,0:T(8,128)S(1)}, f32[128,384]{1,0:T(8,128)S(1)}, u32[]{:S(2)}, u32[]{:S(2)}) collective-permute-start(f32[128,384]{1,0:T(8,128)S(1)} %mix.5.refs_0_.own_ref), channel_id=1, source_target_pairs={{0,4},{1,5},{2,6},{3,7},{4,0},{5,1},{6,2},{7,3},{8,12},{9,13},{10,... | collective-permute-start | bytes 589832 | tf_op jit(solution)/shard_map/ppermute | solution.py:330
  11.1 7.8 %collective-permute-start = (f32[128,512]{1,0:T(8,128)S(1)}, f32[128,512]{1,0:T(8,128)S(1)}, u32[]{:S(2)}, u32[]{:S(2)}) collective-permute-start(f32[128,512]{1,0:T(8,128)S(1)} %mix.6.refs_0_.own_ref), channel_id=1, source_target_pairs={{0,2},{1,3},{2,0},{3,1},{4,6},{5,7},{6,4},{7,5},{8,10},{9,11},{10,... | collective-permute-start | bytes 786440 | tf_op jit(solution)/shard_map/ppermute | solution.py:330
  13.9 1.5 %collective-permute-start.3 = (f32[128,384]{1,0:T(8,128)S(1)}, f32[128,384]{1,0:T(8,128)S(1)}, u32[]{:S(2)}, u32[]{:S(2)}) collective-permute-start(f32[128,384]{1,0:T(8,128)S(1)} %mix.7.refs_0_.own_ref), channel_id=1, source_target_pairs={{0,1},{1,0},{2,3},{3,2},{4,5},{5,4},{6,7},{7,6},{8,9},{9,8},{10,11... | collective-permute-start | bytes 589832 | tf_op jit(solution)/shard_map/ppermute | solution.py:330
  15.4 12.2 %collective-permute-start.5 = (f32[128,384]{1,0:T(8,128)S(1)}, f32[128,384]{1,0:T(8,128)S(1)}, u32[]{:S(2)}, u32[]{:S(2)}) collective-permute-start(f32[128,384]{1,0:T(8,128)S(1)} %fold.16.refs_0_.own_ref), channel_id=1, source_target_pairs={{0,8},{1,9},{2,10},{3,11},{4,12},{5,13},{6,14},{7,15},{8,0},{9,1},... | collective-permute-start | bytes 589832 | tf_op jit(solution)/shard_map/ppermute | solution.py:330
  16.3 6.5 %collective-permute-start.6 = (f32[128,384]{1,0:T(8,128)S(1)}, f32[128,384]{1,0:T(8,128)S(1)}, u32[]{:S(2)}, u32[]{:S(2)}) collective-permute-start(f32[128,384]{1,0:T(8,128)S(1)} %fold.17.refs_0_.own_ref), channel_id=1, source_target_pairs={{0,2},{1,3},{2,0},{3,1},{4,6},{5,7},{6,4},{7,5},{8,10},{9,11},{10,... | collective-permute-start | bytes 589832 | tf_op jit(solution)/shard_map/ppermute | solution.py:330
  18.0 1.5 %collective-permute-start.7 = (f32[128,384]{1,0:T(8,128)S(1)}, f32[128,384]{1,0:T(8,128)S(1)}, u32[]{:S(2)}, u32[]{:S(2)}) collective-permute-start(f32[128,384]{1,0:T(8,128)S(1)} %fold.18.refs_0_.own_ref), channel_id=1, source_target_pairs={{0,1},{1,0},{2,3},{3,2},{4,5},{5,4},{6,7},{7,6},{8,9},{9,8},{10,11... | collective-permute-start | bytes 589832 | tf_op jit(solution)/shard_map/ppermute | solution.py:330
  18.9 17.6 %collective-permute-start.4 = (f32[128,512]{1,0:T(8,128)S(1)}, f32[128,512]{1,0:T(8,128)S(1)}, u32[]{:S(2)}, u32[]{:S(2)}) collective-permute-start(f32[128,512]{1,0:T(8,128)S(1)} %fold.19.refs_0_.own_ref), channel_id=1, source_target_pairs={{0,4},{1,5},{2,6},{3,7},{4,0},{5,1},{6,2},{7,3},{8,12},{9,13},{10,... | collective-permute-start | bytes 786440 | tf_op jit(solution)/shard_map/ppermute | solution.py:330
  19.5 22.3 %collective-permute-start.11 = (f32[128,384]{1,0:T(8,128)S(1)}, f32[128,384]{1,0:T(8,128)S(1)}, u32[]{:S(2)}, u32[]{:S(2)}) collective-permute-start(f32[128,384]{1,0:T(8,128)S(1)} %fold.20.refs_0_.own_ref), channel_id=1, source_target_pairs={{0,8},{1,9},{2,10},{3,11},{4,12},{5,13},{6,14},{7,15},{8,0},{9,1},... | collective-permute-start | bytes 589832 | tf_op jit(solution)/shard_map/ppermute | solution.py:330
  22.9 20.4 %collective-permute-start.13 = (f32[128,384]{1,0:T(8,128)S(1)}, f32[128,384]{1,0:T(8,128)S(1)}, u32[]{:S(2)}, u32[]{:S(2)}) collective-permute-start(f32[128,384]{1,0:T(8,128)S(1)} %fold.21.refs_0_.own_ref), channel_id=1, source_target_pairs={{0,4},{1,5},{2,6},{3,7},{4,0},{5,1},{6,2},{7,3},{8,12},{9,13},{10,... | collective-permute-start | bytes 589832 | tf_op jit(solution)/shard_map/ppermute | solution.py:330
  27.6 9.0 %collective-permute-start.9 = (f32[128,384]{1,0:T(8,128)S(1)}, f32[128,384]{1,0:T(8,128)S(1)}, u32[]{:S(2)}, u32[]{:S(2)}) collective-permute-start(f32[128,384]{1,0:T(8,128)S(1)} %fold.22.refs_0_.own_ref), channel_id=1, source_target_pairs={{0,2},{1,3},{2,0},{3,1},{4,6},{5,7},{6,4},{7,5},{8,10},{9,11},{10,... | collective-permute-start | bytes 589832 | tf_op jit(solution)/shard_map/ppermute | solution.py:330
  36.5 1.6 %collective-permute-start.8 = (f32[128,512]{1,0:T(8,128)S(1)}, f32[128,512]{1,0:T(8,128)S(1)}, u32[]{:S(2)}, u32[]{:S(2)}) collective-permute-start(f32[128,512]{1,0:T(8,128)S(1)} %fold.23.refs_0_.own_ref), channel_id=1, source_target_pairs={{0,1},{1,0},{2,3},{3,2},{4,5},{5,4},{6,7},{7,6},{8,9},{9,8},{10,11... | collective-permute-start | bytes 786440 | tf_op jit(solution)/shard_map/ppermute | solution.py:330
  36.7 7.4 %collective-permute-start.15 = (f32[128,384]{1,0:T(8,128)S(1)}, f32[128,384]{1,0:T(8,128)S(1)}, u32[]{:S(2)}, u32[]{:S(2)}) collective-permute-start(f32[128,384]{1,0:T(8,128)S(1)} %fold.24.refs_0_.own_ref), channel_id=1, source_target_pairs={{0,4},{1,5},{2,6},{3,7},{4,0},{5,1},{6,2},{7,3},{8,12},{9,13},{10,... | collective-permute-start | bytes 589832 | tf_op jit(solution)/shard_map/ppermute | solution.py:330
  41.0 14.9 %collective-permute-start.10 = (f32[128,512]{1,0:T(8,128)S(1)}, f32[128,512]{1,0:T(8,128)S(1)}, u32[]{:S(2)}, u32[]{:S(2)}) collective-permute-start(f32[128,512]{1,0:T(8,128)S(1)} %fold.25.refs_0_.own_ref), channel_id=1, source_target_pairs={{0,8},{1,9},{2,10},{3,11},{4,12},{5,13},{6,14},{7,15},{8,0},{9,1},... | collective-permute-start | bytes 786440 | tf_op jit(solution)/shard_map/ppermute | solution.py:330
  41.8 7.6 %collective-permute-start.12 = (f32[128,384]{1,0:T(8,128)S(1)}, f32[128,384]{1,0:T(8,128)S(1)}, u32[]{:S(2)}, u32[]{:S(2)}) collective-permute-start(f32[128,384]{1,0:T(8,128)S(1)} %fold.26.refs_0_.own_ref), channel_id=1, source_target_pairs={{0,2},{1,3},{2,0},{3,1},{4,6},{5,7},{6,4},{7,5},{8,10},{9,11},{10,... | collective-permute-start | bytes 589832 | tf_op jit(solution)/shard_map/ppermute | solution.py:330
  43.3 4.8 %collective-permute-start.14 = (f32[128,384]{1,0:T(8,128)S(1)}, f32[128,384]{1,0:T(8,128)S(1)}, u32[]{:S(2)}, u32[]{:S(2)}) collective-permute-start(f32[128,384]{1,0:T(8,128)S(1)} %fold.27.refs_0_.own_ref), channel_id=1, source_target_pairs={{0,1},{1,0},{2,3},{3,2},{4,5},{5,4},{6,7},{7,6},{8,9},{9,8},{10,11... | collective-permute-start | bytes 589832 | tf_op jit(solution)/shard_map/ppermute | solution.py:330
  56.7 2.7 %collective-permute-start.17 = (f32[8,128,256]{2,1,0:T(8,128)S(1)}, f32[8,128,256]{2,1,0:T(8,128)S(1)}, u32[]{:S(2)}, u32[]{:S(2)}) collective-permute-start(f32[8,128,256]{2,1,0:T(8,128)S(1)} %get-tuple-element.52), channel_id=1, source_target_pairs={{0,1},{1,0},{2,3},{3,2},{4,5},{5,4},{6,7},{7,6},{8,9},{9,8},{10,11... | collective-permute-start | bytes 3145736 | tf_op jit(solution)/shard_map/ppermute | solution.py:330
  56.8 4.2 %collective-permute-start.16 = (f32[8,128,256]{2,1,0:T(8,128)S(1)}, f32[8,128,256]{2,1,0:T(8,128)S(1)}, u32[]{:S(2)}, u32[]{:S(2)}) collective-permute-start(f32[8,128,256]{2,1,0:T(8,128)S(1)} %get-tuple-element.49.refs_0_), channel_id=1, source_target_pairs={{0,1},{1,0},{2,3},{3,2},{4,5},{5,4},{6,7},{7,6},{8,9},{9,8},{10,11... | collective-permute-start | bytes 3145736 | tf_op jit(solution)/shard_map/ppermute | solution.py:330
  59.6 9.2 %collective-permute-start.21 = (f32[4,64,256]{2,1,0:T(8,128)S(1)}, f32[4,64,256]{2,1,0:T(8,128)S(1)}, u32[]{:S(2)}, u32[]{:S(2)}) collective-permute-start(f32[4,64,256]{2,1,0:T(8,128)S(1)} %get-tuple-element.60), channel_id=1, source_target_pairs={{0,2},{1,3},{2,0},{3,1},{4,6},{5,7},{6,4},{7,5},{8,10},{9,11},{10,... | collective-permute-start | bytes 786440 | tf_op jit(solution)/shard_map/ppermute | solution.py:330
  61.0 13.6 %collective-permute-start.19 = (f32[4,64,256]{2,1,0:T(8,128)S(1)}, f32[4,64,256]{2,1,0:T(8,128)S(1)}, u32[]{:S(2)}, u32[]{:S(2)}) collective-permute-start(f32[4,64,256]{2,1,0:T(8,128)S(1)} %get-tuple-element.53.refs_0_), channel_id=1, source_target_pairs={{0,8},{1,9},{2,10},{3,11},{4,12},{5,13},{6,14},{7,15},{8,0},{9,1},... | collective-permute-start | bytes 786440 | tf_op jit(solution)/shard_map/ppermute | solution.py:330
  61.2 12.5 %collective-permute-start.20 = (f32[4,64,256]{2,1,0:T(8,128)S(1)}, f32[4,64,256]{2,1,0:T(8,128)S(1)}, u32[]{:S(2)}, u32[]{:S(2)}) collective-permute-start(f32[4,64,256]{2,1,0:T(8,128)S(1)} %get-tuple-element.58.refs_0_), channel_id=1, source_target_pairs={{0,2},{1,3},{2,0},{3,1},{4,6},{5,7},{6,4},{7,5},{8,10},{9,11},{10,... | collective-permute-start | bytes 786440 | tf_op jit(solution)/shard_map/ppermute | solution.py:330
  62.5 14.7 %collective-permute-start.18 = (f32[4,64,256]{2,1,0:T(8,128)S(1)}, f32[4,64,256]{2,1,0:T(8,128)S(1)}, u32[]{:S(2)}, u32[]{:S(2)}) collective-permute-start(f32[4,64,256]{2,1,0:T(8,128)S(1)} %get-tuple-element.55), channel_id=1, source_target_pairs={{0,4},{1,5},{2,6},{3,7},{4,0},{5,1},{6,2},{7,3},{8,12},{9,13},{10,... | collective-permute-start | bytes 786440 | tf_op jit(solution)/shard_map/ppermute | solution.py:330
  68.8 11.2 %collective-permute-start.25 = (f32[2,64,256]{2,1,0:T(8,128)S(1)}, f32[2,64,256]{2,1,0:T(8,128)S(1)}, u32[]{:S(2)}, u32[]{:S(2)}) collective-permute-start(f32[2,64,256]{2,1,0:T(8,128)S(1)} %get-tuple-element.61.refs_0_), channel_id=1, source_target_pairs={{0,4},{1,5},{2,6},{3,7},{4,0},{5,1},{6,2},{7,3},{8,12},{9,13},{10,... | collective-permute-start | bytes 393224 | tf_op jit(solution)/shard_map/ppermute | solution.py:330
  73.6 8.9 %collective-permute-start.23 = (f32[2,64,256]{2,1,0:T(8,128)S(1)}, f32[2,64,256]{2,1,0:T(8,128)S(1)}, u32[]{:S(2)}, u32[]{:S(2)}) collective-permute-start(f32[2,64,256]{2,1,0:T(8,128)S(1)} %get-tuple-element.62.refs_0_), channel_id=1, source_target_pairs={{0,4},{1,5},{2,6},{3,7},{4,0},{5,1},{6,2},{7,3},{8,12},{9,13},{10,... | collective-permute-start | bytes 393224 | tf_op jit(solution)/shard_map/ppermute | solution.py:330
  74.7 6.4 %collective-permute-start.24 = (f32[2,64,256]{2,1,0:T(8,128)S(1)}, f32[2,64,256]{2,1,0:T(8,128)S(1)}, u32[]{:S(2)}, u32[]{:S(2)}) collective-permute-start(f32[2,64,256]{2,1,0:T(8,128)S(1)} %get-tuple-element.63.refs_0_), channel_id=1, source_target_pairs={{0,2},{1,3},{2,0},{3,1},{4,6},{5,7},{6,4},{7,5},{8,10},{9,11},{10,... | collective-permute-start | bytes 393224 | tf_op jit(solution)/shard_map/ppermute | solution.py:330
  77.3 6.8 %collective-permute-start.22 = (f32[2,64,256]{2,1,0:T(8,128)S(1)}, f32[2,64,256]{2,1,0:T(8,128)S(1)}, u32[]{:S(2)}, u32[]{:S(2)}) collective-permute-start(f32[2,64,256]{2,1,0:T(8,128)S(1)} %get-tuple-element.65.refs_0_), channel_id=1, source_target_pairs={{0,2},{1,3},{2,0},{3,1},{4,6},{5,7},{6,4},{7,5},{8,10},{9,11},{10,... | collective-permute-start | bytes 393224 | tf_op jit(solution)/shard_map/ppermute | solution.py:330
  80.1 7.0 %collective-permute-start.27 = (f32[1,64,256]{2,1,0:T(8,128)S(1)}, f32[1,64,256]{2,1,0:T(8,128)S(1)}, u32[]{:S(2)}, u32[]{:S(2)}) collective-permute-start(f32[1,64,256]{2,1,0:T(8,128)S(1)} %get-tuple-element.69.refs_0_), channel_id=1, source_target_pairs={{0,8},{1,9},{2,10},{3,11},{4,12},{5,13},{6,14},{7,15},{8,0},{9,1},... | collective-permute-start | bytes 196616 | tf_op jit(solution)/shard_map/ppermute | solution.py:330
  81.2 6.0 %collective-permute-start.28 = (f32[1,64,256]{2,1,0:T(8,128)S(1)}, f32[1,64,256]{2,1,0:T(8,128)S(1)}, u32[]{:S(2)}, u32[]{:S(2)}) collective-permute-start(f32[1,64,256]{2,1,0:T(8,128)S(1)} %get-tuple-element.70.refs_0_), channel_id=1, source_target_pairs={{0,4},{1,5},{2,6},{3,7},{4,0},{5,1},{6,2},{7,3},{8,12},{9,13},{10,... | collective-permute-start | bytes 196616 | tf_op jit(solution)/shard_map/ppermute | solution.py:330
  82.5 6.7 %collective-permute-start.29 = (f32[1,64,256]{2,1,0:T(8,128)S(1)}, f32[1,64,256]{2,1,0:T(8,128)S(1)}, u32[]{:S(2)}, u32[]{:S(2)}) collective-permute-start(f32[1,64,256]{2,1,0:T(8,128)S(1)} %get-tuple-element.71.refs_0_), channel_id=1, source_target_pairs={{0,8},{1,9},{2,10},{3,11},{4,12},{5,13},{6,14},{7,15},{8,0},{9,1},... | collective-permute-start | bytes 196616 | tf_op jit(solution)/shard_map/ppermute | solution.py:330
  84.1 6.5 %collective-permute-start.26 = (f32[1,64,256]{2,1,0:T(8,128)S(1)}, f32[1,64,256]{2,1,0:T(8,128)S(1)}, u32[]{:S(2)}, u32[]{:S(2)}) collective-permute-start(f32[1,64,256]{2,1,0:T(8,128)S(1)} %get-tuple-element.73.refs_0_), channel_id=1, source_target_pairs={{0,8},{1,9},{2,10},{3,11},{4,12},{5,13},{6,14},{7,15},{8,0},{9,1},... | collective-permute-start | bytes 196616 | tf_op jit(solution)/shard_map/ppermute | solution.py:330

commit v6 on v5

--- a/solution.py
+++ b/solution.py
@@ -14,10 +14,9 @@
 
 
 TILES = (3, 3, 3, 4)
-ORDERS = ((3, 1, 2, 0), (0, 3, 1, 2), (2, 0, 3, 1), (1, 2, 0, 3))
-FIRST = (0, 2, 3, 1)
+ORDERS = ((3, 0, 2, 1), ("in", "mid", "out", 0, 1), (1, 0, "in", "mid", "out"), (1, 2, 0, 3))
+FIRST = (1, 2, 0, 3)
 PATIENCE = 1.8
-RULE = 1
 
 
 def quotient(index, divisor, limit):
@@ -111,6 +110,47 @@
 
     shape = jax.ShapeDtypeStruct(own.shape, F32 if factor is None else BF16)
     return call("fold", kernel, (me, own, got), (SMEM, VMEM, VMEM), shape, after)
+
+
+def pair(me, own, got, quarter, after):
+    def kernel(me_ref, own_ref, got_ref, *refs):
+        sign = jnp.where(me_ref[0] // quarter == 2, -1.0, 1.0).astype(F32)
+        refs[-1][0] = got_ref[...] + own_ref[...]
+        refs[-1][1] = (got_ref[...] - own_ref[...]) * sign
+
+    shape = jax.ShapeDtypeStruct((2, *own.shape), F32)
+    return call("pair", kernel, (me, own, got), (SMEM, VMEM, VMEM), shape, after)
+
+
+def meet(me, own, got, quarter, after):
+    def kernel(me_ref, own_ref, got_ref, *refs):
+        keep, give = refs[-2:]
+        third = me_ref[0] // quarter == 2
+
+        @pl.when(third)
+        def _():
+            keep[...] = got_ref[0] - own_ref[0]
+            give[...] = got_ref[1] - own_ref[1]
+
+        @pl.when(jnp.logical_not(third))
+        def _():
+            keep[...] = got_ref[1] + own_ref[1]
+            give[...] = got_ref[0] + own_ref[0]
+
+    shapes = [jax.ShapeDtypeStruct(own.shape[1:], F32)] * 2
+    return call("meet", kernel, (me, own, got), (SMEM, VMEM, VMEM), shapes, after)
+
+
+def settle(me, own, got, quarter, after, factor=None):
+    def kernel(me_ref, own_ref, got_ref, *refs):
+        place = me_ref[0] // quarter
+        total = jnp.where(jnp.logical_or(place == 0, place == 3), got_ref[...], own_ref[...])
+        if factor is not None:
+            total = total * factor
+        refs[-1][...] = total.astype(refs[-1].dtype)
+
+    shape = jax.ShapeDtypeStruct(own.shape, F32 if factor is None else BF16)
+    return call("settle", kernel, (me, own, got), (SMEM, VMEM, VMEM), shape, after)
 
 
 def load(me, weight, rows, after, limit, distances=(), share=0):
@@ -232,14 +272,16 @@
 class Links:
     def __init__(self, bits):
         self.bits = bits
-        self.taken = {bit: [] for bit in bits}
-
-    def needs(self, bit, size):
-        if bit == self.bits[0]:
-            return {bit: size * 8e-6}
-        if bit != self.bits[-1]:
-            return {bit: size * 80e-6}
-        return {bit: size * 160e-6, self.bits[-2]: size * 80e-6}
+        self.taken = {link: [] for link in bits[:-2] + ["in", "mid", "out"]}
+
+    def needs(self, stage, size):
+        if stage == self.bits[0]:
+            return {stage: size * 8e-6}
+        if stage == self.bits[-1]:
+            return {"mid": size * 160e-6, "in": size * 112e-6, "out": size * 112e-6}
+        if stage == self.bits[-2]:
+            return {"in": size * 80e-6, "out": size * 80e-6}
+        return {stage: size * 80e-6}
 
     def free(self, bit, now):
         share, until = 1.0, float("inf")
@@ -282,10 +324,12 @@
     def start(c, stage):
         nonlocal clock
         clock += 0.9
-        flights.append((links.send(orders[c][stage], tokens * sizes[c], clock), len(done), c, stage))
+        what = orders[c][stage]
+        size = tokens * sizes[c] * (2 if what == "mid" else 1)
+        flights.append((links.send(what, size, clock), len(done), c, stage))
 
     while wait or flights:
-        flights.sort(key=lambda flight: (flight[3] if RULE else 0, flight))
+        flights.sort()
         arrival = flights[0][0] if flights else float("inf")
         if wait and arrival > clock:
             done.append(("mix", wait[0]))
@@ -300,7 +344,7 @@
                 done.append(("tick", c))
             clock = max(clock, arrival) + 0.1
             done.append(("fold", c))
-            if stage + 1 < len(bits):
+            if stage + 1 < len(orders[c]):
                 start(c, stage + 1)
             elif flights or wait:
                 if c in loads:
@@ -344,8 +388,14 @@
     assert all(begin < end for begin, end in zip(edges[:-1], edges[1:]))
     spans = list(zip(edges[:-1], edges[1:]))
     sizes = [end - begin for begin, end in spans]
-    roles = [bits[:1], bits[1:-2], bits[-2:-1], bits[-1:]]
-    orders = [sum((roles[role] for role in order), []) for order in ORDERS]
+    roles = {0: bits[:1], 1: bits[1:-2], 2: bits[-2:-1], 3: bits[-1:]}
+    orders = [sum((roles.get(role, [role]) for role in order), []) for order in ORDERS]
+    quarter = shards // 4
+    lines = {
+        "in": [(d + end, d + to) for d in range(quarter) for end, to in ((0, quarter), (3 * quarter, 2 * quarter))],
+        "mid": [(d + end, d + 3 * quarter - end) for d in range(quarter) for end in (quarter, 2 * quarter)],
+    }
+    lines["out"] = [(to, end) for end, to in lines["in"]]
     first = FIRST
     loads = [c for what, c in plan(bits, tokens, sizes, orders, first, ()) if what in ("step", "last")]
     total = None
@@ -361,11 +411,21 @@
             loaded[c] = ran(load(me, down_weight, spans[c], after, room // 2**20, *wanted))[0]
             room -= loaded[c].size * 2
         elif what == "fold":
-            bit = orders[c][stages[c]]
+            stage = orders[c][stages[c]]
             stages[c] += 1
-            got = swap(chunks[c], bit)
-            end = stages[c] == len(bits)
-            chunks[c] = ran(fold(me, chunks[c], got, bit, after, factor if end else None))
+            scale = factor if stages[c] == len(orders[c]) else None
+            if stage == "in":
+                got = lax.ppermute(chunks[c], "tensor", lines["in"])
+                chunks[c] = ran(pair(me, chunks[c], got, quarter, after))
+            elif stage == "mid":
+                got = lax.ppermute(chunks[c], "tensor", lines["mid"])
+                chunks[c] = ran(meet(me, chunks[c], got, quarter, after))
+            elif stage == "out":
+                keep, give = chunks[c]
+                got = lax.ppermute(give, "tensor", lines["out"])
+                chunks[c] = ran(settle(me, keep, got, quarter, after, scale))
+            else:
+                chunks[c] = ran(fold(me, chunks[c], swap(chunks[c], stage), stage, after, scale))
         elif what == "tick":
             ran(tick(after))
         elif what == "step":

time: 91.6 us -> 98.3 us (1.073)
  starting transfers between devices: 28.5 us -> 44.3 us
  waiting for transfers between devices: 37 us -> 27.4 us
    ppermute x30 -> x26, waiting for transfers between devices: 37 us -> 22.9 us  [swap(): return lax.ppermute(x, 'tensor', [(d, d ^ bit) for d in range(shards)])]
    ppermute x0 -> x6, starting transfers between devices: none -> 13.2 us  [the longest x2 9.04 us: body(): got = lax.ppermute(chunks[c], 'tensor', lines['in'])]
    ppermute x0 -> x6, waiting for transfers between devices: none -> 4.48 us  [the longest x2 2.32 us: body(): got = lax.ppermute(give, 'tensor', lines['out'])]
    ppermute x30 -> x26, starting transfers between devices: 28.5 us -> 31.1 us  [swap(): return lax.ppermute(x, 'tensor', [(d, d ^ bit) for d in range(shards)])]
    pallas_call x44 -> x47, Pallas kernels: 23.7 us -> 24 us  [call(): pl.pallas_call(kernel, out_shape=shapes, in_specs=list(specs) + [UNREAD]...]
  transfers between devices with their start and end apart: 30 -> 32, of which waited for: 21 -> 16; matrix products, arithmetic and copies ran while one was open for 0% -> 0% of each run, Pallas kernels for 23% -> 22%
where the time goes in v6:
time: 98.3 us; the launch traced here: 97.9 us
  starting transfers between devices  44.3 us (45%)
  waiting for transfers between devices  27.4 us (28%)
  Pallas kernels  24 us (24%)
  local copies, waits for them, and re-layouts  1.75 us (2%)
    ppermute x26, starting transfers between devices, swap(): return lax.ppermute(x, 'tensor', [(d, d ^ bit) for d in range(shards)])  31.1 us
    pallas_call x47, Pallas kernels, call(): pl.pallas_call(kernel, out_shape=shapes, in_specs=list(specs) + [UNREAD]...  24 us
    ppermute x26, waiting for transfers between devices, swap(): return lax.ppermute(x, 'tensor', [(d, d ^ bit) for d in range(shards)])  22.9 us
    ppermute x2, starting transfers between devices, body(): got = lax.ppermute(chunks[c], 'tensor', lines['in'])  9.04 us
    ppermute x2, starting transfers between devices, body(): got = lax.ppermute(give, 'tensor', lines['out'])  2.76 us
    ppermute x2, waiting for transfers between devices, body(): got = lax.ppermute(give, 'tensor', lines['out'])  2.32 us
    ppermute x2, waiting for transfers between devices, body(): got = lax.ppermute(chunks[c], 'tensor', lines['in'])  2.16 us
  transfers between devices with their start and end apart: 32, of which 16 were waited for; matrix products, arithmetic and copies ran while one was open for 0% of the time, Pallas kernels for 22%

profile of v6, /device:TPU:0, one launch (start us, length us, event | category | flops | bytes accessed | tf_op | source)
XLA Modules:
  0.0 97.9 jit_solution(12580147625925958447)
XLA Ops:
  0.0 1.0 %copy-done = bf16[128,1664]{1,0:T(8,128)(2,1)S(1)} copy-done((bf16[128,1664]{1,0:T(8,128)(2,1)S(1)}, bf16[128,1664]{1,0:T(8,128)(2,1)}, u32[]{:S(2)}) %copy-start) | copy-done | bytes 426008
  1.0 0.7 copy-done.1
  1.8 1.2 %mix.4.refs_0_.own_ref = f32[128,384]{1,0:T(8,128)S(1)} custom-call(bf16[128,1664]{1,0:T(8,128)(2,1)S(1)} %copy-done, f32[52,52]{1,0:T(8,128)S(1)} %copy-done.1), custom_call_target="tpu_custom_call" | custom-call | flops 10000000000 | bytes 100000000 | tf_op jit(solution)/shard_map/mix/pallas_call | solution.py:83
  2.9 4.9 %collective-permute-start.1 = (f32[128,384]{1,0:T(8,128)S(1)}, f32[128,384]{1,0:T(8,128)S(1)}, u32[]{:S(2)}, u32[]{:S(2)}) collective-permute-start(f32[128,384]{1,0:T(8,128)S(1)} %mix.4.refs_0_.own_ref), channel_id=1, source_target_pairs={{0,4},{12,8},{1,5},{13,9},{2,6},{14,10},{3,7},{15,11},{16,20},{28,... | collective-permute-start | bytes 589832 | tf_op jit(solution)/shard_map/ppermute | solution.py:418
  7.9 1.2 %mix.5.refs_0_.own_ref = f32[128,384]{1,0:T(8,128)S(1)} custom-call(bf16[128,1664]{1,0:T(8,128)(2,1)S(1)} %copy-done, f32[52,52]{1,0:T(8,128)S(1)} %copy-done.1, f32[128,384]{1,0:T(8,128)S(1)} %mix.4.refs_0_.own_ref), custom_call_target="tpu_custom_call" | custom-call | flops 10000000000 | bytes 100000000 | tf_op jit(solution)/shard_map/mix/pallas_call | solution.py:83
  9.1 1.6 %collective-permute-start = (f32[128,384]{1,0:T(8,128)S(1)}, f32[128,384]{1,0:T(8,128)S(1)}, u32[]{:S(2)}, u32[]{:S(2)}) collective-permute-start(f32[128,384]{1,0:T(8,128)S(1)} %mix.5.refs_0_.own_ref), channel_id=1, source_target_pairs={{0,2},{1,3},{2,0},{3,1},{4,6},{5,7},{6,4},{7,5},{8,10},{9,11},{10,... | collective-permute-start | bytes 589832 | tf_op jit(solution)/shard_map/ppermute | solution.py:374
  10.7 1.2 %mix.6.refs_0_.own_ref = f32[128,384]{1,0:T(8,128)S(1)} custom-call(bf16[128,1664]{1,0:T(8,128)(2,1)S(1)} %copy-done, f32[52,52]{1,0:T(8,128)S(1)} %copy-done.1, f32[128,384]{1,0:T(8,128)S(1)} %mix.5.refs_0_.own_ref), custom_call_target="tpu_custom_call" | custom-call | flops 10000000000 | bytes 100000000 | tf_op jit(solution)/shard_map/mix/pallas_call | solution.py:83
  11.9 0.5 collective-permute-start.4
  12.3 1.2 %mix.7.refs_0_.own_ref = f32[128,512]{1,0:T(8,128)S(1)} custom-call(bf16[128,1664]{1,0:T(8,128)(2,1)S(1)} %copy-done, f32[52,52]{1,0:T(8,128)S(1)} %copy-done.1, f32[128,384]{1,0:T(8,128)S(1)} %mix.6.refs_0_.own_ref), custom_call_target="tpu_custom_call" | custom-call | flops 10000000000 | bytes 100000000 | tf_op jit(solution)/shard_map/mix/pallas_call | solution.py:83
  13.5 0.6 collective-permute-start.5
  14.1 1.4 %collective-permute-done.got_ref = f32[128,384]{1,0:T(8,128)S(1)} collective-permute-done((f32[128,384]{1,0:T(8,128)S(1)}, f32[128,384]{1,0:T(8,128)S(1)}, u32[]{:S(2)}, u32[]{:S(2)}) %collective-permute-start) | collective-permute-done | bytes 196640 | tf_op jit(solution)/shard_map/ppermute | solution.py:374
  15.6 0.1 collective-permute-start.2
  15.7 0.7 collective-permute-start.10
  16.4 0.7 collective-permute-done.2.got_ref
  17.1 4.1 %collective-permute-start.3 = (f32[128,384]{1,0:T(8,128)S(1)}, f32[128,384]{1,0:T(8,128)S(1)}, u32[]{:S(2)}, u32[]{:S(2)}) collective-permute-start(f32[128,384]{1,0:T(8,128)S(1)} %fold.13.refs_0_.own_ref), channel_id=1, source_target_pairs={{0,4},{12,8},{1,5},{13,9},{2,6},{14,10},{3,7},{15,11},{16,20},{28,... | collective-permute-start | bytes 589832 | tf_op jit(solution)/shard_map/ppermute | solution.py:418
  21.2 2.8 %load.4 = (bf16[384,8192]{1,0:T(8,128)(2,1)S(1)}, f32[8,128]{1,0:T(8,128)S(1)}) custom-call(s32[1]{0:T(128)} %bitcast.me_ref, bf16[1664,8192]{1,0:T(8,128)(2,1)} %weight_ref.7, f32[128,384]{1,0:T(8,128)S(1)} %fold.13.refs_0_.own_ref), custom_call_target="tpu_custom_call" | custom-call | flops 10000000000 | bytes 100000000 | tf_op jit(solution)/shard_map/load/pallas_call | solution.py:83
  24.1 0.1 collective-permute-start.9
  24.2 0.1 collective-permute-start.7
  24.3 2.2 %collective-permute-done.3.got_ref = f32[128,384]{1,0:T(8,128)S(1)} collective-permute-done((f32[128,384]{1,0:T(8,128)S(1)}, f32[128,384]{1,0:T(8,128)S(1)}, u32[]{:S(2)}, u32[]{:S(2)}) %collective-permute-start.3) | collective-permute-done | bytes 196640 | tf_op jit(solution)/shard_map/ppermute | solution.py:418
  26.6 2.8 %load.5 = (bf16[384,8192]{1,0:T(8,128)(2,1)S(1)}, f32[8,128]{1,0:T(8,128)S(1)}) custom-call(s32[1]{0:T(128)} %bitcast.me_ref, bf16[1664,8192]{1,0:T(8,128)(2,1)} %weight_ref.7, f32[128,384]{1,0:T(8,128)S(1)} %fold.16.refs_0_.own_ref), custom_call_target="tpu_custom_call" | custom-call | flops 10000000000 | bytes 100000000 | tf_op jit(solution)/shard_map/load/pallas_call | solution.py:83
  29.4 2.5 %collective-permute-start.8 = (f32[128,384]{1,0:T(8,128)S(1)}, f32[128,384]{1,0:T(8,128)S(1)}, u32[]{:S(2)}, u32[]{:S(2)}) collective-permute-start(f32[128,384]{1,0:T(8,128)S(1)} %fold.16.refs_0_.own_ref), channel_id=1, source_target_pairs={{0,4},{1,5},{2,6},{3,7},{4,0},{5,1},{6,2},{7,3},{8,12},{9,13},{10,... | collective-permute-start | bytes 589832 | tf_op jit(solution)/shard_map/ppermute | solution.py:374
  31.9 0.7 collective-permute-start.6
  32.7 1.3 %collective-permute-start.14 = (f32[128,384]{1,0:T(8,128)S(1)}, f32[128,384]{1,0:T(8,128)S(1)}, u32[]{:S(2)}, u32[]{:S(2)}) collective-permute-start(f32[128,384]{1,0:T(8,128)S(1)} %get-tuple-element.47.refs_0_), channel_id=1, source_target_pairs={{4,0},{8,12},{5,1},{9,13},{6,2},{10,14},{7,3},{11,15},{20,16},{24,... | collective-permute-start | bytes 589832 | tf_op jit(solution)/shard_map/ppermute | solution.py:425
  34.1 3.4 %load.6 = (bf16[512,8192]{1,0:T(8,128)(2,1)S(1)}, f32[8,128]{1,0:T(8,128)S(1)}) custom-call(s32[1]{0:T(128)} %bitcast.me_ref, bf16[1664,8192]{1,0:T(8,128)(2,1)} %weight_ref.7, f32[128,512]{1,0:T(8,128)S(1)} %fold.17.refs_0_.own_ref), custom_call_target="tpu_custom_call" | custom-call | flops 10000000000 | bytes 100000000 | tf_op jit(solution)/shard_map/load/pallas_call | solution.py:83
  37.6 3.7 %collective-permute-start.13 = (f32[128,512]{1,0:T(8,128)S(1)}, f32[128,512]{1,0:T(8,128)S(1)}, u32[]{:S(2)}, u32[]{:S(2)}) collective-permute-start(f32[128,512]{1,0:T(8,128)S(1)} %fold.18.refs_0_.own_ref), channel_id=1, source_target_pairs={{0,8},{1,9},{2,10},{3,11},{4,12},{5,13},{6,14},{7,15},{8,0},{9,1},... | collective-permute-start | bytes 786440 | tf_op jit(solution)/shard_map/ppermute | solution.py:374
  41.3 1.6 %collective-permute-start.17 = (f32[128,384]{1,0:T(8,128)S(1)}, f32[128,384]{1,0:T(8,128)S(1)}, u32[]{:S(2)}, u32[]{:S(2)}) collective-permute-start(f32[128,384]{1,0:T(8,128)S(1)} %fold.19.refs_0_.own_ref), channel_id=1, source_target_pairs={{0,2},{1,3},{2,0},{3,1},{4,6},{5,7},{6,4},{7,5},{8,10},{9,11},{10,... | collective-permute-start | bytes 589832 | tf_op jit(solution)/shard_map/ppermute | solution.py:374
  43.0 0.1 collective-permute-start.15
  43.1 1.5 %collective-permute-start.12 = (f32[128,384]{1,0:T(8,128)S(1)}, f32[128,384]{1,0:T(8,128)S(1)}, u32[]{:S(2)}, u32[]{:S(2)}) collective-permute-start(f32[128,384]{1,0:T(8,128)S(1)} %get-tuple-element.50.refs_0_), channel_id=1, source_target_pairs={{4,0},{8,12},{5,1},{9,13},{6,2},{10,14},{7,3},{11,15},{20,16},{24,... | collective-permute-start | bytes 589832 | tf_op jit(solution)/shard_map/ppermute | solution.py:425
  44.6 0.6 collective-permute-start.16
  45.2 3.8 %collective-permute-done.17.got_ref = f32[128,384]{1,0:T(8,128)S(1)} collective-permute-done((f32[128,384]{1,0:T(8,128)S(1)}, f32[128,384]{1,0:T(8,128)S(1)}, u32[]{:S(2)}, u32[]{:S(2)}) %collective-permute-start.17) | collective-permute-done | bytes 196640 | tf_op jit(solution)/shard_map/ppermute | solution.py:374
  49.0 1.3 %step.3.refs_0_.refs_2_ = f32[16,128,512]{2,1,0:T(8,128)S(1)} custom-call(bf16[128,384]{1,0:T(8,128)(2,1)S(1)} %fold.21.refs_0_.refs_2_, bf16[384,8192]{1,0:T(8,128)(2,1)S(1)} %get-tuple-element.52.refs_1_, bf16[128,384]{1,0:T(8,128)(2,1)S(1)} %fold.21.refs_0_.refs_2_), custom_call_target="tpu_custom_call" | custom-call | flops 10000000000 | bytes 100000000 | tf_op jit(solution)/shard_map/step/pallas_call | solution.py:83
  50.3 3.0 %load.7 = (bf16[384,8192]{1,0:T(8,128)(2,1)S(1)}, f32[8,128]{1,0:T(8,128)S(1)}) custom-call(s32[1]{0:T(128)} %bitcast.me_ref, bf16[1664,8192]{1,0:T(8,128)(2,1)} %weight_ref.7, f32[16,128,512]{2,1,0:T(8,128)S(1)} %step.3.refs_0_.refs_2_), custom_call_target="tpu_custom_call" | custom-call | flops 10000000000 | bytes 100000000 | tf_op jit(solution)/shard_map/load/pallas_call | solution.py:83
  53.3 1.4 %step.4.refs_0_.refs_2_ = f32[16,128,512]{2,1,0:T(8,128)S(1)} custom-call(bf16[128,384]{1,0:T(8,128)(2,1)S(1)} %fold.22.refs_0_.refs_3_, bf16[384,8192]{1,0:T(8,128)(2,1)S(1)} %get-tuple-element.54.refs_1_, f32[16,128,512]{2,1,0:T(8,128)S(1)} %step.3.refs_0_.refs_2_, bf16[128,384]{1,0:T(8,128)(2,1)S(1)} %fold.22.refs_0_.refs_3_), custom_call_target="tpu_custom_call" | custom-call | flops 10000000000 | bytes 100000000 | tf_op jit(solution)/shard_map/step/pallas_call | solution.py:83
  54.8 1.5 %step.5.refs_0_.total_ref = f32[16,128,512]{2,1,0:T(8,128)S(1)} custom-call(bf16[128,512]{1,0:T(8,128)(2,1)S(1)} %fold.23.refs_0_.refs_3_, bf16[512,8192]{1,0:T(8,128)(2,1)S(1)} %get-tuple-element.55.refs_1_, f32[16,128,512]{2,1,0:T(8,128)S(1)} %step.4.refs_0_.refs_2_, bf16[128,512]{1,0:T(8,128)(2,1)S(1)} %fold.23.refs_0_.refs_3_), custom_call_target="tpu_custom_call" | custom-call | flops 10000000000 | bytes 100000000 | tf_op jit(solution)/shard_map/step/pallas_call | solution.py:83
  56.3 2.3 %collective-permute-done.12.got_ref = f32[128,384]{1,0:T(8,128)S(1)} collective-permute-done((f32[128,384]{1,0:T(8,128)S(1)}, f32[128,384]{1,0:T(8,128)S(1)}, u32[]{:S(2)}, u32[]{:S(2)}) %collective-permute-start.12) | collective-permute-done | bytes 196640 | tf_op jit(solution)/shard_map/ppermute | solution.py:425
  58.6 0.7 product.2
  59.4 0.2 collective-permute-start.19
  59.5 0.4 collective-permute-start.18
  59.9 0.8 product.3
  60.7 1.4 %collective-permute-done.19.got_ref = f32[8,128,256]{2,1,0:T(8,128)S(1)} collective-permute-done((f32[8,128,256]{2,1,0:T(8,128)S(1)}, f32[8,128,256]{2,1,0:T(8,128)S(1)}, u32[]{:S(2)}, u32[]{:S(2)}) %collective-permute-start.19) | collective-permute-done | bytes 1048608 | tf_op jit(solution)/shard_map/ppermute | solution.py:374
  62.1 0.1 halve.10
  62.2 1.6 %collective-permute-start.23 = (f32[4,64,256]{2,1,0:T(8,128)S(1)}, f32[4,64,256]{2,1,0:T(8,128)S(1)}, u32[]{:S(2)}, u32[]{:S(2)}) collective-permute-start(f32[4,64,256]{2,1,0:T(8,128)S(1)} %get-tuple-element.68), channel_id=1, source_target_pairs={{0,2},{1,3},{2,0},{3,1},{4,6},{5,7},{6,4},{7,5},{8,10},{9,11},{10,... | collective-permute-start | bytes 786440 | tf_op jit(solution)/shard_map/ppermute | solution.py:374
  63.8 5.1 %collective-permute-start.21 = (f32[4,64,256]{2,1,0:T(8,128)S(1)}, f32[4,64,256]{2,1,0:T(8,128)S(1)}, u32[]{:S(2)}, u32[]{:S(2)}) collective-permute-start(f32[4,64,256]{2,1,0:T(8,128)S(1)} %get-tuple-element.61.refs_0_), channel_id=1, source_target_pairs={{0,8},{1,9},{2,10},{3,11},{4,12},{5,13},{6,14},{7,15},{8,0},{9,1},... | collective-permute-start | bytes 786440 | tf_op jit(solution)/shard_map/ppermute | solution.py:374
  69.0 0.1 halve.11
  69.1 0.6 collective-permute-start.22
  69.7 1.0 collective-permute-done.23.got_ref
  70.7 4.0 %collective-permute-start.27 = (f32[2,64,256]{2,1,0:T(8,128)S(1)}, f32[2,64,256]{2,1,0:T(8,128)S(1)}, u32[]{:S(2)}, u32[]{:S(2)}) collective-permute-start(f32[2,64,256]{2,1,0:T(8,128)S(1)} %get-tuple-element.69.refs_0_), channel_id=1, source_target_pairs={{0,4},{1,5},{2,6},{3,7},{4,0},{5,1},{6,2},{7,3},{8,12},{9,13},{10,... | collective-permute-start | bytes 393224 | tf_op jit(solution)/shard_map/ppermute | solution.py:374
  74.6 2.3 %collective-permute-done.22.got_ref = f32[4,64,256]{2,1,0:T(8,128)S(1)} collective-permute-done((f32[4,64,256]{2,1,0:T(8,128)S(1)}, f32[4,64,256]{2,1,0:T(8,128)S(1)}, u32[]{:S(2)}, u32[]{:S(2)}) %collective-permute-start.22) | collective-permute-done | bytes 262176 | tf_op jit(solution)/shard_map/ppermute | solution.py:374
  77.0 2.5 %collective-permute-start.25 = (f32[2,64,256]{2,1,0:T(8,128)S(1)}, f32[2,64,256]{2,1,0:T(8,128)S(1)}, u32[]{:S(2)}, u32[]{:S(2)}) collective-permute-start(f32[2,64,256]{2,1,0:T(8,128)S(1)} %get-tuple-element.70.refs_0_), channel_id=1, source_target_pairs={{0,4},{1,5},{2,6},{3,7},{4,0},{5,1},{6,2},{7,3},{8,12},{9,13},{10,... | collective-permute-start | bytes 393224 | tf_op jit(solution)/shard_map/ppermute | solution.py:374
  79.5 1.6 %collective-permute-done.21.got_ref = f32[4,64,256]{2,1,0:T(8,128)S(1)} collective-permute-done((f32[4,64,256]{2,1,0:T(8,128)S(1)}, f32[4,64,256]{2,1,0:T(8,128)S(1)}, u32[]{:S(2)}, u32[]{:S(2)}) %collective-permute-start.21) | collective-permute-done | bytes 262176 | tf_op jit(solution)/shard_map/ppermute | solution.py:374
  81.1 0.6 collective-permute-start.26
  81.6 2.8 %collective-permute-done.20.got_ref = f32[4,64,256]{2,1,0:T(8,128)S(1)} collective-permute-done((f32[4,64,256]{2,1,0:T(8,128)S(1)}, f32[4,64,256]{2,1,0:T(8,128)S(1)}, u32[]{:S(2)}, u32[]{:S(2)}) %collective-permute-start.20) | collective-permute-done | bytes 262176 | tf_op jit(solution)/shard_map/ppermute | solution.py:374
  84.5 1.6 %collective-permute-start.24 = (f32[2,64,256]{2,1,0:T(8,128)S(1)}, f32[2,64,256]{2,1,0:T(8,128)S(1)}, u32[]{:S(2)}, u32[]{:S(2)}) collective-permute-start(f32[2,64,256]{2,1,0:T(8,128)S(1)} %get-tuple-element.73.refs_0_), channel_id=1, source_target_pairs={{0,2},{1,3},{2,0},{3,1},{4,6},{5,7},{6,4},{7,5},{8,10},{9,11},{10,... | collective-permute-start | bytes 393224 | tf_op jit(solution)/shard_map/ppermute | solution.py:374
  86.0 0.9 collective-permute-done.27.got_ref
  86.9 0.1 collective-permute-start.29
  87.0 0.5 collective-permute-done.26.got_ref
  87.5 0.1 collective-permute-start.30
  87.6 1.6 %collective-permute-done.25.got_ref = f32[2,64,256]{2,1,0:T(8,128)S(1)} collective-permute-done((f32[2,64,256]{2,1,0:T(8,128)S(1)}, f32[2,64,256]{2,1,0:T(8,128)S(1)}, u32[]{:S(2)}, u32[]{:S(2)}) %collective-permute-start.25) | collective-permute-done | bytes 131104 | tf_op jit(solution)/shard_map/ppermute | solution.py:374
  89.2 0.9 collective-permute-start.31
  90.1 2.2 %collective-permute-start.28 = (f32[1,64,256]{2,1,0:T(8,128)S(1)}, f32[1,64,256]{2,1,0:T(8,128)S(1)}, u32[]{:S(2)}, u32[]{:S(2)}) collective-permute-start(f32[1,64,256]{2,1,0:T(8,128)S(1)} %get-tuple-element.81.refs_0_), channel_id=1, source_target_pairs={{0,8},{1,9},{2,10},{3,11},{4,12},{5,13},{6,14},{7,15},{8,0},{9,1},... | collective-permute-start | bytes 196616 | tf_op jit(solution)/shard_map/ppermute | solution.py:374
  92.3 2.4 %collective-permute-done.29.got_ref = f32[1,64,256]{2,1,0:T(8,128)S(1)} collective-permute-done((f32[1,64,256]{2,1,0:T(8,128)S(1)}, f32[1,64,256]{2,1,0:T(8,128)S(1)}, u32[]{:S(2)}, u32[]{:S(2)}) %collective-permute-start.29) | collective-permute-done | bytes 65568 | tf_op jit(solution)/shard_map/ppermute | solution.py:374
  94.8 1.1 %collective-permute-done.31.got_ref = f32[1,64,256]{2,1,0:T(8,128)S(1)} collective-permute-done((f32[1,64,256]{2,1,0:T(8,128)S(1)}, f32[1,64,256]{2,1,0:T(8,128)S(1)}, u32[]{:S(2)}, u32[]{:S(2)}) %collective-permute-start.31) | collective-permute-done | bytes 65568 | tf_op jit(solution)/shard_map/ppermute | solution.py:374
  95.9 1.4 %collective-permute-done.28.got_ref = f32[1,64,256]{2,1,0:T(8,128)S(1)} collective-permute-done((f32[1,64,256]{2,1,0:T(8,128)S(1)}, f32[1,64,256]{2,1,0:T(8,128)S(1)}, u32[]{:S(2)}, u32[]{:S(2)}) %collective-permute-start.28) | collective-permute-done | bytes 65568 | tf_op jit(solution)/shard_map/ppermute | solution.py:374
  97.3 0.7 finish.7
  (51 shorter events, 0.9 us)
Async XLA Ops:
  0.0 1.0 %copy-start = (bf16[128,1664]{1,0:T(8,128)(2,1)S(1)}, bf16[128,1664]{1,0:T(8,128)(2,1)}, u32[]{:S(2)}) copy-start(bf16[128,1664]{1,0:T(8,128)(2,1)} %activations.7) | copy-start | bytes 1277956
  1.0 0.7 copy-start.1
  2.9 11.1 %collective-permute-start.1 = (f32[128,384]{1,0:T(8,128)S(1)}, f32[128,384]{1,0:T(8,128)S(1)}, u32[]{:S(2)}, u32[]{:S(2)}) collective-permute-start(f32[128,384]{1,0:T(8,128)S(1)} %mix.4.refs_0_.own_ref), channel_id=1, source_target_pairs={{0,4},{12,8},{1,5},{13,9},{2,6},{14,10},{3,7},{15,11},{16,20},{28,... | collective-permute-start | bytes 589832 | tf_op jit(solution)/shard_map/ppermute | solution.py:418
  9.1 6.5 %collective-permute-start = (f32[128,384]{1,0:T(8,128)S(1)}, f32[128,384]{1,0:T(8,128)S(1)}, u32[]{:S(2)}, u32[]{:S(2)}) collective-permute-start(f32[128,384]{1,0:T(8,128)S(1)} %mix.5.refs_0_.own_ref), channel_id=1, source_target_pairs={{0,2},{1,3},{2,0},{3,1},{4,6},{5,7},{6,4},{7,5},{8,10},{9,11},{10,... | collective-permute-start | bytes 589832 | tf_op jit(solution)/shard_map/ppermute | solution.py:374
  11.9 12.3 %collective-permute-start.4 = (f32[128,384]{1,0:T(8,128)S(1)}, f32[128,384]{1,0:T(8,128)S(1)}, u32[]{:S(2)}, u32[]{:S(2)}) collective-permute-start(f32[128,384]{1,0:T(8,128)S(1)} %mix.6.refs_0_.own_ref), channel_id=1, source_target_pairs={{0,8},{1,9},{2,10},{3,11},{4,12},{5,13},{6,14},{7,15},{8,0},{9,1},... | collective-permute-start | bytes 589832 | tf_op jit(solution)/shard_map/ppermute | solution.py:374
  13.5 10.6 %collective-permute-start.5 = (f32[128,512]{1,0:T(8,128)S(1)}, f32[128,512]{1,0:T(8,128)S(1)}, u32[]{:S(2)}, u32[]{:S(2)}) collective-permute-start(f32[128,512]{1,0:T(8,128)S(1)} %mix.7.refs_0_.own_ref), channel_id=1, source_target_pairs={{0,2},{1,3},{2,0},{3,1},{4,6},{5,7},{6,4},{7,5},{8,10},{9,11},{10,... | collective-permute-start | bytes 786440 | tf_op jit(solution)/shard_map/ppermute | solution.py:374
  15.6 1.5 %collective-permute-start.2 = (f32[128,384]{1,0:T(8,128)S(1)}, f32[128,384]{1,0:T(8,128)S(1)}, u32[]{:S(2)}, u32[]{:S(2)}) collective-permute-start(f32[128,384]{1,0:T(8,128)S(1)} %fold.12.refs_0_.own_ref), channel_id=1, source_target_pairs={{0,1},{1,0},{2,3},{3,2},{4,5},{5,4},{6,7},{7,6},{8,9},{9,8},{10,11... | collective-permute-start | bytes 589832 | tf_op jit(solution)/shard_map/ppermute | solution.py:374
  15.7 16.9 %collective-permute-start.10 = (f32[2,128,384]{2,1,0:T(8,128)S(1)}, f32[2,128,384]{2,1,0:T(8,128)S(1)}, u32[]{:S(2)}, u32[]{:S(2)}) collective-permute-start(f32[2,128,384]{2,1,0:T(8,128)S(1)} %pair.2.refs_0_.own_ref), channel_id=1, source_target_pairs={{4,8},{8,4},{5,9},{9,5},{6,10},{10,6},{7,11},{11,7},{20,24},{24,20... | collective-permute-start | bytes 1179656 | tf_op jit(solution)/shard_map/ppermute | solution.py:421
  17.1 9.3 %collective-permute-start.3 = (f32[128,384]{1,0:T(8,128)S(1)}, f32[128,384]{1,0:T(8,128)S(1)}, u32[]{:S(2)}, u32[]{:S(2)}) collective-permute-start(f32[128,384]{1,0:T(8,128)S(1)} %fold.13.refs_0_.own_ref), channel_id=1, source_target_pairs={{0,4},{12,8},{1,5},{13,9},{2,6},{14,10},{3,7},{15,11},{16,20},{28,... | collective-permute-start | bytes 589832 | tf_op jit(solution)/shard_map/ppermute | solution.py:418
  24.1 9.9 %collective-permute-start.9 = (f32[128,512]{1,0:T(8,128)S(1)}, f32[128,512]{1,0:T(8,128)S(1)}, u32[]{:S(2)}, u32[]{:S(2)}) collective-permute-start(f32[128,512]{1,0:T(8,128)S(1)} %fold.14.refs_0_.own_ref), channel_id=1, source_target_pairs={{0,4},{1,5},{2,6},{3,7},{4,0},{5,1},{6,2},{7,3},{8,12},{9,13},{10,... | collective-permute-start | bytes 786440 | tf_op jit(solution)/shard_map/ppermute | solution.py:374
  24.2 2.3 %collective-permute-start.7 = (f32[128,384]{1,0:T(8,128)S(1)}, f32[128,384]{1,0:T(8,128)S(1)}, u32[]{:S(2)}, u32[]{:S(2)}) collective-permute-start(f32[128,384]{1,0:T(8,128)S(1)} %fold.15.refs_0_.own_ref), channel_id=1, source_target_pairs={{0,1},{1,0},{2,3},{3,2},{4,5},{5,4},{6,7},{7,6},{8,9},{9,8},{10,11... | collective-permute-start | bytes 589832 | tf_op jit(solution)/shard_map/ppermute | solution.py:374
  29.4 11.9 %collective-permute-start.8 = (f32[128,384]{1,0:T(8,128)S(1)}, f32[128,384]{1,0:T(8,128)S(1)}, u32[]{:S(2)}, u32[]{:S(2)}) collective-permute-start(f32[128,384]{1,0:T(8,128)S(1)} %fold.16.refs_0_.own_ref), channel_id=1, source_target_pairs={{0,4},{1,5},{2,6},{3,7},{4,0},{5,1},{6,2},{7,3},{8,12},{9,13},{10,... | collective-permute-start | bytes 589832 | tf_op jit(solution)/shard_map/ppermute | solution.py:374
  31.9 11.0 %collective-permute-start.6 = (f32[2,128,384]{2,1,0:T(8,128)S(1)}, f32[2,128,384]{2,1,0:T(8,128)S(1)}, u32[]{:S(2)}, u32[]{:S(2)}) collective-permute-start(f32[2,128,384]{2,1,0:T(8,128)S(1)} %pair.3.refs_0_.own_ref), channel_id=1, source_target_pairs={{4,8},{8,4},{5,9},{9,5},{6,10},{10,6},{7,11},{11,7},{20,24},{24,20... | collective-permute-start | bytes 1179656 | tf_op jit(solution)/shard_map/ppermute | solution.py:421
  32.7 10.3 %collective-permute-start.14 = (f32[128,384]{1,0:T(8,128)S(1)}, f32[128,384]{1,0:T(8,128)S(1)}, u32[]{:S(2)}, u32[]{:S(2)}) collective-permute-start(f32[128,384]{1,0:T(8,128)S(1)} %get-tuple-element.47.refs_0_), channel_id=1, source_target_pairs={{4,0},{8,12},{5,1},{9,13},{6,2},{10,14},{7,3},{11,15},{20,16},{24,... | collective-permute-start | bytes 589832 | tf_op jit(solution)/shard_map/ppermute | solution.py:425
  34.0 3.5 %collective-permute-start.11 = (f32[128,512]{1,0:T(8,128)S(1)}, f32[128,512]{1,0:T(8,128)S(1)}, u32[]{:S(2)}, u32[]{:S(2)}) collective-permute-start(f32[128,512]{1,0:T(8,128)S(1)} %fold.17.refs_0_.own_ref), channel_id=1, source_target_pairs={{0,1},{1,0},{2,3},{3,2},{4,5},{5,4},{6,7},{7,6},{8,9},{9,8},{10,11... | collective-permute-start | bytes 786440 | tf_op jit(solution)/shard_map/ppermute | solution.py:374
  37.6 17.1 %collective-permute-start.13 = (f32[128,512]{1,0:T(8,128)S(1)}, f32[128,512]{1,0:T(8,128)S(1)}, u32[]{:S(2)}, u32[]{:S(2)}) collective-permute-start(f32[128,512]{1,0:T(8,128)S(1)} %fold.18.refs_0_.own_ref), channel_id=1, source_target_pairs={{0,8},{1,9},{2,10},{3,11},{4,12},{5,13},{6,14},{7,15},{8,0},{9,1},... | collective-permute-start | bytes 786440 | tf_op jit(solution)/shard_map/ppermute | solution.py:374
  41.3 7.7 %collective-permute-start.17 = (f32[128,384]{1,0:T(8,128)S(1)}, f32[128,384]{1,0:T(8,128)S(1)}, u32[]{:S(2)}, u32[]{:S(2)}) collective-permute-start(f32[128,384]{1,0:T(8,128)S(1)} %fold.19.refs_0_.own_ref), channel_id=1, source_target_pairs={{0,2},{1,3},{2,0},{3,1},{4,6},{5,7},{6,4},{7,5},{8,10},{9,11},{10,... | collective-permute-start | bytes 589832 | tf_op jit(solution)/shard_map/ppermute | solution.py:374
  43.0 1.6 %collective-permute-start.15 = (f32[128,384]{1,0:T(8,128)S(1)}, f32[128,384]{1,0:T(8,128)S(1)}, u32[]{:S(2)}, u32[]{:S(2)}) collective-permute-start(f32[128,384]{1,0:T(8,128)S(1)} %settle.2.refs_0_.own_ref), channel_id=1, source_target_pairs={{0,1},{1,0},{2,3},{3,2},{4,5},{5,4},{6,7},{7,6},{8,9},{9,8},{10,11... | collective-permute-start | bytes 589832 | tf_op jit(solution)/shard_map/ppermute | solution.py:374
  43.1 15.5 %collective-permute-start.12 = (f32[128,384]{1,0:T(8,128)S(1)}, f32[128,384]{1,0:T(8,128)S(1)}, u32[]{:S(2)}, u32[]{:S(2)}) collective-permute-start(f32[128,384]{1,0:T(8,128)S(1)} %get-tuple-element.50.refs_0_), channel_id=1, source_target_pairs={{4,0},{8,12},{5,1},{9,13},{6,2},{10,14},{7,3},{11,15},{20,16},{24,... | collective-permute-start | bytes 589832 | tf_op jit(solution)/shard_map/ppermute | solution.py:425
  44.6 8.7 %collective-permute-start.16 = (f32[128,384]{1,0:T(8,128)S(1)}, f32[128,384]{1,0:T(8,128)S(1)}, u32[]{:S(2)}, u32[]{:S(2)}) collective-permute-start(f32[128,384]{1,0:T(8,128)S(1)} %fold.20.refs_0_.own_ref), channel_id=1, source_target_pairs={{0,2},{1,3},{2,0},{3,1},{4,6},{5,7},{6,4},{7,5},{8,10},{9,11},{10,... | collective-permute-start | bytes 589832 | tf_op jit(solution)/shard_map/ppermute | solution.py:374
  59.4 2.7 %collective-permute-start.19 = (f32[8,128,256]{2,1,0:T(8,128)S(1)}, f32[8,128,256]{2,1,0:T(8,128)S(1)}, u32[]{:S(2)}, u32[]{:S(2)}) collective-permute-start(f32[8,128,256]{2,1,0:T(8,128)S(1)} %get-tuple-element.60), channel_id=1, source_target_pairs={{0,1},{1,0},{2,3},{3,2},{4,5},{5,4},{6,7},{7,6},{8,9},{9,8},{10,11... | collective-permute-start | bytes 3145736 | tf_op jit(solution)/shard_map/ppermute | solution.py:374
  59.5 9.4 %collective-permute-start.18 = (f32[8,128,256]{2,1,0:T(8,128)S(1)}, f32[8,128,256]{2,1,0:T(8,128)S(1)}, u32[]{:S(2)}, u32[]{:S(2)}) collective-permute-start(f32[8,128,256]{2,1,0:T(8,128)S(1)} %get-tuple-element.57.refs_0_), channel_id=1, source_target_pairs={{0,1},{1,0},{2,3},{3,2},{4,5},{5,4},{6,7},{7,6},{8,9},{9,8},{10,11... | collective-permute-start | bytes 3145736 | tf_op jit(solution)/shard_map/ppermute | solution.py:374
  62.2 8.4 %collective-permute-start.23 = (f32[4,64,256]{2,1,0:T(8,128)S(1)}, f32[4,64,256]{2,1,0:T(8,128)S(1)}, u32[]{:S(2)}, u32[]{:S(2)}) collective-permute-start(f32[4,64,256]{2,1,0:T(8,128)S(1)} %get-tuple-element.68), channel_id=1, source_target_pairs={{0,2},{1,3},{2,0},{3,1},{4,6},{5,7},{6,4},{7,5},{8,10},{9,11},{10,... | collective-permute-start | bytes 786440 | tf_op jit(solution)/shard_map/ppermute | solution.py:374
  63.8 17.2 %collective-permute-start.21 = (f32[4,64,256]{2,1,0:T(8,128)S(1)}, f32[4,64,256]{2,1,0:T(8,128)S(1)}, u32[]{:S(2)}, u32[]{:S(2)}) collective-permute-start(f32[4,64,256]{2,1,0:T(8,128)S(1)} %get-tuple-element.61.refs_0_), channel_id=1, source_target_pairs={{0,8},{1,9},{2,10},{3,11},{4,12},{5,13},{6,14},{7,15},{8,0},{9,1},... | collective-permute-start | bytes 786440 | tf_op jit(solution)/shard_map/ppermute | solution.py:374
  69.1 7.9 %collective-permute-start.22 = (f32[4,64,256]{2,1,0:T(8,128)S(1)}, f32[4,64,256]{2,1,0:T(8,128)S(1)}, u32[]{:S(2)}, u32[]{:S(2)}) collective-permute-start(f32[4,64,256]{2,1,0:T(8,128)S(1)} %get-tuple-element.66.refs_0_), channel_id=1, source_target_pairs={{0,2},{1,3},{2,0},{3,1},{4,6},{5,7},{6,4},{7,5},{8,10},{9,11},{10,... | collective-permute-start | bytes 786440 | tf_op jit(solution)/shard_map/ppermute | solution.py:374
  69.7 14.8 %collective-permute-start.20 = (f32[4,64,256]{2,1,0:T(8,128)S(1)}, f32[4,64,256]{2,1,0:T(8,128)S(1)}, u32[]{:S(2)}, u32[]{:S(2)}) collective-permute-start(f32[4,64,256]{2,1,0:T(8,128)S(1)} %get-tuple-element.63), channel_id=1, source_target_pairs={{0,4},{1,5},{2,6},{3,7},{4,0},{5,1},{6,2},{7,3},{8,12},{9,13},{10,... | collective-permute-start | bytes 786440 | tf_op jit(solution)/shard_map/ppermute | solution.py:374
  70.7 16.2 %collective-permute-start.27 = (f32[2,64,256]{2,1,0:T(8,128)S(1)}, f32[2,64,256]{2,1,0:T(8,128)S(1)}, u32[]{:S(2)}, u32[]{:S(2)}) collective-permute-start(f32[2,64,256]{2,1,0:T(8,128)S(1)} %get-tuple-element.69.refs_0_), channel_id=1, source_target_pairs={{0,4},{1,5},{2,6},{3,7},{4,0},{5,1},{6,2},{7,3},{8,12},{9,13},{10,... | collective-permute-start | bytes 393224 | tf_op jit(solution)/shard_map/ppermute | solution.py:374
  77.0 12.3 %collective-permute-start.25 = (f32[2,64,256]{2,1,0:T(8,128)S(1)}, f32[2,64,256]{2,1,0:T(8,128)S(1)}, u32[]{:S(2)}, u32[]{:S(2)}) collective-permute-start(f32[2,64,256]{2,1,0:T(8,128)S(1)} %get-tuple-element.70.refs_0_), channel_id=1, source_target_pairs={{0,4},{1,5},{2,6},{3,7},{4,0},{5,1},{6,2},{7,3},{8,12},{9,13},{10,... | collective-permute-start | bytes 393224 | tf_op jit(solution)/shard_map/ppermute | solution.py:374
  81.1 6.4 %collective-permute-start.26 = (f32[2,64,256]{2,1,0:T(8,128)S(1)}, f32[2,64,256]{2,1,0:T(8,128)S(1)}, u32[]{:S(2)}, u32[]{:S(2)}) collective-permute-start(f32[2,64,256]{2,1,0:T(8,128)S(1)} %get-tuple-element.71.refs_0_), channel_id=1, source_target_pairs={{0,2},{1,3},{2,0},{3,1},{4,6},{5,7},{6,4},{7,5},{8,10},{9,11},{10,... | collective-permute-start | bytes 393224 | tf_op jit(solution)/shard_map/ppermute | solution.py:374
  84.5 5.6 %collective-permute-start.24 = (f32[2,64,256]{2,1,0:T(8,128)S(1)}, f32[2,64,256]{2,1,0:T(8,128)S(1)}, u32[]{:S(2)}, u32[]{:S(2)}) collective-permute-start(f32[2,64,256]{2,1,0:T(8,128)S(1)} %get-tuple-element.73.refs_0_), channel_id=1, source_target_pairs={{0,2},{1,3},{2,0},{3,1},{4,6},{5,7},{6,4},{7,5},{8,10},{9,11},{10,... | collective-permute-start | bytes 393224 | tf_op jit(solution)/shard_map/ppermute | solution.py:374
  86.9 7.8 %collective-permute-start.29 = (f32[1,64,256]{2,1,0:T(8,128)S(1)}, f32[1,64,256]{2,1,0:T(8,128)S(1)}, u32[]{:S(2)}, u32[]{:S(2)}) collective-permute-start(f32[1,64,256]{2,1,0:T(8,128)S(1)} %get-tuple-element.77.refs_0_), channel_id=1, source_target_pairs={{0,8},{1,9},{2,10},{3,11},{4,12},{5,13},{6,14},{7,15},{8,0},{9,1},... | collective-permute-start | bytes 196616 | tf_op jit(solution)/shard_map/ppermute | solution.py:374
  87.5 7.2 %collective-permute-start.30 = (f32[1,64,256]{2,1,0:T(8,128)S(1)}, f32[1,64,256]{2,1,0:T(8,128)S(1)}, u32[]{:S(2)}, u32[]{:S(2)}) collective-permute-start(f32[1,64,256]{2,1,0:T(8,128)S(1)} %get-tuple-element.78.refs_0_), channel_id=1, source_target_pairs={{0,4},{1,5},{2,6},{3,7},{4,0},{5,1},{6,2},{7,3},{8,12},{9,13},{10,... | collective-permute-start | bytes 196616 | tf_op jit(solution)/shard_map/ppermute | solution.py:374
  89.2 6.6 %collective-permute-start.31 = (f32[1,64,256]{2,1,0:T(8,128)S(1)}, f32[1,64,256]{2,1,0:T(8,128)S(1)}, u32[]{:S(2)}, u32[]{:S(2)}) collective-permute-start(f32[1,64,256]{2,1,0:T(8,128)S(1)} %get-tuple-element.79.refs_0_), channel_id=1, source_target_pairs={{0,8},{1,9},{2,10},{3,11},{4,12},{5,13},{6,14},{7,15},{8,0},{9,1},... | collective-permute-start | bytes 196616 | tf_op jit(solution)/shard_map/ppermute | solution.py:374
  90.1 7.1 %collective-permute-start.28 = (f32[1,64,256]{2,1,0:T(8,128)S(1)}, f32[1,64,256]{2,1,0:T(8,128)S(1)}, u32[]{:S(2)}, u32[]{:S(2)}) collective-permute-start(f32[1,64,256]{2,1,0:T(8,128)S(1)} %get-tuple-element.81.refs_0_), channel_id=1, source_target_pairs={{0,8},{1,9},{2,10},{3,11},{4,12},{5,13},{6,14},{7,15},{8,0},{9,1},... | collective-permute-start | bytes 196616 | tf_op jit(solution)/shard_map/ppermute | solution.py:374

commit v7 on v5

--- a/solution.py
+++ b/solution.py
@@ -13,11 +13,7 @@
 BF16 = jnp.bfloat16
 
 
-TILES = (3, 3, 3, 4)
-ORDERS = ((3, 1, 2, 0), (0, 3, 1, 2), (2, 0, 3, 1), (1, 2, 0, 3))
-FIRST = (0, 2, 3, 1)
-PATIENCE = 1.8
-RULE = 1
+TILES = (6, 7)
 
 
 def quotient(index, divisor, limit):
@@ -101,16 +97,34 @@
     return call("mix", kernel, (activations, small), (VMEM, VMEM), shape, after)
 
 
-def fold(me, own, got, bit, after, factor=None):
-    def kernel(me_ref, own_ref, got_ref, *refs):
-        sign = jnp.where((me_ref[0] & bit) != 0, -1.0, 1.0).astype(F32)
-        total = got_ref[...] + own_ref[...] * sign
-        if factor is not None:
-            total = total * factor
-        refs[-1][...] = total.astype(refs[-1].dtype)
-
-    shape = jax.ShapeDtypeStruct(own.shape, F32 if factor is None else BF16)
-    return call("fold", kernel, (me, own, got), (SMEM, VMEM, VMEM), shape, after)
+def spread(blocks, after):
+    shards, rows, cols = blocks.shape
+
+    def kernel(blocks_ref, *refs):
+        out = refs[-1]
+        for at in range(0, cols, LANES):
+            end = min(at + LANES, cols)
+            values = [blocks_ref[s, :, at:end] for s in range(shards)]
+            reach = 1
+            while reach < shards:
+                values = [
+                    values[s ^ reach] - values[s] if s & reach else values[s] + values[s ^ reach]
+                    for s in range(shards)
+                ]
+                reach *= 2
+            for s in range(shards):
+                out[s, :, at:end] = values[s]
+
+    shape = jax.ShapeDtypeStruct(blocks.shape, F32)
+    return call("spread", kernel, (blocks,), (VMEM,), shape, after)
+
+
+def settle(values, factor, after):
+    def kernel(values_ref, *refs):
+        refs[-1][...] = (values_ref[...] * factor).astype(BF16)
+
+    shape = jax.ShapeDtypeStruct(values.shape, BF16)
+    return call("settle", kernel, (values,), (VMEM,), shape, after)
 
 
 def load(me, weight, rows, after, limit, distances=(), share=0):
@@ -270,51 +284,6 @@
         return now + 0.3
 
 
-def plan(bits, tokens, sizes, orders, first, loads):
-    links = Links(bits)
-    clock = 1.8
-    flights = []
-    done = []
-    wait = list(first)
-    loads = list(loads)
-    missing = list(loads)
-
-    def start(c, stage):
-        nonlocal clock
-        clock += 0.9
-        flights.append((links.send(orders[c][stage], tokens * sizes[c], clock), len(done), c, stage))
-
-    while wait or flights:
-        flights.sort(key=lambda flight: (flight[3] if RULE else 0, flight))
-        arrival = flights[0][0] if flights else float("inf")
-        if wait and arrival > clock:
-            done.append(("mix", wait[0]))
-            clock += 1.2
-            start(wait.pop(0), 0)
-        elif loads and arrival - clock > PATIENCE:
-            done.append(("load", loads.pop(0)))
-            clock += 2.8
-        else:
-            _, began, c, stage = flights.pop(0)
-            if began == len(done):
-                done.append(("tick", c))
-            clock = max(clock, arrival) + 0.1
-            done.append(("fold", c))
-            if stage + 1 < len(bits):
-                start(c, stage + 1)
-            elif flights or wait:
-                if c in loads:
-                    loads.remove(c)
-                    done.append(("load", c))
-                    clock += 2.8
-                done.append(("step", c))
-                clock += 1.3
-            else:
-                done += [("load", c) for c in loads]
-                done.append(("last", c))
-    return done
-
-
 def body(activations, rotation_small, down_weight):
     shards = lax.axis_size("tensor")
     me = lax.axis_index("tensor").astype(jnp.int32).reshape(1)
@@ -343,32 +312,26 @@
     edges = [min(local, end * LANES) for end in ends]
     assert all(begin < end for begin, end in zip(edges[:-1], edges[1:]))
     spans = list(zip(edges[:-1], edges[1:]))
-    sizes = [end - begin for begin, end in spans]
-    roles = [bits[:1], bits[1:-2], bits[-2:-1], bits[-1:]]
-    orders = [sum((roles[role] for role in order), []) for order in ORDERS]
-    first = FIRST
-    loads = [c for what, c in plan(bits, tokens, sizes, orders, first, ()) if what in ("step", "last")]
+    count = len(spans)
+
+    def exchange(x):
+        return lax.all_to_all(x, "tensor", split_axis=0, concat_axis=0)
+
+    room = 40 * 2**20
+    chunks, loaded = [], []
+    for span in spans:
+        x = ran(mix(activations, rotation_small, (0, tokens), span, after))
+        chunks.append(exchange(x.reshape(shards, tokens // shards, -1)))
+    for c, span in enumerate(spans):
+        wanted = (distances, share) if c == count - 1 else ()
+        loaded.append(ran(load(me, down_weight, span, after, room // 2**20, *wanted))[0])
+        room -= loaded[c].size * 2
+    for c in range(count):
+        chunks[c] = exchange(ran(spread(chunks[c], after))).reshape(tokens, -1)
     total = None
-    loaded = {}
-    chunks = {}
-    stages = [0] * len(spans)
-    room = 40 * 2**20
-    for what, c in plan(bits, tokens, sizes, orders, first, loads):
-        if what == "mix":
-            chunks[c] = ran(mix(activations, rotation_small, (0, tokens), spans[c], after))
-        elif what == "load":
-            wanted = (distances, share) if c == loads[-1] else ()
-            loaded[c] = ran(load(me, down_weight, spans[c], after, room // 2**20, *wanted))[0]
-            room -= loaded[c].size * 2
-        elif what == "fold":
-            bit = orders[c][stages[c]]
-            stages[c] += 1
-            got = swap(chunks[c], bit)
-            end = stages[c] == len(bits)
-            chunks[c] = ran(fold(me, chunks[c], got, bit, after, factor if end else None))
-        elif what == "tick":
-            ran(tick(after))
-        elif what == "step":
+    for c in range(count):
+        chunks[c] = ran(settle(chunks[c], factor, after))
+        if c < count - 1:
             total = ran(step(chunks[c], loaded[c], total, shards, after))
 
     inner = bits[1:]
@@ -407,7 +370,7 @@
         held = pieces + [(rows, part, None)] if last else []
         pieces.append((rows, part, ran(finish(held, keep, got, tokens, width, parts, after))))
 
-    last_chunk, last_columns = chunks[loads[-1]], loaded[loads[-1]]
+    last_chunk, last_columns = chunks[-1], loaded[-1]
     sends = ran(product(me, last_chunk, last_columns, total, 0, distances[:len(near)], parts, after))
     clock += 0.9
     kernels += 1

time: 91.6 us -> 132 us (1.44)
  local copies, waits for them, and re-layouts: 1.75 us -> 27.6 us
  waiting for transfers between devices: 37 us -> 45.4 us
  starting transfers between devices: 28.5 us -> 35.8 us
  Pallas kernels: 23.7 us -> 22 us
    all_to_all x0 -> x4, waiting for transfers between devices: none -> 28.6 us  [exchange(): return lax.all_to_all(x, 'tensor', split_axis=0, concat_axis=0)]
    unnamed x4 -> x22, local copies, waits for them, and re-layouts: 1.75 us -> 27.6 us
    all_to_all x0 -> x4, starting transfers between devices: none -> 20.8 us  [exchange(): return lax.all_to_all(x, 'tensor', split_axis=0, concat_axis=0)]
    ppermute x30 -> x14, waiting for transfers between devices: 37 us -> 16.8 us  [swap(): return lax.ppermute(x, 'tensor', [(d, d ^ bit) for d in range(shards)])]
    ppermute x30 -> x14, starting transfers between devices: 28.5 us -> 14.9 us  [swap(): return lax.ppermute(x, 'tensor', [(d, d ^ bit) for d in range(shards)])]
    pallas_call x44 -> x25, Pallas kernels: 23.7 us -> 22 us  [call(): pl.pallas_call(kernel, out_shape=shapes, in_specs=list(specs) + [UNREAD]...]
  transfers between devices with their start and end apart: 30 -> 18, of which waited for: 21 -> 13; matrix products, arithmetic and copies ran while one was open for 0% -> 0% of each run, Pallas kernels for 23% -> 14%
where the time goes in v7:
time: 132 us; the launch traced here: 131 us
  waiting for transfers between devices  45.4 us (34%)
  starting transfers between devices  35.8 us (27%)
  local copies, waits for them, and re-layouts  27.6 us (21%)
  Pallas kernels  22 us (17%)
    all_to_all x4, waiting for transfers between devices, exchange(): return lax.all_to_all(x, 'tensor', split_axis=0, concat_axis=0)  28.6 us
    unnamed x22, local copies, waits for them, and re-layouts  27.6 us
    pallas_call x25, Pallas kernels, call(): pl.pallas_call(kernel, out_shape=shapes, in_specs=list(specs) + [UNREAD]...  22 us
    all_to_all x4, starting transfers between devices, exchange(): return lax.all_to_all(x, 'tensor', split_axis=0, concat_axis=0)  20.8 us
    ppermute x14, waiting for transfers between devices, swap(): return lax.ppermute(x, 'tensor', [(d, d ^ bit) for d in range(shards)])  16.8 us
    ppermute x14, starting transfers between devices, swap(): return lax.ppermute(x, 'tensor', [(d, d ^ bit) for d in range(shards)])  14.9 us
  transfers between devices with their start and end apart: 18, of which 13 were waited for; matrix products, arithmetic and copies ran while one was open for 0% of the time, Pallas kernels for 14%

profile of v7, /device:TPU:0, one launch (start us, length us, event | category | flops | bytes accessed | tf_op | source)
XLA Modules:
  0.0 131.0 jit_solution(6180770060609854074)
XLA Ops:
  0.0 0.0 copy-start
  0.0 1.0 copy-done
  1.0 0.7 copy-done.2
  1.8 2.2 %mix.2.refs_0_ = f32[128,768]{1,0:T(8,128)} custom-call(bf16[128,1664]{1,0:T(8,128)(2,1)S(1)} %copy-done, f32[52,52]{1,0:T(8,128)S(1)} %copy-done.2), custom_call_target="tpu_custom_call" | custom-call | flops 10000000000 | bytes 100000000 | tf_op jit(solution)/shard_map/mix/pallas_call | solution.py:80
  4.0 7.4 %all-to-all-start.1 = ((f32[16,8,768]{2,1,0:T(8,128)}), f32[16,8,768]{2,1,0:T(8,128)S(1)}, u32[]{:S(2)}, u32[]{:S(2)}) async-start(f32[16,8,768]{2,1,0:T(8,128)} %bitcast.2), calls=%async_computation.1 | async-start | bytes 786432 | tf_op jit(solution)/shard_map/all_to_all | solution.py:318
  11.4 0.0 copy-done.1
  11.4 0.0 copy-done.3
  11.4 2.6 %mix.3.refs_0_ = f32[128,896]{1,0:T(8,128)} custom-call(bf16[128,1664]{1,0:T(8,128)(2,1)S(1)} %copy-done.1, f32[52,52]{1,0:T(8,128)S(1)} %copy-done.3, f32[128,768]{1,0:T(8,128)} %mix.2.refs_0_), custom_call_target="tpu_custom_call" | custom-call | flops 10000000000 | bytes 100000000 | tf_op jit(solution)/shard_map/mix/pallas_call | solution.py:80
  14.0 4.6 %load.2 = (bf16[768,8192]{1,0:T(8,128)(2,1)S(1)}, f32[8,128]{1,0:T(8,128)S(1)}) custom-call(s32[1]{0:T(128)} %bitcast.me_ref, bf16[1664,8192]{1,0:T(8,128)(2,1)} %weight_ref.3, f32[128,896]{1,0:T(8,128)} %mix.3.refs_0_), custom_call_target="tpu_custom_call" | custom-call | flops 10000000000 | bytes 100000000 | tf_op jit(solution)/shard_map/load/pallas_call | solution.py:80
  18.6 0.0 copy-start.6
  18.6 4.6 %copy-done.6 = bf16[768,8192]{1,0:T(8,128)(2,1)} copy-done((bf16[768,8192]{1,0:T(8,128)(2,1)}, bf16[768,8192]{1,0:T(8,128)(2,1)S(1)}, u32[]{:S(2)}) %copy-start.6) | copy-done | bytes 12582936
  23.3 5.4 %load.3 = (bf16[896,8192]{1,0:T(8,128)(2,1)S(1)}, f32[8,128]{1,0:T(8,128)S(1)}) custom-call(s32[1]{0:T(128)} %bitcast.me_ref, bf16[1664,8192]{1,0:T(8,128)(2,1)} %weight_ref.3, f32[8,128]{1,0:T(8,128)S(1)} %get-tuple-element.37.refs_0_), custom_call_target="tpu_custom_call" | custom-call | flops 10000000000 | bytes 100000000 | tf_op jit(solution)/shard_map/load/pallas_call | solution.py:80
  28.7 0.0 copy-start.4
  28.7 5.2 %copy-done.4 = bf16[896,8192]{1,0:T(8,128)(2,1)} copy-done((bf16[896,8192]{1,0:T(8,128)(2,1)}, bf16[896,8192]{1,0:T(8,128)(2,1)S(1)}, u32[]{:S(2)}) %copy-start.4) | copy-done | bytes 14680088
  33.9 0.0 all-to-all-done.1.blocks_ref
  33.9 6.0 %all-to-all-start = ((f32[16,8,896]{2,1,0:T(8,128)}), f32[16,8,896]{2,1,0:T(8,128)S(1)}, u32[]{:S(2)}, u32[]{:S(2)}) async-start(f32[16,8,896]{2,1,0:T(8,128)} %bitcast.1), calls=%async_computation | async-start | bytes 917504 | tf_op jit(solution)/shard_map/all_to_all | solution.py:318
  39.9 0.8 spread.2.refs_0_
  40.7 12.4 %all-to-all-done.blocks_ref = f32[16,8,896]{2,1,0:T(8,128)S(1)} async-done(((f32[16,8,896]{2,1,0:T(8,128)}), f32[16,8,896]{2,1,0:T(8,128)S(1)}, u32[]{:S(2)}, u32[]{:S(2)}) %all-to-all-start) | async-done | bytes 458784 | tf_op jit(solution)/shard_map/all_to_all | solution.py:318
  53.2 3.9 %all-to-all-start.3 = ((f32[16,8,768]{2,1,0:T(8,128)}), f32[16,8,768]{2,1,0:T(8,128)S(1)}, u32[]{:S(2)}, u32[]{:S(2)}) async-start(f32[16,8,768]{2,1,0:T(8,128)} %spread.2.refs_0_), calls=%async_computation.3 | async-start | bytes 786432 | tf_op jit(solution)/shard_map/all_to_all | solution.py:318
  57.1 0.8 spread.3.refs_0_
  57.9 11.4 %all-to-all-done.3 = f32[16,8,768]{2,1,0:T(8,128)S(1)} async-done(((f32[16,8,768]{2,1,0:T(8,128)}), f32[16,8,768]{2,1,0:T(8,128)S(1)}, u32[]{:S(2)}, u32[]{:S(2)}) %all-to-all-start.3) | async-done | bytes 393248 | tf_op jit(solution)/shard_map/all_to_all | solution.py:318
  69.3 3.6 %all-to-all-start.2 = ((f32[16,8,896]{2,1,0:T(8,128)}), f32[16,8,896]{2,1,0:T(8,128)S(1)}, u32[]{:S(2)}, u32[]{:S(2)}) async-start(f32[16,8,896]{2,1,0:T(8,128)} %spread.3.refs_0_), calls=%async_computation.2 | async-start | bytes 917504 | tf_op jit(solution)/shard_map/all_to_all | solution.py:318
  72.9 0.0 copy-start.7
  72.9 4.6 %copy-done.7 = bf16[768,8192]{1,0:T(8,128)(2,1)S(1)} copy-done((bf16[768,8192]{1,0:T(8,128)(2,1)S(1)}, bf16[768,8192]{1,0:T(8,128)(2,1)}, u32[]{:S(2)}) %copy-start.7) | copy-done | bytes 12582936
  77.5 1.8 %step.1.refs_0_.total_ref = f32[16,128,512]{2,1,0:T(8,128)S(1)} custom-call(bf16[128,768]{1,0:T(8,128)(2,1)S(1)} %settle.2.refs_0_.refs_2_, bf16[768,8192]{1,0:T(8,128)(2,1)S(1)} %copy-done.7, bf16[128,768]{1,0:T(8,128)(2,1)S(1)} %settle.2.refs_0_.refs_2_), custom_call_target="tpu_custom_call" | custom-call | flops 10000000000 | bytes 100000000 | tf_op jit(solution)/shard_map/step/pallas_call | solution.py:80
  79.3 0.0 copy-start.8
  79.3 2.0 %copy-done.8 = f32[16,128,512]{2,1,0:T(8,128)} copy-done((f32[16,128,512]{2,1,0:T(8,128)}, f32[16,128,512]{2,1,0:T(8,128)S(1)}, u32[]{:S(2)}) %copy-start.8) | copy-done | bytes 4194328
  81.3 4.8 %all-to-all-done.2 = f32[16,8,896]{2,1,0:T(8,128)S(1)} async-done(((f32[16,8,896]{2,1,0:T(8,128)}), f32[16,8,896]{2,1,0:T(8,128)S(1)}, u32[]{:S(2)}, u32[]{:S(2)}) %all-to-all-start.2) | async-done | bytes 458784 | tf_op jit(solution)/shard_map/all_to_all | solution.py:318
  86.0 2.2 %copy-done.9 = f32[16,128,512]{2,1,0:T(8,128)S(1)} copy-done((f32[16,128,512]{2,1,0:T(8,128)S(1)}, f32[16,128,512]{2,1,0:T(8,128)}, u32[]{:S(2)}) %copy-start.9) | copy-done | bytes 4194328
  88.3 2.1 %copy-done.10 = f32[16,128,512]{2,1,0:T(8,128)S(1)} copy-done((f32[16,128,512]{2,1,0:T(8,128)S(1)}, f32[16,128,512]{2,1,0:T(8,128)}, u32[]{:S(2)}) %copy-start.10) | copy-done | bytes 4194328
  90.4 5.2 %copy-done.5 = bf16[896,8192]{1,0:T(8,128)(2,1)S(1)} copy-done((bf16[896,8192]{1,0:T(8,128)(2,1)S(1)}, bf16[896,8192]{1,0:T(8,128)(2,1)}, u32[]{:S(2)}) %copy-start.5) | copy-done | bytes 14680088
  95.6 1.3 product.2
  96.9 0.2 collective-permute-start.1
  97.0 0.4 collective-permute-start
  97.4 1.3 product.3
  98.7 0.9 collective-permute-done.1.got_ref
  99.6 0.1 halve.10
  99.7 0.9 collective-permute-start.5
  100.6 1.4 %collective-permute-start.3 = (f32[4,64,256]{2,1,0:T(8,128)S(1)}, f32[4,64,256]{2,1,0:T(8,128)S(1)}, u32[]{:S(2)}, u32[]{:S(2)}) collective-permute-start(f32[4,64,256]{2,1,0:T(8,128)S(1)} %get-tuple-element.45.refs_0_), channel_id=1, source_target_pairs={{0,8},{1,9},{2,10},{3,11},{4,12},{5,13},{6,14},{7,15},{8,0},{9,1},... | collective-permute-start | bytes 786440 | tf_op jit(solution)/shard_map/ppermute | solution.py:299
  101.9 0.0 collective-permute-done.got_ref
  101.9 0.1 halve.11
  102.0 1.5 %collective-permute-start.2 = (f32[4,64,256]{2,1,0:T(8,128)S(1)}, f32[4,64,256]{2,1,0:T(8,128)S(1)}, u32[]{:S(2)}, u32[]{:S(2)}) collective-permute-start(f32[4,64,256]{2,1,0:T(8,128)S(1)} %get-tuple-element.47), channel_id=1, source_target_pairs={{0,4},{1,5},{2,6},{3,7},{4,0},{5,1},{6,2},{7,3},{8,12},{9,13},{10,... | collective-permute-start | bytes 786440 | tf_op jit(solution)/shard_map/ppermute | solution.py:299
  103.6 0.5 collective-permute-start.4
  104.1 4.8 %collective-permute-done.5.got_ref = f32[4,64,256]{2,1,0:T(8,128)S(1)} collective-permute-done((f32[4,64,256]{2,1,0:T(8,128)S(1)}, f32[4,64,256]{2,1,0:T(8,128)S(1)}, u32[]{:S(2)}, u32[]{:S(2)}) %collective-permute-start.5) | collective-permute-done | bytes 262176 | tf_op jit(solution)/shard_map/ppermute | solution.py:299
  108.9 1.3 collective-permute-start.9
  110.2 3.5 %collective-permute-done.4.got_ref = f32[4,64,256]{2,1,0:T(8,128)S(1)} collective-permute-done((f32[4,64,256]{2,1,0:T(8,128)S(1)}, f32[4,64,256]{2,1,0:T(8,128)S(1)}, u32[]{:S(2)}, u32[]{:S(2)}) %collective-permute-start.4) | collective-permute-done | bytes 262176 | tf_op jit(solution)/shard_map/ppermute | solution.py:299
  113.8 1.5 %collective-permute-start.7 = (f32[2,64,256]{2,1,0:T(8,128)S(1)}, f32[2,64,256]{2,1,0:T(8,128)S(1)}, u32[]{:S(2)}, u32[]{:S(2)}) collective-permute-start(f32[2,64,256]{2,1,0:T(8,128)S(1)} %get-tuple-element.54.refs_0_), channel_id=1, source_target_pairs={{0,4},{1,5},{2,6},{3,7},{4,0},{5,1},{6,2},{7,3},{8,12},{9,13},{10,... | collective-permute-start | bytes 393224 | tf_op jit(solution)/shard_map/ppermute | solution.py:299
  115.3 0.2 collective-permute-done.3.got_ref
  115.5 1.1 collective-permute-start.8
  116.6 0.0 collective-permute-done.2.got_ref
  116.6 1.1 collective-permute-start.6
  117.7 1.1 collective-permute-done.9.got_ref
  118.8 1.7 %collective-permute-start.11 = (f32[1,64,256]{2,1,0:T(8,128)S(1)}, f32[1,64,256]{2,1,0:T(8,128)S(1)}, u32[]{:S(2)}, u32[]{:S(2)}) collective-permute-start(f32[1,64,256]{2,1,0:T(8,128)S(1)} %get-tuple-element.61.refs_0_), channel_id=1, source_target_pairs={{0,8},{1,9},{2,10},{3,11},{4,12},{5,13},{6,14},{7,15},{8,0},{9,1},... | collective-permute-start | bytes 196616 | tf_op jit(solution)/shard_map/ppermute | solution.py:299
  120.5 1.0 collective-permute-done.8.got_ref
  121.6 0.3 collective-permute-start.12
  121.9 0.0 collective-permute-done.7.got_ref
  122.0 2.9 %collective-permute-start.13 = (f32[1,64,256]{2,1,0:T(8,128)S(1)}, f32[1,64,256]{2,1,0:T(8,128)S(1)}, u32[]{:S(2)}, u32[]{:S(2)}) collective-permute-start(f32[1,64,256]{2,1,0:T(8,128)S(1)} %get-tuple-element.63.refs_0_), channel_id=1, source_target_pairs={{0,8},{1,9},{2,10},{3,11},{4,12},{5,13},{6,14},{7,15},{8,0},{9,1},... | collective-permute-start | bytes 196616 | tf_op jit(solution)/shard_map/ppermute | solution.py:299
  124.9 0.0 collective-permute-done.6.got_ref
  124.9 0.1 collective-permute-start.10
  125.0 0.9 collective-permute-done.11.got_ref
  125.9 1.3 collective-permute-done.12.got_ref
  127.2 2.4 %collective-permute-done.13.got_ref = f32[1,64,256]{2,1,0:T(8,128)S(1)} collective-permute-done((f32[1,64,256]{2,1,0:T(8,128)S(1)}, f32[1,64,256]{2,1,0:T(8,128)S(1)}, u32[]{:S(2)}, u32[]{:S(2)}) %collective-permute-start.13) | collective-permute-done | bytes 65568 | tf_op jit(solution)/shard_map/ppermute | solution.py:299
  129.7 0.7 collective-permute-done.10.got_ref
  130.4 0.7 finish.7
  (19 shorter events, 0.3 us)
Async XLA Ops:
  0.0 1.0 copy-start
  1.0 0.7 copy-start.2
  1.8 9.6 %copy-start.1 = (bf16[128,1664]{1,0:T(8,128)(2,1)S(1)}, bf16[128,1664]{1,0:T(8,128)(2,1)}, u32[]{:S(2)}) copy-start(bf16[128,1664]{1,0:T(8,128)(2,1)} %activations.3) | copy-start | bytes 1277956
  1.8 9.7 %copy-start.3 = (f32[52,52]{1,0:T(8,128)S(1)}, f32[52,52]{1,0:T(8,128)}, u32[]{:S(2)}) copy-start(f32[52,52]{1,0:T(8,128)} %small.3) | copy-start | bytes 32452
  4.0 29.9 %all-to-all-start.1 = ((f32[16,8,768]{2,1,0:T(8,128)}), f32[16,8,768]{2,1,0:T(8,128)S(1)}, u32[]{:S(2)}, u32[]{:S(2)}) async-start(f32[16,8,768]{2,1,0:T(8,128)} %bitcast.2), calls=%async_computation.1 | async-start | bytes 786432 | tf_op jit(solution)/shard_map/all_to_all | solution.py:318
  18.6 4.6 %copy-start.6 = (bf16[768,8192]{1,0:T(8,128)(2,1)}, bf16[768,8192]{1,0:T(8,128)(2,1)S(1)}, u32[]{:S(2)}) copy-start(bf16[768,8192]{1,0:T(8,128)(2,1)S(1)} %get-tuple-element.39.refs_1_) | copy-start | bytes 37748740
  28.7 5.2 %copy-start.4 = (bf16[896,8192]{1,0:T(8,128)(2,1)}, bf16[896,8192]{1,0:T(8,128)(2,1)S(1)}, u32[]{:S(2)}) copy-start(bf16[896,8192]{1,0:T(8,128)(2,1)S(1)} %get-tuple-element.40.columns_ref) | copy-start | bytes 44040196
  33.9 19.3 %all-to-all-start = ((f32[16,8,896]{2,1,0:T(8,128)}), f32[16,8,896]{2,1,0:T(8,128)S(1)}, u32[]{:S(2)}, u32[]{:S(2)}) async-start(f32[16,8,896]{2,1,0:T(8,128)} %bitcast.1), calls=%async_computation | async-start | bytes 917504 | tf_op jit(solution)/shard_map/all_to_all | solution.py:318
  53.2 16.1 %all-to-all-start.3 = ((f32[16,8,768]{2,1,0:T(8,128)}), f32[16,8,768]{2,1,0:T(8,128)S(1)}, u32[]{:S(2)}, u32[]{:S(2)}) async-start(f32[16,8,768]{2,1,0:T(8,128)} %spread.2.refs_0_), calls=%async_computation.3 | async-start | bytes 786432 | tf_op jit(solution)/shard_map/all_to_all | solution.py:318
  69.3 16.8 %all-to-all-start.2 = ((f32[16,8,896]{2,1,0:T(8,128)}), f32[16,8,896]{2,1,0:T(8,128)S(1)}, u32[]{:S(2)}, u32[]{:S(2)}) async-start(f32[16,8,896]{2,1,0:T(8,128)} %spread.3.refs_0_), calls=%async_computation.2 | async-start | bytes 917504 | tf_op jit(solution)/shard_map/all_to_all | solution.py:318
  72.9 4.6 %copy-start.7 = (bf16[768,8192]{1,0:T(8,128)(2,1)S(1)}, bf16[768,8192]{1,0:T(8,128)(2,1)}, u32[]{:S(2)}) copy-start(bf16[768,8192]{1,0:T(8,128)(2,1)} %copy-done.6) | copy-start | bytes 37748740
  79.3 2.0 %copy-start.8 = (f32[16,128,512]{2,1,0:T(8,128)}, f32[16,128,512]{2,1,0:T(8,128)S(1)}, u32[]{:S(2)}) copy-start(f32[16,128,512]{2,1,0:T(8,128)S(1)} %step.1.refs_0_.total_ref) | copy-start | bytes 12582916
  86.0 2.2 %copy-start.9 = (f32[16,128,512]{2,1,0:T(8,128)S(1)}, f32[16,128,512]{2,1,0:T(8,128)}, u32[]{:S(2)}) copy-start(f32[16,128,512]{2,1,0:T(8,128)} %copy-done.8) | copy-start | bytes 12582916
  88.2 2.2 %copy-start.10 = (f32[16,128,512]{2,1,0:T(8,128)S(1)}, f32[16,128,512]{2,1,0:T(8,128)}, u32[]{:S(2)}) copy-start(f32[16,128,512]{2,1,0:T(8,128)} %copy-done.8) | copy-start | bytes 12582916
  90.4 5.2 %copy-start.5 = (bf16[896,8192]{1,0:T(8,128)(2,1)S(1)}, bf16[896,8192]{1,0:T(8,128)(2,1)}, u32[]{:S(2)}) copy-start(bf16[896,8192]{1,0:T(8,128)(2,1)} %copy-done.4) | copy-start | bytes 44040196
  96.9 2.7 %collective-permute-start.1 = (f32[8,128,256]{2,1,0:T(8,128)S(1)}, f32[8,128,256]{2,1,0:T(8,128)S(1)}, u32[]{:S(2)}, u32[]{:S(2)}) collective-permute-start(f32[8,128,256]{2,1,0:T(8,128)S(1)} %get-tuple-element.44), channel_id=1, source_target_pairs={{0,1},{1,0},{2,3},{3,2},{4,5},{5,4},{6,7},{7,6},{8,9},{9,8},{10,11... | collective-permute-start | bytes 3145736 | tf_op jit(solution)/shard_map/ppermute | solution.py:299
  97.0 4.9 %collective-permute-start = (f32[8,128,256]{2,1,0:T(8,128)S(1)}, f32[8,128,256]{2,1,0:T(8,128)S(1)}, u32[]{:S(2)}, u32[]{:S(2)}) collective-permute-start(f32[8,128,256]{2,1,0:T(8,128)S(1)} %get-tuple-element.41.refs_0_), channel_id=1, source_target_pairs={{0,1},{1,0},{2,3},{3,2},{4,5},{5,4},{6,7},{7,6},{8,9},{9,8},{10,11... | collective-permute-start | bytes 3145736 | tf_op jit(solution)/shard_map/ppermute | solution.py:299
  99.7 9.2 %collective-permute-start.5 = (f32[4,64,256]{2,1,0:T(8,128)S(1)}, f32[4,64,256]{2,1,0:T(8,128)S(1)}, u32[]{:S(2)}, u32[]{:S(2)}) collective-permute-start(f32[4,64,256]{2,1,0:T(8,128)S(1)} %get-tuple-element.52), channel_id=1, source_target_pairs={{0,2},{1,3},{2,0},{3,1},{4,6},{5,7},{6,4},{7,5},{8,10},{9,11},{10,... | collective-permute-start | bytes 786440 | tf_op jit(solution)/shard_map/ppermute | solution.py:299
  100.6 14.9 %collective-permute-start.3 = (f32[4,64,256]{2,1,0:T(8,128)S(1)}, f32[4,64,256]{2,1,0:T(8,128)S(1)}, u32[]{:S(2)}, u32[]{:S(2)}) collective-permute-start(f32[4,64,256]{2,1,0:T(8,128)S(1)} %get-tuple-element.45.refs_0_), channel_id=1, source_target_pairs={{0,8},{1,9},{2,10},{3,11},{4,12},{5,13},{6,14},{7,15},{8,0},{9,1},... | collective-permute-start | bytes 786440 | tf_op jit(solution)/shard_map/ppermute | solution.py:299
  102.0 14.5 %collective-permute-start.2 = (f32[4,64,256]{2,1,0:T(8,128)S(1)}, f32[4,64,256]{2,1,0:T(8,128)S(1)}, u32[]{:S(2)}, u32[]{:S(2)}) collective-permute-start(f32[4,64,256]{2,1,0:T(8,128)S(1)} %get-tuple-element.47), channel_id=1, source_target_pairs={{0,4},{1,5},{2,6},{3,7},{4,0},{5,1},{6,2},{7,3},{8,12},{9,13},{10,... | collective-permute-start | bytes 786440 | tf_op jit(solution)/shard_map/ppermute | solution.py:299
  103.6 10.1 %collective-permute-start.4 = (f32[4,64,256]{2,1,0:T(8,128)S(1)}, f32[4,64,256]{2,1,0:T(8,128)S(1)}, u32[]{:S(2)}, u32[]{:S(2)}) collective-permute-start(f32[4,64,256]{2,1,0:T(8,128)S(1)} %get-tuple-element.50.refs_0_), channel_id=1, source_target_pairs={{0,2},{1,3},{2,0},{3,1},{4,6},{5,7},{6,4},{7,5},{8,10},{9,11},{10,... | collective-permute-start | bytes 786440 | tf_op jit(solution)/shard_map/ppermute | solution.py:299
  108.9 9.8 %collective-permute-start.9 = (f32[2,64,256]{2,1,0:T(8,128)S(1)}, f32[2,64,256]{2,1,0:T(8,128)S(1)}, u32[]{:S(2)}, u32[]{:S(2)}) collective-permute-start(f32[2,64,256]{2,1,0:T(8,128)S(1)} %get-tuple-element.53.refs_0_), channel_id=1, source_target_pairs={{0,4},{1,5},{2,6},{3,7},{4,0},{5,1},{6,2},{7,3},{8,12},{9,13},{10,... | collective-permute-start | bytes 393224 | tf_op jit(solution)/shard_map/ppermute | solution.py:299
  113.8 8.2 %collective-permute-start.7 = (f32[2,64,256]{2,1,0:T(8,128)S(1)}, f32[2,64,256]{2,1,0:T(8,128)S(1)}, u32[]{:S(2)}, u32[]{:S(2)}) collective-permute-start(f32[2,64,256]{2,1,0:T(8,128)S(1)} %get-tuple-element.54.refs_0_), channel_id=1, source_target_pairs={{0,4},{1,5},{2,6},{3,7},{4,0},{5,1},{6,2},{7,3},{8,12},{9,13},{10,... | collective-permute-start | bytes 393224 | tf_op jit(solution)/shard_map/ppermute | solution.py:299
  115.5 6.1 %collective-permute-start.8 = (f32[2,64,256]{2,1,0:T(8,128)S(1)}, f32[2,64,256]{2,1,0:T(8,128)S(1)}, u32[]{:S(2)}, u32[]{:S(2)}) collective-permute-start(f32[2,64,256]{2,1,0:T(8,128)S(1)} %get-tuple-element.55.refs_0_), channel_id=1, source_target_pairs={{0,2},{1,3},{2,0},{3,1},{4,6},{5,7},{6,4},{7,5},{8,10},{9,11},{10,... | collective-permute-start | bytes 393224 | tf_op jit(solution)/shard_map/ppermute | solution.py:299
  116.6 8.3 %collective-permute-start.6 = (f32[2,64,256]{2,1,0:T(8,128)S(1)}, f32[2,64,256]{2,1,0:T(8,128)S(1)}, u32[]{:S(2)}, u32[]{:S(2)}) collective-permute-start(f32[2,64,256]{2,1,0:T(8,128)S(1)} %get-tuple-element.57.refs_0_), channel_id=1, source_target_pairs={{0,2},{1,3},{2,0},{3,1},{4,6},{5,7},{6,4},{7,5},{8,10},{9,11},{10,... | collective-permute-start | bytes 393224 | tf_op jit(solution)/shard_map/ppermute | solution.py:299
  118.8 7.1 %collective-permute-start.11 = (f32[1,64,256]{2,1,0:T(8,128)S(1)}, f32[1,64,256]{2,1,0:T(8,128)S(1)}, u32[]{:S(2)}, u32[]{:S(2)}) collective-permute-start(f32[1,64,256]{2,1,0:T(8,128)S(1)} %get-tuple-element.61.refs_0_), channel_id=1, source_target_pairs={{0,8},{1,9},{2,10},{3,11},{4,12},{5,13},{6,14},{7,15},{8,0},{9,1},... | collective-permute-start | bytes 196616 | tf_op jit(solution)/shard_map/ppermute | solution.py:299
  121.6 5.6 %collective-permute-start.12 = (f32[1,64,256]{2,1,0:T(8,128)S(1)}, f32[1,64,256]{2,1,0:T(8,128)S(1)}, u32[]{:S(2)}, u32[]{:S(2)}) collective-permute-start(f32[1,64,256]{2,1,0:T(8,128)S(1)} %get-tuple-element.62.refs_0_), channel_id=1, source_target_pairs={{0,4},{1,5},{2,6},{3,7},{4,0},{5,1},{6,2},{7,3},{8,12},{9,13},{10,... | collective-permute-start | bytes 196616 | tf_op jit(solution)/shard_map/ppermute | solution.py:299
  122.0 7.7 %collective-permute-start.13 = (f32[1,64,256]{2,1,0:T(8,128)S(1)}, f32[1,64,256]{2,1,0:T(8,128)S(1)}, u32[]{:S(2)}, u32[]{:S(2)}) collective-permute-start(f32[1,64,256]{2,1,0:T(8,128)S(1)} %get-tuple-element.63.refs_0_), channel_id=1, source_target_pairs={{0,8},{1,9},{2,10},{3,11},{4,12},{5,13},{6,14},{7,15},{8,0},{9,1},... | collective-permute-start | bytes 196616 | tf_op jit(solution)/shard_map/ppermute | solution.py:299
  124.9 5.4 %collective-permute-start.10 = (f32[1,64,256]{2,1,0:T(8,128)S(1)}, f32[1,64,256]{2,1,0:T(8,128)S(1)}, u32[]{:S(2)}, u32[]{:S(2)}) collective-permute-start(f32[1,64,256]{2,1,0:T(8,128)S(1)} %get-tuple-element.65.refs_0_), channel_id=1, source_target_pairs={{0,8},{1,9},{2,10},{3,11},{4,12},{5,13},{6,14},{7,15},{8,0},{9,1},... | collective-permute-start | bytes 196616 | tf_op jit(solution)/shard_map/ppermute | solution.py:299

commit v8 on v6

--- a/solution.py
+++ b/solution.py
@@ -13,10 +13,11 @@
 BF16 = jnp.bfloat16
 
 
-TILES = (3, 3, 3, 4)
-ORDERS = ((3, 0, 2, 1), ("in", "mid", "out", 0, 1), (1, 0, "in", "mid", "out"), (1, 2, 0, 3))
-FIRST = (1, 2, 0, 3)
+TILES = (4, 4, 5)
+ORDERS = ((1, 3, 0, 2), (2, 1, 0, 3), (3, 0, 2, 1))
+FIRST = (2, 1, 0)
 PATIENCE = 1.8
+PIECES = 4
 
 
 def quotient(index, divisor, limit):
@@ -79,7 +80,7 @@
 COST = pl.CostEstimate(flops=10**10, bytes_accessed=10**8, transcendentals=0)
 
 
-def call(name, kernel, operands, specs, shapes, after, scratch=(), limit=16):
+def call(name, kernel, operands, specs, shapes, after, scratch=(), limit=12):
     return pl.pallas_call(
         kernel,
         out_shape=shapes,
@@ -159,8 +160,13 @@
     def kernel(me_ref, weight_ref, *refs):
         out, mark, sems = refs[-3:]
         copies = []
-        if not distances:
-            copies.append(pltpu.make_async_copy(weight_ref.at[begin:end, :], out, sems.at[0]))
+        rows_each = (end - begin) // PIECES // 16 * 16
+        for i in range(PIECES if not distances else 0):
+            low = i * rows_each
+            high = low + rows_each if i + 1 < PIECES else end - begin
+            copies.append(
+                pltpu.make_async_copy(weight_ref.at[begin + low:begin + high, :], out.at[low:high, :], sems.at[i])
+            )
         for i, distance in enumerate(distances):
             column = pl.multiple_of((distance ^ me_ref[0]) * share, LANES)
             copies.append(
@@ -185,7 +191,7 @@
         (SMEM, pl.BlockSpec(memory_space=pltpu.HBM)),
         shapes,
         after,
-        [pltpu.SemaphoreType.DMA((max(1, len(distances)),))],
+        [pltpu.SemaphoreType.DMA((max(PIECES, len(distances)),))],
         limit,
     )
 
@@ -278,7 +284,7 @@
         if stage == self.bits[0]:
             return {stage: size * 8e-6}
         if stage == self.bits[-1]:
-            return {"mid": size * 160e-6, "in": size * 112e-6, "out": size * 112e-6}
+            return {"mid": size * 160e-6, "in": size * 100e-6, "out": size * 100e-6}
         if stage == self.bits[-2]:
             return {"in": size * 80e-6, "out": size * 80e-6}
         return {stage: size * 80e-6}
@@ -323,7 +329,7 @@
 
     def start(c, stage):
         nonlocal clock
-        clock += 0.9
+        clock += 1.2
         what = orders[c][stage]
         size = tokens * sizes[c] * (2 if what == "mid" else 1)
         flights.append((links.send(what, size, clock), len(done), c, stage))

time: 98.3 us -> 93.6 us (0.952)
  starting transfers between devices: 44.3 us -> 34.3 us
  waiting for transfers between devices: 27.4 us -> 35.6 us
  Pallas kernels: 24 us -> 21.4 us
    ppermute x6 -> x0, starting transfers between devices: 13.2 us -> none  [the longest x2 9.04 us: body(): got = lax.ppermute(chunks[c], 'tensor', lines['in'])]
    ppermute x26, waiting for transfers between devices: 22.9 us -> 35.6 us  [swap(): return lax.ppermute(x, 'tensor', [(d, d ^ bit) for d in range(shards)])]
    ppermute x6 -> x0, waiting for transfers between devices: 4.48 us -> none  [the longest x2 2.32 us: body(): got = lax.ppermute(give, 'tensor', lines['out'])]
    ppermute x26, starting transfers between devices: 31.1 us -> 34.3 us  [swap(): return lax.ppermute(x, 'tensor', [(d, d ^ bit) for d in range(shards)])]
    pallas_call x47 -> x37, Pallas kernels: 24 us -> 21.4 us  [call(): pl.pallas_call(kernel, out_shape=shapes, in_specs=list(specs) + [UNREAD]...]
  transfers between devices with their start and end apart: 32 -> 26, of which waited for: 16 -> 15; matrix products, arithmetic and copies ran while one was open for 0% -> 0% of each run, Pallas kernels for 22% -> 20%
where the time goes in v8:
time: 93.6 us; the launch traced here: 93.4 us
  waiting for transfers between devices  35.6 us (38%)
  starting transfers between devices  34.3 us (37%)
  Pallas kernels  21.4 us (23%)
  local copies, waits for them, and re-layouts  1.75 us (2%)
    ppermute x26, waiting for transfers between devices, swap(): return lax.ppermute(x, 'tensor', [(d, d ^ bit) for d in range(shards)])  35.6 us
    ppermute x26, starting transfers between devices, swap(): return lax.ppermute(x, 'tensor', [(d, d ^ bit) for d in range(shards)])  34.3 us
    pallas_call x37, Pallas kernels, call(): pl.pallas_call(kernel, out_shape=shapes, in_specs=list(specs) + [UNREAD]...  21.4 us
  transfers between devices with their start and end apart: 26, of which 15 were waited for; matrix products, arithmetic and copies ran while one was open for 0% of the time, Pallas kernels for 20%

profile of v8, /device:TPU:0, one launch (start us, length us, event | category | flops | bytes accessed | tf_op | source)
XLA Modules:
  0.0 93.4 jit_solution(2559358581292971156)
XLA Ops:
  0.0 1.0 %copy-done = bf16[128,1664]{1,0:T(8,128)(2,1)S(1)} copy-done((bf16[128,1664]{1,0:T(8,128)(2,1)S(1)}, bf16[128,1664]{1,0:T(8,128)(2,1)}, u32[]{:S(2)}) %copy-start) | copy-done | bytes 426008
  1.0 0.7 copy-done.1
  1.8 1.5 %mix.3.refs_0_.own_ref = f32[128,640]{1,0:T(8,128)S(1)} custom-call(bf16[128,1664]{1,0:T(8,128)(2,1)S(1)} %copy-done, f32[52,52]{1,0:T(8,128)S(1)} %copy-done.1), custom_call_target="tpu_custom_call" | custom-call | flops 10000000000 | bytes 100000000 | tf_op jit(solution)/shard_map/mix/pallas_call | solution.py:84
  3.3 4.1 %collective-permute-start.3 = (f32[128,640]{1,0:T(8,128)S(1)}, f32[128,640]{1,0:T(8,128)S(1)}, u32[]{:S(2)}, u32[]{:S(2)}) collective-permute-start(f32[128,640]{1,0:T(8,128)S(1)} %mix.3.refs_0_.own_ref), channel_id=1, source_target_pairs={{0,8},{1,9},{2,10},{3,11},{4,12},{5,13},{6,14},{7,15},{8,0},{9,1},... | collective-permute-start | bytes 983048 | tf_op jit(solution)/shard_map/ppermute | solution.py:380
  7.4 1.2 %mix.4.refs_0_.own_ref = f32[128,512]{1,0:T(8,128)S(1)} custom-call(bf16[128,1664]{1,0:T(8,128)(2,1)S(1)} %copy-done, f32[52,52]{1,0:T(8,128)S(1)} %copy-done.1, f32[128,640]{1,0:T(8,128)S(1)} %mix.3.refs_0_.own_ref), custom_call_target="tpu_custom_call" | custom-call | flops 10000000000 | bytes 100000000 | tf_op jit(solution)/shard_map/mix/pallas_call | solution.py:84
  8.6 1.6 %collective-permute-start.2 = (f32[128,512]{1,0:T(8,128)S(1)}, f32[128,512]{1,0:T(8,128)S(1)}, u32[]{:S(2)}, u32[]{:S(2)}) collective-permute-start(f32[128,512]{1,0:T(8,128)S(1)} %mix.4.refs_0_.own_ref), channel_id=1, source_target_pairs={{0,4},{1,5},{2,6},{3,7},{4,0},{5,1},{6,2},{7,3},{8,12},{9,13},{10,... | collective-permute-start | bytes 786440 | tf_op jit(solution)/shard_map/ppermute | solution.py:380
  10.2 1.2 %mix.5.refs_0_.own_ref = f32[128,512]{1,0:T(8,128)S(1)} custom-call(bf16[128,1664]{1,0:T(8,128)(2,1)S(1)} %copy-done, f32[52,52]{1,0:T(8,128)S(1)} %copy-done.1, f32[128,512]{1,0:T(8,128)S(1)} %mix.4.refs_0_.own_ref), custom_call_target="tpu_custom_call" | custom-call | flops 10000000000 | bytes 100000000 | tf_op jit(solution)/shard_map/mix/pallas_call | solution.py:84
  11.4 1.6 %collective-permute-start = (f32[128,512]{1,0:T(8,128)S(1)}, f32[128,512]{1,0:T(8,128)S(1)}, u32[]{:S(2)}, u32[]{:S(2)}) collective-permute-start(f32[128,512]{1,0:T(8,128)S(1)} %mix.5.refs_0_.own_ref), channel_id=1, source_target_pairs={{0,2},{1,3},{2,0},{3,1},{4,6},{5,7},{6,4},{7,5},{8,10},{9,11},{10,... | collective-permute-start | bytes 786440 | tf_op jit(solution)/shard_map/ppermute | solution.py:380
  13.0 4.1 %load.3 = (bf16[640,8192]{1,0:T(8,128)(2,1)S(1)}, f32[8,128]{1,0:T(8,128)S(1)}) custom-call(s32[1]{0:T(128)} %bitcast.me_ref, bf16[1664,8192]{1,0:T(8,128)(2,1)} %weight_ref.5, f32[128,512]{1,0:T(8,128)S(1)} %mix.5.refs_0_.own_ref), custom_call_target="tpu_custom_call" | custom-call | flops 10000000000 | bytes 100000000 | tf_op jit(solution)/shard_map/load/pallas_call | solution.py:84
  17.1 3.5 %load.4 = (bf16[512,8192]{1,0:T(8,128)(2,1)S(1)}, f32[8,128]{1,0:T(8,128)S(1)}) custom-call(s32[1]{0:T(128)} %bitcast.me_ref, bf16[1664,8192]{1,0:T(8,128)(2,1)} %weight_ref.5, f32[8,128]{1,0:T(8,128)S(1)} %get-tuple-element.39.refs_0_), custom_call_target="tpu_custom_call" | custom-call | flops 10000000000 | bytes 100000000 | tf_op jit(solution)/shard_map/load/pallas_call | solution.py:84
  20.7 0.4 collective-permute-start.1
  21.1 1.2 %collective-permute-done.3.got_ref = f32[128,640]{1,0:T(8,128)S(1)} collective-permute-done((f32[128,640]{1,0:T(8,128)S(1)}, f32[128,640]{1,0:T(8,128)S(1)}, u32[]{:S(2)}, u32[]{:S(2)}) %collective-permute-start.3) | collective-permute-done | bytes 327712 | tf_op jit(solution)/shard_map/ppermute | solution.py:380
  22.3 0.1 collective-permute-start.5
  22.3 0.0 collective-permute-done.2.got_ref
  22.4 7.2 %collective-permute-start.4 = (f32[128,512]{1,0:T(8,128)S(1)}, f32[128,512]{1,0:T(8,128)S(1)}, u32[]{:S(2)}, u32[]{:S(2)}) collective-permute-start(f32[128,512]{1,0:T(8,128)S(1)} %fold.14.refs_0_.own_ref), channel_id=1, source_target_pairs={{0,2},{1,3},{2,0},{3,1},{4,6},{5,7},{6,4},{7,5},{8,10},{9,11},{10,... | collective-permute-start | bytes 786440 | tf_op jit(solution)/shard_map/ppermute | solution.py:380
  29.6 0.0 collective-permute-done.5.got_ref
  29.6 3.6 %load.5 = (bf16[512,8192]{1,0:T(8,128)(2,1)S(1)}, f32[8,128]{1,0:T(8,128)S(1)}) custom-call(s32[1]{0:T(128)} %bitcast.me_ref, bf16[1664,8192]{1,0:T(8,128)(2,1)} %weight_ref.5, f32[128,640]{1,0:T(8,128)S(1)} %fold.15.refs_0_.own_ref), custom_call_target="tpu_custom_call" | custom-call | flops 10000000000 | bytes 100000000 | tf_op jit(solution)/shard_map/load/pallas_call | solution.py:84
  33.2 0.8 collective-permute-start.10
  34.0 2.5 %collective-permute-done.4.got_ref = f32[128,512]{1,0:T(8,128)S(1)} collective-permute-done((f32[128,512]{1,0:T(8,128)S(1)}, f32[128,512]{1,0:T(8,128)S(1)}, u32[]{:S(2)}, u32[]{:S(2)}) %collective-permute-start.4) | collective-permute-done | bytes 262176 | tf_op jit(solution)/shard_map/ppermute | solution.py:380
  36.6 0.1 collective-permute-start.7
  36.7 0.5 collective-permute-start.6
  37.3 0.9 collective-permute-done.7.got_ref
  38.2 0.9 collective-permute-start.9
  39.1 0.0 collective-permute-done.6.got_ref
  39.2 3.5 %collective-permute-start.8 = (f32[128,512]{1,0:T(8,128)S(1)}, f32[128,512]{1,0:T(8,128)S(1)}, u32[]{:S(2)}, u32[]{:S(2)}) collective-permute-start(f32[128,512]{1,0:T(8,128)S(1)} %fold.19.refs_0_.own_ref), channel_id=1, source_target_pairs={{0,4},{1,5},{2,6},{3,7},{4,0},{5,1},{6,2},{7,3},{8,12},{9,13},{10,... | collective-permute-start | bytes 786440 | tf_op jit(solution)/shard_map/ppermute | solution.py:380
  42.7 4.2 %collective-permute-done.10.got_ref = f32[128,640]{1,0:T(8,128)S(1)} collective-permute-done((f32[128,640]{1,0:T(8,128)S(1)}, f32[128,640]{1,0:T(8,128)S(1)}, u32[]{:S(2)}, u32[]{:S(2)}) %collective-permute-start.10) | collective-permute-done | bytes 327712 | tf_op jit(solution)/shard_map/ppermute | solution.py:380
  46.9 1.2 %collective-permute-start.11 = (f32[128,640]{1,0:T(8,128)S(1)}, f32[128,640]{1,0:T(8,128)S(1)}, u32[]{:S(2)}, u32[]{:S(2)}) collective-permute-start(f32[128,640]{1,0:T(8,128)S(1)} %fold.20.refs_0_.own_ref), channel_id=1, source_target_pairs={{0,2},{1,3},{2,0},{3,1},{4,6},{5,7},{6,4},{7,5},{8,10},{9,11},{10,... | collective-permute-start | bytes 983048 | tf_op jit(solution)/shard_map/ppermute | solution.py:380
  48.1 7.0 %collective-permute-done.11.got_ref = f32[128,640]{1,0:T(8,128)S(1)} collective-permute-done((f32[128,640]{1,0:T(8,128)S(1)}, f32[128,640]{1,0:T(8,128)S(1)}, u32[]{:S(2)}, u32[]{:S(2)}) %collective-permute-start.11) | collective-permute-done | bytes 327712 | tf_op jit(solution)/shard_map/ppermute | solution.py:380
  55.2 1.8 %step.2.refs_0_.refs_2_ = f32[16,128,512]{2,1,0:T(8,128)S(1)} custom-call(bf16[128,640]{1,0:T(8,128)(2,1)S(1)} %fold.21.refs_0_.refs_2_, bf16[640,8192]{1,0:T(8,128)(2,1)S(1)} %get-tuple-element.42.refs_1_, bf16[128,640]{1,0:T(8,128)(2,1)S(1)} %fold.21.refs_0_.refs_2_), custom_call_target="tpu_custom_call" | custom-call | flops 10000000000 | bytes 100000000 | tf_op jit(solution)/shard_map/step/pallas_call | solution.py:84
  57.1 1.4 %step.3.refs_0_.total_ref = f32[16,128,512]{2,1,0:T(8,128)S(1)} custom-call(bf16[128,512]{1,0:T(8,128)(2,1)S(1)} %fold.22.refs_0_.refs_3_, bf16[512,8192]{1,0:T(8,128)(2,1)S(1)} %get-tuple-element.43.refs_1_, f32[16,128,512]{2,1,0:T(8,128)S(1)} %step.2.refs_0_.refs_2_, bf16[128,512]{1,0:T(8,128)(2,1)S(1)} %fold.22.refs_0_.refs_3_), custom_call_target="tpu_custom_call" | custom-call | flops 10000000000 | bytes 100000000 | tf_op jit(solution)/shard_map/step/pallas_call | solution.py:84
  58.5 0.0 collective-permute-done.8.got_ref
  58.5 0.8 product.2
  59.4 0.1 collective-permute-start.13
  59.4 0.5 collective-permute-start.12
  59.9 0.8 product.3
  60.7 1.3 %collective-permute-done.13.got_ref = f32[8,128,256]{2,1,0:T(8,128)S(1)} collective-permute-done((f32[8,128,256]{2,1,0:T(8,128)S(1)}, f32[8,128,256]{2,1,0:T(8,128)S(1)}, u32[]{:S(2)}, u32[]{:S(2)}) %collective-permute-start.13) | collective-permute-done | bytes 1048608 | tf_op jit(solution)/shard_map/ppermute | solution.py:380
  62.1 0.1 halve.10
  62.2 0.3 collective-permute-start.17
  62.5 0.8 collective-permute-start.15
  63.3 0.2 collective-permute-done.12.got_ref
  63.6 0.1 halve.11
  63.7 0.8 collective-permute-start.16
  64.5 1.4 %collective-permute-start.14 = (f32[4,64,256]{2,1,0:T(8,128)S(1)}, f32[4,64,256]{2,1,0:T(8,128)S(1)}, u32[]{:S(2)}, u32[]{:S(2)}) collective-permute-start(f32[4,64,256]{2,1,0:T(8,128)S(1)} %get-tuple-element.51), channel_id=1, source_target_pairs={{0,4},{1,5},{2,6},{3,7},{4,0},{5,1},{6,2},{7,3},{8,12},{9,13},{10,... | collective-permute-start | bytes 786440 | tf_op jit(solution)/shard_map/ppermute | solution.py:380
  65.8 5.6 %collective-permute-done.17.got_ref = f32[4,64,256]{2,1,0:T(8,128)S(1)} collective-permute-done((f32[4,64,256]{2,1,0:T(8,128)S(1)}, f32[4,64,256]{2,1,0:T(8,128)S(1)}, u32[]{:S(2)}, u32[]{:S(2)}) %collective-permute-start.17) | collective-permute-done | bytes 262176 | tf_op jit(solution)/shard_map/ppermute | solution.py:380
  71.4 0.1 collective-permute-start.21
  71.5 4.7 %collective-permute-done.16.got_ref = f32[4,64,256]{2,1,0:T(8,128)S(1)} collective-permute-done((f32[4,64,256]{2,1,0:T(8,128)S(1)}, f32[4,64,256]{2,1,0:T(8,128)S(1)}, u32[]{:S(2)}, u32[]{:S(2)}) %collective-permute-start.16) | collective-permute-done | bytes 262176 | tf_op jit(solution)/shard_map/ppermute | solution.py:380
  76.2 0.1 collective-permute-start.19
  76.3 0.0 collective-permute-done.15.got_ref
  76.4 1.2 %collective-permute-start.20 = (f32[2,64,256]{2,1,0:T(8,128)S(1)}, f32[2,64,256]{2,1,0:T(8,128)S(1)}, u32[]{:S(2)}, u32[]{:S(2)}) collective-permute-start(f32[2,64,256]{2,1,0:T(8,128)S(1)} %get-tuple-element.59.refs_0_), channel_id=1, source_target_pairs={{0,2},{1,3},{2,0},{3,1},{4,6},{5,7},{6,4},{7,5},{8,10},{9,11},{10,... | collective-permute-start | bytes 393224 | tf_op jit(solution)/shard_map/ppermute | solution.py:380
  77.5 1.7 %collective-permute-done.14.got_ref = f32[4,64,256]{2,1,0:T(8,128)S(1)} collective-permute-done((f32[4,64,256]{2,1,0:T(8,128)S(1)}, f32[4,64,256]{2,1,0:T(8,128)S(1)}, u32[]{:S(2)}, u32[]{:S(2)}) %collective-permute-start.14) | collective-permute-done | bytes 262176 | tf_op jit(solution)/shard_map/ppermute | solution.py:380
  79.2 1.3 %collective-permute-start.18 = (f32[2,64,256]{2,1,0:T(8,128)S(1)}, f32[2,64,256]{2,1,0:T(8,128)S(1)}, u32[]{:S(2)}, u32[]{:S(2)}) collective-permute-start(f32[2,64,256]{2,1,0:T(8,128)S(1)} %get-tuple-element.61.refs_0_), channel_id=1, source_target_pairs={{0,2},{1,3},{2,0},{3,1},{4,6},{5,7},{6,4},{7,5},{8,10},{9,11},{10,... | collective-permute-start | bytes 393224 | tf_op jit(solution)/shard_map/ppermute | solution.py:380
  80.6 1.4 %collective-permute-done.21.got_ref = f32[2,64,256]{2,1,0:T(8,128)S(1)} collective-permute-done((f32[2,64,256]{2,1,0:T(8,128)S(1)}, f32[2,64,256]{2,1,0:T(8,128)S(1)}, u32[]{:S(2)}, u32[]{:S(2)}) %collective-permute-start.21) | collective-permute-done | bytes 131104 | tf_op jit(solution)/shard_map/ppermute | solution.py:380
  82.0 0.5 collective-permute-start.23
  82.5 0.3 collective-permute-done.20.got_ref
  82.8 2.2 %collective-permute-start.24 = (f32[1,64,256]{2,1,0:T(8,128)S(1)}, f32[1,64,256]{2,1,0:T(8,128)S(1)}, u32[]{:S(2)}, u32[]{:S(2)}) collective-permute-start(f32[1,64,256]{2,1,0:T(8,128)S(1)} %get-tuple-element.66.refs_0_), channel_id=1, source_target_pairs={{0,4},{1,5},{2,6},{3,7},{4,0},{5,1},{6,2},{7,3},{8,12},{9,13},{10,... | collective-permute-start | bytes 196616 | tf_op jit(solution)/shard_map/ppermute | solution.py:380
  85.1 0.0 collective-permute-done.19.got_ref
  85.1 1.0 %collective-permute-start.25 = (f32[1,64,256]{2,1,0:T(8,128)S(1)}, f32[1,64,256]{2,1,0:T(8,128)S(1)}, u32[]{:S(2)}, u32[]{:S(2)}) collective-permute-start(f32[1,64,256]{2,1,0:T(8,128)S(1)} %get-tuple-element.67.refs_0_), channel_id=1, source_target_pairs={{0,8},{1,9},{2,10},{3,11},{4,12},{5,13},{6,14},{7,15},{8,0},{9,1},... | collective-permute-start | bytes 196616 | tf_op jit(solution)/shard_map/ppermute | solution.py:380
  86.1 0.0 collective-permute-done.18.got_ref
  86.2 2.0 %collective-permute-start.22 = (f32[1,64,256]{2,1,0:T(8,128)S(1)}, f32[1,64,256]{2,1,0:T(8,128)S(1)}, u32[]{:S(2)}, u32[]{:S(2)}) collective-permute-start(f32[1,64,256]{2,1,0:T(8,128)S(1)} %get-tuple-element.69.refs_0_), channel_id=1, source_target_pairs={{0,8},{1,9},{2,10},{3,11},{4,12},{5,13},{6,14},{7,15},{8,0},{9,1},... | collective-permute-start | bytes 196616 | tf_op jit(solution)/shard_map/ppermute | solution.py:380
  88.2 1.8 %collective-permute-done.23.got_ref = f32[1,64,256]{2,1,0:T(8,128)S(1)} collective-permute-done((f32[1,64,256]{2,1,0:T(8,128)S(1)}, f32[1,64,256]{2,1,0:T(8,128)S(1)}, u32[]{:S(2)}, u32[]{:S(2)}) %collective-permute-start.23) | collective-permute-done | bytes 65568 | tf_op jit(solution)/shard_map/ppermute | solution.py:380
  90.0 0.0 collective-permute-done.24.got_ref
  90.0 1.3 %collective-permute-done.25.got_ref = f32[1,64,256]{2,1,0:T(8,128)S(1)} collective-permute-done((f32[1,64,256]{2,1,0:T(8,128)S(1)}, f32[1,64,256]{2,1,0:T(8,128)S(1)}, u32[]{:S(2)}, u32[]{:S(2)}) %collective-permute-start.25) | collective-permute-done | bytes 65568 | tf_op jit(solution)/shard_map/ppermute | solution.py:380
  91.3 1.4 %collective-permute-done.22.got_ref = f32[1,64,256]{2,1,0:T(8,128)S(1)} collective-permute-done((f32[1,64,256]{2,1,0:T(8,128)S(1)}, f32[1,64,256]{2,1,0:T(8,128)S(1)}, u32[]{:S(2)}, u32[]{:S(2)}) %collective-permute-start.22) | collective-permute-done | bytes 65568 | tf_op jit(solution)/shard_map/ppermute | solution.py:380
  92.7 0.7 finish.7
  (29 shorter events, 0.6 us)
Async XLA Ops:
  0.0 1.0 %copy-start = (bf16[128,1664]{1,0:T(8,128)(2,1)S(1)}, bf16[128,1664]{1,0:T(8,128)(2,1)}, u32[]{:S(2)}) copy-start(bf16[128,1664]{1,0:T(8,128)(2,1)} %activations.5) | copy-start | bytes 1277956
  1.0 0.7 copy-start.1
  3.3 18.9 %collective-permute-start.3 = (f32[128,640]{1,0:T(8,128)S(1)}, f32[128,640]{1,0:T(8,128)S(1)}, u32[]{:S(2)}, u32[]{:S(2)}) collective-permute-start(f32[128,640]{1,0:T(8,128)S(1)} %mix.3.refs_0_.own_ref), channel_id=1, source_target_pairs={{0,8},{1,9},{2,10},{3,11},{4,12},{5,13},{6,14},{7,15},{8,0},{9,1},... | collective-permute-start | bytes 983048 | tf_op jit(solution)/shard_map/ppermute | solution.py:380
  8.6 13.8 %collective-permute-start.2 = (f32[128,512]{1,0:T(8,128)S(1)}, f32[128,512]{1,0:T(8,128)S(1)}, u32[]{:S(2)}, u32[]{:S(2)}) collective-permute-start(f32[128,512]{1,0:T(8,128)S(1)} %mix.4.refs_0_.own_ref), channel_id=1, source_target_pairs={{0,4},{1,5},{2,6},{3,7},{4,0},{5,1},{6,2},{7,3},{8,12},{9,13},{10,... | collective-permute-start | bytes 786440 | tf_op jit(solution)/shard_map/ppermute | solution.py:380
  11.4 9.2 %collective-permute-start = (f32[128,512]{1,0:T(8,128)S(1)}, f32[128,512]{1,0:T(8,128)S(1)}, u32[]{:S(2)}, u32[]{:S(2)}) collective-permute-start(f32[128,512]{1,0:T(8,128)S(1)} %mix.5.refs_0_.own_ref), channel_id=1, source_target_pairs={{0,2},{1,3},{2,0},{3,1},{4,6},{5,7},{6,4},{7,5},{8,10},{9,11},{10,... | collective-permute-start | bytes 786440 | tf_op jit(solution)/shard_map/ppermute | solution.py:380
  20.7 16.0 %collective-permute-start.1 = (f32[128,512]{1,0:T(8,128)S(1)}, f32[128,512]{1,0:T(8,128)S(1)}, u32[]{:S(2)}, u32[]{:S(2)}) collective-permute-start(f32[128,512]{1,0:T(8,128)S(1)} %fold.12.refs_0_.own_ref), channel_id=1, source_target_pairs={{0,8},{1,9},{2,10},{3,11},{4,12},{5,13},{6,14},{7,15},{8,0},{9,1},... | collective-permute-start | bytes 786440 | tf_op jit(solution)/shard_map/ppermute | solution.py:380
  22.3 7.3 %collective-permute-start.5 = (f32[128,640]{1,0:T(8,128)S(1)}, f32[128,640]{1,0:T(8,128)S(1)}, u32[]{:S(2)}, u32[]{:S(2)}) collective-permute-start(f32[128,640]{1,0:T(8,128)S(1)} %fold.13.refs_0_.own_ref), channel_id=1, source_target_pairs={{0,1},{1,0},{2,3},{3,2},{4,5},{5,4},{6,7},{7,6},{8,9},{9,8},{10,11... | collective-permute-start | bytes 983048 | tf_op jit(solution)/shard_map/ppermute | solution.py:380
  22.4 14.2 %collective-permute-start.4 = (f32[128,512]{1,0:T(8,128)S(1)}, f32[128,512]{1,0:T(8,128)S(1)}, u32[]{:S(2)}, u32[]{:S(2)}) collective-permute-start(f32[128,512]{1,0:T(8,128)S(1)} %fold.14.refs_0_.own_ref), channel_id=1, source_target_pairs={{0,2},{1,3},{2,0},{3,1},{4,6},{5,7},{6,4},{7,5},{8,10},{9,11},{10,... | collective-permute-start | bytes 786440 | tf_op jit(solution)/shard_map/ppermute | solution.py:380
  33.2 13.7 %collective-permute-start.10 = (f32[128,640]{1,0:T(8,128)S(1)}, f32[128,640]{1,0:T(8,128)S(1)}, u32[]{:S(2)}, u32[]{:S(2)}) collective-permute-start(f32[128,640]{1,0:T(8,128)S(1)} %fold.15.refs_0_.own_ref), channel_id=1, source_target_pairs={{0,4},{1,5},{2,6},{3,7},{4,0},{5,1},{6,2},{7,3},{8,12},{9,13},{10,... | collective-permute-start | bytes 983048 | tf_op jit(solution)/shard_map/ppermute | solution.py:380
  36.6 1.6 %collective-permute-start.7 = (f32[128,512]{1,0:T(8,128)S(1)}, f32[128,512]{1,0:T(8,128)S(1)}, u32[]{:S(2)}, u32[]{:S(2)}) collective-permute-start(f32[128,512]{1,0:T(8,128)S(1)} %fold.16.refs_0_.own_ref), channel_id=1, source_target_pairs={{0,1},{1,0},{2,3},{3,2},{4,5},{5,4},{6,7},{7,6},{8,9},{9,8},{10,11... | collective-permute-start | bytes 786440 | tf_op jit(solution)/shard_map/ppermute | solution.py:380
  36.7 2.4 %collective-permute-start.6 = (f32[128,512]{1,0:T(8,128)S(1)}, f32[128,512]{1,0:T(8,128)S(1)}, u32[]{:S(2)}, u32[]{:S(2)}) collective-permute-start(f32[128,512]{1,0:T(8,128)S(1)} %fold.17.refs_0_.own_ref), channel_id=1, source_target_pairs={{0,1},{1,0},{2,3},{3,2},{4,5},{5,4},{6,7},{7,6},{8,9},{9,8},{10,11... | collective-permute-start | bytes 786440 | tf_op jit(solution)/shard_map/ppermute | solution.py:380
  38.2 18.8 %collective-permute-start.9 = (f32[128,512]{1,0:T(8,128)S(1)}, f32[128,512]{1,0:T(8,128)S(1)}, u32[]{:S(2)}, u32[]{:S(2)}) collective-permute-start(f32[128,512]{1,0:T(8,128)S(1)} %fold.18.refs_0_.own_ref), channel_id=1, source_target_pairs={{0,8},{1,9},{2,10},{3,11},{4,12},{5,13},{6,14},{7,15},{8,0},{9,1},... | collective-permute-start | bytes 786440 | tf_op jit(solution)/shard_map/ppermute | solution.py:380
  39.2 19.3 %collective-permute-start.8 = (f32[128,512]{1,0:T(8,128)S(1)}, f32[128,512]{1,0:T(8,128)S(1)}, u32[]{:S(2)}, u32[]{:S(2)}) collective-permute-start(f32[128,512]{1,0:T(8,128)S(1)} %fold.19.refs_0_.own_ref), channel_id=1, source_target_pairs={{0,4},{1,5},{2,6},{3,7},{4,0},{5,1},{6,2},{7,3},{8,12},{9,13},{10,... | collective-permute-start | bytes 786440 | tf_op jit(solution)/shard_map/ppermute | solution.py:380
  46.9 8.2 %collective-permute-start.11 = (f32[128,640]{1,0:T(8,128)S(1)}, f32[128,640]{1,0:T(8,128)S(1)}, u32[]{:S(2)}, u32[]{:S(2)}) collective-permute-start(f32[128,640]{1,0:T(8,128)S(1)} %fold.20.refs_0_.own_ref), channel_id=1, source_target_pairs={{0,2},{1,3},{2,0},{3,1},{4,6},{5,7},{6,4},{7,5},{8,10},{9,11},{10,... | collective-permute-start | bytes 983048 | tf_op jit(solution)/shard_map/ppermute | solution.py:380
  59.4 2.7 %collective-permute-start.13 = (f32[8,128,256]{2,1,0:T(8,128)S(1)}, f32[8,128,256]{2,1,0:T(8,128)S(1)}, u32[]{:S(2)}, u32[]{:S(2)}) collective-permute-start(f32[8,128,256]{2,1,0:T(8,128)S(1)} %get-tuple-element.48), channel_id=1, source_target_pairs={{0,1},{1,0},{2,3},{3,2},{4,5},{5,4},{6,7},{7,6},{8,9},{9,8},{10,11... | collective-permute-start | bytes 3145736 | tf_op jit(solution)/shard_map/ppermute | solution.py:380
  59.4 4.1 %collective-permute-start.12 = (f32[8,128,256]{2,1,0:T(8,128)S(1)}, f32[8,128,256]{2,1,0:T(8,128)S(1)}, u32[]{:S(2)}, u32[]{:S(2)}) collective-permute-start(f32[8,128,256]{2,1,0:T(8,128)S(1)} %get-tuple-element.45.refs_0_), channel_id=1, source_target_pairs={{0,1},{1,0},{2,3},{3,2},{4,5},{5,4},{6,7},{7,6},{8,9},{9,8},{10,11... | collective-permute-start | bytes 3145736 | tf_op jit(solution)/shard_map/ppermute | solution.py:380
  62.2 9.2 %collective-permute-start.17 = (f32[4,64,256]{2,1,0:T(8,128)S(1)}, f32[4,64,256]{2,1,0:T(8,128)S(1)}, u32[]{:S(2)}, u32[]{:S(2)}) collective-permute-start(f32[4,64,256]{2,1,0:T(8,128)S(1)} %get-tuple-element.56), channel_id=1, source_target_pairs={{0,2},{1,3},{2,0},{3,1},{4,6},{5,7},{6,4},{7,5},{8,10},{9,11},{10,... | collective-permute-start | bytes 786440 | tf_op jit(solution)/shard_map/ppermute | solution.py:380
  62.5 13.8 %collective-permute-start.15 = (f32[4,64,256]{2,1,0:T(8,128)S(1)}, f32[4,64,256]{2,1,0:T(8,128)S(1)}, u32[]{:S(2)}, u32[]{:S(2)}) collective-permute-start(f32[4,64,256]{2,1,0:T(8,128)S(1)} %get-tuple-element.49.refs_0_), channel_id=1, source_target_pairs={{0,8},{1,9},{2,10},{3,11},{4,12},{5,13},{6,14},{7,15},{8,0},{9,1},... | collective-permute-start | bytes 786440 | tf_op jit(solution)/shard_map/ppermute | solution.py:380
  63.7 12.5 %collective-permute-start.16 = (f32[4,64,256]{2,1,0:T(8,128)S(1)}, f32[4,64,256]{2,1,0:T(8,128)S(1)}, u32[]{:S(2)}, u32[]{:S(2)}) collective-permute-start(f32[4,64,256]{2,1,0:T(8,128)S(1)} %get-tuple-element.54.refs_0_), channel_id=1, source_target_pairs={{0,2},{1,3},{2,0},{3,1},{4,6},{5,7},{6,4},{7,5},{8,10},{9,11},{10,... | collective-permute-start | bytes 786440 | tf_op jit(solution)/shard_map/ppermute | solution.py:380
  64.5 14.8 %collective-permute-start.14 = (f32[4,64,256]{2,1,0:T(8,128)S(1)}, f32[4,64,256]{2,1,0:T(8,128)S(1)}, u32[]{:S(2)}, u32[]{:S(2)}) collective-permute-start(f32[4,64,256]{2,1,0:T(8,128)S(1)} %get-tuple-element.51), channel_id=1, source_target_pairs={{0,4},{1,5},{2,6},{3,7},{4,0},{5,1},{6,2},{7,3},{8,12},{9,13},{10,... | collective-permute-start | bytes 786440 | tf_op jit(solution)/shard_map/ppermute | solution.py:380
  71.4 10.6 %collective-permute-start.21 = (f32[2,64,256]{2,1,0:T(8,128)S(1)}, f32[2,64,256]{2,1,0:T(8,128)S(1)}, u32[]{:S(2)}, u32[]{:S(2)}) collective-permute-start(f32[2,64,256]{2,1,0:T(8,128)S(1)} %get-tuple-element.57.refs_0_), channel_id=1, source_target_pairs={{0,4},{1,5},{2,6},{3,7},{4,0},{5,1},{6,2},{7,3},{8,12},{9,13},{10,... | collective-permute-start | bytes 393224 | tf_op jit(solution)/shard_map/ppermute | solution.py:380
  76.2 8.8 %collective-permute-start.19 = (f32[2,64,256]{2,1,0:T(8,128)S(1)}, f32[2,64,256]{2,1,0:T(8,128)S(1)}, u32[]{:S(2)}, u32[]{:S(2)}) collective-permute-start(f32[2,64,256]{2,1,0:T(8,128)S(1)} %get-tuple-element.58.refs_0_), channel_id=1, source_target_pairs={{0,4},{1,5},{2,6},{3,7},{4,0},{5,1},{6,2},{7,3},{8,12},{9,13},{10,... | collective-permute-start | bytes 393224 | tf_op jit(solution)/shard_map/ppermute | solution.py:380
  76.4 6.4 %collective-permute-start.20 = (f32[2,64,256]{2,1,0:T(8,128)S(1)}, f32[2,64,256]{2,1,0:T(8,128)S(1)}, u32[]{:S(2)}, u32[]{:S(2)}) collective-permute-start(f32[2,64,256]{2,1,0:T(8,128)S(1)} %get-tuple-element.59.refs_0_), channel_id=1, source_target_pairs={{0,2},{1,3},{2,0},{3,1},{4,6},{5,7},{6,4},{7,5},{8,10},{9,11},{10,... | collective-permute-start | bytes 393224 | tf_op jit(solution)/shard_map/ppermute | solution.py:380
  79.2 6.9 %collective-permute-start.18 = (f32[2,64,256]{2,1,0:T(8,128)S(1)}, f32[2,64,256]{2,1,0:T(8,128)S(1)}, u32[]{:S(2)}, u32[]{:S(2)}) collective-permute-start(f32[2,64,256]{2,1,0:T(8,128)S(1)} %get-tuple-element.61.refs_0_), channel_id=1, source_target_pairs={{0,2},{1,3},{2,0},{3,1},{4,6},{5,7},{6,4},{7,5},{8,10},{9,11},{10,... | collective-permute-start | bytes 393224 | tf_op jit(solution)/shard_map/ppermute | solution.py:380
  82.0 7.9 %collective-permute-start.23 = (f32[1,64,256]{2,1,0:T(8,128)S(1)}, f32[1,64,256]{2,1,0:T(8,128)S(1)}, u32[]{:S(2)}, u32[]{:S(2)}) collective-permute-start(f32[1,64,256]{2,1,0:T(8,128)S(1)} %get-tuple-element.65.refs_0_), channel_id=1, source_target_pairs={{0,8},{1,9},{2,10},{3,11},{4,12},{5,13},{6,14},{7,15},{8,0},{9,1},... | collective-permute-start | bytes 196616 | tf_op jit(solution)/shard_map/ppermute | solution.py:380
  82.8 7.1 %collective-permute-start.24 = (f32[1,64,256]{2,1,0:T(8,128)S(1)}, f32[1,64,256]{2,1,0:T(8,128)S(1)}, u32[]{:S(2)}, u32[]{:S(2)}) collective-permute-start(f32[1,64,256]{2,1,0:T(8,128)S(1)} %get-tuple-element.66.refs_0_), channel_id=1, source_target_pairs={{0,4},{1,5},{2,6},{3,7},{4,0},{5,1},{6,2},{7,3},{8,12},{9,13},{10,... | collective-permute-start | bytes 196616 | tf_op jit(solution)/shard_map/ppermute | solution.py:380
  85.1 6.2 %collective-permute-start.25 = (f32[1,64,256]{2,1,0:T(8,128)S(1)}, f32[1,64,256]{2,1,0:T(8,128)S(1)}, u32[]{:S(2)}, u32[]{:S(2)}) collective-permute-start(f32[1,64,256]{2,1,0:T(8,128)S(1)} %get-tuple-element.67.refs_0_), channel_id=1, source_target_pairs={{0,8},{1,9},{2,10},{3,11},{4,12},{5,13},{6,14},{7,15},{8,0},{9,1},... | collective-permute-start | bytes 196616 | tf_op jit(solution)/shard_map/ppermute | solution.py:380
  86.2 6.5 %collective-permute-start.22 = (f32[1,64,256]{2,1,0:T(8,128)S(1)}, f32[1,64,256]{2,1,0:T(8,128)S(1)}, u32[]{:S(2)}, u32[]{:S(2)}) collective-permute-start(f32[1,64,256]{2,1,0:T(8,128)S(1)} %get-tuple-element.69.refs_0_), channel_id=1, source_target_pairs={{0,8},{1,9},{2,10},{3,11},{4,12},{5,13},{6,14},{7,15},{8,0},{9,1},... | collective-permute-start | bytes 196616 | tf_op jit(solution)/shard_map/ppermute | solution.py:380

commit v9 on v7

--- a/solution.py
+++ b/solution.py
@@ -13,7 +13,8 @@
 BF16 = jnp.bfloat16
 
 
-TILES = (6, 7)
+PIECES = 4
+PERM = (0, 1, 3, 2)
 
 
 def quotient(index, divisor, limit):
@@ -76,7 +77,7 @@
 COST = pl.CostEstimate(flops=10**10, bytes_accessed=10**8, transcendentals=0)
 
 
-def call(name, kernel, operands, specs, shapes, after, scratch=(), limit=16):
+def call(name, kernel, operands, specs, shapes, after, scratch=(), limit=12):
     return pl.pallas_call(
         kernel,
         out_shape=shapes,
@@ -97,89 +98,100 @@
     return call("mix", kernel, (activations, small), (VMEM, VMEM), shape, after)
 
 
-def spread(blocks, after):
-    shards, rows, cols = blocks.shape
-
-    def kernel(blocks_ref, *refs):
-        out = refs[-1]
-        for at in range(0, cols, LANES):
-            end = min(at + LANES, cols)
-            values = [blocks_ref[s, :, at:end] for s in range(shards)]
-            reach = 1
-            while reach < shards:
-                values = [
-                    values[s ^ reach] - values[s] if s & reach else values[s] + values[s ^ reach]
-                    for s in range(shards)
-                ]
-                reach *= 2
-            for s in range(shards):
-                out[s, :, at:end] = values[s]
-
-    shape = jax.ShapeDtypeStruct(blocks.shape, F32)
-    return call("spread", kernel, (blocks,), (VMEM,), shape, after)
-
-
-def settle(values, factor, after):
-    def kernel(values_ref, *refs):
-        refs[-1][...] = (values_ref[...] * factor).astype(BF16)
-
-    shape = jax.ShapeDtypeStruct(values.shape, BF16)
-    return call("settle", kernel, (values,), (VMEM,), shape, after)
-
-
-def load(me, weight, rows, after, limit, distances=(), share=0):
+def fetch(me, weight, out, sems, rows, distances):
     begin, end = rows
+    copies = []
+    if not distances:
+        each = (end - begin) // PIECES // 16 * 16
+        for i in range(PIECES):
+            low, high = i * each, (i + 1) * each if i + 1 < PIECES else end - begin
+            copies.append(
+                pltpu.make_async_copy(weight.at[begin + low:begin + high, :], out.at[low:high, :], sems.at[i])
+            )
+    for i, distance in enumerate(distances):
+        share = weight.shape[1] // len(distances)
+        column = pl.multiple_of((distance ^ me) * share, LANES)
+        copies.append(
+            pltpu.make_async_copy(
+                weight.at[begin:end, pl.ds(column, share)], out.at[:, pl.ds(i * share, share)], sems.at[i]
+            )
+        )
+    for copy in copies:
+        copy.start()
+    return copies
+
+
+def loading(name, work, operands, specs, shape, after, me, weight, rows, distances, limit):
+    count = len(operands)
 
     def kernel(me_ref, weight_ref, *refs):
-        out, mark, sems = refs[-3:]
-        copies = []
-        if not distances:
-            copies.append(pltpu.make_async_copy(weight_ref.at[begin:end, :], out, sems.at[0]))
-        for i, distance in enumerate(distances):
-            column = pl.multiple_of((distance ^ me_ref[0]) * share, LANES)
-            copies.append(
-                pltpu.make_async_copy(
-                    weight_ref.at[begin:end, pl.ds(column, share)], out.at[:, pl.ds(i * share, share)], sems.at[i]
-                )
-            )
-        for copy in copies:
-            copy.start()
-        mark[...] = jnp.zeros_like(mark)
+        columns, out, sems = refs[-3:]
+        copies = fetch(me_ref[0], weight_ref, columns, sems, rows, distances)
+        work(me_ref, refs[:count], out)
         for copy in copies:
             copy.wait()
 
-    shapes = [
-        jax.ShapeDtypeStruct((end - begin, weight.shape[1]), BF16),
-        jax.ShapeDtypeStruct((8, LANES), F32),
-    ]
-    return call(
-        "load",
+    columns = jax.ShapeDtypeStruct((rows[1] - rows[0], weight.shape[1]), BF16)
+    outs = call(
+        name,
         kernel,
-        (me, weight),
-        (SMEM, pl.BlockSpec(memory_space=pltpu.HBM)),
-        shapes,
+        (me, weight, *operands),
+        [SMEM, pl.BlockSpec(memory_space=pltpu.HBM), *specs],
+        [columns, shape],
         after,
-        [pltpu.SemaphoreType.DMA((max(1, len(distances)),))],
+        [pltpu.SemaphoreType.DMA((max(PIECES, len(distances)),))],
         limit,
     )
-
-
-def step(chunk, columns, total, shards, after):
+    return outs[1], outs[0]
+
+
+def load(me, weight, rows, distances, limit, after):
+    def work(me_ref, refs, out):
+        out[...] = jnp.zeros_like(out)
+
+    shape = jax.ShapeDtypeStruct((8, LANES), F32)
+    return loading("load", work, (), (), shape, after, me, weight, rows, distances, limit)
+
+
+def fold(me, own, got, bit, after, factor=None, *more):
+    def work(me_ref, refs, out):
+        own_ref, got_ref = refs
+        sign = jnp.where((me_ref[0] & bit) != 0, -1.0, 1.0).astype(F32)
+        total = got_ref[...] + own_ref[...] * sign
+        if factor is not None:
+            total = total * factor
+        out[...] = total.astype(out.dtype)
+
+    def kernel(me_ref, *refs):
+        work(me_ref, refs[:2], refs[-1])
+
+    shape = jax.ShapeDtypeStruct(own.shape, F32 if factor is None else BF16)
+    if more:
+        return loading("fold", work, (own, got), (VMEM, VMEM), shape, after, me, *more)
+    return call("fold", kernel, (me, own, got), (SMEM, VMEM, VMEM), shape, after)
+
+
+def step(me, chunk, columns, total, shards, after, *more):
     tokens = chunk.shape[0]
     share = columns.shape[1] // shards
     group = max(1, 1024 // share)
     values = [chunk, columns] + ([] if total is None else [total])
 
-    def kernel(*refs):
-        out = refs[-1]
+    def work(me_ref, refs, out):
         for at in range(0, shards, group):
             sums = jnp.dot(refs[0][...], refs[1][:, at * share:(at + group) * share], preferred_element_type=F32)
             for i in range(group):
                 term = sums[:, i * share:(i + 1) * share]
                 out[at + i] = term if total is None else refs[2][at + i] + term
 
+    def kernel(*refs):
+        work(None, refs, refs[-1])
+
     shape = jax.ShapeDtypeStruct((shards, tokens, share), F32)
-    return call("step", kernel, values, [VMEM] * len(values), shape, after)
+    specs = [VMEM] * len(values)
+    if more:
+        return loading("step", work, values, specs, shape, after, me, *more)
+    return call("step", kernel, values, specs, shape, after)
 
 
 def product(me, chunk, columns, total, begin, distances, parts, after):
@@ -308,31 +320,45 @@
     distances = [d | bits[0] for d in near] + near
 
     tiles = -(-local // LANES)
-    ends = [round(tiles * sum(TILES[:c]) / sum(TILES)) for c in range(len(TILES) + 1)]
-    edges = [min(local, end * LANES) for end in ends]
-    assert all(begin < end for begin, end in zip(edges[:-1], edges[1:]))
+    count = min(4, len(bits), tiles)
+    edges = [min(local, (tiles * c // count) * LANES) for c in range(count)] + [local]
     spans = list(zip(edges[:-1], edges[1:]))
-    count = len(spans)
-
-    def exchange(x):
-        return lax.all_to_all(x, "tensor", split_axis=0, concat_axis=0)
-
+    chunks = []
+    for span in spans:
+        chunks.append(ran(mix(activations, rotation_small, (0, tokens), span, after)))
+    cycle = bits[-1:] + bits[1:-1] + bits[:1]
+    events = sorted((phase, cycle[(phase - c) % len(bits)], c) for phase in range(len(bits)) for c in range(count))
+    final = [c for phase, _, c in events if phase == len(bits) - 1]
+    loads = [final[i] for i in (PERM if count == len(PERM) else range(count))]
+    total = None
+    loaded = []
     room = 40 * 2**20
-    chunks, loaded = [], []
-    for span in spans:
-        x = ran(mix(activations, rotation_small, (0, tokens), span, after))
-        chunks.append(exchange(x.reshape(shards, tokens // shards, -1)))
-    for c, span in enumerate(spans):
-        wanted = (distances, share) if c == count - 1 else ()
-        loaded.append(ran(load(me, down_weight, span, after, room // 2**20, *wanted))[0])
-        room -= loaded[c].size * 2
-    for c in range(count):
-        chunks[c] = exchange(ran(spread(chunks[c], after))).reshape(tokens, -1)
-    total = None
-    for c in range(count):
-        chunks[c] = ran(settle(chunks[c], factor, after))
-        if c < count - 1:
-            total = ran(step(chunks[c], loaded[c], total, shards, after))
+
+    def wanted():
+        nonlocal room
+        c = loads[len(loaded)]
+        limit = room // 2**20
+        room -= (spans[c][1] - spans[c][0]) * down_weight.shape[1] * 2
+        return me, down_weight, spans[c], distances if c == final[-1] else (), limit
+
+    for number, (phase, bit, c) in enumerate(events):
+        got = swap(chunks[c], bit)
+        last = phase == len(bits) - 1
+        scale = factor if last else None
+        if number == count + 1 and len(loaded) < count - 1:
+            chunks[c], columns = ran(fold(me, chunks[c], got, bit, after, scale, *wanted()[1:]), 0)
+            loaded.append(columns)
+        else:
+            chunks[c] = ran(fold(me, chunks[c], got, bit, after, scale))
+        while number == 0 and len(loaded) < count - 2:
+            loaded.append(ran(load(*wanted(), after), 0)[1])
+        if last and c != final[-1]:
+            columns = loaded[loads.index(c)]
+            if len(loaded) < count:
+                total, columns = ran(step(me, chunks[c], columns, total, shards, after, *wanted()[1:]), 0)
+                loaded.append(columns)
+            else:
+                total = ran(step(me, chunks[c], columns, total, shards, after))
 
     inner = bits[1:]
     late = inner[-1:] + inner[:-1]
@@ -370,7 +396,7 @@
         held = pieces + [(rows, part, None)] if last else []
         pieces.append((rows, part, ran(finish(held, keep, got, tokens, width, parts, after))))
 
-    last_chunk, last_columns = chunks[-1], loaded[-1]
+    last_chunk, last_columns = chunks[final[-1]], loaded[loads.index(final[-1])]
     sends = ran(product(me, last_chunk, last_columns, total, 0, distances[:len(near)], parts, after))
     clock += 0.9
     kernels += 1

time: 132 us -> 92.5 us (0.70)
  local copies, waits for them, and re-layouts: 27.6 us -> 5.97 us
  waiting for transfers between devices: 45.4 us -> 27.9 us
  Pallas kernels: 22 us -> 23.9 us
  starting transfers between devices: 35.8 us -> 34.1 us
    all_to_all x4 -> x0, waiting for transfers between devices: 28.6 us -> none  [exchange(): return lax.all_to_all(x, 'tensor', split_axis=0, concat_axis=0)]
    unnamed x22 -> x10, local copies, waits for them, and re-layouts: 27.6 us -> 5.97 us
    all_to_all x4 -> x0, starting transfers between devices: 20.8 us -> none  [exchange(): return lax.all_to_all(x, 'tensor', split_axis=0, concat_axis=0)]
    ppermute x14 -> x30, starting transfers between devices: 14.9 us -> 34.1 us  [swap(): return lax.ppermute(x, 'tensor', [(d, d ^ bit) for d in range(shards)])]
    ppermute x14 -> x30, waiting for transfers between devices: 16.8 us -> 27.9 us  [swap(): return lax.ppermute(x, 'tensor', [(d, d ^ bit) for d in range(shards)])]
    pallas_call x25 -> x41, Pallas kernels: 22 us -> 23.9 us  [call(): pl.pallas_call(kernel, out_shape=shapes, in_specs=list(specs) + [UNREAD]...]
  transfers between devices with their start and end apart: 18 -> 30, of which waited for: 13 -> 15; matrix products, arithmetic and copies ran while one was open for 0% -> 0% of each run, Pallas kernels for 14% -> 23%
where the time goes in v9:
time: 92.5 us; the launch traced here: 92.3 us
  starting transfers between devices  34.1 us (37%)
  waiting for transfers between devices  27.9 us (30%)
  Pallas kernels  23.9 us (26%)
  local copies, waits for them, and re-layouts  5.97 us (6%)
    ppermute x30, starting transfers between devices, swap(): return lax.ppermute(x, 'tensor', [(d, d ^ bit) for d in range(shards)])  34.1 us
    ppermute x30, waiting for transfers between devices, swap(): return lax.ppermute(x, 'tensor', [(d, d ^ bit) for d in range(shards)])  27.9 us
    pallas_call x41, Pallas kernels, call(): pl.pallas_call(kernel, out_shape=shapes, in_specs=list(specs) + [UNREAD]...  23.9 us
    unnamed x10, local copies, waits for them, and re-layouts  5.97 us
  transfers between devices with their start and end apart: 30, of which 15 were waited for; matrix products, arithmetic and copies ran while one was open for 0% of the time, Pallas kernels for 23%

profile of v9, /device:TPU:0, one launch (start us, length us, event | category | flops | bytes accessed | tf_op | source)
XLA Modules:
  0.0 92.3 jit_solution(10619676894271541346)
XLA Ops:
  0.0 1.0 %copy-done = bf16[128,1664]{1,0:T(8,128)(2,1)S(1)} copy-done((bf16[128,1664]{1,0:T(8,128)(2,1)S(1)}, bf16[128,1664]{1,0:T(8,128)(2,1)}, u32[]{:S(2)}) %copy-start) | copy-done | bytes 426008
  1.0 0.7 copy-done.1
  1.8 1.2 %mix.4.refs_0_ = f32[128,384]{1,0:T(8,128)S(1)} custom-call(bf16[128,1664]{1,0:T(8,128)(2,1)S(1)} %copy-done, f32[52,52]{1,0:T(8,128)S(1)} %copy-done.1), custom_call_target="tpu_custom_call" | custom-call | flops 10000000000 | bytes 100000000 | tf_op jit(solution)/shard_map/mix/pallas_call | solution.py:81
  2.9 4.1 %collective-permute-start.3 = (f32[128,384]{1,0:T(8,128)S(1)}, f32[128,384]{1,0:T(8,128)S(1)}, u32[]{:S(2)}, u32[]{:S(2)}) collective-permute-start(f32[128,384]{1,0:T(8,128)S(1)} %mix.4.refs_0_), channel_id=1, source_target_pairs={{0,8},{1,9},{2,10},{3,11},{4,12},{5,13},{6,14},{7,15},{8,0},{9,1},... | collective-permute-start | bytes 589832 | tf_op jit(solution)/shard_map/ppermute | solution.py:311
  7.0 1.2 %mix.5.refs_0_ = f32[128,384]{1,0:T(8,128)S(1)} custom-call(bf16[128,1664]{1,0:T(8,128)(2,1)S(1)} %copy-done, f32[52,52]{1,0:T(8,128)S(1)} %copy-done.1, f32[128,384]{1,0:T(8,128)S(1)} %mix.4.refs_0_), custom_call_target="tpu_custom_call" | custom-call | flops 10000000000 | bytes 100000000 | tf_op jit(solution)/shard_map/mix/pallas_call | solution.py:81
  8.2 0.1 collective-permute-start.1
  8.3 1.2 %mix.6.refs_0_ = f32[128,384]{1,0:T(8,128)S(1)} custom-call(bf16[128,1664]{1,0:T(8,128)(2,1)S(1)} %copy-done, f32[52,52]{1,0:T(8,128)S(1)} %copy-done.1, f32[128,384]{1,0:T(8,128)S(1)} %mix.5.refs_0_), custom_call_target="tpu_custom_call" | custom-call | flops 10000000000 | bytes 100000000 | tf_op jit(solution)/shard_map/mix/pallas_call | solution.py:81
  9.5 1.6 %collective-permute-start.4 = (f32[128,384]{1,0:T(8,128)S(1)}, f32[128,384]{1,0:T(8,128)S(1)}, u32[]{:S(2)}, u32[]{:S(2)}) collective-permute-start(f32[128,384]{1,0:T(8,128)S(1)} %mix.6.refs_0_), channel_id=1, source_target_pairs={{0,4},{1,5},{2,6},{3,7},{4,0},{5,1},{6,2},{7,3},{8,12},{9,13},{10,... | collective-permute-start | bytes 589832 | tf_op jit(solution)/shard_map/ppermute | solution.py:311
  11.2 1.2 %mix.7.refs_2_.refs_0_ = f32[128,512]{1,0:T(8,128)S(1)} custom-call(bf16[128,1664]{1,0:T(8,128)(2,1)S(1)} %copy-done, f32[52,52]{1,0:T(8,128)S(1)} %copy-done.1, f32[128,384]{1,0:T(8,128)S(1)} %mix.6.refs_0_), custom_call_target="tpu_custom_call" | custom-call | flops 10000000000 | bytes 100000000 | tf_op jit(solution)/shard_map/mix/pallas_call | solution.py:81
  12.3 1.6 %collective-permute-start = (f32[128,512]{1,0:T(8,128)S(1)}, f32[128,512]{1,0:T(8,128)S(1)}, u32[]{:S(2)}, u32[]{:S(2)}) collective-permute-start(f32[128,512]{1,0:T(8,128)S(1)} %mix.7.refs_2_.refs_0_), channel_id=1, source_target_pairs={{0,2},{1,3},{2,0},{3,1},{4,6},{5,7},{6,4},{7,5},{8,10},{9,11},{10,... | collective-permute-start | bytes 786440 | tf_op jit(solution)/shard_map/ppermute | solution.py:311
  14.0 0.4 collective-permute-start.8
  14.4 2.9 %load.2 = (bf16[384,8192]{1,0:T(8,128)(2,1)S(1)}, f32[8,128]{1,0:T(8,128)S(1)}) custom-call(s32[1]{0:T(128)} %bitcast.me_ref, bf16[1664,8192]{1,0:T(8,128)(2,1)} %weight_ref.7, f32[128,384]{1,0:T(8,128)S(1)} %fold.16.refs_0_), custom_call_target="tpu_custom_call" | custom-call | flops 10000000000 | bytes 100000000 | tf_op jit(solution)/shard_map/load/pallas_call | solution.py:81
  17.2 2.9 %load.3 = (bf16[384,8192]{1,0:T(8,128)(2,1)S(1)}, f32[8,128]{1,0:T(8,128)S(1)}) custom-call(s32[1]{0:T(128)} %bitcast.me_ref, bf16[1664,8192]{1,0:T(8,128)(2,1)} %weight_ref.7, f32[8,128]{1,0:T(8,128)S(1)} %get-tuple-element.41.refs_0_), custom_call_target="tpu_custom_call" | custom-call | flops 10000000000 | bytes 100000000 | tf_op jit(solution)/shard_map/load/pallas_call | solution.py:81
  20.1 2.7 %copy-done.2 = bf16[384,8192]{1,0:T(8,128)(2,1)} copy-done((bf16[384,8192]{1,0:T(8,128)(2,1)}, bf16[384,8192]{1,0:T(8,128)(2,1)S(1)}, u32[]{:S(2)}) %copy-start.2) | copy-done | bytes 6291480
  22.8 0.5 collective-permute-start.2
  23.4 0.1 collective-permute-start.6
  23.5 0.3 collective-permute-start.5
  23.8 1.1 %collective-permute-done.6.refs_1_ = f32[128,384]{1,0:T(8,128)S(1)} collective-permute-done((f32[128,384]{1,0:T(8,128)S(1)}, f32[128,384]{1,0:T(8,128)S(1)}, u32[]{:S(2)}, u32[]{:S(2)}) %collective-permute-start.6) | collective-permute-done | bytes 196640 | tf_op jit(solution)/shard_map/ppermute | solution.py:311
  24.9 2.7 %collective-permute-start.12 = (f32[128,384]{1,0:T(8,128)S(1)}, f32[128,384]{1,0:T(8,128)S(1)}, u32[]{:S(2)}, u32[]{:S(2)}) collective-permute-start(f32[128,384]{1,0:T(8,128)S(1)} %fold.20.refs_2_.refs_0_), channel_id=1, source_target_pairs={{0,8},{1,9},{2,10},{3,11},{4,12},{5,13},{6,14},{7,15},{8,0},{9,1},... | collective-permute-start | bytes 589832 | tf_op jit(solution)/shard_map/ppermute | solution.py:311
  27.6 3.3 %collective-permute-done.5.refs_1_ = f32[128,384]{1,0:T(8,128)S(1)} collective-permute-done((f32[128,384]{1,0:T(8,128)S(1)}, f32[128,384]{1,0:T(8,128)S(1)}, u32[]{:S(2)}, u32[]{:S(2)}) %collective-permute-start.5) | collective-permute-done | bytes 196640 | tf_op jit(solution)/shard_map/ppermute | solution.py:311
  30.8 3.6 %fold.21 = (bf16[512,8192]{1,0:T(8,128)(2,1)S(1)}, f32[128,384]{1,0:T(8,128)S(1)}) custom-call(s32[1]{0:T(128)} %bitcast.me_ref, bf16[1664,8192]{1,0:T(8,128)(2,1)} %weight_ref.7, f32[128,384]{1,0:T(8,128)S(1)} %fold.19.refs_2_.refs_0_, f32[128,384]{1,0:T(8,128)S(1)} %collective-permute-done.5.refs_1_, f32[128,384]{1,0:T(8,128)S(1)} %fold.20.refs_2_.refs_0_), custom_call_target="tpu_custom_call" | custom-call | flops 10000000000 | bytes 100000000 | tf_op jit(solution)/shard_map/fold/pallas_call | solution.py:81
  34.4 1.6 %collective-permute-start.13 = (f32[128,384]{1,0:T(8,128)S(1)}, f32[128,384]{1,0:T(8,128)S(1)}, u32[]{:S(2)}, u32[]{:S(2)}) collective-permute-start(f32[128,384]{1,0:T(8,128)S(1)} %get-tuple-element.43.refs_2_.refs_0_), channel_id=1, source_target_pairs={{0,4},{1,5},{2,6},{3,7},{4,0},{5,1},{6,2},{7,3},{8,12},{9,13},{10,... | collective-permute-start | bytes 589832 | tf_op jit(solution)/shard_map/ppermute | solution.py:311
  36.1 0.1 collective-permute-start.7
  36.2 0.6 collective-permute-start.10
  36.8 0.9 collective-permute-done.7.refs_1_
  37.8 2.6 %collective-permute-start.9 = (f32[128,512]{1,0:T(8,128)S(1)}, f32[128,512]{1,0:T(8,128)S(1)}, u32[]{:S(2)}, u32[]{:S(2)}) collective-permute-start(f32[128,512]{1,0:T(8,128)S(1)} %fold.24.refs_2_.refs_0_), channel_id=1, source_target_pairs={{0,8},{1,9},{2,10},{3,11},{4,12},{5,13},{6,14},{7,15},{8,0},{9,1},... | collective-permute-start | bytes 786440 | tf_op jit(solution)/shard_map/ppermute | solution.py:311
  40.4 3.2 %collective-permute-done.10.refs_1_ = f32[128,384]{1,0:T(8,128)S(1)} collective-permute-done((f32[128,384]{1,0:T(8,128)S(1)}, f32[128,384]{1,0:T(8,128)S(1)}, u32[]{:S(2)}, u32[]{:S(2)}) %collective-permute-start.10) | collective-permute-done | bytes 196640 | tf_op jit(solution)/shard_map/ppermute | solution.py:311
  43.6 0.5 collective-permute-start.11
  44.2 0.1 collective-permute-start.15
  44.3 0.4 collective-permute-start.14
  44.6 1.0 %collective-permute-done.15.refs_1_ = f32[128,384]{1,0:T(8,128)S(1)} collective-permute-done((f32[128,384]{1,0:T(8,128)S(1)}, f32[128,384]{1,0:T(8,128)S(1)}, u32[]{:S(2)}, u32[]{:S(2)}) %collective-permute-start.15) | collective-permute-done | bytes 196640 | tf_op jit(solution)/shard_map/ppermute | solution.py:311
  45.7 4.1 %step.3 = (bf16[384,8192]{1,0:T(8,128)(2,1)S(1)}, f32[16,128,512]{2,1,0:T(8,128)S(1)}) custom-call(s32[1]{0:T(128)} %bitcast.me_ref, bf16[1664,8192]{1,0:T(8,128)(2,1)} %weight_ref.7, bf16[128,384]{1,0:T(8,128)(2,1)S(1)} %fold.28.refs_0_.refs_2_, bf16[384,8192]{1,0:T(8,128)(2,1)S(1)} %get-tuple-element.44.refs_1_, bf16[128,384]{1,0:T(8,128)(2,1)S(1)} %fold.28.refs_0_.refs_2_), custom_call_target="tpu_custom_call" | custom-call | flops 10000000000 | bytes 100000000 | tf_op jit(solution)/shard_map/step/pallas_call | solution.py:81
  49.8 1.8 %collective-permute-done.14.refs_1_ = f32[128,384]{1,0:T(8,128)S(1)} collective-permute-done((f32[128,384]{1,0:T(8,128)S(1)}, f32[128,384]{1,0:T(8,128)S(1)}, u32[]{:S(2)}, u32[]{:S(2)}) %collective-permute-start.14) | collective-permute-done | bytes 196640 | tf_op jit(solution)/shard_map/ppermute | solution.py:311
  51.7 1.5 %slice-done.1 = s8[2097152]{0:T(1024)(128)(4,1)S(1)} async-done(((s8[6291456]{0:T(1024)(128)(4,1)}), s8[2097152]{0:T(1024)(128)(4,1)S(1)}, s32[]{:S(2)}) %slice-start.1) | async-done | bytes 2097176
  53.2 1.3 %step.4.refs_2_ = f32[16,128,512]{2,1,0:T(8,128)S(1)} custom-call(bf16[128,384]{1,0:T(8,128)(2,1)S(1)} %fold.29.refs_0_.refs_3_, bf16[384,8192]{1,0:T(8,128)(2,1)S(1)} %bitcast.2, f32[16,128,512]{2,1,0:T(8,128)S(1)} %get-tuple-element.45.refs_2_, bf16[128,384]{1,0:T(8,128)(2,1)S(1)} %fold.29.refs_0_.refs_3_), custom_call_target="tpu_custom_call" | custom-call | flops 10000000000 | bytes 100000000 | tf_op jit(solution)/shard_map/step/pallas_call | solution.py:81
  54.6 1.3 %step.5.refs_2_.total_ref = f32[16,128,512]{2,1,0:T(8,128)S(1)} custom-call(bf16[128,384]{1,0:T(8,128)(2,1)S(1)} %fold.30.refs_0_.refs_3_, bf16[384,8192]{1,0:T(8,128)(2,1)S(1)} %get-tuple-element.47.refs_1_, f32[16,128,512]{2,1,0:T(8,128)S(1)} %step.4.refs_2_, bf16[128,384]{1,0:T(8,128)(2,1)S(1)} %fold.30.refs_0_.refs_3_), custom_call_target="tpu_custom_call" | custom-call | flops 10000000000 | bytes 100000000 | tf_op jit(solution)/shard_map/step/pallas_call | solution.py:81
  56.0 0.8 product.2
  56.8 0.1 collective-permute-start.17
  56.9 0.5 collective-permute-start.16
  57.4 0.8 product.3
  58.2 1.3 %collective-permute-done.17.got_ref = f32[8,128,256]{2,1,0:T(8,128)S(1)} collective-permute-done((f32[8,128,256]{2,1,0:T(8,128)S(1)}, f32[8,128,256]{2,1,0:T(8,128)S(1)}, u32[]{:S(2)}, u32[]{:S(2)}) %collective-permute-start.17) | collective-permute-done | bytes 1048608 | tf_op jit(solution)/shard_map/ppermute | solution.py:311
  59.5 0.1 halve.10
  59.6 0.3 collective-permute-start.21
  60.0 2.8 %collective-permute-start.19 = (f32[4,64,256]{2,1,0:T(8,128)S(1)}, f32[4,64,256]{2,1,0:T(8,128)S(1)}, u32[]{:S(2)}, u32[]{:S(2)}) collective-permute-start(f32[4,64,256]{2,1,0:T(8,128)S(1)} %get-tuple-element.53.refs_0_), channel_id=1, source_target_pairs={{0,8},{1,9},{2,10},{3,11},{4,12},{5,13},{6,14},{7,15},{8,0},{9,1},... | collective-permute-start | bytes 786440 | tf_op jit(solution)/shard_map/ppermute | solution.py:311
  62.8 0.1 halve.11
  62.9 1.6 %collective-permute-start.20 = (f32[4,64,256]{2,1,0:T(8,128)S(1)}, f32[4,64,256]{2,1,0:T(8,128)S(1)}, u32[]{:S(2)}, u32[]{:S(2)}) collective-permute-start(f32[4,64,256]{2,1,0:T(8,128)S(1)} %get-tuple-element.58.refs_0_), channel_id=1, source_target_pairs={{0,2},{1,3},{2,0},{3,1},{4,6},{5,7},{6,4},{7,5},{8,10},{9,11},{10,... | collective-permute-start | bytes 786440 | tf_op jit(solution)/shard_map/ppermute | solution.py:311
  64.5 1.6 %collective-permute-start.18 = (f32[4,64,256]{2,1,0:T(8,128)S(1)}, f32[4,64,256]{2,1,0:T(8,128)S(1)}, u32[]{:S(2)}, u32[]{:S(2)}) collective-permute-start(f32[4,64,256]{2,1,0:T(8,128)S(1)} %get-tuple-element.55), channel_id=1, source_target_pairs={{0,4},{1,5},{2,6},{3,7},{4,0},{5,1},{6,2},{7,3},{8,12},{9,13},{10,... | collective-permute-start | bytes 786440 | tf_op jit(solution)/shard_map/ppermute | solution.py:311
  66.1 2.8 %collective-permute-done.21.got_ref = f32[4,64,256]{2,1,0:T(8,128)S(1)} collective-permute-done((f32[4,64,256]{2,1,0:T(8,128)S(1)}, f32[4,64,256]{2,1,0:T(8,128)S(1)}, u32[]{:S(2)}, u32[]{:S(2)}) %collective-permute-start.21) | collective-permute-done | bytes 262176 | tf_op jit(solution)/shard_map/ppermute | solution.py:311
  68.9 1.6 %collective-permute-start.25 = (f32[2,64,256]{2,1,0:T(8,128)S(1)}, f32[2,64,256]{2,1,0:T(8,128)S(1)}, u32[]{:S(2)}, u32[]{:S(2)}) collective-permute-start(f32[2,64,256]{2,1,0:T(8,128)S(1)} %get-tuple-element.61.refs_0_), channel_id=1, source_target_pairs={{0,4},{1,5},{2,6},{3,7},{4,0},{5,1},{6,2},{7,3},{8,12},{9,13},{10,... | collective-permute-start | bytes 393224 | tf_op jit(solution)/shard_map/ppermute | solution.py:311
  70.5 3.1 %collective-permute-done.20.got_ref = f32[4,64,256]{2,1,0:T(8,128)S(1)} collective-permute-done((f32[4,64,256]{2,1,0:T(8,128)S(1)}, f32[4,64,256]{2,1,0:T(8,128)S(1)}, u32[]{:S(2)}, u32[]{:S(2)}) %collective-permute-start.20) | collective-permute-done | bytes 262176 | tf_op jit(solution)/shard_map/ppermute | solution.py:311
  73.7 1.6 %collective-permute-start.23 = (f32[2,64,256]{2,1,0:T(8,128)S(1)}, f32[2,64,256]{2,1,0:T(8,128)S(1)}, u32[]{:S(2)}, u32[]{:S(2)}) collective-permute-start(f32[2,64,256]{2,1,0:T(8,128)S(1)} %get-tuple-element.62.refs_0_), channel_id=1, source_target_pairs={{0,4},{1,5},{2,6},{3,7},{4,0},{5,1},{6,2},{7,3},{8,12},{9,13},{10,... | collective-permute-start | bytes 393224 | tf_op jit(solution)/shard_map/ppermute | solution.py:311
  75.4 1.1 %collective-permute-start.24 = (f32[2,64,256]{2,1,0:T(8,128)S(1)}, f32[2,64,256]{2,1,0:T(8,128)S(1)}, u32[]{:S(2)}, u32[]{:S(2)}) collective-permute-start(f32[2,64,256]{2,1,0:T(8,128)S(1)} %get-tuple-element.63.refs_0_), channel_id=1, source_target_pairs={{0,2},{1,3},{2,0},{3,1},{4,6},{5,7},{6,4},{7,5},{8,10},{9,11},{10,... | collective-permute-start | bytes 393224 | tf_op jit(solution)/shard_map/ppermute | solution.py:311
  76.5 1.7 %collective-permute-done.18.got_ref = f32[4,64,256]{2,1,0:T(8,128)S(1)} collective-permute-done((f32[4,64,256]{2,1,0:T(8,128)S(1)}, f32[4,64,256]{2,1,0:T(8,128)S(1)}, u32[]{:S(2)}, u32[]{:S(2)}) %collective-permute-start.18) | collective-permute-done | bytes 262176 | tf_op jit(solution)/shard_map/ppermute | solution.py:311
  78.2 0.6 collective-permute-start.22
  78.8 1.8 %collective-permute-done.25.got_ref = f32[2,64,256]{2,1,0:T(8,128)S(1)} collective-permute-done((f32[2,64,256]{2,1,0:T(8,128)S(1)}, f32[2,64,256]{2,1,0:T(8,128)S(1)}, u32[]{:S(2)}, u32[]{:S(2)}) %collective-permute-start.25) | collective-permute-done | bytes 131104 | tf_op jit(solution)/shard_map/ppermute | solution.py:311
  80.7 0.1 collective-permute-start.27
  80.8 0.5 collective-permute-done.24.got_ref
  81.3 1.9 %collective-permute-start.28 = (f32[1,64,256]{2,1,0:T(8,128)S(1)}, f32[1,64,256]{2,1,0:T(8,128)S(1)}, u32[]{:S(2)}, u32[]{:S(2)}) collective-permute-start(f32[1,64,256]{2,1,0:T(8,128)S(1)} %get-tuple-element.70.refs_0_), channel_id=1, source_target_pairs={{0,4},{1,5},{2,6},{3,7},{4,0},{5,1},{6,2},{7,3},{8,12},{9,13},{10,... | collective-permute-start | bytes 196616 | tf_op jit(solution)/shard_map/ppermute | solution.py:311
  83.2 2.4 %collective-permute-start.29 = (f32[1,64,256]{2,1,0:T(8,128)S(1)}, f32[1,64,256]{2,1,0:T(8,128)S(1)}, u32[]{:S(2)}, u32[]{:S(2)}) collective-permute-start(f32[1,64,256]{2,1,0:T(8,128)S(1)} %get-tuple-element.71.refs_0_), channel_id=1, source_target_pairs={{0,8},{1,9},{2,10},{3,11},{4,12},{5,13},{6,14},{7,15},{8,0},{9,1},... | collective-permute-start | bytes 196616 | tf_op jit(solution)/shard_map/ppermute | solution.py:311
  85.6 0.7 collective-permute-start.26
  86.3 1.2 %collective-permute-done.27.got_ref = f32[1,64,256]{2,1,0:T(8,128)S(1)} collective-permute-done((f32[1,64,256]{2,1,0:T(8,128)S(1)}, f32[1,64,256]{2,1,0:T(8,128)S(1)}, u32[]{:S(2)}, u32[]{:S(2)}) %collective-permute-start.27) | collective-permute-done | bytes 65568 | tf_op jit(solution)/shard_map/ppermute | solution.py:311
  87.5 3.4 %collective-permute-done.29.got_ref = f32[1,64,256]{2,1,0:T(8,128)S(1)} collective-permute-done((f32[1,64,256]{2,1,0:T(8,128)S(1)}, f32[1,64,256]{2,1,0:T(8,128)S(1)}, u32[]{:S(2)}, u32[]{:S(2)}) %collective-permute-start.29) | collective-permute-done | bytes 65568 | tf_op jit(solution)/shard_map/ppermute | solution.py:311
  90.9 0.7 collective-permute-done.26.got_ref
  91.6 0.7 finish.7
  (48 shorter events, 0.7 us)
Async XLA Ops:
  0.0 1.0 %copy-start = (bf16[128,1664]{1,0:T(8,128)(2,1)S(1)}, bf16[128,1664]{1,0:T(8,128)(2,1)}, u32[]{:S(2)}) copy-start(bf16[128,1664]{1,0:T(8,128)(2,1)} %activations.7) | copy-start | bytes 1277956
  1.0 0.7 copy-start.1
  2.9 20.5 %collective-permute-start.3 = (f32[128,384]{1,0:T(8,128)S(1)}, f32[128,384]{1,0:T(8,128)S(1)}, u32[]{:S(2)}, u32[]{:S(2)}) collective-permute-start(f32[128,384]{1,0:T(8,128)S(1)} %mix.4.refs_0_), channel_id=1, source_target_pairs={{0,8},{1,9},{2,10},{3,11},{4,12},{5,13},{6,14},{7,15},{8,0},{9,1},... | collective-permute-start | bytes 589832 | tf_op jit(solution)/shard_map/ppermute | solution.py:311
  8.2 5.7 %collective-permute-start.1 = (f32[128,384]{1,0:T(8,128)S(1)}, f32[128,384]{1,0:T(8,128)S(1)}, u32[]{:S(2)}, u32[]{:S(2)}) collective-permute-start(f32[128,384]{1,0:T(8,128)S(1)} %mix.5.refs_0_), channel_id=1, source_target_pairs={{0,1},{1,0},{2,3},{3,2},{4,5},{5,4},{6,7},{7,6},{8,9},{9,8},{10,11... | collective-permute-start | bytes 589832 | tf_op jit(solution)/shard_map/ppermute | solution.py:311
  9.5 13.8 %collective-permute-start.4 = (f32[128,384]{1,0:T(8,128)S(1)}, f32[128,384]{1,0:T(8,128)S(1)}, u32[]{:S(2)}, u32[]{:S(2)}) collective-permute-start(f32[128,384]{1,0:T(8,128)S(1)} %mix.6.refs_0_), channel_id=1, source_target_pairs={{0,4},{1,5},{2,6},{3,7},{4,0},{5,1},{6,2},{7,3},{8,12},{9,13},{10,... | collective-permute-start | bytes 589832 | tf_op jit(solution)/shard_map/ppermute | solution.py:311
  12.3 10.4 %collective-permute-start = (f32[128,512]{1,0:T(8,128)S(1)}, f32[128,512]{1,0:T(8,128)S(1)}, u32[]{:S(2)}, u32[]{:S(2)}) collective-permute-start(f32[128,512]{1,0:T(8,128)S(1)} %mix.7.refs_2_.refs_0_), channel_id=1, source_target_pairs={{0,2},{1,3},{2,0},{3,1},{4,6},{5,7},{6,4},{7,5},{8,10},{9,11},{10,... | collective-permute-start | bytes 786440 | tf_op jit(solution)/shard_map/ppermute | solution.py:311
  14.0 22.2 %collective-permute-start.8 = (f32[128,384]{1,0:T(8,128)S(1)}, f32[128,384]{1,0:T(8,128)S(1)}, u32[]{:S(2)}, u32[]{:S(2)}) collective-permute-start(f32[128,384]{1,0:T(8,128)S(1)} %fold.16.refs_0_), channel_id=1, source_target_pairs={{0,8},{1,9},{2,10},{3,11},{4,12},{5,13},{6,14},{7,15},{8,0},{9,1},... | collective-permute-start | bytes 589832 | tf_op jit(solution)/shard_map/ppermute | solution.py:311
  20.1 2.7 %copy-start.2 = (bf16[384,8192]{1,0:T(8,128)(2,1)}, bf16[384,8192]{1,0:T(8,128)(2,1)S(1)}, u32[]{:S(2)}) copy-start(bf16[384,8192]{1,0:T(8,128)(2,1)S(1)} %get-tuple-element.46.refs_1_) | copy-start | bytes 18874372
  22.8 13.3 %collective-permute-start.2 = (f32[128,512]{1,0:T(8,128)S(1)}, f32[128,512]{1,0:T(8,128)S(1)}, u32[]{:S(2)}, u32[]{:S(2)}) collective-permute-start(f32[128,512]{1,0:T(8,128)S(1)} %fold.17.refs_2_.refs_0_), channel_id=1, source_target_pairs={{0,4},{1,5},{2,6},{3,7},{4,0},{5,1},{6,2},{7,3},{8,12},{9,13},{10,... | collective-permute-start | bytes 786440 | tf_op jit(solution)/shard_map/ppermute | solution.py:311
  23.4 1.5 %collective-permute-start.6 = (f32[128,384]{1,0:T(8,128)S(1)}, f32[128,384]{1,0:T(8,128)S(1)}, u32[]{:S(2)}, u32[]{:S(2)}) collective-permute-start(f32[128,384]{1,0:T(8,128)S(1)} %fold.18.refs_2_.refs_0_), channel_id=1, source_target_pairs={{0,1},{1,0},{2,3},{3,2},{4,5},{5,4},{6,7},{7,6},{8,9},{9,8},{10,11... | collective-permute-start | bytes 589832 | tf_op jit(solution)/shard_map/ppermute | solution.py:311
  23.5 7.4 %collective-permute-start.5 = (f32[128,384]{1,0:T(8,128)S(1)}, f32[128,384]{1,0:T(8,128)S(1)}, u32[]{:S(2)}, u32[]{:S(2)}) collective-permute-start(f32[128,384]{1,0:T(8,128)S(1)} %fold.19.refs_2_.refs_0_), channel_id=1, source_target_pairs={{0,2},{1,3},{2,0},{3,1},{4,6},{5,7},{6,4},{7,5},{8,10},{9,11},{10,... | collective-permute-start | bytes 589832 | tf_op jit(solution)/shard_map/ppermute | solution.py:311
  24.9 19.3 %collective-permute-start.12 = (f32[128,384]{1,0:T(8,128)S(1)}, f32[128,384]{1,0:T(8,128)S(1)}, u32[]{:S(2)}, u32[]{:S(2)}) collective-permute-start(f32[128,384]{1,0:T(8,128)S(1)} %fold.20.refs_2_.refs_0_), channel_id=1, source_target_pairs={{0,8},{1,9},{2,10},{3,11},{4,12},{5,13},{6,14},{7,15},{8,0},{9,1},... | collective-permute-start | bytes 589832 | tf_op jit(solution)/shard_map/ppermute | solution.py:311
  34.4 9.7 %collective-permute-start.13 = (f32[128,384]{1,0:T(8,128)S(1)}, f32[128,384]{1,0:T(8,128)S(1)}, u32[]{:S(2)}, u32[]{:S(2)}) collective-permute-start(f32[128,384]{1,0:T(8,128)S(1)} %get-tuple-element.43.refs_2_.refs_0_), channel_id=1, source_target_pairs={{0,4},{1,5},{2,6},{3,7},{4,0},{5,1},{6,2},{7,3},{8,12},{9,13},{10,... | collective-permute-start | bytes 589832 | tf_op jit(solution)/shard_map/ppermute | solution.py:311
  36.1 1.6 %collective-permute-start.7 = (f32[128,512]{1,0:T(8,128)S(1)}, f32[128,512]{1,0:T(8,128)S(1)}, u32[]{:S(2)}, u32[]{:S(2)}) collective-permute-start(f32[128,512]{1,0:T(8,128)S(1)} %fold.22.refs_2_.refs_0_), channel_id=1, source_target_pairs={{0,1},{1,0},{2,3},{3,2},{4,5},{5,4},{6,7},{7,6},{8,9},{9,8},{10,11... | collective-permute-start | bytes 786440 | tf_op jit(solution)/shard_map/ppermute | solution.py:311
  36.2 7.4 %collective-permute-start.10 = (f32[128,384]{1,0:T(8,128)S(1)}, f32[128,384]{1,0:T(8,128)S(1)}, u32[]{:S(2)}, u32[]{:S(2)}) collective-permute-start(f32[128,384]{1,0:T(8,128)S(1)} %fold.23.refs_2_.refs_0_), channel_id=1, source_target_pairs={{0,2},{1,3},{2,0},{3,1},{4,6},{5,7},{6,4},{7,5},{8,10},{9,11},{10,... | collective-permute-start | bytes 589832 | tf_op jit(solution)/shard_map/ppermute | solution.py:311
  37.8 18.2 %collective-permute-start.9 = (f32[128,512]{1,0:T(8,128)S(1)}, f32[128,512]{1,0:T(8,128)S(1)}, u32[]{:S(2)}, u32[]{:S(2)}) collective-permute-start(f32[128,512]{1,0:T(8,128)S(1)} %fold.24.refs_2_.refs_0_), channel_id=1, source_target_pairs={{0,8},{1,9},{2,10},{3,11},{4,12},{5,13},{6,14},{7,15},{8,0},{9,1},... | collective-permute-start | bytes 786440 | tf_op jit(solution)/shard_map/ppermute | solution.py:311
  43.6 10.9 %collective-permute-start.11 = (f32[128,384]{1,0:T(8,128)S(1)}, f32[128,384]{1,0:T(8,128)S(1)}, u32[]{:S(2)}, u32[]{:S(2)}) collective-permute-start(f32[128,384]{1,0:T(8,128)S(1)} %fold.25.refs_2_.refs_0_), channel_id=1, source_target_pairs={{0,4},{1,5},{2,6},{3,7},{4,0},{5,1},{6,2},{7,3},{8,12},{9,13},{10,... | collective-permute-start | bytes 589832 | tf_op jit(solution)/shard_map/ppermute | solution.py:311
  44.2 1.5 %collective-permute-start.15 = (f32[128,384]{1,0:T(8,128)S(1)}, f32[128,384]{1,0:T(8,128)S(1)}, u32[]{:S(2)}, u32[]{:S(2)}) collective-permute-start(f32[128,384]{1,0:T(8,128)S(1)} %fold.26.refs_2_.refs_0_), channel_id=1, source_target_pairs={{0,1},{1,0},{2,3},{3,2},{4,5},{5,4},{6,7},{7,6},{8,9},{9,8},{10,11... | collective-permute-start | bytes 589832 | tf_op jit(solution)/shard_map/ppermute | solution.py:311
  44.3 7.4 %collective-permute-start.14 = (f32[128,384]{1,0:T(8,128)S(1)}, f32[128,384]{1,0:T(8,128)S(1)}, u32[]{:S(2)}, u32[]{:S(2)}) collective-permute-start(f32[128,384]{1,0:T(8,128)S(1)} %fold.27.refs_2_.refs_0_), channel_id=1, source_target_pairs={{0,2},{1,3},{2,0},{3,1},{4,6},{5,7},{6,4},{7,5},{8,10},{9,11},{10,... | collective-permute-start | bytes 589832 | tf_op jit(solution)/shard_map/ppermute | solution.py:311
  45.7 6.0 %slice-start = ((s8[6291456]{0:T(1024)(128)(4,1)}), s8[4194304]{0:T(1024)(128)(4,1)S(1)}, s32[]{:S(2)}) async-start(s8[6291456]{0:T(1024)(128)(4,1)} %bitcast.1), calls=%async_computation | async-start | bytes 8388608
  51.6 1.6 %slice-start.1 = ((s8[6291456]{0:T(1024)(128)(4,1)}), s8[2097152]{0:T(1024)(128)(4,1)S(1)}, s32[]{:S(2)}) async-start(s8[6291456]{0:T(1024)(128)(4,1)} %bitcast.1), calls=%async_computation.1 | async-start | bytes 4194304
  56.8 2.7 %collective-permute-start.17 = (f32[8,128,256]{2,1,0:T(8,128)S(1)}, f32[8,128,256]{2,1,0:T(8,128)S(1)}, u32[]{:S(2)}, u32[]{:S(2)}) collective-permute-start(f32[8,128,256]{2,1,0:T(8,128)S(1)} %get-tuple-element.52), channel_id=1, source_target_pairs={{0,1},{1,0},{2,3},{3,2},{4,5},{5,4},{6,7},{7,6},{8,9},{9,8},{10,11... | collective-permute-start | bytes 3145736 | tf_op jit(solution)/shard_map/ppermute | solution.py:311
  56.9 5.9 %collective-permute-start.16 = (f32[8,128,256]{2,1,0:T(8,128)S(1)}, f32[8,128,256]{2,1,0:T(8,128)S(1)}, u32[]{:S(2)}, u32[]{:S(2)}) collective-permute-start(f32[8,128,256]{2,1,0:T(8,128)S(1)} %get-tuple-element.49.refs_0_), channel_id=1, source_target_pairs={{0,1},{1,0},{2,3},{3,2},{4,5},{5,4},{6,7},{7,6},{8,9},{9,8},{10,11... | collective-permute-start | bytes 3145736 | tf_op jit(solution)/shard_map/ppermute | solution.py:311
  59.6 9.2 %collective-permute-start.21 = (f32[4,64,256]{2,1,0:T(8,128)S(1)}, f32[4,64,256]{2,1,0:T(8,128)S(1)}, u32[]{:S(2)}, u32[]{:S(2)}) collective-permute-start(f32[4,64,256]{2,1,0:T(8,128)S(1)} %get-tuple-element.60), channel_id=1, source_target_pairs={{0,2},{1,3},{2,0},{3,1},{4,6},{5,7},{6,4},{7,5},{8,10},{9,11},{10,... | collective-permute-start | bytes 786440 | tf_op jit(solution)/shard_map/ppermute | solution.py:311
  60.0 15.4 %collective-permute-start.19 = (f32[4,64,256]{2,1,0:T(8,128)S(1)}, f32[4,64,256]{2,1,0:T(8,128)S(1)}, u32[]{:S(2)}, u32[]{:S(2)}) collective-permute-start(f32[4,64,256]{2,1,0:T(8,128)S(1)} %get-tuple-element.53.refs_0_), channel_id=1, source_target_pairs={{0,8},{1,9},{2,10},{3,11},{4,12},{5,13},{6,14},{7,15},{8,0},{9,1},... | collective-permute-start | bytes 786440 | tf_op jit(solution)/shard_map/ppermute | solution.py:311
  62.9 10.8 %collective-permute-start.20 = (f32[4,64,256]{2,1,0:T(8,128)S(1)}, f32[4,64,256]{2,1,0:T(8,128)S(1)}, u32[]{:S(2)}, u32[]{:S(2)}) collective-permute-start(f32[4,64,256]{2,1,0:T(8,128)S(1)} %get-tuple-element.58.refs_0_), channel_id=1, source_target_pairs={{0,2},{1,3},{2,0},{3,1},{4,6},{5,7},{6,4},{7,5},{8,10},{9,11},{10,... | collective-permute-start | bytes 786440 | tf_op jit(solution)/shard_map/ppermute | solution.py:311
  64.5 13.7 %collective-permute-start.18 = (f32[4,64,256]{2,1,0:T(8,128)S(1)}, f32[4,64,256]{2,1,0:T(8,128)S(1)}, u32[]{:S(2)}, u32[]{:S(2)}) collective-permute-start(f32[4,64,256]{2,1,0:T(8,128)S(1)} %get-tuple-element.55), channel_id=1, source_target_pairs={{0,4},{1,5},{2,6},{3,7},{4,0},{5,1},{6,2},{7,3},{8,12},{9,13},{10,... | collective-permute-start | bytes 786440 | tf_op jit(solution)/shard_map/ppermute | solution.py:311
  68.9 11.8 %collective-permute-start.25 = (f32[2,64,256]{2,1,0:T(8,128)S(1)}, f32[2,64,256]{2,1,0:T(8,128)S(1)}, u32[]{:S(2)}, u32[]{:S(2)}) collective-permute-start(f32[2,64,256]{2,1,0:T(8,128)S(1)} %get-tuple-element.61.refs_0_), channel_id=1, source_target_pairs={{0,4},{1,5},{2,6},{3,7},{4,0},{5,1},{6,2},{7,3},{8,12},{9,13},{10,... | collective-permute-start | bytes 393224 | tf_op jit(solution)/shard_map/ppermute | solution.py:311
  73.7 9.5 %collective-permute-start.23 = (f32[2,64,256]{2,1,0:T(8,128)S(1)}, f32[2,64,256]{2,1,0:T(8,128)S(1)}, u32[]{:S(2)}, u32[]{:S(2)}) collective-permute-start(f32[2,64,256]{2,1,0:T(8,128)S(1)} %get-tuple-element.62.refs_0_), channel_id=1, source_target_pairs={{0,4},{1,5},{2,6},{3,7},{4,0},{5,1},{6,2},{7,3},{8,12},{9,13},{10,... | collective-permute-start | bytes 393224 | tf_op jit(solution)/shard_map/ppermute | solution.py:311
  75.4 5.9 %collective-permute-start.24 = (f32[2,64,256]{2,1,0:T(8,128)S(1)}, f32[2,64,256]{2,1,0:T(8,128)S(1)}, u32[]{:S(2)}, u32[]{:S(2)}) collective-permute-start(f32[2,64,256]{2,1,0:T(8,128)S(1)} %get-tuple-element.63.refs_0_), channel_id=1, source_target_pairs={{0,2},{1,3},{2,0},{3,1},{4,6},{5,7},{6,4},{7,5},{8,10},{9,11},{10,... | collective-permute-start | bytes 393224 | tf_op jit(solution)/shard_map/ppermute | solution.py:311
  78.2 7.4 %collective-permute-start.22 = (f32[2,64,256]{2,1,0:T(8,128)S(1)}, f32[2,64,256]{2,1,0:T(8,128)S(1)}, u32[]{:S(2)}, u32[]{:S(2)}) collective-permute-start(f32[2,64,256]{2,1,0:T(8,128)S(1)} %get-tuple-element.65.refs_0_), channel_id=1, source_target_pairs={{0,2},{1,3},{2,0},{3,1},{4,6},{5,7},{6,4},{7,5},{8,10},{9,11},{10,... | collective-permute-start | bytes 393224 | tf_op jit(solution)/shard_map/ppermute | solution.py:311
  80.7 6.7 %collective-permute-start.27 = (f32[1,64,256]{2,1,0:T(8,128)S(1)}, f32[1,64,256]{2,1,0:T(8,128)S(1)}, u32[]{:S(2)}, u32[]{:S(2)}) collective-permute-start(f32[1,64,256]{2,1,0:T(8,128)S(1)} %get-tuple-element.69.refs_0_), channel_id=1, source_target_pairs={{0,8},{1,9},{2,10},{3,11},{4,12},{5,13},{6,14},{7,15},{8,0},{9,1},... | collective-permute-start | bytes 196616 | tf_op jit(solution)/shard_map/ppermute | solution.py:311
  81.3 6.1 %collective-permute-start.28 = (f32[1,64,256]{2,1,0:T(8,128)S(1)}, f32[1,64,256]{2,1,0:T(8,128)S(1)}, u32[]{:S(2)}, u32[]{:S(2)}) collective-permute-start(f32[1,64,256]{2,1,0:T(8,128)S(1)} %get-tuple-element.70.refs_0_), channel_id=1, source_target_pairs={{0,4},{1,5},{2,6},{3,7},{4,0},{5,1},{6,2},{7,3},{8,12},{9,13},{10,... | collective-permute-start | bytes 196616 | tf_op jit(solution)/shard_map/ppermute | solution.py:311
  83.2 7.7 %collective-permute-start.29 = (f32[1,64,256]{2,1,0:T(8,128)S(1)}, f32[1,64,256]{2,1,0:T(8,128)S(1)}, u32[]{:S(2)}, u32[]{:S(2)}) collective-permute-start(f32[1,64,256]{2,1,0:T(8,128)S(1)} %get-tuple-element.71.refs_0_), channel_id=1, source_target_pairs={{0,8},{1,9},{2,10},{3,11},{4,12},{5,13},{6,14},{7,15},{8,0},{9,1},... | collective-permute-start | bytes 196616 | tf_op jit(solution)/shard_map/ppermute | solution.py:311
  85.6 6.0 %collective-permute-start.26 = (f32[1,64,256]{2,1,0:T(8,128)S(1)}, f32[1,64,256]{2,1,0:T(8,128)S(1)}, u32[]{:S(2)}, u32[]{:S(2)}) collective-permute-start(f32[1,64,256]{2,1,0:T(8,128)S(1)} %get-tuple-element.73.refs_0_), channel_id=1, source_target_pairs={{0,8},{1,9},{2,10},{3,11},{4,12},{5,13},{6,14},{7,15},{8,0},{9,1},... | collective-permute-start | bytes 196616 | tf_op jit(solution)/shard_map/ppermute | solution.py:311

commit v10 on v9

--- a/solution.py
+++ b/solution.py
@@ -77,7 +77,7 @@
 COST = pl.CostEstimate(flops=10**10, bytes_accessed=10**8, transcendentals=0)
 
 
-def call(name, kernel, operands, specs, shapes, after, scratch=(), limit=12):
+def call(name, kernel, operands, specs, shapes, after, scratch=(), limit=8):
     return pl.pallas_call(
         kernel,
         out_shape=shapes,
@@ -332,12 +332,12 @@
     loads = [final[i] for i in (PERM if count == len(PERM) else range(count))]
     total = None
     loaded = []
-    room = 40 * 2**20
+    room = 37 * 2**20
 
     def wanted():
         nonlocal room
         c = loads[len(loaded)]
-        limit = room // 2**20
+        limit = room // 2**20 + (0 if loaded else 3)
         room -= (spans[c][1] - spans[c][0]) * down_weight.shape[1] * 2
         return me, down_weight, spans[c], distances if c == final[-1] else (), limit
 

time: 92.5 us -> 92 us (level)
  waiting for transfers between devices: 27.9 us -> 38.5 us
  starting transfers between devices: 34.1 us -> 27.5 us
  local copies, waits for them, and re-layouts: 5.97 us -> 1.75 us
    ppermute x30, waiting for transfers between devices: 27.9 us -> 38.5 us  [swap(): return lax.ppermute(x, 'tensor', [(d, d ^ bit) for d in range(shards)])]
    ppermute x30, starting transfers between devices: 34.1 us -> 27.5 us  [swap(): return lax.ppermute(x, 'tensor', [(d, d ^ bit) for d in range(shards)])]
    unnamed x10 -> x4, local copies, waits for them, and re-layouts: 5.97 us -> 1.75 us
  transfers between devices with their start and end apart: 30 -> 30, of which waited for: 15 -> 19; matrix products, arithmetic and copies ran while one was open for 0% -> 0% of each run, Pallas kernels for 23% -> 23%
where the time goes in v10:
time: 92 us; the launch traced here: 91.8 us
  waiting for transfers between devices  38.5 us (42%)
  starting transfers between devices  27.5 us (30%)
  Pallas kernels  23.7 us (26%)
  local copies, waits for them, and re-layouts  1.75 us (2%)
    ppermute x30, waiting for transfers between devices, swap(): return lax.ppermute(x, 'tensor', [(d, d ^ bit) for d in range(shards)])  38.5 us
    ppermute x30, starting transfers between devices, swap(): return lax.ppermute(x, 'tensor', [(d, d ^ bit) for d in range(shards)])  27.5 us
    pallas_call x41, Pallas kernels, call(): pl.pallas_call(kernel, out_shape=shapes, in_specs=list(specs) + [UNREAD]...  23.7 us
  transfers between devices with their start and end apart: 30, of which 19 were waited for; matrix products, arithmetic and copies ran while one was open for 0% of the time, Pallas kernels for 23%

profile of v10, /device:TPU:0, one launch (start us, length us, event | category | flops | bytes accessed | tf_op | source)
XLA Modules:
  0.0 91.8 jit_solution(5744920570235532486)
XLA Ops:
  0.0 1.0 %copy-done = bf16[128,1664]{1,0:T(8,128)(2,1)S(1)} copy-done((bf16[128,1664]{1,0:T(8,128)(2,1)S(1)}, bf16[128,1664]{1,0:T(8,128)(2,1)}, u32[]{:S(2)}) %copy-start) | copy-done | bytes 426008
  1.0 0.7 copy-done.1
  1.8 1.2 %mix.4.refs_0_ = f32[128,384]{1,0:T(8,128)S(1)} custom-call(bf16[128,1664]{1,0:T(8,128)(2,1)S(1)} %copy-done, f32[52,52]{1,0:T(8,128)S(1)} %copy-done.1), custom_call_target="tpu_custom_call" | custom-call | flops 10000000000 | bytes 100000000 | tf_op jit(solution)/shard_map/mix/pallas_call | solution.py:81
  2.9 4.1 %collective-permute-start.3 = (f32[128,384]{1,0:T(8,128)S(1)}, f32[128,384]{1,0:T(8,128)S(1)}, u32[]{:S(2)}, u32[]{:S(2)}) collective-permute-start(f32[128,384]{1,0:T(8,128)S(1)} %mix.4.refs_0_), channel_id=1, source_target_pairs={{0,8},{1,9},{2,10},{3,11},{4,12},{5,13},{6,14},{7,15},{8,0},{9,1},... | collective-permute-start | bytes 589832 | tf_op jit(solution)/shard_map/ppermute | solution.py:311
  7.0 1.2 %mix.5.refs_0_ = f32[128,384]{1,0:T(8,128)S(1)} custom-call(bf16[128,1664]{1,0:T(8,128)(2,1)S(1)} %copy-done, f32[52,52]{1,0:T(8,128)S(1)} %copy-done.1, f32[128,384]{1,0:T(8,128)S(1)} %mix.4.refs_0_), custom_call_target="tpu_custom_call" | custom-call | flops 10000000000 | bytes 100000000 | tf_op jit(solution)/shard_map/mix/pallas_call | solution.py:81
  8.2 0.1 collective-permute-start.1
  8.3 1.2 %mix.6.refs_0_ = f32[128,384]{1,0:T(8,128)S(1)} custom-call(bf16[128,1664]{1,0:T(8,128)(2,1)S(1)} %copy-done, f32[52,52]{1,0:T(8,128)S(1)} %copy-done.1, f32[128,384]{1,0:T(8,128)S(1)} %mix.5.refs_0_), custom_call_target="tpu_custom_call" | custom-call | flops 10000000000 | bytes 100000000 | tf_op jit(solution)/shard_map/mix/pallas_call | solution.py:81
  9.5 1.6 %collective-permute-start.4 = (f32[128,384]{1,0:T(8,128)S(1)}, f32[128,384]{1,0:T(8,128)S(1)}, u32[]{:S(2)}, u32[]{:S(2)}) collective-permute-start(f32[128,384]{1,0:T(8,128)S(1)} %mix.6.refs_0_), channel_id=1, source_target_pairs={{0,4},{1,5},{2,6},{3,7},{4,0},{5,1},{6,2},{7,3},{8,12},{9,13},{10,... | collective-permute-start | bytes 589832 | tf_op jit(solution)/shard_map/ppermute | solution.py:311
  11.2 1.2 %mix.7.refs_2_.refs_0_ = f32[128,512]{1,0:T(8,128)S(1)} custom-call(bf16[128,1664]{1,0:T(8,128)(2,1)S(1)} %copy-done, f32[52,52]{1,0:T(8,128)S(1)} %copy-done.1, f32[128,384]{1,0:T(8,128)S(1)} %mix.6.refs_0_), custom_call_target="tpu_custom_call" | custom-call | flops 10000000000 | bytes 100000000 | tf_op jit(solution)/shard_map/mix/pallas_call | solution.py:81
  12.3 1.6 %collective-permute-start = (f32[128,512]{1,0:T(8,128)S(1)}, f32[128,512]{1,0:T(8,128)S(1)}, u32[]{:S(2)}, u32[]{:S(2)}) collective-permute-start(f32[128,512]{1,0:T(8,128)S(1)} %mix.7.refs_2_.refs_0_), channel_id=1, source_target_pairs={{0,2},{1,3},{2,0},{3,1},{4,6},{5,7},{6,4},{7,5},{8,10},{9,11},{10,... | collective-permute-start | bytes 786440 | tf_op jit(solution)/shard_map/ppermute | solution.py:311
  14.0 0.4 collective-permute-start.8
  14.4 2.9 %load.2 = (bf16[384,8192]{1,0:T(8,128)(2,1)S(1)}, f32[8,128]{1,0:T(8,128)S(1)}) custom-call(s32[1]{0:T(128)} %bitcast.me_ref, bf16[1664,8192]{1,0:T(8,128)(2,1)} %weight_ref.7, f32[128,384]{1,0:T(8,128)S(1)} %fold.16.refs_0_), custom_call_target="tpu_custom_call" | custom-call | flops 10000000000 | bytes 100000000 | tf_op jit(solution)/shard_map/load/pallas_call | solution.py:81
  17.2 2.9 %load.3 = (bf16[384,8192]{1,0:T(8,128)(2,1)S(1)}, f32[8,128]{1,0:T(8,128)S(1)}) custom-call(s32[1]{0:T(128)} %bitcast.me_ref, bf16[1664,8192]{1,0:T(8,128)(2,1)} %weight_ref.7, f32[8,128]{1,0:T(8,128)S(1)} %get-tuple-element.41.refs_0_), custom_call_target="tpu_custom_call" | custom-call | flops 10000000000 | bytes 100000000 | tf_op jit(solution)/shard_map/load/pallas_call | solution.py:81
  20.1 0.7 collective-permute-done.refs_1_
  20.9 0.5 collective-permute-start.2
  21.4 0.1 collective-permute-start.6
  21.5 1.6 %collective-permute-start.5 = (f32[128,384]{1,0:T(8,128)S(1)}, f32[128,384]{1,0:T(8,128)S(1)}, u32[]{:S(2)}, u32[]{:S(2)}) collective-permute-start(f32[128,384]{1,0:T(8,128)S(1)} %fold.19.refs_2_.refs_0_), channel_id=1, source_target_pairs={{0,2},{1,3},{2,0},{3,1},{4,6},{5,7},{6,4},{7,5},{8,10},{9,11},{10,... | collective-permute-start | bytes 589832 | tf_op jit(solution)/shard_map/ppermute | solution.py:311
  23.2 1.7 %collective-permute-start.12 = (f32[128,384]{1,0:T(8,128)S(1)}, f32[128,384]{1,0:T(8,128)S(1)}, u32[]{:S(2)}, u32[]{:S(2)}) collective-permute-start(f32[128,384]{1,0:T(8,128)S(1)} %fold.20.refs_2_.refs_0_), channel_id=1, source_target_pairs={{0,8},{1,9},{2,10},{3,11},{4,12},{5,13},{6,14},{7,15},{8,0},{9,1},... | collective-permute-start | bytes 589832 | tf_op jit(solution)/shard_map/ppermute | solution.py:311
  24.9 4.0 %collective-permute-done.5.refs_1_ = f32[128,384]{1,0:T(8,128)S(1)} collective-permute-done((f32[128,384]{1,0:T(8,128)S(1)}, f32[128,384]{1,0:T(8,128)S(1)}, u32[]{:S(2)}, u32[]{:S(2)}) %collective-permute-start.5) | collective-permute-done | bytes 196640 | tf_op jit(solution)/shard_map/ppermute | solution.py:311
  28.9 3.6 %fold.21 = (bf16[512,8192]{1,0:T(8,128)(2,1)S(1)}, f32[128,384]{1,0:T(8,128)S(1)}) custom-call(s32[1]{0:T(128)} %bitcast.me_ref, bf16[1664,8192]{1,0:T(8,128)(2,1)} %weight_ref.7, f32[128,384]{1,0:T(8,128)S(1)} %fold.19.refs_2_.refs_0_, f32[128,384]{1,0:T(8,128)S(1)} %collective-permute-done.5.refs_1_, f32[128,384]{1,0:T(8,128)S(1)} %fold.20.refs_2_.refs_0_), custom_call_target="tpu_custom_call" | custom-call | flops 10000000000 | bytes 100000000 | tf_op jit(solution)/shard_map/fold/pallas_call | solution.py:81
  32.5 1.6 %collective-permute-start.13 = (f32[128,384]{1,0:T(8,128)S(1)}, f32[128,384]{1,0:T(8,128)S(1)}, u32[]{:S(2)}, u32[]{:S(2)}) collective-permute-start(f32[128,384]{1,0:T(8,128)S(1)} %get-tuple-element.43.refs_2_.refs_0_), channel_id=1, source_target_pairs={{0,4},{1,5},{2,6},{3,7},{4,0},{5,1},{6,2},{7,3},{8,12},{9,13},{10,... | collective-permute-start | bytes 589832 | tf_op jit(solution)/shard_map/ppermute | solution.py:311
  34.1 1.6 %collective-permute-done.2.refs_1_ = f32[128,512]{1,0:T(8,128)S(1)} collective-permute-done((f32[128,512]{1,0:T(8,128)S(1)}, f32[128,512]{1,0:T(8,128)S(1)}, u32[]{:S(2)}, u32[]{:S(2)}) %collective-permute-start.2) | collective-permute-done | bytes 262176 | tf_op jit(solution)/shard_map/ppermute | solution.py:311
  35.7 0.1 collective-permute-start.7
  35.9 1.4 %collective-permute-done.7.refs_1_ = f32[128,512]{1,0:T(8,128)S(1)} collective-permute-done((f32[128,512]{1,0:T(8,128)S(1)}, f32[128,512]{1,0:T(8,128)S(1)}, u32[]{:S(2)}, u32[]{:S(2)}) %collective-permute-start.7) | collective-permute-done | bytes 262176 | tf_op jit(solution)/shard_map/ppermute | solution.py:311
  37.4 0.4 collective-permute-start.9
  37.7 5.5 %collective-permute-done.10.refs_1_ = f32[128,384]{1,0:T(8,128)S(1)} collective-permute-done((f32[128,384]{1,0:T(8,128)S(1)}, f32[128,384]{1,0:T(8,128)S(1)}, u32[]{:S(2)}, u32[]{:S(2)}) %collective-permute-start.10) | collective-permute-done | bytes 196640 | tf_op jit(solution)/shard_map/ppermute | solution.py:311
  43.2 0.1 collective-permute-start.11
  43.4 0.1 collective-permute-start.15
  43.5 0.4 collective-permute-start.14
  43.9 0.9 %collective-permute-done.15.refs_1_ = f32[128,384]{1,0:T(8,128)S(1)} collective-permute-done((f32[128,384]{1,0:T(8,128)S(1)}, f32[128,384]{1,0:T(8,128)S(1)}, u32[]{:S(2)}, u32[]{:S(2)}) %collective-permute-start.15) | collective-permute-done | bytes 196640 | tf_op jit(solution)/shard_map/ppermute | solution.py:311
  44.9 4.0 %step.3 = (bf16[384,8192]{1,0:T(8,128)(2,1)S(1)}, f32[16,128,512]{2,1,0:T(8,128)S(1)}) custom-call(s32[1]{0:T(128)} %bitcast.me_ref, bf16[1664,8192]{1,0:T(8,128)(2,1)} %weight_ref.7, bf16[128,384]{1,0:T(8,128)(2,1)S(1)} %fold.28.refs_0_.refs_2_, bf16[384,8192]{1,0:T(8,128)(2,1)S(1)} %get-tuple-element.44.refs_1_, bf16[128,384]{1,0:T(8,128)(2,1)S(1)} %fold.28.refs_0_.refs_2_), custom_call_target="tpu_custom_call" | custom-call | flops 10000000000 | bytes 100000000 | tf_op jit(solution)/shard_map/step/pallas_call | solution.py:81
  48.9 2.0 %collective-permute-done.14.refs_1_ = f32[128,384]{1,0:T(8,128)S(1)} collective-permute-done((f32[128,384]{1,0:T(8,128)S(1)}, f32[128,384]{1,0:T(8,128)S(1)}, u32[]{:S(2)}, u32[]{:S(2)}) %collective-permute-start.14) | collective-permute-done | bytes 196640 | tf_op jit(solution)/shard_map/ppermute | solution.py:311
  50.9 1.3 %step.4.refs_2_ = f32[16,128,512]{2,1,0:T(8,128)S(1)} custom-call(bf16[128,384]{1,0:T(8,128)(2,1)S(1)} %fold.29.refs_0_.refs_3_, bf16[384,8192]{1,0:T(8,128)(2,1)S(1)} %get-tuple-element.46.refs_1_, f32[16,128,512]{2,1,0:T(8,128)S(1)} %get-tuple-element.45.refs_2_, bf16[128,384]{1,0:T(8,128)(2,1)S(1)} %fold.29.refs_0_.refs_3_), custom_call_target="tpu_custom_call" | custom-call | flops 10000000000 | bytes 100000000 | tf_op jit(solution)/shard_map/step/pallas_call | solution.py:81
  52.2 3.1 %collective-permute-done.11.refs_1_ = f32[128,384]{1,0:T(8,128)S(1)} collective-permute-done((f32[128,384]{1,0:T(8,128)S(1)}, f32[128,384]{1,0:T(8,128)S(1)}, u32[]{:S(2)}, u32[]{:S(2)}) %collective-permute-start.11) | collective-permute-done | bytes 196640 | tf_op jit(solution)/shard_map/ppermute | solution.py:311
  55.4 1.3 %step.5.refs_2_.total_ref = f32[16,128,512]{2,1,0:T(8,128)S(1)} custom-call(bf16[128,384]{1,0:T(8,128)(2,1)S(1)} %fold.30.refs_0_.refs_3_, bf16[384,8192]{1,0:T(8,128)(2,1)S(1)} %get-tuple-element.47.refs_1_, f32[16,128,512]{2,1,0:T(8,128)S(1)} %step.4.refs_2_, bf16[128,384]{1,0:T(8,128)(2,1)S(1)} %fold.30.refs_0_.refs_3_), custom_call_target="tpu_custom_call" | custom-call | flops 10000000000 | bytes 100000000 | tf_op jit(solution)/shard_map/step/pallas_call | solution.py:81
  56.7 0.8 product.2
  57.5 0.1 collective-permute-start.17
  57.6 0.5 collective-permute-start.16
  58.1 0.8 product.3
  58.9 1.3 %collective-permute-done.17.got_ref = f32[8,128,256]{2,1,0:T(8,128)S(1)} collective-permute-done((f32[8,128,256]{2,1,0:T(8,128)S(1)}, f32[8,128,256]{2,1,0:T(8,128)S(1)}, u32[]{:S(2)}, u32[]{:S(2)}) %collective-permute-start.17) | collective-permute-done | bytes 1048608 | tf_op jit(solution)/shard_map/ppermute | solution.py:311
  60.2 0.1 halve.10
  60.3 0.6 collective-permute-start.21
  60.9 0.5 collective-permute-start.19
  61.4 0.3 collective-permute-done.16.got_ref
  61.7 0.1 halve.11
  61.8 0.8 collective-permute-start.20
  62.6 2.2 %collective-permute-start.18 = (f32[4,64,256]{2,1,0:T(8,128)S(1)}, f32[4,64,256]{2,1,0:T(8,128)S(1)}, u32[]{:S(2)}, u32[]{:S(2)}) collective-permute-start(f32[4,64,256]{2,1,0:T(8,128)S(1)} %get-tuple-element.55), channel_id=1, source_target_pairs={{0,4},{1,5},{2,6},{3,7},{4,0},{5,1},{6,2},{7,3},{8,12},{9,13},{10,... | collective-permute-start | bytes 786440 | tf_op jit(solution)/shard_map/ppermute | solution.py:311
  64.8 4.7 %collective-permute-done.21.got_ref = f32[4,64,256]{2,1,0:T(8,128)S(1)} collective-permute-done((f32[4,64,256]{2,1,0:T(8,128)S(1)}, f32[4,64,256]{2,1,0:T(8,128)S(1)}, u32[]{:S(2)}, u32[]{:S(2)}) %collective-permute-start.21) | collective-permute-done | bytes 262176 | tf_op jit(solution)/shard_map/ppermute | solution.py:311
  69.6 0.1 collective-permute-start.25
  69.7 4.7 %collective-permute-done.20.got_ref = f32[4,64,256]{2,1,0:T(8,128)S(1)} collective-permute-done((f32[4,64,256]{2,1,0:T(8,128)S(1)}, f32[4,64,256]{2,1,0:T(8,128)S(1)}, u32[]{:S(2)}, u32[]{:S(2)}) %collective-permute-start.20) | collective-permute-done | bytes 262176 | tf_op jit(solution)/shard_map/ppermute | solution.py:311
  74.5 0.9 collective-permute-done.19.got_ref
  75.4 0.9 collective-permute-start.24
  76.2 0.6 collective-permute-done.18.got_ref
  76.9 2.0 %collective-permute-start.22 = (f32[2,64,256]{2,1,0:T(8,128)S(1)}, f32[2,64,256]{2,1,0:T(8,128)S(1)}, u32[]{:S(2)}, u32[]{:S(2)}) collective-permute-start(f32[2,64,256]{2,1,0:T(8,128)S(1)} %get-tuple-element.65.refs_0_), channel_id=1, source_target_pairs={{0,2},{1,3},{2,0},{3,1},{4,6},{5,7},{6,4},{7,5},{8,10},{9,11},{10,... | collective-permute-start | bytes 393224 | tf_op jit(solution)/shard_map/ppermute | solution.py:311
  78.9 0.8 collective-permute-done.25.got_ref
  79.7 1.0 %collective-permute-start.27 = (f32[1,64,256]{2,1,0:T(8,128)S(1)}, f32[1,64,256]{2,1,0:T(8,128)S(1)}, u32[]{:S(2)}, u32[]{:S(2)}) collective-permute-start(f32[1,64,256]{2,1,0:T(8,128)S(1)} %get-tuple-element.69.refs_0_), channel_id=1, source_target_pairs={{0,8},{1,9},{2,10},{3,11},{4,12},{5,13},{6,14},{7,15},{8,0},{9,1},... | collective-permute-start | bytes 196616 | tf_op jit(solution)/shard_map/ppermute | solution.py:311
  80.7 1.1 %collective-permute-done.24.got_ref = f32[2,64,256]{2,1,0:T(8,128)S(1)} collective-permute-done((f32[2,64,256]{2,1,0:T(8,128)S(1)}, f32[2,64,256]{2,1,0:T(8,128)S(1)}, u32[]{:S(2)}, u32[]{:S(2)}) %collective-permute-start.24) | collective-permute-done | bytes 131104 | tf_op jit(solution)/shard_map/ppermute | solution.py:311
  81.8 1.4 %collective-permute-start.28 = (f32[1,64,256]{2,1,0:T(8,128)S(1)}, f32[1,64,256]{2,1,0:T(8,128)S(1)}, u32[]{:S(2)}, u32[]{:S(2)}) collective-permute-start(f32[1,64,256]{2,1,0:T(8,128)S(1)} %get-tuple-element.70.refs_0_), channel_id=1, source_target_pairs={{0,4},{1,5},{2,6},{3,7},{4,0},{5,1},{6,2},{7,3},{8,12},{9,13},{10,... | collective-permute-start | bytes 196616 | tf_op jit(solution)/shard_map/ppermute | solution.py:311
  83.3 0.9 collective-permute-start.29
  84.2 2.2 %collective-permute-start.26 = (f32[1,64,256]{2,1,0:T(8,128)S(1)}, f32[1,64,256]{2,1,0:T(8,128)S(1)}, u32[]{:S(2)}, u32[]{:S(2)}) collective-permute-start(f32[1,64,256]{2,1,0:T(8,128)S(1)} %get-tuple-element.73.refs_0_), channel_id=1, source_target_pairs={{0,8},{1,9},{2,10},{3,11},{4,12},{5,13},{6,14},{7,15},{8,0},{9,1},... | collective-permute-start | bytes 196616 | tf_op jit(solution)/shard_map/ppermute | solution.py:311
  86.4 1.2 %collective-permute-done.27.got_ref = f32[1,64,256]{2,1,0:T(8,128)S(1)} collective-permute-done((f32[1,64,256]{2,1,0:T(8,128)S(1)}, f32[1,64,256]{2,1,0:T(8,128)S(1)}, u32[]{:S(2)}, u32[]{:S(2)}) %collective-permute-start.27) | collective-permute-done | bytes 65568 | tf_op jit(solution)/shard_map/ppermute | solution.py:311
  87.6 2.8 %collective-permute-done.29.got_ref = f32[1,64,256]{2,1,0:T(8,128)S(1)} collective-permute-done((f32[1,64,256]{2,1,0:T(8,128)S(1)}, f32[1,64,256]{2,1,0:T(8,128)S(1)}, u32[]{:S(2)}, u32[]{:S(2)}) %collective-permute-start.29) | collective-permute-done | bytes 65568 | tf_op jit(solution)/shard_map/ppermute | solution.py:311
  90.5 0.7 collective-permute-done.26.got_ref
  91.2 0.7 finish.7
  (41 shorter events, 0.8 us)
Async XLA Ops:
  0.0 1.0 %copy-start = (bf16[128,1664]{1,0:T(8,128)(2,1)S(1)}, bf16[128,1664]{1,0:T(8,128)(2,1)}, u32[]{:S(2)}) copy-start(bf16[128,1664]{1,0:T(8,128)(2,1)} %activations.7) | copy-start | bytes 1277956
  1.0 0.7 copy-start.1
  2.9 18.5 %collective-permute-start.3 = (f32[128,384]{1,0:T(8,128)S(1)}, f32[128,384]{1,0:T(8,128)S(1)}, u32[]{:S(2)}, u32[]{:S(2)}) collective-permute-start(f32[128,384]{1,0:T(8,128)S(1)} %mix.4.refs_0_), channel_id=1, source_target_pairs={{0,8},{1,9},{2,10},{3,11},{4,12},{5,13},{6,14},{7,15},{8,0},{9,1},... | collective-permute-start | bytes 589832 | tf_op jit(solution)/shard_map/ppermute | solution.py:311
  8.2 5.7 %collective-permute-start.1 = (f32[128,384]{1,0:T(8,128)S(1)}, f32[128,384]{1,0:T(8,128)S(1)}, u32[]{:S(2)}, u32[]{:S(2)}) collective-permute-start(f32[128,384]{1,0:T(8,128)S(1)} %mix.5.refs_0_), channel_id=1, source_target_pairs={{0,1},{1,0},{2,3},{3,2},{4,5},{5,4},{6,7},{7,6},{8,9},{9,8},{10,11... | collective-permute-start | bytes 589832 | tf_op jit(solution)/shard_map/ppermute | solution.py:311
  9.5 11.9 %collective-permute-start.4 = (f32[128,384]{1,0:T(8,128)S(1)}, f32[128,384]{1,0:T(8,128)S(1)}, u32[]{:S(2)}, u32[]{:S(2)}) collective-permute-start(f32[128,384]{1,0:T(8,128)S(1)} %mix.6.refs_0_), channel_id=1, source_target_pairs={{0,4},{1,5},{2,6},{3,7},{4,0},{5,1},{6,2},{7,3},{8,12},{9,13},{10,... | collective-permute-start | bytes 589832 | tf_op jit(solution)/shard_map/ppermute | solution.py:311
  12.3 8.5 %collective-permute-start = (f32[128,512]{1,0:T(8,128)S(1)}, f32[128,512]{1,0:T(8,128)S(1)}, u32[]{:S(2)}, u32[]{:S(2)}) collective-permute-start(f32[128,512]{1,0:T(8,128)S(1)} %mix.7.refs_2_.refs_0_), channel_id=1, source_target_pairs={{0,2},{1,3},{2,0},{3,1},{4,6},{5,7},{6,4},{7,5},{8,10},{9,11},{10,... | collective-permute-start | bytes 786440 | tf_op jit(solution)/shard_map/ppermute | solution.py:311
  14.0 21.9 %collective-permute-start.8 = (f32[128,384]{1,0:T(8,128)S(1)}, f32[128,384]{1,0:T(8,128)S(1)}, u32[]{:S(2)}, u32[]{:S(2)}) collective-permute-start(f32[128,384]{1,0:T(8,128)S(1)} %fold.16.refs_0_), channel_id=1, source_target_pairs={{0,8},{1,9},{2,10},{3,11},{4,12},{5,13},{6,14},{7,15},{8,0},{9,1},... | collective-permute-start | bytes 589832 | tf_op jit(solution)/shard_map/ppermute | solution.py:311
  20.9 14.8 %collective-permute-start.2 = (f32[128,512]{1,0:T(8,128)S(1)}, f32[128,512]{1,0:T(8,128)S(1)}, u32[]{:S(2)}, u32[]{:S(2)}) collective-permute-start(f32[128,512]{1,0:T(8,128)S(1)} %fold.17.refs_2_.refs_0_), channel_id=1, source_target_pairs={{0,4},{1,5},{2,6},{3,7},{4,0},{5,1},{6,2},{7,3},{8,12},{9,13},{10,... | collective-permute-start | bytes 786440 | tf_op jit(solution)/shard_map/ppermute | solution.py:311
  21.4 1.7 %collective-permute-start.6 = (f32[128,384]{1,0:T(8,128)S(1)}, f32[128,384]{1,0:T(8,128)S(1)}, u32[]{:S(2)}, u32[]{:S(2)}) collective-permute-start(f32[128,384]{1,0:T(8,128)S(1)} %fold.18.refs_2_.refs_0_), channel_id=1, source_target_pairs={{0,1},{1,0},{2,3},{3,2},{4,5},{5,4},{6,7},{7,6},{8,9},{9,8},{10,11... | collective-permute-start | bytes 589832 | tf_op jit(solution)/shard_map/ppermute | solution.py:311
  21.5 7.4 %collective-permute-start.5 = (f32[128,384]{1,0:T(8,128)S(1)}, f32[128,384]{1,0:T(8,128)S(1)}, u32[]{:S(2)}, u32[]{:S(2)}) collective-permute-start(f32[128,384]{1,0:T(8,128)S(1)} %fold.19.refs_2_.refs_0_), channel_id=1, source_target_pairs={{0,2},{1,3},{2,0},{3,1},{4,6},{5,7},{6,4},{7,5},{8,10},{9,11},{10,... | collective-permute-start | bytes 589832 | tf_op jit(solution)/shard_map/ppermute | solution.py:311
  23.2 20.3 %collective-permute-start.12 = (f32[128,384]{1,0:T(8,128)S(1)}, f32[128,384]{1,0:T(8,128)S(1)}, u32[]{:S(2)}, u32[]{:S(2)}) collective-permute-start(f32[128,384]{1,0:T(8,128)S(1)} %fold.20.refs_2_.refs_0_), channel_id=1, source_target_pairs={{0,8},{1,9},{2,10},{3,11},{4,12},{5,13},{6,14},{7,15},{8,0},{9,1},... | collective-permute-start | bytes 589832 | tf_op jit(solution)/shard_map/ppermute | solution.py:311
  32.5 10.8 %collective-permute-start.13 = (f32[128,384]{1,0:T(8,128)S(1)}, f32[128,384]{1,0:T(8,128)S(1)}, u32[]{:S(2)}, u32[]{:S(2)}) collective-permute-start(f32[128,384]{1,0:T(8,128)S(1)} %get-tuple-element.43.refs_2_.refs_0_), channel_id=1, source_target_pairs={{0,4},{1,5},{2,6},{3,7},{4,0},{5,1},{6,2},{7,3},{8,12},{9,13},{10,... | collective-permute-start | bytes 589832 | tf_op jit(solution)/shard_map/ppermute | solution.py:311
  35.7 1.6 %collective-permute-start.7 = (f32[128,512]{1,0:T(8,128)S(1)}, f32[128,512]{1,0:T(8,128)S(1)}, u32[]{:S(2)}, u32[]{:S(2)}) collective-permute-start(f32[128,512]{1,0:T(8,128)S(1)} %fold.22.refs_2_.refs_0_), channel_id=1, source_target_pairs={{0,1},{1,0},{2,3},{3,2},{4,5},{5,4},{6,7},{7,6},{8,9},{9,8},{10,11... | collective-permute-start | bytes 786440 | tf_op jit(solution)/shard_map/ppermute | solution.py:311
  35.9 7.4 %collective-permute-start.10 = (f32[128,384]{1,0:T(8,128)S(1)}, f32[128,384]{1,0:T(8,128)S(1)}, u32[]{:S(2)}, u32[]{:S(2)}) collective-permute-start(f32[128,384]{1,0:T(8,128)S(1)} %fold.23.refs_2_.refs_0_), channel_id=1, source_target_pairs={{0,2},{1,3},{2,0},{3,1},{4,6},{5,7},{6,4},{7,5},{8,10},{9,11},{10,... | collective-permute-start | bytes 589832 | tf_op jit(solution)/shard_map/ppermute | solution.py:311
  37.4 19.3 %collective-permute-start.9 = (f32[128,512]{1,0:T(8,128)S(1)}, f32[128,512]{1,0:T(8,128)S(1)}, u32[]{:S(2)}, u32[]{:S(2)}) collective-permute-start(f32[128,512]{1,0:T(8,128)S(1)} %fold.24.refs_2_.refs_0_), channel_id=1, source_target_pairs={{0,8},{1,9},{2,10},{3,11},{4,12},{5,13},{6,14},{7,15},{8,0},{9,1},... | collective-permute-start | bytes 786440 | tf_op jit(solution)/shard_map/ppermute | solution.py:311
  43.2 12.1 %collective-permute-start.11 = (f32[128,384]{1,0:T(8,128)S(1)}, f32[128,384]{1,0:T(8,128)S(1)}, u32[]{:S(2)}, u32[]{:S(2)}) collective-permute-start(f32[128,384]{1,0:T(8,128)S(1)} %fold.25.refs_2_.refs_0_), channel_id=1, source_target_pairs={{0,4},{1,5},{2,6},{3,7},{4,0},{5,1},{6,2},{7,3},{8,12},{9,13},{10,... | collective-permute-start | bytes 589832 | tf_op jit(solution)/shard_map/ppermute | solution.py:311
  43.4 1.5 %collective-permute-start.15 = (f32[128,384]{1,0:T(8,128)S(1)}, f32[128,384]{1,0:T(8,128)S(1)}, u32[]{:S(2)}, u32[]{:S(2)}) collective-permute-start(f32[128,384]{1,0:T(8,128)S(1)} %fold.26.refs_2_.refs_0_), channel_id=1, source_target_pairs={{0,1},{1,0},{2,3},{3,2},{4,5},{5,4},{6,7},{7,6},{8,9},{9,8},{10,11... | collective-permute-start | bytes 589832 | tf_op jit(solution)/shard_map/ppermute | solution.py:311
  43.5 7.4 %collective-permute-start.14 = (f32[128,384]{1,0:T(8,128)S(1)}, f32[128,384]{1,0:T(8,128)S(1)}, u32[]{:S(2)}, u32[]{:S(2)}) collective-permute-start(f32[128,384]{1,0:T(8,128)S(1)} %fold.27.refs_2_.refs_0_), channel_id=1, source_target_pairs={{0,2},{1,3},{2,0},{3,1},{4,6},{5,7},{6,4},{7,5},{8,10},{9,11},{10,... | collective-permute-start | bytes 589832 | tf_op jit(solution)/shard_map/ppermute | solution.py:311
  57.5 2.7 %collective-permute-start.17 = (f32[8,128,256]{2,1,0:T(8,128)S(1)}, f32[8,128,256]{2,1,0:T(8,128)S(1)}, u32[]{:S(2)}, u32[]{:S(2)}) collective-permute-start(f32[8,128,256]{2,1,0:T(8,128)S(1)} %get-tuple-element.52), channel_id=1, source_target_pairs={{0,1},{1,0},{2,3},{3,2},{4,5},{5,4},{6,7},{7,6},{8,9},{9,8},{10,11... | collective-permute-start | bytes 3145736 | tf_op jit(solution)/shard_map/ppermute | solution.py:311
  57.6 4.1 %collective-permute-start.16 = (f32[8,128,256]{2,1,0:T(8,128)S(1)}, f32[8,128,256]{2,1,0:T(8,128)S(1)}, u32[]{:S(2)}, u32[]{:S(2)}) collective-permute-start(f32[8,128,256]{2,1,0:T(8,128)S(1)} %get-tuple-element.49.refs_0_), channel_id=1, source_target_pairs={{0,1},{1,0},{2,3},{3,2},{4,5},{5,4},{6,7},{7,6},{8,9},{9,8},{10,11... | collective-permute-start | bytes 3145736 | tf_op jit(solution)/shard_map/ppermute | solution.py:311
  60.3 9.2 %collective-permute-start.21 = (f32[4,64,256]{2,1,0:T(8,128)S(1)}, f32[4,64,256]{2,1,0:T(8,128)S(1)}, u32[]{:S(2)}, u32[]{:S(2)}) collective-permute-start(f32[4,64,256]{2,1,0:T(8,128)S(1)} %get-tuple-element.60), channel_id=1, source_target_pairs={{0,2},{1,3},{2,0},{3,1},{4,6},{5,7},{6,4},{7,5},{8,10},{9,11},{10,... | collective-permute-start | bytes 786440 | tf_op jit(solution)/shard_map/ppermute | solution.py:311
  60.9 14.5 %collective-permute-start.19 = (f32[4,64,256]{2,1,0:T(8,128)S(1)}, f32[4,64,256]{2,1,0:T(8,128)S(1)}, u32[]{:S(2)}, u32[]{:S(2)}) collective-permute-start(f32[4,64,256]{2,1,0:T(8,128)S(1)} %get-tuple-element.53.refs_0_), channel_id=1, source_target_pairs={{0,8},{1,9},{2,10},{3,11},{4,12},{5,13},{6,14},{7,15},{8,0},{9,1},... | collective-permute-start | bytes 786440 | tf_op jit(solution)/shard_map/ppermute | solution.py:311
  61.8 12.5 %collective-permute-start.20 = (f32[4,64,256]{2,1,0:T(8,128)S(1)}, f32[4,64,256]{2,1,0:T(8,128)S(1)}, u32[]{:S(2)}, u32[]{:S(2)}) collective-permute-start(f32[4,64,256]{2,1,0:T(8,128)S(1)} %get-tuple-element.58.refs_0_), channel_id=1, source_target_pairs={{0,2},{1,3},{2,0},{3,1},{4,6},{5,7},{6,4},{7,5},{8,10},{9,11},{10,... | collective-permute-start | bytes 786440 | tf_op jit(solution)/shard_map/ppermute | solution.py:311
  62.6 14.3 %collective-permute-start.18 = (f32[4,64,256]{2,1,0:T(8,128)S(1)}, f32[4,64,256]{2,1,0:T(8,128)S(1)}, u32[]{:S(2)}, u32[]{:S(2)}) collective-permute-start(f32[4,64,256]{2,1,0:T(8,128)S(1)} %get-tuple-element.55), channel_id=1, source_target_pairs={{0,4},{1,5},{2,6},{3,7},{4,0},{5,1},{6,2},{7,3},{8,12},{9,13},{10,... | collective-permute-start | bytes 786440 | tf_op jit(solution)/shard_map/ppermute | solution.py:311
  69.6 10.1 %collective-permute-start.25 = (f32[2,64,256]{2,1,0:T(8,128)S(1)}, f32[2,64,256]{2,1,0:T(8,128)S(1)}, u32[]{:S(2)}, u32[]{:S(2)}) collective-permute-start(f32[2,64,256]{2,1,0:T(8,128)S(1)} %get-tuple-element.61.refs_0_), channel_id=1, source_target_pairs={{0,4},{1,5},{2,6},{3,7},{4,0},{5,1},{6,2},{7,3},{8,12},{9,13},{10,... | collective-permute-start | bytes 393224 | tf_op jit(solution)/shard_map/ppermute | solution.py:311
  74.4 8.9 %collective-permute-start.23 = (f32[2,64,256]{2,1,0:T(8,128)S(1)}, f32[2,64,256]{2,1,0:T(8,128)S(1)}, u32[]{:S(2)}, u32[]{:S(2)}) collective-permute-start(f32[2,64,256]{2,1,0:T(8,128)S(1)} %get-tuple-element.62.refs_0_), channel_id=1, source_target_pairs={{0,4},{1,5},{2,6},{3,7},{4,0},{5,1},{6,2},{7,3},{8,12},{9,13},{10,... | collective-permute-start | bytes 393224 | tf_op jit(solution)/shard_map/ppermute | solution.py:311
  75.4 6.4 %collective-permute-start.24 = (f32[2,64,256]{2,1,0:T(8,128)S(1)}, f32[2,64,256]{2,1,0:T(8,128)S(1)}, u32[]{:S(2)}, u32[]{:S(2)}) collective-permute-start(f32[2,64,256]{2,1,0:T(8,128)S(1)} %get-tuple-element.63.refs_0_), channel_id=1, source_target_pairs={{0,2},{1,3},{2,0},{3,1},{4,6},{5,7},{6,4},{7,5},{8,10},{9,11},{10,... | collective-permute-start | bytes 393224 | tf_op jit(solution)/shard_map/ppermute | solution.py:311
  76.9 7.3 %collective-permute-start.22 = (f32[2,64,256]{2,1,0:T(8,128)S(1)}, f32[2,64,256]{2,1,0:T(8,128)S(1)}, u32[]{:S(2)}, u32[]{:S(2)}) collective-permute-start(f32[2,64,256]{2,1,0:T(8,128)S(1)} %get-tuple-element.65.refs_0_), channel_id=1, source_target_pairs={{0,2},{1,3},{2,0},{3,1},{4,6},{5,7},{6,4},{7,5},{8,10},{9,11},{10,... | collective-permute-start | bytes 393224 | tf_op jit(solution)/shard_map/ppermute | solution.py:311
  79.7 7.9 %collective-permute-start.27 = (f32[1,64,256]{2,1,0:T(8,128)S(1)}, f32[1,64,256]{2,1,0:T(8,128)S(1)}, u32[]{:S(2)}, u32[]{:S(2)}) collective-permute-start(f32[1,64,256]{2,1,0:T(8,128)S(1)} %get-tuple-element.69.refs_0_), channel_id=1, source_target_pairs={{0,8},{1,9},{2,10},{3,11},{4,12},{5,13},{6,14},{7,15},{8,0},{9,1},... | collective-permute-start | bytes 196616 | tf_op jit(solution)/shard_map/ppermute | solution.py:311
  81.8 5.8 %collective-permute-start.28 = (f32[1,64,256]{2,1,0:T(8,128)S(1)}, f32[1,64,256]{2,1,0:T(8,128)S(1)}, u32[]{:S(2)}, u32[]{:S(2)}) collective-permute-start(f32[1,64,256]{2,1,0:T(8,128)S(1)} %get-tuple-element.70.refs_0_), channel_id=1, source_target_pairs={{0,4},{1,5},{2,6},{3,7},{4,0},{5,1},{6,2},{7,3},{8,12},{9,13},{10,... | collective-permute-start | bytes 196616 | tf_op jit(solution)/shard_map/ppermute | solution.py:311
  83.3 7.2 %collective-permute-start.29 = (f32[1,64,256]{2,1,0:T(8,128)S(1)}, f32[1,64,256]{2,1,0:T(8,128)S(1)}, u32[]{:S(2)}, u32[]{:S(2)}) collective-permute-start(f32[1,64,256]{2,1,0:T(8,128)S(1)} %get-tuple-element.71.refs_0_), channel_id=1, source_target_pairs={{0,8},{1,9},{2,10},{3,11},{4,12},{5,13},{6,14},{7,15},{8,0},{9,1},... | collective-permute-start | bytes 196616 | tf_op jit(solution)/shard_map/ppermute | solution.py:311
  84.2 7.0 %collective-permute-start.26 = (f32[1,64,256]{2,1,0:T(8,128)S(1)}, f32[1,64,256]{2,1,0:T(8,128)S(1)}, u32[]{:S(2)}, u32[]{:S(2)}) collective-permute-start(f32[1,64,256]{2,1,0:T(8,128)S(1)} %get-tuple-element.73.refs_0_), channel_id=1, source_target_pairs={{0,8},{1,9},{2,10},{3,11},{4,12},{5,13},{6,14},{7,15},{8,0},{9,1},... | collective-permute-start | bytes 196616 | tf_op jit(solution)/shard_map/ppermute | solution.py:311

commit v11 on v10

--- a/solution.py
+++ b/solution.py
@@ -13,6 +13,7 @@
 BF16 = jnp.bfloat16
 
 
+TILES = (4, 3, 3, 3)
 PIECES = 4
 PERM = (0, 1, 3, 2)
 
@@ -320,14 +321,17 @@
     distances = [d | bits[0] for d in near] + near
 
     tiles = -(-local // LANES)
-    count = min(4, len(bits), tiles)
-    edges = [min(local, (tiles * c // count) * LANES) for c in range(count)] + [local]
+    count = len(TILES)
+    edges = [min(local, round(tiles * sum(TILES[:c]) / sum(TILES)) * LANES) for c in range(count + 1)]
+    assert all(begin < end for begin, end in zip(edges[:-1], edges[1:]))
     spans = list(zip(edges[:-1], edges[1:]))
     chunks = []
     for span in spans:
         chunks.append(ran(mix(activations, rotation_small, (0, tokens), span, after)))
-    cycle = bits[-1:] + bits[1:-1] + bits[:1]
-    events = sorted((phase, cycle[(phase - c) % len(bits)], c) for phase in range(len(bits)) for c in range(count))
+    cycle = bits[:0:-1] + bits[:1]
+    rank = {bit: place for place, bit in enumerate(bits[:-2] + bits[:-3:-1])}
+    events = [(phase, cycle[(phase - c) % len(bits)], c) for phase in range(len(bits)) for c in range(count)]
+    events.sort(key=lambda event: (event[0], rank[event[1]]))
     final = [c for phase, _, c in events if phase == len(bits) - 1]
     loads = [final[i] for i in (PERM if count == len(PERM) else range(count))]
     total = None

time: 92 us -> 94 us (1.022)
  starting transfers between devices: 27.5 us -> 39 us
  waiting for transfers between devices: 38.5 us -> 30.2 us
  Pallas kernels: 23.7 us -> 22.5 us
    ppermute x30, starting transfers between devices: 27.5 us -> 39 us  [swap(): return lax.ppermute(x, 'tensor', [(d, d ^ bit) for d in range(shards)])]
    ppermute x30, waiting for transfers between devices: 38.5 us -> 30.2 us  [swap(): return lax.ppermute(x, 'tensor', [(d, d ^ bit) for d in range(shards)])]
    pallas_call x41, Pallas kernels: 23.7 us -> 22.5 us  [call(): pl.pallas_call(kernel, out_shape=shapes, in_specs=list(specs) + [UNREAD]...]
  transfers between devices with their start and end apart: 30 -> 30, of which waited for: 19 -> 16; matrix products, arithmetic and copies ran while one was open for 0% -> 0% of each run, Pallas kernels for 23% -> 21%
where the time goes in v11:
time: 94 us; the launch traced here: 93.8 us
  starting transfers between devices  39 us (41%)
  waiting for transfers between devices  30.2 us (32%)
  Pallas kernels  22.5 us (24%)
  local copies, waits for them, and re-layouts  1.75 us (2%)
    ppermute x30, starting transfers between devices, swap(): return lax.ppermute(x, 'tensor', [(d, d ^ bit) for d in range(shards)])  39 us
    ppermute x30, waiting for transfers between devices, swap(): return lax.ppermute(x, 'tensor', [(d, d ^ bit) for d in range(shards)])  30.2 us
    pallas_call x41, Pallas kernels, call(): pl.pallas_call(kernel, out_shape=shapes, in_specs=list(specs) + [UNREAD]...  22.5 us
  transfers between devices with their start and end apart: 30, of which 16 were waited for; matrix products, arithmetic and copies ran while one was open for 0% of the time, Pallas kernels for 21%

profile of v11, /device:TPU:0, one launch (start us, length us, event | category | flops | bytes accessed | tf_op | source)
XLA Modules:
  0.0 93.8 jit_solution(18219575025732505995)
XLA Ops:
  0.0 1.0 %copy-done = bf16[128,1664]{1,0:T(8,128)(2,1)S(1)} copy-done((bf16[128,1664]{1,0:T(8,128)(2,1)S(1)}, bf16[128,1664]{1,0:T(8,128)(2,1)}, u32[]{:S(2)}) %copy-start) | copy-done | bytes 426008
  1.0 0.7 copy-done.1
  1.8 1.2 %mix.4.refs_0_ = f32[128,512]{1,0:T(8,128)S(1)} custom-call(bf16[128,1664]{1,0:T(8,128)(2,1)S(1)} %copy-done, f32[52,52]{1,0:T(8,128)S(1)} %copy-done.1), custom_call_target="tpu_custom_call" | custom-call | flops 10000000000 | bytes 100000000 | tf_op jit(solution)/shard_map/mix/pallas_call | solution.py:82
  2.9 4.1 %collective-permute-start.4 = (f32[128,512]{1,0:T(8,128)S(1)}, f32[128,512]{1,0:T(8,128)S(1)}, u32[]{:S(2)}, u32[]{:S(2)}) collective-permute-start(f32[128,512]{1,0:T(8,128)S(1)} %mix.4.refs_0_), channel_id=1, source_target_pairs={{0,8},{1,9},{2,10},{3,11},{4,12},{5,13},{6,14},{7,15},{8,0},{9,1},... | collective-permute-start | bytes 786440 | tf_op jit(solution)/shard_map/ppermute | solution.py:312
  7.0 1.2 %mix.5.refs_0_ = f32[128,384]{1,0:T(8,128)S(1)} custom-call(bf16[128,1664]{1,0:T(8,128)(2,1)S(1)} %copy-done, f32[52,52]{1,0:T(8,128)S(1)} %copy-done.1, f32[128,512]{1,0:T(8,128)S(1)} %mix.4.refs_0_), custom_call_target="tpu_custom_call" | custom-call | flops 10000000000 | bytes 100000000 | tf_op jit(solution)/shard_map/mix/pallas_call | solution.py:82
  8.2 0.1 collective-permute-start.1
  8.3 1.2 %mix.6.refs_0_ = f32[128,384]{1,0:T(8,128)S(1)} custom-call(bf16[128,1664]{1,0:T(8,128)(2,1)S(1)} %copy-done, f32[52,52]{1,0:T(8,128)S(1)} %copy-done.1, f32[128,384]{1,0:T(8,128)S(1)} %mix.5.refs_0_), custom_call_target="tpu_custom_call" | custom-call | flops 10000000000 | bytes 100000000 | tf_op jit(solution)/shard_map/mix/pallas_call | solution.py:82
  9.5 1.6 %collective-permute-start = (f32[128,384]{1,0:T(8,128)S(1)}, f32[128,384]{1,0:T(8,128)S(1)}, u32[]{:S(2)}, u32[]{:S(2)}) collective-permute-start(f32[128,384]{1,0:T(8,128)S(1)} %mix.6.refs_0_), channel_id=1, source_target_pairs={{0,2},{1,3},{2,0},{3,1},{4,6},{5,7},{6,4},{7,5},{8,10},{9,11},{10,... | collective-permute-start | bytes 589832 | tf_op jit(solution)/shard_map/ppermute | solution.py:312
  11.1 1.2 %mix.7.refs_2_.refs_0_ = f32[128,384]{1,0:T(8,128)S(1)} custom-call(bf16[128,1664]{1,0:T(8,128)(2,1)S(1)} %copy-done, f32[52,52]{1,0:T(8,128)S(1)} %copy-done.1, f32[128,384]{1,0:T(8,128)S(1)} %mix.6.refs_0_), custom_call_target="tpu_custom_call" | custom-call | flops 10000000000 | bytes 100000000 | tf_op jit(solution)/shard_map/mix/pallas_call | solution.py:82
  12.3 1.6 %collective-permute-start.3 = (f32[128,384]{1,0:T(8,128)S(1)}, f32[128,384]{1,0:T(8,128)S(1)}, u32[]{:S(2)}, u32[]{:S(2)}) collective-permute-start(f32[128,384]{1,0:T(8,128)S(1)} %mix.7.refs_2_.refs_0_), channel_id=1, source_target_pairs={{0,4},{1,5},{2,6},{3,7},{4,0},{5,1},{6,2},{7,3},{8,12},{9,13},{10,... | collective-permute-start | bytes 589832 | tf_op jit(solution)/shard_map/ppermute | solution.py:312
  14.0 0.4 collective-permute-start.7
  14.4 3.5 %load.2 = (bf16[512,8192]{1,0:T(8,128)(2,1)S(1)}, f32[8,128]{1,0:T(8,128)S(1)}) custom-call(s32[1]{0:T(128)} %bitcast.me_ref, bf16[1664,8192]{1,0:T(8,128)(2,1)} %weight_ref.7, f32[128,384]{1,0:T(8,128)S(1)} %fold.16.refs_0_), custom_call_target="tpu_custom_call" | custom-call | flops 10000000000 | bytes 100000000 | tf_op jit(solution)/shard_map/load/pallas_call | solution.py:82
  17.9 2.9 %load.3 = (bf16[384,8192]{1,0:T(8,128)(2,1)S(1)}, f32[8,128]{1,0:T(8,128)S(1)}) custom-call(s32[1]{0:T(128)} %bitcast.me_ref, bf16[1664,8192]{1,0:T(8,128)(2,1)} %weight_ref.7, f32[8,128]{1,0:T(8,128)S(1)} %get-tuple-element.41.refs_0_), custom_call_target="tpu_custom_call" | custom-call | flops 10000000000 | bytes 100000000 | tf_op jit(solution)/shard_map/load/pallas_call | solution.py:82
  20.7 0.0 collective-permute-done.refs_1_
  20.8 0.1 collective-permute-start.2
  20.9 3.2 %collective-permute-done.4.refs_1_ = f32[128,512]{1,0:T(8,128)S(1)} collective-permute-done((f32[128,512]{1,0:T(8,128)S(1)}, f32[128,512]{1,0:T(8,128)S(1)}, u32[]{:S(2)}, u32[]{:S(2)}) %collective-permute-start.4) | collective-permute-done | bytes 262176 | tf_op jit(solution)/shard_map/ppermute | solution.py:312
  24.1 0.1 collective-permute-start.6
  24.2 1.9 %collective-permute-start.8 = (f32[128,384]{1,0:T(8,128)S(1)}, f32[128,384]{1,0:T(8,128)S(1)}, u32[]{:S(2)}, u32[]{:S(2)}) collective-permute-start(f32[128,384]{1,0:T(8,128)S(1)} %fold.19.refs_2_.refs_0_), channel_id=1, source_target_pairs={{0,2},{1,3},{2,0},{3,1},{4,6},{5,7},{6,4},{7,5},{8,10},{9,11},{10,... | collective-permute-start | bytes 589832 | tf_op jit(solution)/shard_map/ppermute | solution.py:312
  26.2 3.1 %collective-permute-start.5 = (f32[128,384]{1,0:T(8,128)S(1)}, f32[128,384]{1,0:T(8,128)S(1)}, u32[]{:S(2)}, u32[]{:S(2)}) collective-permute-start(f32[128,384]{1,0:T(8,128)S(1)} %fold.20.refs_2_.refs_0_), channel_id=1, source_target_pairs={{0,8},{1,9},{2,10},{3,11},{4,12},{5,13},{6,14},{7,15},{8,0},{9,1},... | collective-permute-start | bytes 589832 | tf_op jit(solution)/shard_map/ppermute | solution.py:312
  29.2 1.1 %collective-permute-done.8.refs_1_ = f32[128,384]{1,0:T(8,128)S(1)} collective-permute-done((f32[128,384]{1,0:T(8,128)S(1)}, f32[128,384]{1,0:T(8,128)S(1)}, u32[]{:S(2)}, u32[]{:S(2)}) %collective-permute-start.8) | collective-permute-done | bytes 196640 | tf_op jit(solution)/shard_map/ppermute | solution.py:312
  30.4 3.0 %fold.21 = (bf16[384,8192]{1,0:T(8,128)(2,1)S(1)}, f32[128,384]{1,0:T(8,128)S(1)}) custom-call(s32[1]{0:T(128)} %bitcast.me_ref, bf16[1664,8192]{1,0:T(8,128)(2,1)} %weight_ref.7, f32[128,384]{1,0:T(8,128)S(1)} %fold.19.refs_2_.refs_0_, f32[128,384]{1,0:T(8,128)S(1)} %collective-permute-done.8.refs_1_, f32[128,384]{1,0:T(8,128)S(1)} %fold.20.refs_2_.refs_0_), custom_call_target="tpu_custom_call" | custom-call | flops 10000000000 | bytes 100000000 | tf_op jit(solution)/shard_map/fold/pallas_call | solution.py:82
  33.3 0.1 collective-permute-start.10
  33.5 1.7 %collective-permute-start.13 = (f32[128,384]{1,0:T(8,128)S(1)}, f32[128,384]{1,0:T(8,128)S(1)}, u32[]{:S(2)}, u32[]{:S(2)}) collective-permute-start(f32[128,384]{1,0:T(8,128)S(1)} %fold.22.refs_2_.refs_0_), channel_id=1, source_target_pairs={{0,4},{1,5},{2,6},{3,7},{4,0},{5,1},{6,2},{7,3},{8,12},{9,13},{10,... | collective-permute-start | bytes 589832 | tf_op jit(solution)/shard_map/ppermute | solution.py:312
  35.1 0.3 collective-permute-done.6.refs_1_
  35.4 4.0 %collective-permute-start.9 = (f32[128,512]{1,0:T(8,128)S(1)}, f32[128,512]{1,0:T(8,128)S(1)}, u32[]{:S(2)}, u32[]{:S(2)}) collective-permute-start(f32[128,512]{1,0:T(8,128)S(1)} %fold.23.refs_2_.refs_0_), channel_id=1, source_target_pairs={{0,2},{1,3},{2,0},{3,1},{4,6},{5,7},{6,4},{7,5},{8,10},{9,11},{10,... | collective-permute-start | bytes 786440 | tf_op jit(solution)/shard_map/ppermute | solution.py:312
  39.4 1.3 %collective-permute-start.12 = (f32[128,384]{1,0:T(8,128)S(1)}, f32[128,384]{1,0:T(8,128)S(1)}, u32[]{:S(2)}, u32[]{:S(2)}) collective-permute-start(f32[128,384]{1,0:T(8,128)S(1)} %fold.24.refs_2_.refs_0_), channel_id=1, source_target_pairs={{0,8},{1,9},{2,10},{3,11},{4,12},{5,13},{6,14},{7,15},{8,0},{9,1},... | collective-permute-start | bytes 589832 | tf_op jit(solution)/shard_map/ppermute | solution.py:312
  40.7 4.2 %collective-permute-done.9.refs_1_ = f32[128,512]{1,0:T(8,128)S(1)} collective-permute-done((f32[128,512]{1,0:T(8,128)S(1)}, f32[128,512]{1,0:T(8,128)S(1)}, u32[]{:S(2)}, u32[]{:S(2)}) %collective-permute-start.9) | collective-permute-done | bytes 262176 | tf_op jit(solution)/shard_map/ppermute | solution.py:312
  44.9 0.1 collective-permute-start.15
  45.0 0.1 collective-permute-start.11
  45.2 1.8 %collective-permute-start.14 = (f32[128,384]{1,0:T(8,128)S(1)}, f32[128,384]{1,0:T(8,128)S(1)}, u32[]{:S(2)}, u32[]{:S(2)}) collective-permute-start(f32[128,384]{1,0:T(8,128)S(1)} %fold.27.refs_2_.refs_0_), channel_id=1, source_target_pairs={{0,2},{1,3},{2,0},{3,1},{4,6},{5,7},{6,4},{7,5},{8,10},{9,11},{10,... | collective-permute-start | bytes 589832 | tf_op jit(solution)/shard_map/ppermute | solution.py:312
  47.0 2.9 %step.3 = (bf16[384,8192]{1,0:T(8,128)(2,1)S(1)}, f32[16,128,512]{2,1,0:T(8,128)S(1)}) custom-call(s32[1]{0:T(128)} %bitcast.me_ref, bf16[1664,8192]{1,0:T(8,128)(2,1)} %weight_ref.7, bf16[128,512]{1,0:T(8,128)(2,1)S(1)} %fold.28.refs_0_.refs_2_, bf16[512,8192]{1,0:T(8,128)(2,1)S(1)} %get-tuple-element.44.refs_1_, bf16[128,512]{1,0:T(8,128)(2,1)S(1)} %fold.28.refs_0_.refs_2_), custom_call_target="tpu_custom_call" | custom-call | flops 10000000000 | bytes 100000000 | tf_op jit(solution)/shard_map/step/pallas_call | solution.py:82
  49.9 2.6 %collective-permute-done.14.refs_1_ = f32[128,384]{1,0:T(8,128)S(1)} collective-permute-done((f32[128,384]{1,0:T(8,128)S(1)}, f32[128,384]{1,0:T(8,128)S(1)}, u32[]{:S(2)}, u32[]{:S(2)}) %collective-permute-start.14) | collective-permute-done | bytes 196640 | tf_op jit(solution)/shard_map/ppermute | solution.py:312
  52.6 1.3 %step.4.refs_2_ = f32[16,128,512]{2,1,0:T(8,128)S(1)} custom-call(bf16[128,384]{1,0:T(8,128)(2,1)S(1)} %fold.29.refs_0_.refs_3_, bf16[384,8192]{1,0:T(8,128)(2,1)S(1)} %get-tuple-element.46.refs_1_, f32[16,128,512]{2,1,0:T(8,128)S(1)} %get-tuple-element.45.refs_2_, bf16[128,384]{1,0:T(8,128)(2,1)S(1)} %fold.29.refs_0_.refs_3_), custom_call_target="tpu_custom_call" | custom-call | flops 10000000000 | bytes 100000000 | tf_op jit(solution)/shard_map/step/pallas_call | solution.py:82
  53.9 1.3 %step.5.refs_2_.total_ref = f32[16,128,512]{2,1,0:T(8,128)S(1)} custom-call(bf16[128,384]{1,0:T(8,128)(2,1)S(1)} %fold.30.refs_0_.refs_3_, bf16[384,8192]{1,0:T(8,128)(2,1)S(1)} %get-tuple-element.47.refs_1_, f32[16,128,512]{2,1,0:T(8,128)S(1)} %step.4.refs_2_, bf16[128,384]{1,0:T(8,128)(2,1)S(1)} %fold.30.refs_0_.refs_3_), custom_call_target="tpu_custom_call" | custom-call | flops 10000000000 | bytes 100000000 | tf_op jit(solution)/shard_map/step/pallas_call | solution.py:82
  55.3 0.7 product.2
  56.0 0.1 collective-permute-start.17
  56.1 0.5 collective-permute-start.16
  56.6 0.8 product.3
  57.4 1.4 %collective-permute-done.17.got_ref = f32[8,128,256]{2,1,0:T(8,128)S(1)} collective-permute-done((f32[8,128,256]{2,1,0:T(8,128)S(1)}, f32[8,128,256]{2,1,0:T(8,128)S(1)}, u32[]{:S(2)}, u32[]{:S(2)}) %collective-permute-start.17) | collective-permute-done | bytes 1048608 | tf_op jit(solution)/shard_map/ppermute | solution.py:312
  58.7 0.1 halve.10
  58.9 1.8 %collective-permute-start.21 = (f32[4,64,256]{2,1,0:T(8,128)S(1)}, f32[4,64,256]{2,1,0:T(8,128)S(1)}, u32[]{:S(2)}, u32[]{:S(2)}) collective-permute-start(f32[4,64,256]{2,1,0:T(8,128)S(1)} %get-tuple-element.60), channel_id=1, source_target_pairs={{0,2},{1,3},{2,0},{3,1},{4,6},{5,7},{6,4},{7,5},{8,10},{9,11},{10,... | collective-permute-start | bytes 786440 | tf_op jit(solution)/shard_map/ppermute | solution.py:312
  60.7 4.3 %collective-permute-start.19 = (f32[4,64,256]{2,1,0:T(8,128)S(1)}, f32[4,64,256]{2,1,0:T(8,128)S(1)}, u32[]{:S(2)}, u32[]{:S(2)}) collective-permute-start(f32[4,64,256]{2,1,0:T(8,128)S(1)} %get-tuple-element.53.refs_0_), channel_id=1, source_target_pairs={{0,8},{1,9},{2,10},{3,11},{4,12},{5,13},{6,14},{7,15},{8,0},{9,1},... | collective-permute-start | bytes 786440 | tf_op jit(solution)/shard_map/ppermute | solution.py:312
  64.9 0.1 halve.11
  65.1 0.4 collective-permute-start.20
  65.4 0.3 collective-permute-start.18
  65.7 1.6 %collective-permute-done.21.got_ref = f32[4,64,256]{2,1,0:T(8,128)S(1)} collective-permute-done((f32[4,64,256]{2,1,0:T(8,128)S(1)}, f32[4,64,256]{2,1,0:T(8,128)S(1)}, u32[]{:S(2)}, u32[]{:S(2)}) %collective-permute-start.21) | collective-permute-done | bytes 262176 | tf_op jit(solution)/shard_map/ppermute | solution.py:312
  67.4 2.6 %collective-permute-start.25 = (f32[2,64,256]{2,1,0:T(8,128)S(1)}, f32[2,64,256]{2,1,0:T(8,128)S(1)}, u32[]{:S(2)}, u32[]{:S(2)}) collective-permute-start(f32[2,64,256]{2,1,0:T(8,128)S(1)} %get-tuple-element.61.refs_0_), channel_id=1, source_target_pairs={{0,4},{1,5},{2,6},{3,7},{4,0},{5,1},{6,2},{7,3},{8,12},{9,13},{10,... | collective-permute-start | bytes 393224 | tf_op jit(solution)/shard_map/ppermute | solution.py:312
  69.9 3.0 %collective-permute-done.20.got_ref = f32[4,64,256]{2,1,0:T(8,128)S(1)} collective-permute-done((f32[4,64,256]{2,1,0:T(8,128)S(1)}, f32[4,64,256]{2,1,0:T(8,128)S(1)}, u32[]{:S(2)}, u32[]{:S(2)}) %collective-permute-start.20) | collective-permute-done | bytes 262176 | tf_op jit(solution)/shard_map/ppermute | solution.py:312
  72.9 1.8 %collective-permute-start.23 = (f32[2,64,256]{2,1,0:T(8,128)S(1)}, f32[2,64,256]{2,1,0:T(8,128)S(1)}, u32[]{:S(2)}, u32[]{:S(2)}) collective-permute-start(f32[2,64,256]{2,1,0:T(8,128)S(1)} %get-tuple-element.62.refs_0_), channel_id=1, source_target_pairs={{0,4},{1,5},{2,6},{3,7},{4,0},{5,1},{6,2},{7,3},{8,12},{9,13},{10,... | collective-permute-start | bytes 393224 | tf_op jit(solution)/shard_map/ppermute | solution.py:312
  74.7 2.0 %collective-permute-done.19.got_ref = f32[4,64,256]{2,1,0:T(8,128)S(1)} collective-permute-done((f32[4,64,256]{2,1,0:T(8,128)S(1)}, f32[4,64,256]{2,1,0:T(8,128)S(1)}, u32[]{:S(2)}, u32[]{:S(2)}) %collective-permute-start.19) | collective-permute-done | bytes 262176 | tf_op jit(solution)/shard_map/ppermute | solution.py:312
  76.8 0.4 collective-permute-start.24
  77.2 3.0 %collective-permute-done.18.got_ref = f32[4,64,256]{2,1,0:T(8,128)S(1)} collective-permute-done((f32[4,64,256]{2,1,0:T(8,128)S(1)}, f32[4,64,256]{2,1,0:T(8,128)S(1)}, u32[]{:S(2)}, u32[]{:S(2)}) %collective-permute-start.18) | collective-permute-done | bytes 262176 | tf_op jit(solution)/shard_map/ppermute | solution.py:312
  80.2 1.8 %collective-permute-start.22 = (f32[2,64,256]{2,1,0:T(8,128)S(1)}, f32[2,64,256]{2,1,0:T(8,128)S(1)}, u32[]{:S(2)}, u32[]{:S(2)}) collective-permute-start(f32[2,64,256]{2,1,0:T(8,128)S(1)} %get-tuple-element.65.refs_0_), channel_id=1, source_target_pairs={{0,2},{1,3},{2,0},{3,1},{4,6},{5,7},{6,4},{7,5},{8,10},{9,11},{10,... | collective-permute-start | bytes 393224 | tf_op jit(solution)/shard_map/ppermute | solution.py:312
  82.0 0.7 collective-permute-done.25.got_ref
  82.7 0.1 collective-permute-start.27
  82.8 0.4 collective-permute-done.24.got_ref
  83.2 0.1 collective-permute-start.28
  83.3 1.9 %collective-permute-done.23.got_ref = f32[2,64,256]{2,1,0:T(8,128)S(1)} collective-permute-done((f32[2,64,256]{2,1,0:T(8,128)S(1)}, f32[2,64,256]{2,1,0:T(8,128)S(1)}, u32[]{:S(2)}, u32[]{:S(2)}) %collective-permute-start.23) | collective-permute-done | bytes 131104 | tf_op jit(solution)/shard_map/ppermute | solution.py:312
  85.2 0.8 collective-permute-start.29
  86.0 2.3 %collective-permute-start.26 = (f32[1,64,256]{2,1,0:T(8,128)S(1)}, f32[1,64,256]{2,1,0:T(8,128)S(1)}, u32[]{:S(2)}, u32[]{:S(2)}) collective-permute-start(f32[1,64,256]{2,1,0:T(8,128)S(1)} %get-tuple-element.73.refs_0_), channel_id=1, source_target_pairs={{0,8},{1,9},{2,10},{3,11},{4,12},{5,13},{6,14},{7,15},{8,0},{9,1},... | collective-permute-start | bytes 196616 | tf_op jit(solution)/shard_map/ppermute | solution.py:312
  88.3 2.4 %collective-permute-done.27.got_ref = f32[1,64,256]{2,1,0:T(8,128)S(1)} collective-permute-done((f32[1,64,256]{2,1,0:T(8,128)S(1)}, f32[1,64,256]{2,1,0:T(8,128)S(1)}, u32[]{:S(2)}, u32[]{:S(2)}) %collective-permute-start.27) | collective-permute-done | bytes 65568 | tf_op jit(solution)/shard_map/ppermute | solution.py:312
  90.7 1.1 %collective-permute-done.29.got_ref = f32[1,64,256]{2,1,0:T(8,128)S(1)} collective-permute-done((f32[1,64,256]{2,1,0:T(8,128)S(1)}, f32[1,64,256]{2,1,0:T(8,128)S(1)}, u32[]{:S(2)}, u32[]{:S(2)}) %collective-permute-start.29) | collective-permute-done | bytes 65568 | tf_op jit(solution)/shard_map/ppermute | solution.py:312
  91.8 1.4 %collective-permute-done.26.got_ref = f32[1,64,256]{2,1,0:T(8,128)S(1)} collective-permute-done((f32[1,64,256]{2,1,0:T(8,128)S(1)}, f32[1,64,256]{2,1,0:T(8,128)S(1)}, u32[]{:S(2)}, u32[]{:S(2)}) %collective-permute-start.26) | collective-permute-done | bytes 65568 | tf_op jit(solution)/shard_map/ppermute | solution.py:312
  93.2 0.7 finish.7
  (41 shorter events, 0.7 us)
Async XLA Ops:
  0.0 1.0 %copy-start = (bf16[128,1664]{1,0:T(8,128)(2,1)S(1)}, bf16[128,1664]{1,0:T(8,128)(2,1)}, u32[]{:S(2)}) copy-start(bf16[128,1664]{1,0:T(8,128)(2,1)} %activations.7) | copy-start | bytes 1277956
  1.0 0.7 copy-start.1
  2.9 21.1 %collective-permute-start.4 = (f32[128,512]{1,0:T(8,128)S(1)}, f32[128,512]{1,0:T(8,128)S(1)}, u32[]{:S(2)}, u32[]{:S(2)}) collective-permute-start(f32[128,512]{1,0:T(8,128)S(1)} %mix.4.refs_0_), channel_id=1, source_target_pairs={{0,8},{1,9},{2,10},{3,11},{4,12},{5,13},{6,14},{7,15},{8,0},{9,1},... | collective-permute-start | bytes 786440 | tf_op jit(solution)/shard_map/ppermute | solution.py:312
  8.2 5.7 %collective-permute-start.1 = (f32[128,384]{1,0:T(8,128)S(1)}, f32[128,384]{1,0:T(8,128)S(1)}, u32[]{:S(2)}, u32[]{:S(2)}) collective-permute-start(f32[128,384]{1,0:T(8,128)S(1)} %mix.5.refs_0_), channel_id=1, source_target_pairs={{0,1},{1,0},{2,3},{3,2},{4,5},{5,4},{6,7},{7,6},{8,9},{9,8},{10,11... | collective-permute-start | bytes 589832 | tf_op jit(solution)/shard_map/ppermute | solution.py:312
  9.5 11.2 %collective-permute-start = (f32[128,384]{1,0:T(8,128)S(1)}, f32[128,384]{1,0:T(8,128)S(1)}, u32[]{:S(2)}, u32[]{:S(2)}) collective-permute-start(f32[128,384]{1,0:T(8,128)S(1)} %mix.6.refs_0_), channel_id=1, source_target_pairs={{0,2},{1,3},{2,0},{3,1},{4,6},{5,7},{6,4},{7,5},{8,10},{9,11},{10,... | collective-permute-start | bytes 589832 | tf_op jit(solution)/shard_map/ppermute | solution.py:312
  12.3 11.9 %collective-permute-start.3 = (f32[128,384]{1,0:T(8,128)S(1)}, f32[128,384]{1,0:T(8,128)S(1)}, u32[]{:S(2)}, u32[]{:S(2)}) collective-permute-start(f32[128,384]{1,0:T(8,128)S(1)} %mix.7.refs_2_.refs_0_), channel_id=1, source_target_pairs={{0,4},{1,5},{2,6},{3,7},{4,0},{5,1},{6,2},{7,3},{8,12},{9,13},{10,... | collective-permute-start | bytes 589832 | tf_op jit(solution)/shard_map/ppermute | solution.py:312
  14.0 19.4 %collective-permute-start.7 = (f32[128,384]{1,0:T(8,128)S(1)}, f32[128,384]{1,0:T(8,128)S(1)}, u32[]{:S(2)}, u32[]{:S(2)}) collective-permute-start(f32[128,384]{1,0:T(8,128)S(1)} %fold.16.refs_0_), channel_id=1, source_target_pairs={{0,8},{1,9},{2,10},{3,11},{4,12},{5,13},{6,14},{7,15},{8,0},{9,1},... | collective-permute-start | bytes 589832 | tf_op jit(solution)/shard_map/ppermute | solution.py:312
  20.8 5.4 %collective-permute-start.2 = (f32[128,384]{1,0:T(8,128)S(1)}, f32[128,384]{1,0:T(8,128)S(1)}, u32[]{:S(2)}, u32[]{:S(2)}) collective-permute-start(f32[128,384]{1,0:T(8,128)S(1)} %fold.17.refs_2_.refs_0_), channel_id=1, source_target_pairs={{0,1},{1,0},{2,3},{3,2},{4,5},{5,4},{6,7},{7,6},{8,9},{9,8},{10,11... | collective-permute-start | bytes 589832 | tf_op jit(solution)/shard_map/ppermute | solution.py:312
  24.1 11.3 %collective-permute-start.6 = (f32[128,512]{1,0:T(8,128)S(1)}, f32[128,512]{1,0:T(8,128)S(1)}, u32[]{:S(2)}, u32[]{:S(2)}) collective-permute-start(f32[128,512]{1,0:T(8,128)S(1)} %fold.18.refs_2_.refs_0_), channel_id=1, source_target_pairs={{0,4},{1,5},{2,6},{3,7},{4,0},{5,1},{6,2},{7,3},{8,12},{9,13},{10,... | collective-permute-start | bytes 786440 | tf_op jit(solution)/shard_map/ppermute | solution.py:312
  24.2 6.1 %collective-permute-start.8 = (f32[128,384]{1,0:T(8,128)S(1)}, f32[128,384]{1,0:T(8,128)S(1)}, u32[]{:S(2)}, u32[]{:S(2)}) collective-permute-start(f32[128,384]{1,0:T(8,128)S(1)} %fold.19.refs_2_.refs_0_), channel_id=1, source_target_pairs={{0,2},{1,3},{2,0},{3,1},{4,6},{5,7},{6,4},{7,5},{8,10},{9,11},{10,... | collective-permute-start | bytes 589832 | tf_op jit(solution)/shard_map/ppermute | solution.py:312
  26.2 18.8 %collective-permute-start.5 = (f32[128,384]{1,0:T(8,128)S(1)}, f32[128,384]{1,0:T(8,128)S(1)}, u32[]{:S(2)}, u32[]{:S(2)}) collective-permute-start(f32[128,384]{1,0:T(8,128)S(1)} %fold.20.refs_2_.refs_0_), channel_id=1, source_target_pairs={{0,8},{1,9},{2,10},{3,11},{4,12},{5,13},{6,14},{7,15},{8,0},{9,1},... | collective-permute-start | bytes 589832 | tf_op jit(solution)/shard_map/ppermute | solution.py:312
  33.3 6.1 %collective-permute-start.10 = (f32[128,384]{1,0:T(8,128)S(1)}, f32[128,384]{1,0:T(8,128)S(1)}, u32[]{:S(2)}, u32[]{:S(2)}) collective-permute-start(f32[128,384]{1,0:T(8,128)S(1)} %get-tuple-element.43.refs_2_.refs_0_), channel_id=1, source_target_pairs={{0,1},{1,0},{2,3},{3,2},{4,5},{5,4},{6,7},{7,6},{8,9},{9,8},{10,11... | collective-permute-start | bytes 589832 | tf_op jit(solution)/shard_map/ppermute | solution.py:312
  33.5 11.7 %collective-permute-start.13 = (f32[128,384]{1,0:T(8,128)S(1)}, f32[128,384]{1,0:T(8,128)S(1)}, u32[]{:S(2)}, u32[]{:S(2)}) collective-permute-start(f32[128,384]{1,0:T(8,128)S(1)} %fold.22.refs_2_.refs_0_), channel_id=1, source_target_pairs={{0,4},{1,5},{2,6},{3,7},{4,0},{5,1},{6,2},{7,3},{8,12},{9,13},{10,... | collective-permute-start | bytes 589832 | tf_op jit(solution)/shard_map/ppermute | solution.py:312
  35.4 9.5 %collective-permute-start.9 = (f32[128,512]{1,0:T(8,128)S(1)}, f32[128,512]{1,0:T(8,128)S(1)}, u32[]{:S(2)}, u32[]{:S(2)}) collective-permute-start(f32[128,512]{1,0:T(8,128)S(1)} %fold.23.refs_2_.refs_0_), channel_id=1, source_target_pairs={{0,2},{1,3},{2,0},{3,1},{4,6},{5,7},{6,4},{7,5},{8,10},{9,11},{10,... | collective-permute-start | bytes 786440 | tf_op jit(solution)/shard_map/ppermute | solution.py:312
  39.4 14.5 %collective-permute-start.12 = (f32[128,384]{1,0:T(8,128)S(1)}, f32[128,384]{1,0:T(8,128)S(1)}, u32[]{:S(2)}, u32[]{:S(2)}) collective-permute-start(f32[128,384]{1,0:T(8,128)S(1)} %fold.24.refs_2_.refs_0_), channel_id=1, source_target_pairs={{0,8},{1,9},{2,10},{3,11},{4,12},{5,13},{6,14},{7,15},{8,0},{9,1},... | collective-permute-start | bytes 589832 | tf_op jit(solution)/shard_map/ppermute | solution.py:312
  44.9 2.1 %collective-permute-start.15 = (f32[128,512]{1,0:T(8,128)S(1)}, f32[128,512]{1,0:T(8,128)S(1)}, u32[]{:S(2)}, u32[]{:S(2)}) collective-permute-start(f32[128,512]{1,0:T(8,128)S(1)} %fold.25.refs_2_.refs_0_), channel_id=1, source_target_pairs={{0,1},{1,0},{2,3},{3,2},{4,5},{5,4},{6,7},{7,6},{8,9},{9,8},{10,11... | collective-permute-start | bytes 786440 | tf_op jit(solution)/shard_map/ppermute | solution.py:312
  45.0 10.2 %collective-permute-start.11 = (f32[128,384]{1,0:T(8,128)S(1)}, f32[128,384]{1,0:T(8,128)S(1)}, u32[]{:S(2)}, u32[]{:S(2)}) collective-permute-start(f32[128,384]{1,0:T(8,128)S(1)} %fold.26.refs_2_.refs_0_), channel_id=1, source_target_pairs={{0,4},{1,5},{2,6},{3,7},{4,0},{5,1},{6,2},{7,3},{8,12},{9,13},{10,... | collective-permute-start | bytes 589832 | tf_op jit(solution)/shard_map/ppermute | solution.py:312
  45.2 7.4 %collective-permute-start.14 = (f32[128,384]{1,0:T(8,128)S(1)}, f32[128,384]{1,0:T(8,128)S(1)}, u32[]{:S(2)}, u32[]{:S(2)}) collective-permute-start(f32[128,384]{1,0:T(8,128)S(1)} %fold.27.refs_2_.refs_0_), channel_id=1, source_target_pairs={{0,2},{1,3},{2,0},{3,1},{4,6},{5,7},{6,4},{7,5},{8,10},{9,11},{10,... | collective-permute-start | bytes 589832 | tf_op jit(solution)/shard_map/ppermute | solution.py:312
  56.0 2.7 %collective-permute-start.17 = (f32[8,128,256]{2,1,0:T(8,128)S(1)}, f32[8,128,256]{2,1,0:T(8,128)S(1)}, u32[]{:S(2)}, u32[]{:S(2)}) collective-permute-start(f32[8,128,256]{2,1,0:T(8,128)S(1)} %get-tuple-element.52), channel_id=1, source_target_pairs={{0,1},{1,0},{2,3},{3,2},{4,5},{5,4},{6,7},{7,6},{8,9},{9,8},{10,11... | collective-permute-start | bytes 3145736 | tf_op jit(solution)/shard_map/ppermute | solution.py:312
  56.1 8.8 %collective-permute-start.16 = (f32[8,128,256]{2,1,0:T(8,128)S(1)}, f32[8,128,256]{2,1,0:T(8,128)S(1)}, u32[]{:S(2)}, u32[]{:S(2)}) collective-permute-start(f32[8,128,256]{2,1,0:T(8,128)S(1)} %get-tuple-element.49.refs_0_), channel_id=1, source_target_pairs={{0,1},{1,0},{2,3},{3,2},{4,5},{5,4},{6,7},{7,6},{8,9},{9,8},{10,11... | collective-permute-start | bytes 3145736 | tf_op jit(solution)/shard_map/ppermute | solution.py:312
  58.9 8.5 %collective-permute-start.21 = (f32[4,64,256]{2,1,0:T(8,128)S(1)}, f32[4,64,256]{2,1,0:T(8,128)S(1)}, u32[]{:S(2)}, u32[]{:S(2)}) collective-permute-start(f32[4,64,256]{2,1,0:T(8,128)S(1)} %get-tuple-element.60), channel_id=1, source_target_pairs={{0,2},{1,3},{2,0},{3,1},{4,6},{5,7},{6,4},{7,5},{8,10},{9,11},{10,... | collective-permute-start | bytes 786440 | tf_op jit(solution)/shard_map/ppermute | solution.py:312
  60.7 16.1 %collective-permute-start.19 = (f32[4,64,256]{2,1,0:T(8,128)S(1)}, f32[4,64,256]{2,1,0:T(8,128)S(1)}, u32[]{:S(2)}, u32[]{:S(2)}) collective-permute-start(f32[4,64,256]{2,1,0:T(8,128)S(1)} %get-tuple-element.53.refs_0_), channel_id=1, source_target_pairs={{0,8},{1,9},{2,10},{3,11},{4,12},{5,13},{6,14},{7,15},{8,0},{9,1},... | collective-permute-start | bytes 786440 | tf_op jit(solution)/shard_map/ppermute | solution.py:312
  65.1 7.9 %collective-permute-start.20 = (f32[4,64,256]{2,1,0:T(8,128)S(1)}, f32[4,64,256]{2,1,0:T(8,128)S(1)}, u32[]{:S(2)}, u32[]{:S(2)}) collective-permute-start(f32[4,64,256]{2,1,0:T(8,128)S(1)} %get-tuple-element.58.refs_0_), channel_id=1, source_target_pairs={{0,2},{1,3},{2,0},{3,1},{4,6},{5,7},{6,4},{7,5},{8,10},{9,11},{10,... | collective-permute-start | bytes 786440 | tf_op jit(solution)/shard_map/ppermute | solution.py:312
  65.4 14.8 %collective-permute-start.18 = (f32[4,64,256]{2,1,0:T(8,128)S(1)}, f32[4,64,256]{2,1,0:T(8,128)S(1)}, u32[]{:S(2)}, u32[]{:S(2)}) collective-permute-start(f32[4,64,256]{2,1,0:T(8,128)S(1)} %get-tuple-element.55), channel_id=1, source_target_pairs={{0,4},{1,5},{2,6},{3,7},{4,0},{5,1},{6,2},{7,3},{8,12},{9,13},{10,... | collective-permute-start | bytes 786440 | tf_op jit(solution)/shard_map/ppermute | solution.py:312
  67.4 15.4 %collective-permute-start.25 = (f32[2,64,256]{2,1,0:T(8,128)S(1)}, f32[2,64,256]{2,1,0:T(8,128)S(1)}, u32[]{:S(2)}, u32[]{:S(2)}) collective-permute-start(f32[2,64,256]{2,1,0:T(8,128)S(1)} %get-tuple-element.61.refs_0_), channel_id=1, source_target_pairs={{0,4},{1,5},{2,6},{3,7},{4,0},{5,1},{6,2},{7,3},{8,12},{9,13},{10,... | collective-permute-start | bytes 393224 | tf_op jit(solution)/shard_map/ppermute | solution.py:312
  72.9 12.2 %collective-permute-start.23 = (f32[2,64,256]{2,1,0:T(8,128)S(1)}, f32[2,64,256]{2,1,0:T(8,128)S(1)}, u32[]{:S(2)}, u32[]{:S(2)}) collective-permute-start(f32[2,64,256]{2,1,0:T(8,128)S(1)} %get-tuple-element.62.refs_0_), channel_id=1, source_target_pairs={{0,4},{1,5},{2,6},{3,7},{4,0},{5,1},{6,2},{7,3},{8,12},{9,13},{10,... | collective-permute-start | bytes 393224 | tf_op jit(solution)/shard_map/ppermute | solution.py:312
  76.8 6.4 %collective-permute-start.24 = (f32[2,64,256]{2,1,0:T(8,128)S(1)}, f32[2,64,256]{2,1,0:T(8,128)S(1)}, u32[]{:S(2)}, u32[]{:S(2)}) collective-permute-start(f32[2,64,256]{2,1,0:T(8,128)S(1)} %get-tuple-element.63.refs_0_), channel_id=1, source_target_pairs={{0,2},{1,3},{2,0},{3,1},{4,6},{5,7},{6,4},{7,5},{8,10},{9,11},{10,... | collective-permute-start | bytes 393224 | tf_op jit(solution)/shard_map/ppermute | solution.py:312
  80.2 5.7 %collective-permute-start.22 = (f32[2,64,256]{2,1,0:T(8,128)S(1)}, f32[2,64,256]{2,1,0:T(8,128)S(1)}, u32[]{:S(2)}, u32[]{:S(2)}) collective-permute-start(f32[2,64,256]{2,1,0:T(8,128)S(1)} %get-tuple-element.65.refs_0_), channel_id=1, source_target_pairs={{0,2},{1,3},{2,0},{3,1},{4,6},{5,7},{6,4},{7,5},{8,10},{9,11},{10,... | collective-permute-start | bytes 393224 | tf_op jit(solution)/shard_map/ppermute | solution.py:312
  82.7 7.9 %collective-permute-start.27 = (f32[1,64,256]{2,1,0:T(8,128)S(1)}, f32[1,64,256]{2,1,0:T(8,128)S(1)}, u32[]{:S(2)}, u32[]{:S(2)}) collective-permute-start(f32[1,64,256]{2,1,0:T(8,128)S(1)} %get-tuple-element.69.refs_0_), channel_id=1, source_target_pairs={{0,8},{1,9},{2,10},{3,11},{4,12},{5,13},{6,14},{7,15},{8,0},{9,1},... | collective-permute-start | bytes 196616 | tf_op jit(solution)/shard_map/ppermute | solution.py:312
  83.2 7.4 %collective-permute-start.28 = (f32[1,64,256]{2,1,0:T(8,128)S(1)}, f32[1,64,256]{2,1,0:T(8,128)S(1)}, u32[]{:S(2)}, u32[]{:S(2)}) collective-permute-start(f32[1,64,256]{2,1,0:T(8,128)S(1)} %get-tuple-element.70.refs_0_), channel_id=1, source_target_pairs={{0,4},{1,5},{2,6},{3,7},{4,0},{5,1},{6,2},{7,3},{8,12},{9,13},{10,... | collective-permute-start | bytes 196616 | tf_op jit(solution)/shard_map/ppermute | solution.py:312
  85.2 6.6 %collective-permute-start.29 = (f32[1,64,256]{2,1,0:T(8,128)S(1)}, f32[1,64,256]{2,1,0:T(8,128)S(1)}, u32[]{:S(2)}, u32[]{:S(2)}) collective-permute-start(f32[1,64,256]{2,1,0:T(8,128)S(1)} %get-tuple-element.71.refs_0_), channel_id=1, source_target_pairs={{0,8},{1,9},{2,10},{3,11},{4,12},{5,13},{6,14},{7,15},{8,0},{9,1},... | collective-permute-start | bytes 196616 | tf_op jit(solution)/shard_map/ppermute | solution.py:312
  86.0 7.2 %collective-permute-start.26 = (f32[1,64,256]{2,1,0:T(8,128)S(1)}, f32[1,64,256]{2,1,0:T(8,128)S(1)}, u32[]{:S(2)}, u32[]{:S(2)}) collective-permute-start(f32[1,64,256]{2,1,0:T(8,128)S(1)} %get-tuple-element.73.refs_0_), channel_id=1, source_target_pairs={{0,8},{1,9},{2,10},{3,11},{4,12},{5,13},{6,14},{7,15},{8,0},{9,1},... | collective-permute-start | bytes 196616 | tf_op jit(solution)/shard_map/ppermute | solution.py:312

commit v12 on v11

--- a/solution.py
+++ b/solution.py
@@ -349,7 +349,7 @@
         got = swap(chunks[c], bit)
         last = phase == len(bits) - 1
         scale = factor if last else None
-        if number == count + 1 and len(loaded) < count - 1:
+        if number == 6 and len(loaded) < count - 1:
             chunks[c], columns = ran(fold(me, chunks[c], got, bit, after, scale, *wanted()[1:]), 0)
             loaded.append(columns)
         else:
@@ -365,12 +365,12 @@
                 total = ran(step(me, chunks[c], columns, total, shards, after))
 
     inner = bits[1:]
-    late = inner[-1:] + inner[:-1]
+    late = inner[:1] + inner[:0:-1]
     swapped = [inner[1], inner[0]] + inner[2:]
     half = tokens // 2
     routes = [
-        [((0, half), inner), ((half, tokens), late)],
-        [((0, half), swapped), ((half, tokens), inner)],
+        [((0, half), swapped), ((half, tokens), late)],
+        [((0, half), inner), ((half, tokens), swapped)],
     ][:parts]
     links = Links(bits)
     clock = 0.0

time: 94 us -> 91.2 us (0.970)
  waiting for transfers between devices: 30.2 us -> 21.8 us
  starting transfers between devices: 39 us -> 44.5 us
    ppermute x30, waiting for transfers between devices: 30.2 us -> 21.8 us  [swap(): return lax.ppermute(x, 'tensor', [(d, d ^ bit) for d in range(shards)])]
    ppermute x30, starting transfers between devices: 39 us -> 44.5 us  [swap(): return lax.ppermute(x, 'tensor', [(d, d ^ bit) for d in range(shards)])]
  transfers between devices with their start and end apart: 30 -> 30, of which waited for: 16 -> 10; matrix products, arithmetic and copies ran while one was open for 0% -> 0% of each run, Pallas kernels for 21% -> 22%
where the time goes in v12:
time: 91.2 us; the launch traced here: 91 us
  starting transfers between devices  44.5 us (49%)
  Pallas kernels  22.6 us (25%)
  waiting for transfers between devices  21.8 us (24%)
  local copies, waits for them, and re-layouts  1.75 us (2%)
    ppermute x30, starting transfers between devices, swap(): return lax.ppermute(x, 'tensor', [(d, d ^ bit) for d in range(shards)])  44.5 us
    pallas_call x41, Pallas kernels, call(): pl.pallas_call(kernel, out_shape=shapes, in_specs=list(specs) + [UNREAD]...  22.6 us
    ppermute x30, waiting for transfers between devices, swap(): return lax.ppermute(x, 'tensor', [(d, d ^ bit) for d in range(shards)])  21.8 us
  transfers between devices with their start and end apart: 30, of which 10 were waited for; matrix products, arithmetic and copies ran while one was open for 0% of the time, Pallas kernels for 22%

profile of v12, /device:TPU:0, one launch (start us, length us, event | category | flops | bytes accessed | tf_op | source)
XLA Modules:
  0.0 91.0 jit_solution(270411540418894538)
XLA Ops:
  0.0 1.0 %copy-done = bf16[128,1664]{1,0:T(8,128)(2,1)S(1)} copy-done((bf16[128,1664]{1,0:T(8,128)(2,1)S(1)}, bf16[128,1664]{1,0:T(8,128)(2,1)}, u32[]{:S(2)}) %copy-start) | copy-done | bytes 426008
  1.0 0.7 copy-done.1
  1.8 1.2 %mix.4.refs_0_ = f32[128,512]{1,0:T(8,128)S(1)} custom-call(bf16[128,1664]{1,0:T(8,128)(2,1)S(1)} %copy-done, f32[52,52]{1,0:T(8,128)S(1)} %copy-done.1), custom_call_target="tpu_custom_call" | custom-call | flops 10000000000 | bytes 100000000 | tf_op jit(solution)/shard_map/mix/pallas_call | solution.py:82
  2.9 4.1 %collective-permute-start.4 = (f32[128,512]{1,0:T(8,128)S(1)}, f32[128,512]{1,0:T(8,128)S(1)}, u32[]{:S(2)}, u32[]{:S(2)}) collective-permute-start(f32[128,512]{1,0:T(8,128)S(1)} %mix.4.refs_0_), channel_id=1, source_target_pairs={{0,8},{1,9},{2,10},{3,11},{4,12},{5,13},{6,14},{7,15},{8,0},{9,1},... | collective-permute-start | bytes 786440 | tf_op jit(solution)/shard_map/ppermute | solution.py:312
  7.0 1.2 %mix.5.refs_0_ = f32[128,384]{1,0:T(8,128)S(1)} custom-call(bf16[128,1664]{1,0:T(8,128)(2,1)S(1)} %copy-done, f32[52,52]{1,0:T(8,128)S(1)} %copy-done.1, f32[128,512]{1,0:T(8,128)S(1)} %mix.4.refs_0_), custom_call_target="tpu_custom_call" | custom-call | flops 10000000000 | bytes 100000000 | tf_op jit(solution)/shard_map/mix/pallas_call | solution.py:82
  8.2 0.1 collective-permute-start.1
  8.3 1.2 %mix.6.refs_0_ = f32[128,384]{1,0:T(8,128)S(1)} custom-call(bf16[128,1664]{1,0:T(8,128)(2,1)S(1)} %copy-done, f32[52,52]{1,0:T(8,128)S(1)} %copy-done.1, f32[128,384]{1,0:T(8,128)S(1)} %mix.5.refs_0_), custom_call_target="tpu_custom_call" | custom-call | flops 10000000000 | bytes 100000000 | tf_op jit(solution)/shard_map/mix/pallas_call | solution.py:82
  9.5 1.6 %collective-permute-start = (f32[128,384]{1,0:T(8,128)S(1)}, f32[128,384]{1,0:T(8,128)S(1)}, u32[]{:S(2)}, u32[]{:S(2)}) collective-permute-start(f32[128,384]{1,0:T(8,128)S(1)} %mix.6.refs_0_), channel_id=1, source_target_pairs={{0,2},{1,3},{2,0},{3,1},{4,6},{5,7},{6,4},{7,5},{8,10},{9,11},{10,... | collective-permute-start | bytes 589832 | tf_op jit(solution)/shard_map/ppermute | solution.py:312
  11.1 1.2 %mix.7.refs_2_.refs_0_ = f32[128,384]{1,0:T(8,128)S(1)} custom-call(bf16[128,1664]{1,0:T(8,128)(2,1)S(1)} %copy-done, f32[52,52]{1,0:T(8,128)S(1)} %copy-done.1, f32[128,384]{1,0:T(8,128)S(1)} %mix.6.refs_0_), custom_call_target="tpu_custom_call" | custom-call | flops 10000000000 | bytes 100000000 | tf_op jit(solution)/shard_map/mix/pallas_call | solution.py:82
  12.3 1.6 %collective-permute-start.3 = (f32[128,384]{1,0:T(8,128)S(1)}, f32[128,384]{1,0:T(8,128)S(1)}, u32[]{:S(2)}, u32[]{:S(2)}) collective-permute-start(f32[128,384]{1,0:T(8,128)S(1)} %mix.7.refs_2_.refs_0_), channel_id=1, source_target_pairs={{0,4},{1,5},{2,6},{3,7},{4,0},{5,1},{6,2},{7,3},{8,12},{9,13},{10,... | collective-permute-start | bytes 589832 | tf_op jit(solution)/shard_map/ppermute | solution.py:312
  14.0 0.4 collective-permute-start.7
  14.4 3.5 %load.2 = (bf16[512,8192]{1,0:T(8,128)(2,1)S(1)}, f32[8,128]{1,0:T(8,128)S(1)}) custom-call(s32[1]{0:T(128)} %bitcast.me_ref, bf16[1664,8192]{1,0:T(8,128)(2,1)} %weight_ref.7, f32[128,384]{1,0:T(8,128)S(1)} %fold.16.refs_0_), custom_call_target="tpu_custom_call" | custom-call | flops 10000000000 | bytes 100000000 | tf_op jit(solution)/shard_map/load/pallas_call | solution.py:82
  17.9 2.9 %load.3 = (bf16[384,8192]{1,0:T(8,128)(2,1)S(1)}, f32[8,128]{1,0:T(8,128)S(1)}) custom-call(s32[1]{0:T(128)} %bitcast.me_ref, bf16[1664,8192]{1,0:T(8,128)(2,1)} %weight_ref.7, f32[8,128]{1,0:T(8,128)S(1)} %get-tuple-element.41.refs_0_), custom_call_target="tpu_custom_call" | custom-call | flops 10000000000 | bytes 100000000 | tf_op jit(solution)/shard_map/load/pallas_call | solution.py:82
  20.7 0.0 collective-permute-done.refs_1_
  20.8 0.1 collective-permute-start.2
  20.9 3.2 %collective-permute-done.4.refs_1_ = f32[128,512]{1,0:T(8,128)S(1)} collective-permute-done((f32[128,512]{1,0:T(8,128)S(1)}, f32[128,512]{1,0:T(8,128)S(1)}, u32[]{:S(2)}, u32[]{:S(2)}) %collective-permute-start.4) | collective-permute-done | bytes 262176 | tf_op jit(solution)/shard_map/ppermute | solution.py:312
  24.1 0.1 collective-permute-start.6
  24.2 0.0 collective-permute-done.3.refs_1_
  24.2 1.9 %collective-permute-start.8 = (f32[128,384]{1,0:T(8,128)S(1)}, f32[128,384]{1,0:T(8,128)S(1)}, u32[]{:S(2)}, u32[]{:S(2)}) collective-permute-start(f32[128,384]{1,0:T(8,128)S(1)} %fold.19.refs_2_.refs_0_), channel_id=1, source_target_pairs={{0,2},{1,3},{2,0},{3,1},{4,6},{5,7},{6,4},{7,5},{8,10},{9,11},{10,... | collective-permute-start | bytes 589832 | tf_op jit(solution)/shard_map/ppermute | solution.py:312
  26.2 3.1 %collective-permute-start.5 = (f32[128,384]{1,0:T(8,128)S(1)}, f32[128,384]{1,0:T(8,128)S(1)}, u32[]{:S(2)}, u32[]{:S(2)}) collective-permute-start(f32[128,384]{1,0:T(8,128)S(1)} %fold.20.refs_2_.refs_0_), channel_id=1, source_target_pairs={{0,8},{1,9},{2,10},{3,11},{4,12},{5,13},{6,14},{7,15},{8,0},{9,1},... | collective-permute-start | bytes 589832 | tf_op jit(solution)/shard_map/ppermute | solution.py:312
  29.2 1.1 %collective-permute-done.8.refs_1_ = f32[128,384]{1,0:T(8,128)S(1)} collective-permute-done((f32[128,384]{1,0:T(8,128)S(1)}, f32[128,384]{1,0:T(8,128)S(1)}, u32[]{:S(2)}, u32[]{:S(2)}) %collective-permute-start.8) | collective-permute-done | bytes 196640 | tf_op jit(solution)/shard_map/ppermute | solution.py:312
  30.4 0.1 collective-permute-start.10
  30.5 0.0 collective-permute-done.7.refs_1_
  30.5 3.0 %fold.22 = (bf16[384,8192]{1,0:T(8,128)(2,1)S(1)}, f32[128,384]{1,0:T(8,128)S(1)}) custom-call(s32[1]{0:T(128)} %bitcast.me_ref, bf16[1664,8192]{1,0:T(8,128)(2,1)} %weight_ref.7, f32[128,384]{1,0:T(8,128)S(1)} %fold.16.refs_0_, f32[128,384]{1,0:T(8,128)S(1)} %collective-permute-done.7.refs_1_, f32[128,384]{1,0:T(8,128)S(1)} %fold.21.refs_2_.refs_0_), custom_call_target="tpu_custom_call" | custom-call | flops 10000000000 | bytes 100000000 | tf_op jit(solution)/shard_map/fold/pallas_call | solution.py:82
  33.4 1.7 %collective-permute-start.13 = (f32[128,384]{1,0:T(8,128)S(1)}, f32[128,384]{1,0:T(8,128)S(1)}, u32[]{:S(2)}, u32[]{:S(2)}) collective-permute-start(f32[128,384]{1,0:T(8,128)S(1)} %get-tuple-element.43.refs_2_.refs_0_), channel_id=1, source_target_pairs={{0,4},{1,5},{2,6},{3,7},{4,0},{5,1},{6,2},{7,3},{8,12},{9,13},{10,... | collective-permute-start | bytes 589832 | tf_op jit(solution)/shard_map/ppermute | solution.py:312
  35.1 0.3 collective-permute-done.6.refs_1_
  35.4 4.0 %collective-permute-start.9 = (f32[128,512]{1,0:T(8,128)S(1)}, f32[128,512]{1,0:T(8,128)S(1)}, u32[]{:S(2)}, u32[]{:S(2)}) collective-permute-start(f32[128,512]{1,0:T(8,128)S(1)} %fold.23.refs_2_.refs_0_), channel_id=1, source_target_pairs={{0,2},{1,3},{2,0},{3,1},{4,6},{5,7},{6,4},{7,5},{8,10},{9,11},{10,... | collective-permute-start | bytes 786440 | tf_op jit(solution)/shard_map/ppermute | solution.py:312
  39.4 0.0 collective-permute-done.10.refs_1_
  39.4 1.3 %collective-permute-start.12 = (f32[128,384]{1,0:T(8,128)S(1)}, f32[128,384]{1,0:T(8,128)S(1)}, u32[]{:S(2)}, u32[]{:S(2)}) collective-permute-start(f32[128,384]{1,0:T(8,128)S(1)} %fold.24.refs_2_.refs_0_), channel_id=1, source_target_pairs={{0,8},{1,9},{2,10},{3,11},{4,12},{5,13},{6,14},{7,15},{8,0},{9,1},... | collective-permute-start | bytes 589832 | tf_op jit(solution)/shard_map/ppermute | solution.py:312
  40.7 4.2 %collective-permute-done.9.refs_1_ = f32[128,512]{1,0:T(8,128)S(1)} collective-permute-done((f32[128,512]{1,0:T(8,128)S(1)}, f32[128,512]{1,0:T(8,128)S(1)}, u32[]{:S(2)}, u32[]{:S(2)}) %collective-permute-start.9) | collective-permute-done | bytes 262176 | tf_op jit(solution)/shard_map/ppermute | solution.py:312
  44.9 0.1 collective-permute-start.15
  45.0 0.0 collective-permute-done.5.refs_1_
  45.0 0.1 collective-permute-start.11
  45.2 1.8 %collective-permute-start.14 = (f32[128,384]{1,0:T(8,128)S(1)}, f32[128,384]{1,0:T(8,128)S(1)}, u32[]{:S(2)}, u32[]{:S(2)}) collective-permute-start(f32[128,384]{1,0:T(8,128)S(1)} %fold.27.refs_2_.refs_0_), channel_id=1, source_target_pairs={{0,2},{1,3},{2,0},{3,1},{4,6},{5,7},{6,4},{7,5},{8,10},{9,11},{10,... | collective-permute-start | bytes 589832 | tf_op jit(solution)/shard_map/ppermute | solution.py:312
  47.0 0.0 collective-permute-done.15.refs_1_
  47.0 2.9 %step.3 = (bf16[384,8192]{1,0:T(8,128)(2,1)S(1)}, f32[16,128,512]{2,1,0:T(8,128)S(1)}) custom-call(s32[1]{0:T(128)} %bitcast.me_ref, bf16[1664,8192]{1,0:T(8,128)(2,1)} %weight_ref.7, bf16[128,512]{1,0:T(8,128)(2,1)S(1)} %fold.28.refs_0_.refs_2_, bf16[512,8192]{1,0:T(8,128)(2,1)S(1)} %get-tuple-element.44.refs_1_, bf16[128,512]{1,0:T(8,128)(2,1)S(1)} %fold.28.refs_0_.refs_2_), custom_call_target="tpu_custom_call" | custom-call | flops 10000000000 | bytes 100000000 | tf_op jit(solution)/shard_map/step/pallas_call | solution.py:82
  49.9 2.6 %collective-permute-done.14.refs_1_ = f32[128,384]{1,0:T(8,128)S(1)} collective-permute-done((f32[128,384]{1,0:T(8,128)S(1)}, f32[128,384]{1,0:T(8,128)S(1)}, u32[]{:S(2)}, u32[]{:S(2)}) %collective-permute-start.14) | collective-permute-done | bytes 196640 | tf_op jit(solution)/shard_map/ppermute | solution.py:312
  52.6 1.3 %step.4.refs_2_ = f32[16,128,512]{2,1,0:T(8,128)S(1)} custom-call(bf16[128,384]{1,0:T(8,128)(2,1)S(1)} %fold.29.refs_0_.refs_3_, bf16[384,8192]{1,0:T(8,128)(2,1)S(1)} %get-tuple-element.46.refs_1_, f32[16,128,512]{2,1,0:T(8,128)S(1)} %get-tuple-element.45.refs_2_, bf16[128,384]{1,0:T(8,128)(2,1)S(1)} %fold.29.refs_0_.refs_3_), custom_call_target="tpu_custom_call" | custom-call | flops 10000000000 | bytes 100000000 | tf_op jit(solution)/shard_map/step/pallas_call | solution.py:82
  53.9 0.0 collective-permute-done.12.refs_1_
  54.0 1.3 %step.5.refs_2_.total_ref = f32[16,128,512]{2,1,0:T(8,128)S(1)} custom-call(bf16[128,384]{1,0:T(8,128)(2,1)S(1)} %fold.30.refs_0_.refs_3_, bf16[384,8192]{1,0:T(8,128)(2,1)S(1)} %get-tuple-element.47.refs_1_, f32[16,128,512]{2,1,0:T(8,128)S(1)} %step.4.refs_2_, bf16[128,384]{1,0:T(8,128)(2,1)S(1)} %fold.30.refs_0_.refs_3_), custom_call_target="tpu_custom_call" | custom-call | flops 10000000000 | bytes 100000000 | tf_op jit(solution)/shard_map/step/pallas_call | solution.py:82
  55.3 0.7 product.2
  56.1 0.1 collective-permute-start.17
  56.2 0.5 collective-permute-start.16
  56.7 0.8 product.3
  57.4 1.4 %collective-permute-done.17.got_ref = f32[8,128,256]{2,1,0:T(8,128)S(1)} collective-permute-done((f32[8,128,256]{2,1,0:T(8,128)S(1)}, f32[8,128,256]{2,1,0:T(8,128)S(1)}, u32[]{:S(2)}, u32[]{:S(2)}) %collective-permute-start.17) | collective-permute-done | bytes 1048608 | tf_op jit(solution)/shard_map/ppermute | solution.py:312
  58.8 0.1 halve.10
  58.9 1.8 %collective-permute-start.21 = (f32[4,64,256]{2,1,0:T(8,128)S(1)}, f32[4,64,256]{2,1,0:T(8,128)S(1)}, u32[]{:S(2)}, u32[]{:S(2)}) collective-permute-start(f32[4,64,256]{2,1,0:T(8,128)S(1)} %get-tuple-element.60), channel_id=1, source_target_pairs={{0,4},{1,5},{2,6},{3,7},{4,0},{5,1},{6,2},{7,3},{8,12},{9,13},{10,... | collective-permute-start | bytes 786440 | tf_op jit(solution)/shard_map/ppermute | solution.py:312
  60.7 1.8 %collective-permute-start.20 = (f32[4,64,256]{2,1,0:T(8,128)S(1)}, f32[4,64,256]{2,1,0:T(8,128)S(1)}, u32[]{:S(2)}, u32[]{:S(2)}) collective-permute-start(f32[4,64,256]{2,1,0:T(8,128)S(1)} %get-tuple-element.53.refs_0_), channel_id=1, source_target_pairs={{0,2},{1,3},{2,0},{3,1},{4,6},{5,7},{6,4},{7,5},{8,10},{9,11},{10,... | collective-permute-start | bytes 786440 | tf_op jit(solution)/shard_map/ppermute | solution.py:312
  62.5 0.1 halve.11
  62.6 0.4 collective-permute-start.19
  63.0 1.0 %collective-permute-start.18 = (f32[4,64,256]{2,1,0:T(8,128)S(1)}, f32[4,64,256]{2,1,0:T(8,128)S(1)}, u32[]{:S(2)}, u32[]{:S(2)}) collective-permute-start(f32[4,64,256]{2,1,0:T(8,128)S(1)} %get-tuple-element.55), channel_id=1, source_target_pairs={{0,2},{1,3},{2,0},{3,1},{4,6},{5,7},{6,4},{7,5},{8,10},{9,11},{10,... | collective-permute-start | bytes 786440 | tf_op jit(solution)/shard_map/ppermute | solution.py:312
  64.0 4.2 %collective-permute-done.21.got_ref = f32[4,64,256]{2,1,0:T(8,128)S(1)} collective-permute-done((f32[4,64,256]{2,1,0:T(8,128)S(1)}, f32[4,64,256]{2,1,0:T(8,128)S(1)}, u32[]{:S(2)}, u32[]{:S(2)}) %collective-permute-start.21) | collective-permute-done | bytes 262176 | tf_op jit(solution)/shard_map/ppermute | solution.py:312
  68.2 1.8 %collective-permute-start.25 = (f32[2,64,256]{2,1,0:T(8,128)S(1)}, f32[2,64,256]{2,1,0:T(8,128)S(1)}, u32[]{:S(2)}, u32[]{:S(2)}) collective-permute-start(f32[2,64,256]{2,1,0:T(8,128)S(1)} %get-tuple-element.61.refs_0_), channel_id=1, source_target_pairs={{0,2},{1,3},{2,0},{3,1},{4,6},{5,7},{6,4},{7,5},{8,10},{9,11},{10,... | collective-permute-start | bytes 393224 | tf_op jit(solution)/shard_map/ppermute | solution.py:312
  70.0 4.3 %collective-permute-start.24 = (f32[2,64,256]{2,1,0:T(8,128)S(1)}, f32[2,64,256]{2,1,0:T(8,128)S(1)}, u32[]{:S(2)}, u32[]{:S(2)}) collective-permute-start(f32[2,64,256]{2,1,0:T(8,128)S(1)} %get-tuple-element.62.refs_0_), channel_id=1, source_target_pairs={{0,8},{1,9},{2,10},{3,11},{4,12},{5,13},{6,14},{7,15},{8,0},{9,1},... | collective-permute-start | bytes 393224 | tf_op jit(solution)/shard_map/ppermute | solution.py:312
  74.4 1.8 %collective-permute-start.23 = (f32[2,64,256]{2,1,0:T(8,128)S(1)}, f32[2,64,256]{2,1,0:T(8,128)S(1)}, u32[]{:S(2)}, u32[]{:S(2)}) collective-permute-start(f32[2,64,256]{2,1,0:T(8,128)S(1)} %get-tuple-element.63.refs_0_), channel_id=1, source_target_pairs={{0,2},{1,3},{2,0},{3,1},{4,6},{5,7},{6,4},{7,5},{8,10},{9,11},{10,... | collective-permute-start | bytes 393224 | tf_op jit(solution)/shard_map/ppermute | solution.py:312
  76.3 1.2 %collective-permute-start.22 = (f32[2,64,256]{2,1,0:T(8,128)S(1)}, f32[2,64,256]{2,1,0:T(8,128)S(1)}, u32[]{:S(2)}, u32[]{:S(2)}) collective-permute-start(f32[2,64,256]{2,1,0:T(8,128)S(1)} %get-tuple-element.65.refs_0_), channel_id=1, source_target_pairs={{0,4},{1,5},{2,6},{3,7},{4,0},{5,1},{6,2},{7,3},{8,12},{9,13},{10,... | collective-permute-start | bytes 393224 | tf_op jit(solution)/shard_map/ppermute | solution.py:312
  77.4 0.6 collective-permute-done.25.got_ref
  78.0 3.0 %collective-permute-start.27 = (f32[1,64,256]{2,1,0:T(8,128)S(1)}, f32[1,64,256]{2,1,0:T(8,128)S(1)}, u32[]{:S(2)}, u32[]{:S(2)}) collective-permute-start(f32[1,64,256]{2,1,0:T(8,128)S(1)} %get-tuple-element.69.refs_0_), channel_id=1, source_target_pairs={{0,8},{1,9},{2,10},{3,11},{4,12},{5,13},{6,14},{7,15},{8,0},{9,1},... | collective-permute-start | bytes 196616 | tf_op jit(solution)/shard_map/ppermute | solution.py:312
  81.1 1.9 %collective-permute-start.28 = (f32[1,64,256]{2,1,0:T(8,128)S(1)}, f32[1,64,256]{2,1,0:T(8,128)S(1)}, u32[]{:S(2)}, u32[]{:S(2)}) collective-permute-start(f32[1,64,256]{2,1,0:T(8,128)S(1)} %get-tuple-element.70.refs_0_), channel_id=1, source_target_pairs={{0,4},{1,5},{2,6},{3,7},{4,0},{5,1},{6,2},{7,3},{8,12},{9,13},{10,... | collective-permute-start | bytes 196616 | tf_op jit(solution)/shard_map/ppermute | solution.py:312
  83.0 0.2 collective-permute-start.29
  83.2 2.8 %collective-permute-start.26 = (f32[1,64,256]{2,1,0:T(8,128)S(1)}, f32[1,64,256]{2,1,0:T(8,128)S(1)}, u32[]{:S(2)}, u32[]{:S(2)}) collective-permute-start(f32[1,64,256]{2,1,0:T(8,128)S(1)} %get-tuple-element.73.refs_0_), channel_id=1, source_target_pairs={{0,8},{1,9},{2,10},{3,11},{4,12},{5,13},{6,14},{7,15},{8,0},{9,1},... | collective-permute-start | bytes 196616 | tf_op jit(solution)/shard_map/ppermute | solution.py:312
  86.1 3.5 %collective-permute-done.29.got_ref = f32[1,64,256]{2,1,0:T(8,128)S(1)} collective-permute-done((f32[1,64,256]{2,1,0:T(8,128)S(1)}, f32[1,64,256]{2,1,0:T(8,128)S(1)}, u32[]{:S(2)}, u32[]{:S(2)}) %collective-permute-start.29) | collective-permute-done | bytes 65568 | tf_op jit(solution)/shard_map/ppermute | solution.py:312
  89.6 0.7 collective-permute-done.26.got_ref
  90.3 0.7 finish.7
  (41 shorter events, 0.7 us)
Async XLA Ops:
  0.0 1.0 %copy-start = (bf16[128,1664]{1,0:T(8,128)(2,1)S(1)}, bf16[128,1664]{1,0:T(8,128)(2,1)}, u32[]{:S(2)}) copy-start(bf16[128,1664]{1,0:T(8,128)(2,1)} %activations.7) | copy-start | bytes 1277956
  1.0 0.7 copy-start.1
  2.9 21.1 %collective-permute-start.4 = (f32[128,512]{1,0:T(8,128)S(1)}, f32[128,512]{1,0:T(8,128)S(1)}, u32[]{:S(2)}, u32[]{:S(2)}) collective-permute-start(f32[128,512]{1,0:T(8,128)S(1)} %mix.4.refs_0_), channel_id=1, source_target_pairs={{0,8},{1,9},{2,10},{3,11},{4,12},{5,13},{6,14},{7,15},{8,0},{9,1},... | collective-permute-start | bytes 786440 | tf_op jit(solution)/shard_map/ppermute | solution.py:312
  8.2 5.7 %collective-permute-start.1 = (f32[128,384]{1,0:T(8,128)S(1)}, f32[128,384]{1,0:T(8,128)S(1)}, u32[]{:S(2)}, u32[]{:S(2)}) collective-permute-start(f32[128,384]{1,0:T(8,128)S(1)} %mix.5.refs_0_), channel_id=1, source_target_pairs={{0,1},{1,0},{2,3},{3,2},{4,5},{5,4},{6,7},{7,6},{8,9},{9,8},{10,11... | collective-permute-start | bytes 589832 | tf_op jit(solution)/shard_map/ppermute | solution.py:312
  9.5 11.2 %collective-permute-start = (f32[128,384]{1,0:T(8,128)S(1)}, f32[128,384]{1,0:T(8,128)S(1)}, u32[]{:S(2)}, u32[]{:S(2)}) collective-permute-start(f32[128,384]{1,0:T(8,128)S(1)} %mix.6.refs_0_), channel_id=1, source_target_pairs={{0,2},{1,3},{2,0},{3,1},{4,6},{5,7},{6,4},{7,5},{8,10},{9,11},{10,... | collective-permute-start | bytes 589832 | tf_op jit(solution)/shard_map/ppermute | solution.py:312
  12.3 11.9 %collective-permute-start.3 = (f32[128,384]{1,0:T(8,128)S(1)}, f32[128,384]{1,0:T(8,128)S(1)}, u32[]{:S(2)}, u32[]{:S(2)}) collective-permute-start(f32[128,384]{1,0:T(8,128)S(1)} %mix.7.refs_2_.refs_0_), channel_id=1, source_target_pairs={{0,4},{1,5},{2,6},{3,7},{4,0},{5,1},{6,2},{7,3},{8,12},{9,13},{10,... | collective-permute-start | bytes 589832 | tf_op jit(solution)/shard_map/ppermute | solution.py:312
  14.0 16.5 %collective-permute-start.7 = (f32[128,384]{1,0:T(8,128)S(1)}, f32[128,384]{1,0:T(8,128)S(1)}, u32[]{:S(2)}, u32[]{:S(2)}) collective-permute-start(f32[128,384]{1,0:T(8,128)S(1)} %fold.16.refs_0_), channel_id=1, source_target_pairs={{0,8},{1,9},{2,10},{3,11},{4,12},{5,13},{6,14},{7,15},{8,0},{9,1},... | collective-permute-start | bytes 589832 | tf_op jit(solution)/shard_map/ppermute | solution.py:312
  20.8 5.4 %collective-permute-start.2 = (f32[128,384]{1,0:T(8,128)S(1)}, f32[128,384]{1,0:T(8,128)S(1)}, u32[]{:S(2)}, u32[]{:S(2)}) collective-permute-start(f32[128,384]{1,0:T(8,128)S(1)} %fold.17.refs_2_.refs_0_), channel_id=1, source_target_pairs={{0,1},{1,0},{2,3},{3,2},{4,5},{5,4},{6,7},{7,6},{8,9},{9,8},{10,11... | collective-permute-start | bytes 589832 | tf_op jit(solution)/shard_map/ppermute | solution.py:312
  24.1 11.3 %collective-permute-start.6 = (f32[128,512]{1,0:T(8,128)S(1)}, f32[128,512]{1,0:T(8,128)S(1)}, u32[]{:S(2)}, u32[]{:S(2)}) collective-permute-start(f32[128,512]{1,0:T(8,128)S(1)} %fold.18.refs_2_.refs_0_), channel_id=1, source_target_pairs={{0,4},{1,5},{2,6},{3,7},{4,0},{5,1},{6,2},{7,3},{8,12},{9,13},{10,... | collective-permute-start | bytes 786440 | tf_op jit(solution)/shard_map/ppermute | solution.py:312
  24.2 6.1 %collective-permute-start.8 = (f32[128,384]{1,0:T(8,128)S(1)}, f32[128,384]{1,0:T(8,128)S(1)}, u32[]{:S(2)}, u32[]{:S(2)}) collective-permute-start(f32[128,384]{1,0:T(8,128)S(1)} %fold.19.refs_2_.refs_0_), channel_id=1, source_target_pairs={{0,2},{1,3},{2,0},{3,1},{4,6},{5,7},{6,4},{7,5},{8,10},{9,11},{10,... | collective-permute-start | bytes 589832 | tf_op jit(solution)/shard_map/ppermute | solution.py:312
  26.2 18.8 %collective-permute-start.5 = (f32[128,384]{1,0:T(8,128)S(1)}, f32[128,384]{1,0:T(8,128)S(1)}, u32[]{:S(2)}, u32[]{:S(2)}) collective-permute-start(f32[128,384]{1,0:T(8,128)S(1)} %fold.20.refs_2_.refs_0_), channel_id=1, source_target_pairs={{0,8},{1,9},{2,10},{3,11},{4,12},{5,13},{6,14},{7,15},{8,0},{9,1},... | collective-permute-start | bytes 589832 | tf_op jit(solution)/shard_map/ppermute | solution.py:312
  30.4 9.0 %collective-permute-start.10 = (f32[128,384]{1,0:T(8,128)S(1)}, f32[128,384]{1,0:T(8,128)S(1)}, u32[]{:S(2)}, u32[]{:S(2)}) collective-permute-start(f32[128,384]{1,0:T(8,128)S(1)} %fold.21.refs_2_.refs_0_), channel_id=1, source_target_pairs={{0,1},{1,0},{2,3},{3,2},{4,5},{5,4},{6,7},{7,6},{8,9},{9,8},{10,11... | collective-permute-start | bytes 589832 | tf_op jit(solution)/shard_map/ppermute | solution.py:312
  33.4 11.7 %collective-permute-start.13 = (f32[128,384]{1,0:T(8,128)S(1)}, f32[128,384]{1,0:T(8,128)S(1)}, u32[]{:S(2)}, u32[]{:S(2)}) collective-permute-start(f32[128,384]{1,0:T(8,128)S(1)} %get-tuple-element.43.refs_2_.refs_0_), channel_id=1, source_target_pairs={{0,4},{1,5},{2,6},{3,7},{4,0},{5,1},{6,2},{7,3},{8,12},{9,13},{10,... | collective-permute-start | bytes 589832 | tf_op jit(solution)/shard_map/ppermute | solution.py:312
  35.4 9.5 %collective-permute-start.9 = (f32[128,512]{1,0:T(8,128)S(1)}, f32[128,512]{1,0:T(8,128)S(1)}, u32[]{:S(2)}, u32[]{:S(2)}) collective-permute-start(f32[128,512]{1,0:T(8,128)S(1)} %fold.23.refs_2_.refs_0_), channel_id=1, source_target_pairs={{0,2},{1,3},{2,0},{3,1},{4,6},{5,7},{6,4},{7,5},{8,10},{9,11},{10,... | collective-permute-start | bytes 786440 | tf_op jit(solution)/shard_map/ppermute | solution.py:312
  39.4 14.5 %collective-permute-start.12 = (f32[128,384]{1,0:T(8,128)S(1)}, f32[128,384]{1,0:T(8,128)S(1)}, u32[]{:S(2)}, u32[]{:S(2)}) collective-permute-start(f32[128,384]{1,0:T(8,128)S(1)} %fold.24.refs_2_.refs_0_), channel_id=1, source_target_pairs={{0,8},{1,9},{2,10},{3,11},{4,12},{5,13},{6,14},{7,15},{8,0},{9,1},... | collective-permute-start | bytes 589832 | tf_op jit(solution)/shard_map/ppermute | solution.py:312
  44.9 2.1 %collective-permute-start.15 = (f32[128,512]{1,0:T(8,128)S(1)}, f32[128,512]{1,0:T(8,128)S(1)}, u32[]{:S(2)}, u32[]{:S(2)}) collective-permute-start(f32[128,512]{1,0:T(8,128)S(1)} %fold.25.refs_2_.refs_0_), channel_id=1, source_target_pairs={{0,1},{1,0},{2,3},{3,2},{4,5},{5,4},{6,7},{7,6},{8,9},{9,8},{10,11... | collective-permute-start | bytes 786440 | tf_op jit(solution)/shard_map/ppermute | solution.py:312
  45.0 10.3 %collective-permute-start.11 = (f32[128,384]{1,0:T(8,128)S(1)}, f32[128,384]{1,0:T(8,128)S(1)}, u32[]{:S(2)}, u32[]{:S(2)}) collective-permute-start(f32[128,384]{1,0:T(8,128)S(1)} %fold.26.refs_2_.refs_0_), channel_id=1, source_target_pairs={{0,4},{1,5},{2,6},{3,7},{4,0},{5,1},{6,2},{7,3},{8,12},{9,13},{10,... | collective-permute-start | bytes 589832 | tf_op jit(solution)/shard_map/ppermute | solution.py:312
  45.2 7.4 %collective-permute-start.14 = (f32[128,384]{1,0:T(8,128)S(1)}, f32[128,384]{1,0:T(8,128)S(1)}, u32[]{:S(2)}, u32[]{:S(2)}) collective-permute-start(f32[128,384]{1,0:T(8,128)S(1)} %fold.27.refs_2_.refs_0_), channel_id=1, source_target_pairs={{0,2},{1,3},{2,0},{3,1},{4,6},{5,7},{6,4},{7,5},{8,10},{9,11},{10,... | collective-permute-start | bytes 589832 | tf_op jit(solution)/shard_map/ppermute | solution.py:312
  56.1 2.7 %collective-permute-start.17 = (f32[8,128,256]{2,1,0:T(8,128)S(1)}, f32[8,128,256]{2,1,0:T(8,128)S(1)}, u32[]{:S(2)}, u32[]{:S(2)}) collective-permute-start(f32[8,128,256]{2,1,0:T(8,128)S(1)} %get-tuple-element.52), channel_id=1, source_target_pairs={{0,1},{1,0},{2,3},{3,2},{4,5},{5,4},{6,7},{7,6},{8,9},{9,8},{10,11... | collective-permute-start | bytes 3145736 | tf_op jit(solution)/shard_map/ppermute | solution.py:312
  56.2 6.3 %collective-permute-start.16 = (f32[8,128,256]{2,1,0:T(8,128)S(1)}, f32[8,128,256]{2,1,0:T(8,128)S(1)}, u32[]{:S(2)}, u32[]{:S(2)}) collective-permute-start(f32[8,128,256]{2,1,0:T(8,128)S(1)} %get-tuple-element.49.refs_0_), channel_id=1, source_target_pairs={{0,1},{1,0},{2,3},{3,2},{4,5},{5,4},{6,7},{7,6},{8,9},{9,8},{10,11... | collective-permute-start | bytes 3145736 | tf_op jit(solution)/shard_map/ppermute | solution.py:312
  58.9 9.2 %collective-permute-start.21 = (f32[4,64,256]{2,1,0:T(8,128)S(1)}, f32[4,64,256]{2,1,0:T(8,128)S(1)}, u32[]{:S(2)}, u32[]{:S(2)}) collective-permute-start(f32[4,64,256]{2,1,0:T(8,128)S(1)} %get-tuple-element.60), channel_id=1, source_target_pairs={{0,4},{1,5},{2,6},{3,7},{4,0},{5,1},{6,2},{7,3},{8,12},{9,13},{10,... | collective-permute-start | bytes 786440 | tf_op jit(solution)/shard_map/ppermute | solution.py:312
  60.7 9.3 %collective-permute-start.20 = (f32[4,64,256]{2,1,0:T(8,128)S(1)}, f32[4,64,256]{2,1,0:T(8,128)S(1)}, u32[]{:S(2)}, u32[]{:S(2)}) collective-permute-start(f32[4,64,256]{2,1,0:T(8,128)S(1)} %get-tuple-element.53.refs_0_), channel_id=1, source_target_pairs={{0,2},{1,3},{2,0},{3,1},{4,6},{5,7},{6,4},{7,5},{8,10},{9,11},{10,... | collective-permute-start | bytes 786440 | tf_op jit(solution)/shard_map/ppermute | solution.py:312
  62.6 11.8 %collective-permute-start.19 = (f32[4,64,256]{2,1,0:T(8,128)S(1)}, f32[4,64,256]{2,1,0:T(8,128)S(1)}, u32[]{:S(2)}, u32[]{:S(2)}) collective-permute-start(f32[4,64,256]{2,1,0:T(8,128)S(1)} %get-tuple-element.57.refs_0_), channel_id=1, source_target_pairs={{0,4},{1,5},{2,6},{3,7},{4,0},{5,1},{6,2},{7,3},{8,12},{9,13},{10,... | collective-permute-start | bytes 786440 | tf_op jit(solution)/shard_map/ppermute | solution.py:312
  63.0 13.3 %collective-permute-start.18 = (f32[4,64,256]{2,1,0:T(8,128)S(1)}, f32[4,64,256]{2,1,0:T(8,128)S(1)}, u32[]{:S(2)}, u32[]{:S(2)}) collective-permute-start(f32[4,64,256]{2,1,0:T(8,128)S(1)} %get-tuple-element.55), channel_id=1, source_target_pairs={{0,2},{1,3},{2,0},{3,1},{4,6},{5,7},{6,4},{7,5},{8,10},{9,11},{10,... | collective-permute-start | bytes 786440 | tf_op jit(solution)/shard_map/ppermute | solution.py:312
  68.2 9.8 %collective-permute-start.25 = (f32[2,64,256]{2,1,0:T(8,128)S(1)}, f32[2,64,256]{2,1,0:T(8,128)S(1)}, u32[]{:S(2)}, u32[]{:S(2)}) collective-permute-start(f32[2,64,256]{2,1,0:T(8,128)S(1)} %get-tuple-element.61.refs_0_), channel_id=1, source_target_pairs={{0,2},{1,3},{2,0},{3,1},{4,6},{5,7},{6,4},{7,5},{8,10},{9,11},{10,... | collective-permute-start | bytes 393224 | tf_op jit(solution)/shard_map/ppermute | solution.py:312
  70.0 11.0 %collective-permute-start.24 = (f32[2,64,256]{2,1,0:T(8,128)S(1)}, f32[2,64,256]{2,1,0:T(8,128)S(1)}, u32[]{:S(2)}, u32[]{:S(2)}) collective-permute-start(f32[2,64,256]{2,1,0:T(8,128)S(1)} %get-tuple-element.62.refs_0_), channel_id=1, source_target_pairs={{0,8},{1,9},{2,10},{3,11},{4,12},{5,13},{6,14},{7,15},{8,0},{9,1},... | collective-permute-start | bytes 393224 | tf_op jit(solution)/shard_map/ppermute | solution.py:312
  74.4 8.6 %collective-permute-start.23 = (f32[2,64,256]{2,1,0:T(8,128)S(1)}, f32[2,64,256]{2,1,0:T(8,128)S(1)}, u32[]{:S(2)}, u32[]{:S(2)}) collective-permute-start(f32[2,64,256]{2,1,0:T(8,128)S(1)} %get-tuple-element.63.refs_0_), channel_id=1, source_target_pairs={{0,2},{1,3},{2,0},{3,1},{4,6},{5,7},{6,4},{7,5},{8,10},{9,11},{10,... | collective-permute-start | bytes 393224 | tf_op jit(solution)/shard_map/ppermute | solution.py:312
  76.3 7.0 %collective-permute-start.22 = (f32[2,64,256]{2,1,0:T(8,128)S(1)}, f32[2,64,256]{2,1,0:T(8,128)S(1)}, u32[]{:S(2)}, u32[]{:S(2)}) collective-permute-start(f32[2,64,256]{2,1,0:T(8,128)S(1)} %get-tuple-element.65.refs_0_), channel_id=1, source_target_pairs={{0,4},{1,5},{2,6},{3,7},{4,0},{5,1},{6,2},{7,3},{8,12},{9,13},{10,... | collective-permute-start | bytes 393224 | tf_op jit(solution)/shard_map/ppermute | solution.py:312
  78.0 8.0 %collective-permute-start.27 = (f32[1,64,256]{2,1,0:T(8,128)S(1)}, f32[1,64,256]{2,1,0:T(8,128)S(1)}, u32[]{:S(2)}, u32[]{:S(2)}) collective-permute-start(f32[1,64,256]{2,1,0:T(8,128)S(1)} %get-tuple-element.69.refs_0_), channel_id=1, source_target_pairs={{0,8},{1,9},{2,10},{3,11},{4,12},{5,13},{6,14},{7,15},{8,0},{9,1},... | collective-permute-start | bytes 196616 | tf_op jit(solution)/shard_map/ppermute | solution.py:312
  81.1 5.0 %collective-permute-start.28 = (f32[1,64,256]{2,1,0:T(8,128)S(1)}, f32[1,64,256]{2,1,0:T(8,128)S(1)}, u32[]{:S(2)}, u32[]{:S(2)}) collective-permute-start(f32[1,64,256]{2,1,0:T(8,128)S(1)} %get-tuple-element.70.refs_0_), channel_id=1, source_target_pairs={{0,4},{1,5},{2,6},{3,7},{4,0},{5,1},{6,2},{7,3},{8,12},{9,13},{10,... | collective-permute-start | bytes 196616 | tf_op jit(solution)/shard_map/ppermute | solution.py:312
  83.0 6.6 %collective-permute-start.29 = (f32[1,64,256]{2,1,0:T(8,128)S(1)}, f32[1,64,256]{2,1,0:T(8,128)S(1)}, u32[]{:S(2)}, u32[]{:S(2)}) collective-permute-start(f32[1,64,256]{2,1,0:T(8,128)S(1)} %get-tuple-element.71.refs_0_), channel_id=1, source_target_pairs={{0,8},{1,9},{2,10},{3,11},{4,12},{5,13},{6,14},{7,15},{8,0},{9,1},... | collective-permute-start | bytes 196616 | tf_op jit(solution)/shard_map/ppermute | solution.py:312
  83.2 7.1 %collective-permute-start.26 = (f32[1,64,256]{2,1,0:T(8,128)S(1)}, f32[1,64,256]{2,1,0:T(8,128)S(1)}, u32[]{:S(2)}, u32[]{:S(2)}) collective-permute-start(f32[1,64,256]{2,1,0:T(8,128)S(1)} %get-tuple-element.73.refs_0_), channel_id=1, source_target_pairs={{0,8},{1,9},{2,10},{3,11},{4,12},{5,13},{6,14},{7,15},{8,0},{9,1},... | collective-permute-start | bytes 196616 | tf_op jit(solution)/shard_map/ppermute | solution.py:312

commit v13 on v12

--- a/solution.py
+++ b/solution.py
@@ -14,8 +14,9 @@
 
 
 TILES = (4, 3, 3, 3)
+DIRECT = 2
 PIECES = 4
-PERM = (0, 1, 3, 2)
+PERM = (0, 3, 2, 1)
 
 
 def quotient(index, divisor, limit):
@@ -195,25 +196,28 @@
     return call("step", kernel, values, specs, shape, after)
 
 
-def product(me, chunk, columns, total, begin, distances, parts, after):
+def product(me, factors, total, begin, distances, parts, after):
     share = total.shape[2]
     width = share // parts
-    group = max(1, min(len(distances), 1024 // share))
-
-    def kernel(me_ref, chunk_ref, columns_ref, total_ref, *refs):
-        outs = refs[-parts:]
-        for at in range(0, len(distances), group):
-            start = (begin + at) * share
-            sums = jnp.dot(
-                chunk_ref[...], columns_ref[:, start:start + group * share], preferred_element_type=F32
-            )
-            for i in range(group):
-                value = total_ref[distances[at + i] ^ me_ref[0]] + sums[:, i * share:(i + 1) * share]
-                for part in range(parts):
-                    outs[part][at + i] = value[:, part * width:(part + 1) * width]
-
-    shapes = [jax.ShapeDtypeStruct((len(distances), chunk.shape[0], width), F32)] * parts
-    return call("product", kernel, (me, chunk, columns, total), [SMEM] + [VMEM] * 3, shapes, after)
+    count = len(factors)
+
+    def kernel(me_ref, total_ref, *refs):
+        chunks, weights, outs = refs[:count], refs[count:2 * count], refs[-parts:]
+        for at, distance in enumerate(distances):
+            owner = distance ^ me_ref[0]
+            value = total_ref[owner]
+            for (_, _, in_order), chunk, columns in zip(factors, chunks, weights):
+                start = (begin + at) * share if in_order else pl.multiple_of(owner * share, LANES)
+                value = value + jnp.dot(
+                    chunk[...], columns[:, pl.ds(start, share)], preferred_element_type=F32
+                )
+            for part in range(parts):
+                outs[part][at] = value[:, part * width:(part + 1) * width]
+
+    tokens = factors[0][0].shape[0]
+    shapes = [jax.ShapeDtypeStruct((len(distances), tokens, width), F32)] * parts
+    operands = (me, total, *[f[0] for f in factors], *[f[1] for f in factors])
+    return call("product", kernel, operands, [SMEM] + [VMEM] * (1 + 2 * count), shapes, after)
 
 
 def halve(own, got, distances, plans, after):
@@ -349,14 +353,14 @@
         got = swap(chunks[c], bit)
         last = phase == len(bits) - 1
         scale = factor if last else None
-        if number == 6 and len(loaded) < count - 1:
+        if number == 1 and len(loaded) < count - 1:
             chunks[c], columns = ran(fold(me, chunks[c], got, bit, after, scale, *wanted()[1:]), 0)
             loaded.append(columns)
         else:
             chunks[c] = ran(fold(me, chunks[c], got, bit, after, scale))
         while number == 0 and len(loaded) < count - 2:
             loaded.append(ran(load(*wanted(), after), 0)[1])
-        if last and c != final[-1]:
+        if last and c in final[:count - DIRECT]:
             columns = loaded[loads.index(c)]
             if len(loaded) < count:
                 total, columns = ran(step(me, chunks[c], columns, total, shards, after, *wanted()[1:]), 0)
@@ -400,13 +404,13 @@
         held = pieces + [(rows, part, None)] if last else []
         pieces.append((rows, part, ran(finish(held, keep, got, tokens, width, parts, after))))
 
-    last_chunk, last_columns = chunks[final[-1]], loaded[loads.index(final[-1])]
-    sends = ran(product(me, last_chunk, last_columns, total, 0, distances[:len(near)], parts, after))
+    factors = [(chunks[c], loaded[loads.index(c)], c == final[-1]) for c in final[count - DIRECT:]]
+    sends = ran(product(me, factors, total, 0, distances[:len(near)], parts, after))
     clock += 0.9
     kernels += 1
     for x in sends:
         send(x, bits[0], None)
-    keeps = ran(product(me, last_chunk, last_columns, total, len(near), near, parts, after))
+    keeps = ran(product(me, factors, total, len(near), near, parts, after))
     clock += 0.9
     kernels += 1
     queue[:] = [

time: 91.2 us -> 90.6 us (level)
  starting transfers between devices: 44.5 us -> 39.4 us
  waiting for transfers between devices: 21.8 us -> 26.6 us
    ppermute x30, starting transfers between devices: 44.5 us -> 39.4 us  [swap(): return lax.ppermute(x, 'tensor', [(d, d ^ bit) for d in range(shards)])]
    ppermute x30, waiting for transfers between devices: 21.8 us -> 26.6 us  [swap(): return lax.ppermute(x, 'tensor', [(d, d ^ bit) for d in range(shards)])]
    pallas_call x41 -> x40, Pallas kernels: 22.6 us -> 22.3 us  [call(): pl.pallas_call(kernel, out_shape=shapes, in_specs=list(specs) + [UNREAD]...]
  transfers between devices with their start and end apart: 30 -> 30, of which waited for: 10 -> 12; matrix products, arithmetic and copies ran while one was open for 0% -> 0% of each run, Pallas kernels for 22% -> 21%
where the time goes in v13:
time: 90.6 us; the launch traced here: 90.4 us
  starting transfers between devices  39.4 us (43%)
  waiting for transfers between devices  26.6 us (29%)
  Pallas kernels  22.3 us (25%)
  local copies, waits for them, and re-layouts  1.75 us (2%)
    ppermute x30, starting transfers between devices, swap(): return lax.ppermute(x, 'tensor', [(d, d ^ bit) for d in range(shards)])  39.4 us
    ppermute x30, waiting for transfers between devices, swap(): return lax.ppermute(x, 'tensor', [(d, d ^ bit) for d in range(shards)])  26.6 us
    pallas_call x40, Pallas kernels, call(): pl.pallas_call(kernel, out_shape=shapes, in_specs=list(specs) + [UNREAD]...  22.3 us
  transfers between devices with their start and end apart: 30, of which 12 were waited for; matrix products, arithmetic and copies ran while one was open for 0% of the time, Pallas kernels for 21%

profile of v13, /device:TPU:0, one launch (start us, length us, event | category | flops | bytes accessed | tf_op | source)
XLA Modules:
  0.0 90.4 jit_solution(13723117312008476872)
XLA Ops:
  0.0 1.0 %copy-done = bf16[128,1664]{1,0:T(8,128)(2,1)S(1)} copy-done((bf16[128,1664]{1,0:T(8,128)(2,1)S(1)}, bf16[128,1664]{1,0:T(8,128)(2,1)}, u32[]{:S(2)}) %copy-start) | copy-done | bytes 426008
  1.0 0.7 copy-done.1
  1.8 1.2 %mix.4.refs_0_ = f32[128,512]{1,0:T(8,128)S(1)} custom-call(bf16[128,1664]{1,0:T(8,128)(2,1)S(1)} %copy-done, f32[52,52]{1,0:T(8,128)S(1)} %copy-done.1), custom_call_target="tpu_custom_call" | custom-call | flops 10000000000 | bytes 100000000 | tf_op jit(solution)/shard_map/mix/pallas_call | solution.py:83
  2.9 4.1 %collective-permute-start.3 = (f32[128,512]{1,0:T(8,128)S(1)}, f32[128,512]{1,0:T(8,128)S(1)}, u32[]{:S(2)}, u32[]{:S(2)}) collective-permute-start(f32[128,512]{1,0:T(8,128)S(1)} %mix.4.refs_0_), channel_id=1, source_target_pairs={{0,8},{1,9},{2,10},{3,11},{4,12},{5,13},{6,14},{7,15},{8,0},{9,1},... | collective-permute-start | bytes 786440 | tf_op jit(solution)/shard_map/ppermute | solution.py:316
  7.0 1.2 %mix.5.refs_0_ = f32[128,384]{1,0:T(8,128)S(1)} custom-call(bf16[128,1664]{1,0:T(8,128)(2,1)S(1)} %copy-done, f32[52,52]{1,0:T(8,128)S(1)} %copy-done.1, f32[128,512]{1,0:T(8,128)S(1)} %mix.4.refs_0_), custom_call_target="tpu_custom_call" | custom-call | flops 10000000000 | bytes 100000000 | tf_op jit(solution)/shard_map/mix/pallas_call | solution.py:83
  8.2 0.1 collective-permute-start
  8.3 1.2 %mix.6.refs_0_ = f32[128,384]{1,0:T(8,128)S(1)} custom-call(bf16[128,1664]{1,0:T(8,128)(2,1)S(1)} %copy-done, f32[52,52]{1,0:T(8,128)S(1)} %copy-done.1, f32[128,384]{1,0:T(8,128)S(1)} %mix.5.refs_0_), custom_call_target="tpu_custom_call" | custom-call | flops 10000000000 | bytes 100000000 | tf_op jit(solution)/shard_map/mix/pallas_call | solution.py:83
  9.5 1.6 %collective-permute-start.4 = (f32[128,384]{1,0:T(8,128)S(1)}, f32[128,384]{1,0:T(8,128)S(1)}, u32[]{:S(2)}, u32[]{:S(2)}) collective-permute-start(f32[128,384]{1,0:T(8,128)S(1)} %mix.6.refs_0_), channel_id=1, source_target_pairs={{0,2},{1,3},{2,0},{3,1},{4,6},{5,7},{6,4},{7,5},{8,10},{9,11},{10,... | collective-permute-start | bytes 589832 | tf_op jit(solution)/shard_map/ppermute | solution.py:316
  11.1 1.2 %mix.7.refs_2_.refs_0_ = f32[128,384]{1,0:T(8,128)S(1)} custom-call(bf16[128,1664]{1,0:T(8,128)(2,1)S(1)} %copy-done, f32[52,52]{1,0:T(8,128)S(1)} %copy-done.1, f32[128,384]{1,0:T(8,128)S(1)} %mix.6.refs_0_), custom_call_target="tpu_custom_call" | custom-call | flops 10000000000 | bytes 100000000 | tf_op jit(solution)/shard_map/mix/pallas_call | solution.py:83
  12.3 1.6 %collective-permute-start.2 = (f32[128,384]{1,0:T(8,128)S(1)}, f32[128,384]{1,0:T(8,128)S(1)}, u32[]{:S(2)}, u32[]{:S(2)}) collective-permute-start(f32[128,384]{1,0:T(8,128)S(1)} %mix.7.refs_2_.refs_0_), channel_id=1, source_target_pairs={{0,4},{1,5},{2,6},{3,7},{4,0},{5,1},{6,2},{7,3},{8,12},{9,13},{10,... | collective-permute-start | bytes 589832 | tf_op jit(solution)/shard_map/ppermute | solution.py:316
  14.0 0.4 collective-permute-start.1
  14.4 3.5 %load.2 = (bf16[512,8192]{1,0:T(8,128)(2,1)S(1)}, f32[8,128]{1,0:T(8,128)S(1)}) custom-call(s32[1]{0:T(128)} %bitcast.me_ref, bf16[1664,8192]{1,0:T(8,128)(2,1)} %weight_ref.7, f32[128,384]{1,0:T(8,128)S(1)} %fold.16.refs_0_), custom_call_target="tpu_custom_call" | custom-call | flops 10000000000 | bytes 100000000 | tf_op jit(solution)/shard_map/load/pallas_call | solution.py:83
  17.9 3.0 %load.3 = (bf16[384,8192]{1,0:T(8,128)(2,1)S(1)}, f32[8,128]{1,0:T(8,128)S(1)}) custom-call(s32[1]{0:T(128)} %bitcast.me_ref, bf16[1664,8192]{1,0:T(8,128)(2,1)} %weight_ref.7, f32[8,128]{1,0:T(8,128)S(1)} %get-tuple-element.41.refs_0_), custom_call_target="tpu_custom_call" | custom-call | flops 10000000000 | bytes 100000000 | tf_op jit(solution)/shard_map/load/pallas_call | solution.py:83
  20.8 0.0 collective-permute-done.4.refs_1_
  20.8 2.9 %fold.17 = (bf16[384,8192]{1,0:T(8,128)(2,1)S(1)}, f32[128,384]{1,0:T(8,128)S(1)}) custom-call(s32[1]{0:T(128)} %bitcast.me_ref, bf16[1664,8192]{1,0:T(8,128)(2,1)} %weight_ref.7, f32[128,384]{1,0:T(8,128)S(1)} %mix.6.refs_0_, f32[128,384]{1,0:T(8,128)S(1)} %collective-permute-done.4.refs_1_, f32[8,128]{1,0:T(8,128)S(1)} %get-tuple-element.42.refs_2_), custom_call_target="tpu_custom_call" | custom-call | flops 10000000000 | bytes 100000000 | tf_op jit(solution)/shard_map/fold/pallas_call | solution.py:83
  23.7 0.1 collective-permute-start.6
  23.8 0.3 collective-permute-done.3.refs_1_
  24.1 0.3 collective-permute-start.9
  24.4 0.0 collective-permute-done.2.refs_1_
  24.4 1.7 %collective-permute-start.5 = (f32[128,384]{1,0:T(8,128)S(1)}, f32[128,384]{1,0:T(8,128)S(1)}, u32[]{:S(2)}, u32[]{:S(2)}) collective-permute-start(f32[128,384]{1,0:T(8,128)S(1)} %fold.19.refs_2_.refs_0_), channel_id=1, source_target_pairs={{0,2},{1,3},{2,0},{3,1},{4,6},{5,7},{6,4},{7,5},{8,10},{9,11},{10,... | collective-permute-start | bytes 589832 | tf_op jit(solution)/shard_map/ppermute | solution.py:316
  26.2 3.1 %collective-permute-start.8 = (f32[128,384]{1,0:T(8,128)S(1)}, f32[128,384]{1,0:T(8,128)S(1)}, u32[]{:S(2)}, u32[]{:S(2)}) collective-permute-start(f32[128,384]{1,0:T(8,128)S(1)} %fold.20.refs_2_.refs_0_), channel_id=1, source_target_pairs={{0,8},{1,9},{2,10},{3,11},{4,12},{5,13},{6,14},{7,15},{8,0},{9,1},... | collective-permute-start | bytes 589832 | tf_op jit(solution)/shard_map/ppermute | solution.py:316
  29.2 2.2 %collective-permute-done.5.refs_1_ = f32[128,384]{1,0:T(8,128)S(1)} collective-permute-done((f32[128,384]{1,0:T(8,128)S(1)}, f32[128,384]{1,0:T(8,128)S(1)}, u32[]{:S(2)}, u32[]{:S(2)}) %collective-permute-start.5) | collective-permute-done | bytes 196640 | tf_op jit(solution)/shard_map/ppermute | solution.py:316
  31.5 0.1 collective-permute-start.11
  31.6 0.0 collective-permute-done.1.refs_1_
  31.6 1.6 %collective-permute-start.7 = (f32[128,384]{1,0:T(8,128)S(1)}, f32[128,384]{1,0:T(8,128)S(1)}, u32[]{:S(2)}, u32[]{:S(2)}) collective-permute-start(f32[128,384]{1,0:T(8,128)S(1)} %fold.22.refs_2_.refs_0_), channel_id=1, source_target_pairs={{0,4},{1,5},{2,6},{3,7},{4,0},{5,1},{6,2},{7,3},{8,12},{9,13},{10,... | collective-permute-start | bytes 589832 | tf_op jit(solution)/shard_map/ppermute | solution.py:316
  33.3 4.3 %collective-permute-done.9.refs_1_ = f32[128,512]{1,0:T(8,128)S(1)} collective-permute-done((f32[128,512]{1,0:T(8,128)S(1)}, f32[128,512]{1,0:T(8,128)S(1)}, u32[]{:S(2)}, u32[]{:S(2)}) %collective-permute-start.9) | collective-permute-done | bytes 262176 | tf_op jit(solution)/shard_map/ppermute | solution.py:316
  37.6 2.0 %collective-permute-start.10 = (f32[128,512]{1,0:T(8,128)S(1)}, f32[128,512]{1,0:T(8,128)S(1)}, u32[]{:S(2)}, u32[]{:S(2)}) collective-permute-start(f32[128,512]{1,0:T(8,128)S(1)} %fold.23.refs_2_.refs_0_), channel_id=1, source_target_pairs={{0,2},{1,3},{2,0},{3,1},{4,6},{5,7},{6,4},{7,5},{8,10},{9,11},{10,... | collective-permute-start | bytes 786440 | tf_op jit(solution)/shard_map/ppermute | solution.py:316
  39.6 1.0 %collective-permute-start.14 = (f32[128,384]{1,0:T(8,128)S(1)}, f32[128,384]{1,0:T(8,128)S(1)}, u32[]{:S(2)}, u32[]{:S(2)}) collective-permute-start(f32[128,384]{1,0:T(8,128)S(1)} %fold.24.refs_2_.refs_0_), channel_id=1, source_target_pairs={{0,8},{1,9},{2,10},{3,11},{4,12},{5,13},{6,14},{7,15},{8,0},{9,1},... | collective-permute-start | bytes 589832 | tf_op jit(solution)/shard_map/ppermute | solution.py:316
  40.6 4.8 %collective-permute-done.10.refs_1_ = f32[128,512]{1,0:T(8,128)S(1)} collective-permute-done((f32[128,512]{1,0:T(8,128)S(1)}, f32[128,512]{1,0:T(8,128)S(1)}, u32[]{:S(2)}, u32[]{:S(2)}) %collective-permute-start.10) | collective-permute-done | bytes 262176 | tf_op jit(solution)/shard_map/ppermute | solution.py:316
  45.4 0.1 collective-permute-start.13
  45.5 0.0 collective-permute-done.8.refs_1_
  45.6 0.1 collective-permute-start.15
  45.7 1.3 %collective-permute-start.12 = (f32[128,384]{1,0:T(8,128)S(1)}, f32[128,384]{1,0:T(8,128)S(1)}, u32[]{:S(2)}, u32[]{:S(2)}) collective-permute-start(f32[128,384]{1,0:T(8,128)S(1)} %fold.27.refs_2_.refs_0_), channel_id=1, source_target_pairs={{0,2},{1,3},{2,0},{3,1},{4,6},{5,7},{6,4},{7,5},{8,10},{9,11},{10,... | collective-permute-start | bytes 589832 | tf_op jit(solution)/shard_map/ppermute | solution.py:316
  47.0 0.1 collective-permute-done.13.refs_1_
  47.1 2.9 %step.2 = (bf16[384,8192]{1,0:T(8,128)(2,1)S(1)}, f32[16,128,512]{2,1,0:T(8,128)S(1)}) custom-call(s32[1]{0:T(128)} %bitcast.me_ref, bf16[1664,8192]{1,0:T(8,128)(2,1)} %weight_ref.7, bf16[128,512]{1,0:T(8,128)(2,1)S(1)} %fold.28.refs_0_.refs_2_, bf16[512,8192]{1,0:T(8,128)(2,1)S(1)} %get-tuple-element.44.refs_1_, bf16[128,512]{1,0:T(8,128)(2,1)S(1)} %fold.28.refs_0_.refs_2_), custom_call_target="tpu_custom_call" | custom-call | flops 10000000000 | bytes 100000000 | tf_op jit(solution)/shard_map/step/pallas_call | solution.py:83
  50.0 3.1 %collective-permute-done.12.refs_1_ = f32[128,384]{1,0:T(8,128)S(1)} collective-permute-done((f32[128,384]{1,0:T(8,128)S(1)}, f32[128,384]{1,0:T(8,128)S(1)}, u32[]{:S(2)}, u32[]{:S(2)}) %collective-permute-start.12) | collective-permute-done | bytes 196640 | tf_op jit(solution)/shard_map/ppermute | solution.py:316
  53.1 1.3 %step.3.refs_2_.total_ref = f32[16,128,512]{2,1,0:T(8,128)S(1)} custom-call(bf16[128,384]{1,0:T(8,128)(2,1)S(1)} %fold.29.refs_0_.refs_3_, bf16[384,8192]{1,0:T(8,128)(2,1)S(1)} %get-tuple-element.46.refs_1_, f32[16,128,512]{2,1,0:T(8,128)S(1)} %get-tuple-element.45.refs_2_, bf16[128,384]{1,0:T(8,128)(2,1)S(1)} %fold.29.refs_0_.refs_3_), custom_call_target="tpu_custom_call" | custom-call | flops 10000000000 | bytes 100000000 | tf_op jit(solution)/shard_map/step/pallas_call | solution.py:83
  54.4 0.0 collective-permute-done.15.refs_1_
  54.4 1.3 %product.2 = (f32[8,128,256]{2,1,0:T(8,128)S(1)}, f32[8,128,256]{2,1,0:T(8,128)S(1)}) custom-call(s32[1]{0:T(128)} %bitcast.me_ref, f32[16,128,512]{2,1,0:T(8,128)S(1)} %step.3.refs_2_.total_ref, bf16[128,384]{1,0:T(8,128)(2,1)S(1)} %fold.30.refs_2_.refs_0_, bf16[128,384]{1,0:T(8,128)(2,1)S(1)} %fold.31.refs_1_.refs_4_, ...), custom_call_target="tpu_custom_call" | custom-call | flops 10000000000 | bytes 100000000 | tf_op jit(solution)/shard_map/product/pallas_call | solution.py:83
  55.8 0.1 collective-permute-start.17
  55.9 0.5 collective-permute-start.16
  56.3 1.3 %product.3 = (f32[8,128,256]{2,1,0:T(8,128)S(1)}, f32[8,128,256]{2,1,0:T(8,128)S(1)}) custom-call(s32[1]{0:T(128)} %bitcast.me_ref, f32[16,128,512]{2,1,0:T(8,128)S(1)} %step.3.refs_2_.total_ref, bf16[128,384]{1,0:T(8,128)(2,1)S(1)} %fold.30.refs_2_.refs_0_, bf16[128,384]{1,0:T(8,128)(2,1)S(1)} %fold.31.refs_1_.refs_4_, ...), custom_call_target="tpu_custom_call" | custom-call | flops 10000000000 | bytes 100000000 | tf_op jit(solution)/shard_map/product/pallas_call | solution.py:83
  57.7 0.8 collective-permute-done.17.got_ref
  58.5 0.1 halve.10
  58.6 1.8 %collective-permute-start.21 = (f32[4,64,256]{2,1,0:T(8,128)S(1)}, f32[4,64,256]{2,1,0:T(8,128)S(1)}, u32[]{:S(2)}, u32[]{:S(2)}) collective-permute-start(f32[4,64,256]{2,1,0:T(8,128)S(1)} %get-tuple-element.60), channel_id=1, source_target_pairs={{0,4},{1,5},{2,6},{3,7},{4,0},{5,1},{6,2},{7,3},{8,12},{9,13},{10,... | collective-permute-start | bytes 786440 | tf_op jit(solution)/shard_map/ppermute | solution.py:316
  60.4 1.2 %collective-permute-start.20 = (f32[4,64,256]{2,1,0:T(8,128)S(1)}, f32[4,64,256]{2,1,0:T(8,128)S(1)}, u32[]{:S(2)}, u32[]{:S(2)}) collective-permute-start(f32[4,64,256]{2,1,0:T(8,128)S(1)} %get-tuple-element.53.refs_0_), channel_id=1, source_target_pairs={{0,2},{1,3},{2,0},{3,1},{4,6},{5,7},{6,4},{7,5},{8,10},{9,11},{10,... | collective-permute-start | bytes 786440 | tf_op jit(solution)/shard_map/ppermute | solution.py:316
  61.6 0.0 collective-permute-done.16.got_ref
  61.6 0.1 halve.11
  61.7 0.4 collective-permute-start.19
  62.1 1.0 %collective-permute-start.18 = (f32[4,64,256]{2,1,0:T(8,128)S(1)}, f32[4,64,256]{2,1,0:T(8,128)S(1)}, u32[]{:S(2)}, u32[]{:S(2)}) collective-permute-start(f32[4,64,256]{2,1,0:T(8,128)S(1)} %get-tuple-element.55), channel_id=1, source_target_pairs={{0,2},{1,3},{2,0},{3,1},{4,6},{5,7},{6,4},{7,5},{8,10},{9,11},{10,... | collective-permute-start | bytes 786440 | tf_op jit(solution)/shard_map/ppermute | solution.py:316
  63.1 4.7 %collective-permute-done.21.got_ref = f32[4,64,256]{2,1,0:T(8,128)S(1)} collective-permute-done((f32[4,64,256]{2,1,0:T(8,128)S(1)}, f32[4,64,256]{2,1,0:T(8,128)S(1)}, u32[]{:S(2)}, u32[]{:S(2)}) %collective-permute-start.21) | collective-permute-done | bytes 262176 | tf_op jit(solution)/shard_map/ppermute | solution.py:316
  67.9 1.3 %collective-permute-start.25 = (f32[2,64,256]{2,1,0:T(8,128)S(1)}, f32[2,64,256]{2,1,0:T(8,128)S(1)}, u32[]{:S(2)}, u32[]{:S(2)}) collective-permute-start(f32[2,64,256]{2,1,0:T(8,128)S(1)} %get-tuple-element.61.refs_0_), channel_id=1, source_target_pairs={{0,2},{1,3},{2,0},{3,1},{4,6},{5,7},{6,4},{7,5},{8,10},{9,11},{10,... | collective-permute-start | bytes 393224 | tf_op jit(solution)/shard_map/ppermute | solution.py:316
  69.1 0.4 collective-permute-done.20.got_ref
  69.6 3.9 %collective-permute-start.24 = (f32[2,64,256]{2,1,0:T(8,128)S(1)}, f32[2,64,256]{2,1,0:T(8,128)S(1)}, u32[]{:S(2)}, u32[]{:S(2)}) collective-permute-start(f32[2,64,256]{2,1,0:T(8,128)S(1)} %get-tuple-element.62.refs_0_), channel_id=1, source_target_pairs={{0,8},{1,9},{2,10},{3,11},{4,12},{5,13},{6,14},{7,15},{8,0},{9,1},... | collective-permute-start | bytes 393224 | tf_op jit(solution)/shard_map/ppermute | solution.py:316
  73.6 1.8 %collective-permute-start.23 = (f32[2,64,256]{2,1,0:T(8,128)S(1)}, f32[2,64,256]{2,1,0:T(8,128)S(1)}, u32[]{:S(2)}, u32[]{:S(2)}) collective-permute-start(f32[2,64,256]{2,1,0:T(8,128)S(1)} %get-tuple-element.63.refs_0_), channel_id=1, source_target_pairs={{0,2},{1,3},{2,0},{3,1},{4,6},{5,7},{6,4},{7,5},{8,10},{9,11},{10,... | collective-permute-start | bytes 393224 | tf_op jit(solution)/shard_map/ppermute | solution.py:316
  75.4 1.0 %collective-permute-start.22 = (f32[2,64,256]{2,1,0:T(8,128)S(1)}, f32[2,64,256]{2,1,0:T(8,128)S(1)}, u32[]{:S(2)}, u32[]{:S(2)}) collective-permute-start(f32[2,64,256]{2,1,0:T(8,128)S(1)} %get-tuple-element.65.refs_0_), channel_id=1, source_target_pairs={{0,4},{1,5},{2,6},{3,7},{4,0},{5,1},{6,2},{7,3},{8,12},{9,13},{10,... | collective-permute-start | bytes 393224 | tf_op jit(solution)/shard_map/ppermute | solution.py:316
  76.4 1.6 %collective-permute-done.25.got_ref = f32[2,64,256]{2,1,0:T(8,128)S(1)} collective-permute-done((f32[2,64,256]{2,1,0:T(8,128)S(1)}, f32[2,64,256]{2,1,0:T(8,128)S(1)}, u32[]{:S(2)}, u32[]{:S(2)}) %collective-permute-start.25) | collective-permute-done | bytes 131104 | tf_op jit(solution)/shard_map/ppermute | solution.py:316
  78.0 2.4 %collective-permute-start.27 = (f32[1,64,256]{2,1,0:T(8,128)S(1)}, f32[1,64,256]{2,1,0:T(8,128)S(1)}, u32[]{:S(2)}, u32[]{:S(2)}) collective-permute-start(f32[1,64,256]{2,1,0:T(8,128)S(1)} %get-tuple-element.69.refs_0_), channel_id=1, source_target_pairs={{0,8},{1,9},{2,10},{3,11},{4,12},{5,13},{6,14},{7,15},{8,0},{9,1},... | collective-permute-start | bytes 196616 | tf_op jit(solution)/shard_map/ppermute | solution.py:316
  80.5 1.9 %collective-permute-start.28 = (f32[1,64,256]{2,1,0:T(8,128)S(1)}, f32[1,64,256]{2,1,0:T(8,128)S(1)}, u32[]{:S(2)}, u32[]{:S(2)}) collective-permute-start(f32[1,64,256]{2,1,0:T(8,128)S(1)} %get-tuple-element.70.refs_0_), channel_id=1, source_target_pairs={{0,4},{1,5},{2,6},{3,7},{4,0},{5,1},{6,2},{7,3},{8,12},{9,13},{10,... | collective-permute-start | bytes 196616 | tf_op jit(solution)/shard_map/ppermute | solution.py:316
  82.4 0.2 collective-permute-start.29
  82.7 2.8 %collective-permute-start.26 = (f32[1,64,256]{2,1,0:T(8,128)S(1)}, f32[1,64,256]{2,1,0:T(8,128)S(1)}, u32[]{:S(2)}, u32[]{:S(2)}) collective-permute-start(f32[1,64,256]{2,1,0:T(8,128)S(1)} %get-tuple-element.73.refs_0_), channel_id=1, source_target_pairs={{0,8},{1,9},{2,10},{3,11},{4,12},{5,13},{6,14},{7,15},{8,0},{9,1},... | collective-permute-start | bytes 196616 | tf_op jit(solution)/shard_map/ppermute | solution.py:316
  85.5 3.5 %collective-permute-done.29.got_ref = f32[1,64,256]{2,1,0:T(8,128)S(1)} collective-permute-done((f32[1,64,256]{2,1,0:T(8,128)S(1)}, f32[1,64,256]{2,1,0:T(8,128)S(1)}, u32[]{:S(2)}, u32[]{:S(2)}) %collective-permute-start.29) | collective-permute-done | bytes 65568 | tf_op jit(solution)/shard_map/ppermute | solution.py:316
  89.0 0.7 collective-permute-done.26.got_ref
  89.7 0.7 finish.7
  (40 shorter events, 0.7 us)
Async XLA Ops:
  0.0 1.0 %copy-start = (bf16[128,1664]{1,0:T(8,128)(2,1)S(1)}, bf16[128,1664]{1,0:T(8,128)(2,1)}, u32[]{:S(2)}) copy-start(bf16[128,1664]{1,0:T(8,128)(2,1)} %activations.7) | copy-start | bytes 1277956
  1.0 0.7 copy-start.1
  2.9 21.1 %collective-permute-start.3 = (f32[128,512]{1,0:T(8,128)S(1)}, f32[128,512]{1,0:T(8,128)S(1)}, u32[]{:S(2)}, u32[]{:S(2)}) collective-permute-start(f32[128,512]{1,0:T(8,128)S(1)} %mix.4.refs_0_), channel_id=1, source_target_pairs={{0,8},{1,9},{2,10},{3,11},{4,12},{5,13},{6,14},{7,15},{8,0},{9,1},... | collective-permute-start | bytes 786440 | tf_op jit(solution)/shard_map/ppermute | solution.py:316
  8.2 5.7 %collective-permute-start = (f32[128,384]{1,0:T(8,128)S(1)}, f32[128,384]{1,0:T(8,128)S(1)}, u32[]{:S(2)}, u32[]{:S(2)}) collective-permute-start(f32[128,384]{1,0:T(8,128)S(1)} %mix.5.refs_0_), channel_id=1, source_target_pairs={{0,1},{1,0},{2,3},{3,2},{4,5},{5,4},{6,7},{7,6},{8,9},{9,8},{10,11... | collective-permute-start | bytes 589832 | tf_op jit(solution)/shard_map/ppermute | solution.py:316
  9.5 11.3 %collective-permute-start.4 = (f32[128,384]{1,0:T(8,128)S(1)}, f32[128,384]{1,0:T(8,128)S(1)}, u32[]{:S(2)}, u32[]{:S(2)}) collective-permute-start(f32[128,384]{1,0:T(8,128)S(1)} %mix.6.refs_0_), channel_id=1, source_target_pairs={{0,2},{1,3},{2,0},{3,1},{4,6},{5,7},{6,4},{7,5},{8,10},{9,11},{10,... | collective-permute-start | bytes 589832 | tf_op jit(solution)/shard_map/ppermute | solution.py:316
  12.3 12.1 %collective-permute-start.2 = (f32[128,384]{1,0:T(8,128)S(1)}, f32[128,384]{1,0:T(8,128)S(1)}, u32[]{:S(2)}, u32[]{:S(2)}) collective-permute-start(f32[128,384]{1,0:T(8,128)S(1)} %mix.7.refs_2_.refs_0_), channel_id=1, source_target_pairs={{0,4},{1,5},{2,6},{3,7},{4,0},{5,1},{6,2},{7,3},{8,12},{9,13},{10,... | collective-permute-start | bytes 589832 | tf_op jit(solution)/shard_map/ppermute | solution.py:316
  14.0 17.6 %collective-permute-start.1 = (f32[128,384]{1,0:T(8,128)S(1)}, f32[128,384]{1,0:T(8,128)S(1)}, u32[]{:S(2)}, u32[]{:S(2)}) collective-permute-start(f32[128,384]{1,0:T(8,128)S(1)} %fold.16.refs_0_), channel_id=1, source_target_pairs={{0,8},{1,9},{2,10},{3,11},{4,12},{5,13},{6,14},{7,15},{8,0},{9,1},... | collective-permute-start | bytes 589832 | tf_op jit(solution)/shard_map/ppermute | solution.py:316
  23.7 2.4 %collective-permute-start.6 = (f32[128,384]{1,0:T(8,128)S(1)}, f32[128,384]{1,0:T(8,128)S(1)}, u32[]{:S(2)}, u32[]{:S(2)}) collective-permute-start(f32[128,384]{1,0:T(8,128)S(1)} %get-tuple-element.43.refs_2_.refs_0_), channel_id=1, source_target_pairs={{0,1},{1,0},{2,3},{3,2},{4,5},{5,4},{6,7},{7,6},{8,9},{9,8},{10,11... | collective-permute-start | bytes 589832 | tf_op jit(solution)/shard_map/ppermute | solution.py:316
  24.1 13.5 %collective-permute-start.9 = (f32[128,512]{1,0:T(8,128)S(1)}, f32[128,512]{1,0:T(8,128)S(1)}, u32[]{:S(2)}, u32[]{:S(2)}) collective-permute-start(f32[128,512]{1,0:T(8,128)S(1)} %fold.18.refs_2_.refs_0_), channel_id=1, source_target_pairs={{0,4},{1,5},{2,6},{3,7},{4,0},{5,1},{6,2},{7,3},{8,12},{9,13},{10,... | collective-permute-start | bytes 786440 | tf_op jit(solution)/shard_map/ppermute | solution.py:316
  24.4 7.1 %collective-permute-start.5 = (f32[128,384]{1,0:T(8,128)S(1)}, f32[128,384]{1,0:T(8,128)S(1)}, u32[]{:S(2)}, u32[]{:S(2)}) collective-permute-start(f32[128,384]{1,0:T(8,128)S(1)} %fold.19.refs_2_.refs_0_), channel_id=1, source_target_pairs={{0,2},{1,3},{2,0},{3,1},{4,6},{5,7},{6,4},{7,5},{8,10},{9,11},{10,... | collective-permute-start | bytes 589832 | tf_op jit(solution)/shard_map/ppermute | solution.py:316
  26.2 19.3 %collective-permute-start.8 = (f32[128,384]{1,0:T(8,128)S(1)}, f32[128,384]{1,0:T(8,128)S(1)}, u32[]{:S(2)}, u32[]{:S(2)}) collective-permute-start(f32[128,384]{1,0:T(8,128)S(1)} %fold.20.refs_2_.refs_0_), channel_id=1, source_target_pairs={{0,8},{1,9},{2,10},{3,11},{4,12},{5,13},{6,14},{7,15},{8,0},{9,1},... | collective-permute-start | bytes 589832 | tf_op jit(solution)/shard_map/ppermute | solution.py:316
  31.5 8.1 %collective-permute-start.11 = (f32[128,384]{1,0:T(8,128)S(1)}, f32[128,384]{1,0:T(8,128)S(1)}, u32[]{:S(2)}, u32[]{:S(2)}) collective-permute-start(f32[128,384]{1,0:T(8,128)S(1)} %fold.21.refs_2_.refs_0_), channel_id=1, source_target_pairs={{0,1},{1,0},{2,3},{3,2},{4,5},{5,4},{6,7},{7,6},{8,9},{9,8},{10,11... | collective-permute-start | bytes 589832 | tf_op jit(solution)/shard_map/ppermute | solution.py:316
  31.6 14.0 %collective-permute-start.7 = (f32[128,384]{1,0:T(8,128)S(1)}, f32[128,384]{1,0:T(8,128)S(1)}, u32[]{:S(2)}, u32[]{:S(2)}) collective-permute-start(f32[128,384]{1,0:T(8,128)S(1)} %fold.22.refs_2_.refs_0_), channel_id=1, source_target_pairs={{0,4},{1,5},{2,6},{3,7},{4,0},{5,1},{6,2},{7,3},{8,12},{9,13},{10,... | collective-permute-start | bytes 589832 | tf_op jit(solution)/shard_map/ppermute | solution.py:316
  37.6 7.8 %collective-permute-start.10 = (f32[128,512]{1,0:T(8,128)S(1)}, f32[128,512]{1,0:T(8,128)S(1)}, u32[]{:S(2)}, u32[]{:S(2)}) collective-permute-start(f32[128,512]{1,0:T(8,128)S(1)} %fold.23.refs_2_.refs_0_), channel_id=1, source_target_pairs={{0,2},{1,3},{2,0},{3,1},{4,6},{5,7},{6,4},{7,5},{8,10},{9,11},{10,... | collective-permute-start | bytes 786440 | tf_op jit(solution)/shard_map/ppermute | solution.py:316
  39.6 14.7 %collective-permute-start.14 = (f32[128,384]{1,0:T(8,128)S(1)}, f32[128,384]{1,0:T(8,128)S(1)}, u32[]{:S(2)}, u32[]{:S(2)}) collective-permute-start(f32[128,384]{1,0:T(8,128)S(1)} %fold.24.refs_2_.refs_0_), channel_id=1, source_target_pairs={{0,8},{1,9},{2,10},{3,11},{4,12},{5,13},{6,14},{7,15},{8,0},{9,1},... | collective-permute-start | bytes 589832 | tf_op jit(solution)/shard_map/ppermute | solution.py:316
  45.4 1.6 %collective-permute-start.13 = (f32[128,512]{1,0:T(8,128)S(1)}, f32[128,512]{1,0:T(8,128)S(1)}, u32[]{:S(2)}, u32[]{:S(2)}) collective-permute-start(f32[128,512]{1,0:T(8,128)S(1)} %fold.25.refs_2_.refs_0_), channel_id=1, source_target_pairs={{0,1},{1,0},{2,3},{3,2},{4,5},{5,4},{6,7},{7,6},{8,9},{9,8},{10,11... | collective-permute-start | bytes 786440 | tf_op jit(solution)/shard_map/ppermute | solution.py:316
  45.6 8.8 %collective-permute-start.15 = (f32[128,384]{1,0:T(8,128)S(1)}, f32[128,384]{1,0:T(8,128)S(1)}, u32[]{:S(2)}, u32[]{:S(2)}) collective-permute-start(f32[128,384]{1,0:T(8,128)S(1)} %fold.26.refs_2_.refs_0_), channel_id=1, source_target_pairs={{0,4},{1,5},{2,6},{3,7},{4,0},{5,1},{6,2},{7,3},{8,12},{9,13},{10,... | collective-permute-start | bytes 589832 | tf_op jit(solution)/shard_map/ppermute | solution.py:316
  45.7 7.4 %collective-permute-start.12 = (f32[128,384]{1,0:T(8,128)S(1)}, f32[128,384]{1,0:T(8,128)S(1)}, u32[]{:S(2)}, u32[]{:S(2)}) collective-permute-start(f32[128,384]{1,0:T(8,128)S(1)} %fold.27.refs_2_.refs_0_), channel_id=1, source_target_pairs={{0,2},{1,3},{2,0},{3,1},{4,6},{5,7},{6,4},{7,5},{8,10},{9,11},{10,... | collective-permute-start | bytes 589832 | tf_op jit(solution)/shard_map/ppermute | solution.py:316
  55.8 2.7 %collective-permute-start.17 = (f32[8,128,256]{2,1,0:T(8,128)S(1)}, f32[8,128,256]{2,1,0:T(8,128)S(1)}, u32[]{:S(2)}, u32[]{:S(2)}) collective-permute-start(f32[8,128,256]{2,1,0:T(8,128)S(1)} %get-tuple-element.52), channel_id=1, source_target_pairs={{0,1},{1,0},{2,3},{3,2},{4,5},{5,4},{6,7},{7,6},{8,9},{9,8},{10,11... | collective-permute-start | bytes 3145736 | tf_op jit(solution)/shard_map/ppermute | solution.py:316
  55.9 5.8 %collective-permute-start.16 = (f32[8,128,256]{2,1,0:T(8,128)S(1)}, f32[8,128,256]{2,1,0:T(8,128)S(1)}, u32[]{:S(2)}, u32[]{:S(2)}) collective-permute-start(f32[8,128,256]{2,1,0:T(8,128)S(1)} %get-tuple-element.49.refs_4_), channel_id=1, source_target_pairs={{0,1},{1,0},{2,3},{3,2},{4,5},{5,4},{6,7},{7,6},{8,9},{9,8},{10,11... | collective-permute-start | bytes 3145736 | tf_op jit(solution)/shard_map/ppermute | solution.py:316
  58.6 9.2 %collective-permute-start.21 = (f32[4,64,256]{2,1,0:T(8,128)S(1)}, f32[4,64,256]{2,1,0:T(8,128)S(1)}, u32[]{:S(2)}, u32[]{:S(2)}) collective-permute-start(f32[4,64,256]{2,1,0:T(8,128)S(1)} %get-tuple-element.60), channel_id=1, source_target_pairs={{0,4},{1,5},{2,6},{3,7},{4,0},{5,1},{6,2},{7,3},{8,12},{9,13},{10,... | collective-permute-start | bytes 786440 | tf_op jit(solution)/shard_map/ppermute | solution.py:316
  60.4 9.2 %collective-permute-start.20 = (f32[4,64,256]{2,1,0:T(8,128)S(1)}, f32[4,64,256]{2,1,0:T(8,128)S(1)}, u32[]{:S(2)}, u32[]{:S(2)}) collective-permute-start(f32[4,64,256]{2,1,0:T(8,128)S(1)} %get-tuple-element.53.refs_0_), channel_id=1, source_target_pairs={{0,2},{1,3},{2,0},{3,1},{4,6},{5,7},{6,4},{7,5},{8,10},{9,11},{10,... | collective-permute-start | bytes 786440 | tf_op jit(solution)/shard_map/ppermute | solution.py:316
  61.7 11.8 %collective-permute-start.19 = (f32[4,64,256]{2,1,0:T(8,128)S(1)}, f32[4,64,256]{2,1,0:T(8,128)S(1)}, u32[]{:S(2)}, u32[]{:S(2)}) collective-permute-start(f32[4,64,256]{2,1,0:T(8,128)S(1)} %get-tuple-element.57.refs_0_), channel_id=1, source_target_pairs={{0,4},{1,5},{2,6},{3,7},{4,0},{5,1},{6,2},{7,3},{8,12},{9,13},{10,... | collective-permute-start | bytes 786440 | tf_op jit(solution)/shard_map/ppermute | solution.py:316
  62.1 13.3 %collective-permute-start.18 = (f32[4,64,256]{2,1,0:T(8,128)S(1)}, f32[4,64,256]{2,1,0:T(8,128)S(1)}, u32[]{:S(2)}, u32[]{:S(2)}) collective-permute-start(f32[4,64,256]{2,1,0:T(8,128)S(1)} %get-tuple-element.55), channel_id=1, source_target_pairs={{0,2},{1,3},{2,0},{3,1},{4,6},{5,7},{6,4},{7,5},{8,10},{9,11},{10,... | collective-permute-start | bytes 786440 | tf_op jit(solution)/shard_map/ppermute | solution.py:316
  67.9 10.2 %collective-permute-start.25 = (f32[2,64,256]{2,1,0:T(8,128)S(1)}, f32[2,64,256]{2,1,0:T(8,128)S(1)}, u32[]{:S(2)}, u32[]{:S(2)}) collective-permute-start(f32[2,64,256]{2,1,0:T(8,128)S(1)} %get-tuple-element.61.refs_0_), channel_id=1, source_target_pairs={{0,2},{1,3},{2,0},{3,1},{4,6},{5,7},{6,4},{7,5},{8,10},{9,11},{10,... | collective-permute-start | bytes 393224 | tf_op jit(solution)/shard_map/ppermute | solution.py:316
  69.6 10.9 %collective-permute-start.24 = (f32[2,64,256]{2,1,0:T(8,128)S(1)}, f32[2,64,256]{2,1,0:T(8,128)S(1)}, u32[]{:S(2)}, u32[]{:S(2)}) collective-permute-start(f32[2,64,256]{2,1,0:T(8,128)S(1)} %get-tuple-element.62.refs_0_), channel_id=1, source_target_pairs={{0,8},{1,9},{2,10},{3,11},{4,12},{5,13},{6,14},{7,15},{8,0},{9,1},... | collective-permute-start | bytes 393224 | tf_op jit(solution)/shard_map/ppermute | solution.py:316
  73.6 8.8 %collective-permute-start.23 = (f32[2,64,256]{2,1,0:T(8,128)S(1)}, f32[2,64,256]{2,1,0:T(8,128)S(1)}, u32[]{:S(2)}, u32[]{:S(2)}) collective-permute-start(f32[2,64,256]{2,1,0:T(8,128)S(1)} %get-tuple-element.63.refs_0_), channel_id=1, source_target_pairs={{0,2},{1,3},{2,0},{3,1},{4,6},{5,7},{6,4},{7,5},{8,10},{9,11},{10,... | collective-permute-start | bytes 393224 | tf_op jit(solution)/shard_map/ppermute | solution.py:316
  75.4 7.2 %collective-permute-start.22 = (f32[2,64,256]{2,1,0:T(8,128)S(1)}, f32[2,64,256]{2,1,0:T(8,128)S(1)}, u32[]{:S(2)}, u32[]{:S(2)}) collective-permute-start(f32[2,64,256]{2,1,0:T(8,128)S(1)} %get-tuple-element.65.refs_0_), channel_id=1, source_target_pairs={{0,4},{1,5},{2,6},{3,7},{4,0},{5,1},{6,2},{7,3},{8,12},{9,13},{10,... | collective-permute-start | bytes 393224 | tf_op jit(solution)/shard_map/ppermute | solution.py:316
  78.0 7.4 %collective-permute-start.27 = (f32[1,64,256]{2,1,0:T(8,128)S(1)}, f32[1,64,256]{2,1,0:T(8,128)S(1)}, u32[]{:S(2)}, u32[]{:S(2)}) collective-permute-start(f32[1,64,256]{2,1,0:T(8,128)S(1)} %get-tuple-element.69.refs_0_), channel_id=1, source_target_pairs={{0,8},{1,9},{2,10},{3,11},{4,12},{5,13},{6,14},{7,15},{8,0},{9,1},... | collective-permute-start | bytes 196616 | tf_op jit(solution)/shard_map/ppermute | solution.py:316
  80.5 5.0 %collective-permute-start.28 = (f32[1,64,256]{2,1,0:T(8,128)S(1)}, f32[1,64,256]{2,1,0:T(8,128)S(1)}, u32[]{:S(2)}, u32[]{:S(2)}) collective-permute-start(f32[1,64,256]{2,1,0:T(8,128)S(1)} %get-tuple-element.70.refs_0_), channel_id=1, source_target_pairs={{0,4},{1,5},{2,6},{3,7},{4,0},{5,1},{6,2},{7,3},{8,12},{9,13},{10,... | collective-permute-start | bytes 196616 | tf_op jit(solution)/shard_map/ppermute | solution.py:316
  82.4 6.6 %collective-permute-start.29 = (f32[1,64,256]{2,1,0:T(8,128)S(1)}, f32[1,64,256]{2,1,0:T(8,128)S(1)}, u32[]{:S(2)}, u32[]{:S(2)}) collective-permute-start(f32[1,64,256]{2,1,0:T(8,128)S(1)} %get-tuple-element.71.refs_0_), channel_id=1, source_target_pairs={{0,8},{1,9},{2,10},{3,11},{4,12},{5,13},{6,14},{7,15},{8,0},{9,1},... | collective-permute-start | bytes 196616 | tf_op jit(solution)/shard_map/ppermute | solution.py:316
  82.7 7.1 %collective-permute-start.26 = (f32[1,64,256]{2,1,0:T(8,128)S(1)}, f32[1,64,256]{2,1,0:T(8,128)S(1)}, u32[]{:S(2)}, u32[]{:S(2)}) collective-permute-start(f32[1,64,256]{2,1,0:T(8,128)S(1)} %get-tuple-element.73.refs_0_), channel_id=1, source_target_pairs={{0,8},{1,9},{2,10},{3,11},{4,12},{5,13},{6,14},{7,15},{8,0},{9,1},... | collective-permute-start | bytes 196616 | tf_op jit(solution)/shard_map/ppermute | solution.py:316

commit v14 on v13

--- a/solution.py
+++ b/solution.py
@@ -13,10 +13,10 @@
 BF16 = jnp.bfloat16
 
 
-TILES = (4, 3, 3, 3)
+TILES = (3, 3, 3, 4)
 DIRECT = 2
 PIECES = 4
-PERM = (0, 3, 2, 1)
+PERM = (0, 1, 3, 2)
 
 
 def quotient(index, divisor, limit):

time: 90.6 us -> 90.2 us (level)
  starting transfers between devices: 39.4 us -> 37.2 us
  Pallas kernels: 22.3 us -> 23.4 us
    ppermute x30, starting transfers between devices: 39.4 us -> 37.2 us  [swap(): return lax.ppermute(x, 'tensor', [(d, d ^ bit) for d in range(shards)])]
    pallas_call x40, Pallas kernels: 22.3 us -> 23.4 us  [call(): pl.pallas_call(kernel, out_shape=shapes, in_specs=list(specs) + [UNREAD]...]
  transfers between devices with their start and end apart: 30 -> 30, of which waited for: 12 -> 13; matrix products, arithmetic and copies ran while one was open for 0% -> 0% of each run, Pallas kernels for 21% -> 23%
where the time goes in v14:
time: 90.2 us; the launch traced here: 90 us
  starting transfers between devices  37.2 us (41%)
  waiting for transfers between devices  27.2 us (30%)
  Pallas kernels  23.4 us (26%)
  local copies, waits for them, and re-layouts  1.75 us (2%)
    ppermute x30, starting transfers between devices, swap(): return lax.ppermute(x, 'tensor', [(d, d ^ bit) for d in range(shards)])  37.2 us
    ppermute x30, waiting for transfers between devices, swap(): return lax.ppermute(x, 'tensor', [(d, d ^ bit) for d in range(shards)])  27.2 us
    pallas_call x40, Pallas kernels, call(): pl.pallas_call(kernel, out_shape=shapes, in_specs=list(specs) + [UNREAD]...  23.4 us
  transfers between devices with their start and end apart: 30, of which 13 were waited for; matrix products, arithmetic and copies ran while one was open for 0% of the time, Pallas kernels for 23%

profile of v14, /device:TPU:0, one launch (start us, length us, event | category | flops | bytes accessed | tf_op | source)
XLA Modules:
  0.0 90.0 jit_solution(8660757666388766050)
XLA Ops:
  0.0 1.0 %copy-done = bf16[128,1664]{1,0:T(8,128)(2,1)S(1)} copy-done((bf16[128,1664]{1,0:T(8,128)(2,1)S(1)}, bf16[128,1664]{1,0:T(8,128)(2,1)}, u32[]{:S(2)}) %copy-start) | copy-done | bytes 426008
  1.0 0.7 copy-done.1
  1.8 1.2 %mix.4.refs_0_ = f32[128,384]{1,0:T(8,128)S(1)} custom-call(bf16[128,1664]{1,0:T(8,128)(2,1)S(1)} %copy-done, f32[52,52]{1,0:T(8,128)S(1)} %copy-done.1), custom_call_target="tpu_custom_call" | custom-call | flops 10000000000 | bytes 100000000 | tf_op jit(solution)/shard_map/mix/pallas_call | solution.py:83
  2.9 4.1 %collective-permute-start.3 = (f32[128,384]{1,0:T(8,128)S(1)}, f32[128,384]{1,0:T(8,128)S(1)}, u32[]{:S(2)}, u32[]{:S(2)}) collective-permute-start(f32[128,384]{1,0:T(8,128)S(1)} %mix.4.refs_0_), channel_id=1, source_target_pairs={{0,8},{1,9},{2,10},{3,11},{4,12},{5,13},{6,14},{7,15},{8,0},{9,1},... | collective-permute-start | bytes 589832 | tf_op jit(solution)/shard_map/ppermute | solution.py:316
  7.0 1.2 %mix.5.refs_0_ = f32[128,384]{1,0:T(8,128)S(1)} custom-call(bf16[128,1664]{1,0:T(8,128)(2,1)S(1)} %copy-done, f32[52,52]{1,0:T(8,128)S(1)} %copy-done.1, f32[128,384]{1,0:T(8,128)S(1)} %mix.4.refs_0_), custom_call_target="tpu_custom_call" | custom-call | flops 10000000000 | bytes 100000000 | tf_op jit(solution)/shard_map/mix/pallas_call | solution.py:83
  8.2 0.1 collective-permute-start
  8.3 1.2 %mix.6.refs_0_ = f32[128,384]{1,0:T(8,128)S(1)} custom-call(bf16[128,1664]{1,0:T(8,128)(2,1)S(1)} %copy-done, f32[52,52]{1,0:T(8,128)S(1)} %copy-done.1, f32[128,384]{1,0:T(8,128)S(1)} %mix.5.refs_0_), custom_call_target="tpu_custom_call" | custom-call | flops 10000000000 | bytes 100000000 | tf_op jit(solution)/shard_map/mix/pallas_call | solution.py:83
  9.5 1.6 %collective-permute-start.4 = (f32[128,384]{1,0:T(8,128)S(1)}, f32[128,384]{1,0:T(8,128)S(1)}, u32[]{:S(2)}, u32[]{:S(2)}) collective-permute-start(f32[128,384]{1,0:T(8,128)S(1)} %mix.6.refs_0_), channel_id=1, source_target_pairs={{0,2},{1,3},{2,0},{3,1},{4,6},{5,7},{6,4},{7,5},{8,10},{9,11},{10,... | collective-permute-start | bytes 589832 | tf_op jit(solution)/shard_map/ppermute | solution.py:316
  11.1 1.2 %mix.7.refs_2_.refs_0_ = f32[128,512]{1,0:T(8,128)S(1)} custom-call(bf16[128,1664]{1,0:T(8,128)(2,1)S(1)} %copy-done, f32[52,52]{1,0:T(8,128)S(1)} %copy-done.1, f32[128,384]{1,0:T(8,128)S(1)} %mix.6.refs_0_), custom_call_target="tpu_custom_call" | custom-call | flops 10000000000 | bytes 100000000 | tf_op jit(solution)/shard_map/mix/pallas_call | solution.py:83
  12.3 1.6 %collective-permute-start.2 = (f32[128,512]{1,0:T(8,128)S(1)}, f32[128,512]{1,0:T(8,128)S(1)}, u32[]{:S(2)}, u32[]{:S(2)}) collective-permute-start(f32[128,512]{1,0:T(8,128)S(1)} %mix.7.refs_2_.refs_0_), channel_id=1, source_target_pairs={{0,4},{1,5},{2,6},{3,7},{4,0},{5,1},{6,2},{7,3},{8,12},{9,13},{10,... | collective-permute-start | bytes 786440 | tf_op jit(solution)/shard_map/ppermute | solution.py:316
  13.9 0.0 collective-permute-done.refs_1_
  14.0 0.4 collective-permute-start.1
  14.4 2.9 %load.2 = (bf16[384,8192]{1,0:T(8,128)(2,1)S(1)}, f32[8,128]{1,0:T(8,128)S(1)}) custom-call(s32[1]{0:T(128)} %bitcast.me_ref, bf16[1664,8192]{1,0:T(8,128)(2,1)} %weight_ref.7, f32[128,384]{1,0:T(8,128)S(1)} %fold.16.refs_0_), custom_call_target="tpu_custom_call" | custom-call | flops 10000000000 | bytes 100000000 | tf_op jit(solution)/shard_map/load/pallas_call | solution.py:83
  17.2 2.9 %load.3 = (bf16[384,8192]{1,0:T(8,128)(2,1)S(1)}, f32[8,128]{1,0:T(8,128)S(1)}) custom-call(s32[1]{0:T(128)} %bitcast.me_ref, bf16[1664,8192]{1,0:T(8,128)(2,1)} %weight_ref.7, f32[8,128]{1,0:T(8,128)S(1)} %get-tuple-element.41.refs_0_), custom_call_target="tpu_custom_call" | custom-call | flops 10000000000 | bytes 100000000 | tf_op jit(solution)/shard_map/load/pallas_call | solution.py:83
  20.1 0.0 collective-permute-done.4.refs_1_
  20.1 3.0 %fold.17 = (bf16[384,8192]{1,0:T(8,128)(2,1)S(1)}, f32[128,384]{1,0:T(8,128)S(1)}) custom-call(s32[1]{0:T(128)} %bitcast.me_ref, bf16[1664,8192]{1,0:T(8,128)(2,1)} %weight_ref.7, f32[128,384]{1,0:T(8,128)S(1)} %mix.6.refs_0_, f32[128,384]{1,0:T(8,128)S(1)} %collective-permute-done.4.refs_1_, f32[8,128]{1,0:T(8,128)S(1)} %get-tuple-element.42.refs_2_), custom_call_target="tpu_custom_call" | custom-call | flops 10000000000 | bytes 100000000 | tf_op jit(solution)/shard_map/fold/pallas_call | solution.py:83
  23.1 0.1 collective-permute-start.6
  23.2 0.5 collective-permute-start.9
  23.7 1.2 %collective-permute-done.2.refs_1_ = f32[128,512]{1,0:T(8,128)S(1)} collective-permute-done((f32[128,512]{1,0:T(8,128)S(1)}, f32[128,512]{1,0:T(8,128)S(1)}, u32[]{:S(2)}, u32[]{:S(2)}) %collective-permute-start.2) | collective-permute-done | bytes 262176 | tf_op jit(solution)/shard_map/ppermute | solution.py:316
  25.0 2.8 %collective-permute-start.5 = (f32[128,512]{1,0:T(8,128)S(1)}, f32[128,512]{1,0:T(8,128)S(1)}, u32[]{:S(2)}, u32[]{:S(2)}) collective-permute-start(f32[128,512]{1,0:T(8,128)S(1)} %fold.19.refs_2_.refs_0_), channel_id=1, source_target_pairs={{0,2},{1,3},{2,0},{3,1},{4,6},{5,7},{6,4},{7,5},{8,10},{9,11},{10,... | collective-permute-start | bytes 786440 | tf_op jit(solution)/shard_map/ppermute | solution.py:316
  27.8 1.7 %collective-permute-start.8 = (f32[128,384]{1,0:T(8,128)S(1)}, f32[128,384]{1,0:T(8,128)S(1)}, u32[]{:S(2)}, u32[]{:S(2)}) collective-permute-start(f32[128,384]{1,0:T(8,128)S(1)} %fold.20.refs_2_.refs_0_), channel_id=1, source_target_pairs={{0,8},{1,9},{2,10},{3,11},{4,12},{5,13},{6,14},{7,15},{8,0},{9,1},... | collective-permute-start | bytes 589832 | tf_op jit(solution)/shard_map/ppermute | solution.py:316
  29.4 4.8 %collective-permute-done.5.refs_1_ = f32[128,512]{1,0:T(8,128)S(1)} collective-permute-done((f32[128,512]{1,0:T(8,128)S(1)}, f32[128,512]{1,0:T(8,128)S(1)}, u32[]{:S(2)}, u32[]{:S(2)}) %collective-permute-start.5) | collective-permute-done | bytes 262176 | tf_op jit(solution)/shard_map/ppermute | solution.py:316
  34.2 0.1 collective-permute-start.11
  34.3 0.0 collective-permute-done.1.refs_1_
  34.3 0.1 collective-permute-start.7
  34.5 1.8 %collective-permute-start.10 = (f32[128,384]{1,0:T(8,128)S(1)}, f32[128,384]{1,0:T(8,128)S(1)}, u32[]{:S(2)}, u32[]{:S(2)}) collective-permute-start(f32[128,384]{1,0:T(8,128)S(1)} %fold.23.refs_2_.refs_0_), channel_id=1, source_target_pairs={{0,2},{1,3},{2,0},{3,1},{4,6},{5,7},{6,4},{7,5},{8,10},{9,11},{10,... | collective-permute-start | bytes 589832 | tf_op jit(solution)/shard_map/ppermute | solution.py:316
  36.3 0.0 collective-permute-done.11.refs_1_
  36.3 3.9 %collective-permute-start.14 = (f32[128,512]{1,0:T(8,128)S(1)}, f32[128,512]{1,0:T(8,128)S(1)}, u32[]{:S(2)}, u32[]{:S(2)}) collective-permute-start(f32[128,512]{1,0:T(8,128)S(1)} %fold.24.refs_2_.refs_0_), channel_id=1, source_target_pairs={{0,8},{1,9},{2,10},{3,11},{4,12},{5,13},{6,14},{7,15},{8,0},{9,1},... | collective-permute-start | bytes 786440 | tf_op jit(solution)/shard_map/ppermute | solution.py:316
  40.2 1.6 %collective-permute-done.10.refs_1_ = f32[128,384]{1,0:T(8,128)S(1)} collective-permute-done((f32[128,384]{1,0:T(8,128)S(1)}, f32[128,384]{1,0:T(8,128)S(1)}, u32[]{:S(2)}, u32[]{:S(2)}) %collective-permute-start.10) | collective-permute-done | bytes 196640 | tf_op jit(solution)/shard_map/ppermute | solution.py:316
  41.8 0.1 collective-permute-start.13
  41.9 0.0 collective-permute-done.8.refs_1_
  42.0 1.8 %collective-permute-start.15 = (f32[128,384]{1,0:T(8,128)S(1)}, f32[128,384]{1,0:T(8,128)S(1)}, u32[]{:S(2)}, u32[]{:S(2)}) collective-permute-start(f32[128,384]{1,0:T(8,128)S(1)} %fold.26.refs_2_.refs_0_), channel_id=1, source_target_pairs={{0,4},{1,5},{2,6},{3,7},{4,0},{5,1},{6,2},{7,3},{8,12},{9,13},{10,... | collective-permute-start | bytes 589832 | tf_op jit(solution)/shard_map/ppermute | solution.py:316
  43.8 2.7 %collective-permute-done.7.refs_1_ = f32[128,384]{1,0:T(8,128)S(1)} collective-permute-done((f32[128,384]{1,0:T(8,128)S(1)}, f32[128,384]{1,0:T(8,128)S(1)}, u32[]{:S(2)}, u32[]{:S(2)}) %collective-permute-start.7) | collective-permute-done | bytes 196640 | tf_op jit(solution)/shard_map/ppermute | solution.py:316
  46.5 1.0 %collective-permute-start.12 = (f32[128,384]{1,0:T(8,128)S(1)}, f32[128,384]{1,0:T(8,128)S(1)}, u32[]{:S(2)}, u32[]{:S(2)}) collective-permute-start(f32[128,384]{1,0:T(8,128)S(1)} %fold.27.refs_2_.refs_0_), channel_id=1, source_target_pairs={{0,2},{1,3},{2,0},{3,1},{4,6},{5,7},{6,4},{7,5},{8,10},{9,11},{10,... | collective-permute-start | bytes 589832 | tf_op jit(solution)/shard_map/ppermute | solution.py:316
  47.5 4.6 %step.2 = (bf16[512,8192]{1,0:T(8,128)(2,1)S(1)}, f32[16,128,512]{2,1,0:T(8,128)S(1)}) custom-call(s32[1]{0:T(128)} %bitcast.me_ref, bf16[1664,8192]{1,0:T(8,128)(2,1)} %weight_ref.7, bf16[128,384]{1,0:T(8,128)(2,1)S(1)} %fold.28.refs_0_.refs_2_, bf16[384,8192]{1,0:T(8,128)(2,1)S(1)} %get-tuple-element.44.refs_1_, bf16[128,384]{1,0:T(8,128)(2,1)S(1)} %fold.28.refs_0_.refs_2_), custom_call_target="tpu_custom_call" | custom-call | flops 10000000000 | bytes 100000000 | tf_op jit(solution)/shard_map/step/pallas_call | solution.py:83
  52.1 1.2 %collective-permute-done.12.refs_1_ = f32[128,384]{1,0:T(8,128)S(1)} collective-permute-done((f32[128,384]{1,0:T(8,128)S(1)}, f32[128,384]{1,0:T(8,128)S(1)}, u32[]{:S(2)}, u32[]{:S(2)}) %collective-permute-start.12) | collective-permute-done | bytes 196640 | tf_op jit(solution)/shard_map/ppermute | solution.py:316
  53.4 1.3 %step.3.refs_2_.total_ref = f32[16,128,512]{2,1,0:T(8,128)S(1)} custom-call(bf16[128,384]{1,0:T(8,128)(2,1)S(1)} %fold.29.refs_0_.refs_3_, bf16[384,8192]{1,0:T(8,128)(2,1)S(1)} %get-tuple-element.46.refs_1_, f32[16,128,512]{2,1,0:T(8,128)S(1)} %get-tuple-element.45.refs_2_, bf16[128,384]{1,0:T(8,128)(2,1)S(1)} %fold.29.refs_0_.refs_3_), custom_call_target="tpu_custom_call" | custom-call | flops 10000000000 | bytes 100000000 | tf_op jit(solution)/shard_map/step/pallas_call | solution.py:83
  54.9 1.3 %product.2 = (f32[8,128,256]{2,1,0:T(8,128)S(1)}, f32[8,128,256]{2,1,0:T(8,128)S(1)}) custom-call(s32[1]{0:T(128)} %bitcast.me_ref, f32[16,128,512]{2,1,0:T(8,128)S(1)} %step.3.refs_2_.total_ref, bf16[128,512]{1,0:T(8,128)(2,1)S(1)} %fold.30.refs_2_.refs_0_, bf16[128,384]{1,0:T(8,128)(2,1)S(1)} %fold.31.refs_1_.refs_4_, ...), custom_call_target="tpu_custom_call" | custom-call | flops 10000000000 | bytes 100000000 | tf_op jit(solution)/shard_map/product/pallas_call | solution.py:83
  56.2 0.1 collective-permute-start.17
  56.2 0.5 collective-permute-start.16
  56.7 1.3 %product.3 = (f32[8,128,256]{2,1,0:T(8,128)S(1)}, f32[8,128,256]{2,1,0:T(8,128)S(1)}) custom-call(s32[1]{0:T(128)} %bitcast.me_ref, f32[16,128,512]{2,1,0:T(8,128)S(1)} %step.3.refs_2_.total_ref, bf16[128,512]{1,0:T(8,128)(2,1)S(1)} %fold.30.refs_2_.refs_0_, bf16[128,384]{1,0:T(8,128)(2,1)S(1)} %fold.31.refs_1_.refs_4_, ...), custom_call_target="tpu_custom_call" | custom-call | flops 10000000000 | bytes 100000000 | tf_op jit(solution)/shard_map/product/pallas_call | solution.py:83
  58.0 0.9 collective-permute-done.17.got_ref
  58.9 0.1 halve.10
  59.0 0.1 collective-permute-start.21
  59.1 1.0 %collective-permute-start.20 = (f32[4,64,256]{2,1,0:T(8,128)S(1)}, f32[4,64,256]{2,1,0:T(8,128)S(1)}, u32[]{:S(2)}, u32[]{:S(2)}) collective-permute-start(f32[4,64,256]{2,1,0:T(8,128)S(1)} %get-tuple-element.53.refs_0_), channel_id=1, source_target_pairs={{0,2},{1,3},{2,0},{3,1},{4,6},{5,7},{6,4},{7,5},{8,10},{9,11},{10,... | collective-permute-start | bytes 786440 | tf_op jit(solution)/shard_map/ppermute | solution.py:316
  60.1 0.3 collective-permute-done.16.got_ref
  60.4 0.1 halve.11
  60.5 1.7 %collective-permute-start.19 = (f32[4,64,256]{2,1,0:T(8,128)S(1)}, f32[4,64,256]{2,1,0:T(8,128)S(1)}, u32[]{:S(2)}, u32[]{:S(2)}) collective-permute-start(f32[4,64,256]{2,1,0:T(8,128)S(1)} %get-tuple-element.57.refs_0_), channel_id=1, source_target_pairs={{0,4},{1,5},{2,6},{3,7},{4,0},{5,1},{6,2},{7,3},{8,12},{9,13},{10,... | collective-permute-start | bytes 786440 | tf_op jit(solution)/shard_map/ppermute | solution.py:316
  62.2 1.1 %collective-permute-start.18 = (f32[4,64,256]{2,1,0:T(8,128)S(1)}, f32[4,64,256]{2,1,0:T(8,128)S(1)}, u32[]{:S(2)}, u32[]{:S(2)}) collective-permute-start(f32[4,64,256]{2,1,0:T(8,128)S(1)} %get-tuple-element.55), channel_id=1, source_target_pairs={{0,2},{1,3},{2,0},{3,1},{4,6},{5,7},{6,4},{7,5},{8,10},{9,11},{10,... | collective-permute-start | bytes 786440 | tf_op jit(solution)/shard_map/ppermute | solution.py:316
  63.3 4.9 %collective-permute-done.21.got_ref = f32[4,64,256]{2,1,0:T(8,128)S(1)} collective-permute-done((f32[4,64,256]{2,1,0:T(8,128)S(1)}, f32[4,64,256]{2,1,0:T(8,128)S(1)}, u32[]{:S(2)}, u32[]{:S(2)}) %collective-permute-start.21) | collective-permute-done | bytes 262176 | tf_op jit(solution)/shard_map/ppermute | solution.py:316
  68.2 1.0 %collective-permute-start.25 = (f32[2,64,256]{2,1,0:T(8,128)S(1)}, f32[2,64,256]{2,1,0:T(8,128)S(1)}, u32[]{:S(2)}, u32[]{:S(2)}) collective-permute-start(f32[2,64,256]{2,1,0:T(8,128)S(1)} %get-tuple-element.61.refs_0_), channel_id=1, source_target_pairs={{0,2},{1,3},{2,0},{3,1},{4,6},{5,7},{6,4},{7,5},{8,10},{9,11},{10,... | collective-permute-start | bytes 393224 | tf_op jit(solution)/shard_map/ppermute | solution.py:316
  69.3 2.3 %collective-permute-start.24 = (f32[2,64,256]{2,1,0:T(8,128)S(1)}, f32[2,64,256]{2,1,0:T(8,128)S(1)}, u32[]{:S(2)}, u32[]{:S(2)}) collective-permute-start(f32[2,64,256]{2,1,0:T(8,128)S(1)} %get-tuple-element.62.refs_0_), channel_id=1, source_target_pairs={{0,8},{1,9},{2,10},{3,11},{4,12},{5,13},{6,14},{7,15},{8,0},{9,1},... | collective-permute-start | bytes 393224 | tf_op jit(solution)/shard_map/ppermute | solution.py:316
  71.5 3.3 %collective-permute-done.19.got_ref = f32[4,64,256]{2,1,0:T(8,128)S(1)} collective-permute-done((f32[4,64,256]{2,1,0:T(8,128)S(1)}, f32[4,64,256]{2,1,0:T(8,128)S(1)}, u32[]{:S(2)}, u32[]{:S(2)}) %collective-permute-start.19) | collective-permute-done | bytes 262176 | tf_op jit(solution)/shard_map/ppermute | solution.py:316
  74.9 1.1 %collective-permute-start.23 = (f32[2,64,256]{2,1,0:T(8,128)S(1)}, f32[2,64,256]{2,1,0:T(8,128)S(1)}, u32[]{:S(2)}, u32[]{:S(2)}) collective-permute-start(f32[2,64,256]{2,1,0:T(8,128)S(1)} %get-tuple-element.63.refs_0_), channel_id=1, source_target_pairs={{0,2},{1,3},{2,0},{3,1},{4,6},{5,7},{6,4},{7,5},{8,10},{9,11},{10,... | collective-permute-start | bytes 393224 | tf_op jit(solution)/shard_map/ppermute | solution.py:316
  76.0 0.1 collective-permute-start.22
  76.1 4.1 %collective-permute-start.27 = (f32[1,64,256]{2,1,0:T(8,128)S(1)}, f32[1,64,256]{2,1,0:T(8,128)S(1)}, u32[]{:S(2)}, u32[]{:S(2)}) collective-permute-start(f32[1,64,256]{2,1,0:T(8,128)S(1)} %get-tuple-element.69.refs_0_), channel_id=1, source_target_pairs={{0,8},{1,9},{2,10},{3,11},{4,12},{5,13},{6,14},{7,15},{8,0},{9,1},... | collective-permute-start | bytes 196616 | tf_op jit(solution)/shard_map/ppermute | solution.py:316
  80.2 0.1 collective-permute-start.28
  80.3 1.5 %collective-permute-start.29 = (f32[1,64,256]{2,1,0:T(8,128)S(1)}, f32[1,64,256]{2,1,0:T(8,128)S(1)}, u32[]{:S(2)}, u32[]{:S(2)}) collective-permute-start(f32[1,64,256]{2,1,0:T(8,128)S(1)} %get-tuple-element.71.refs_0_), channel_id=1, source_target_pairs={{0,8},{1,9},{2,10},{3,11},{4,12},{5,13},{6,14},{7,15},{8,0},{9,1},... | collective-permute-start | bytes 196616 | tf_op jit(solution)/shard_map/ppermute | solution.py:316
  81.9 1.5 %collective-permute-done.22.got_ref = f32[2,64,256]{2,1,0:T(8,128)S(1)} collective-permute-done((f32[2,64,256]{2,1,0:T(8,128)S(1)}, f32[2,64,256]{2,1,0:T(8,128)S(1)}, u32[]{:S(2)}, u32[]{:S(2)}) %collective-permute-start.22) | collective-permute-done | bytes 131104 | tf_op jit(solution)/shard_map/ppermute | solution.py:316
  83.4 1.1 %collective-permute-start.26 = (f32[1,64,256]{2,1,0:T(8,128)S(1)}, f32[1,64,256]{2,1,0:T(8,128)S(1)}, u32[]{:S(2)}, u32[]{:S(2)}) collective-permute-start(f32[1,64,256]{2,1,0:T(8,128)S(1)} %get-tuple-element.73.refs_0_), channel_id=1, source_target_pairs={{0,8},{1,9},{2,10},{3,11},{4,12},{5,13},{6,14},{7,15},{8,0},{9,1},... | collective-permute-start | bytes 196616 | tf_op jit(solution)/shard_map/ppermute | solution.py:316
  84.6 0.1 collective-permute-done.28.got_ref
  84.6 3.2 %collective-permute-done.29.got_ref = f32[1,64,256]{2,1,0:T(8,128)S(1)} collective-permute-done((f32[1,64,256]{2,1,0:T(8,128)S(1)}, f32[1,64,256]{2,1,0:T(8,128)S(1)}, u32[]{:S(2)}, u32[]{:S(2)}) %collective-permute-start.29) | collective-permute-done | bytes 65568 | tf_op jit(solution)/shard_map/ppermute | solution.py:316
  87.9 1.5 %collective-permute-done.26.got_ref = f32[1,64,256]{2,1,0:T(8,128)S(1)} collective-permute-done((f32[1,64,256]{2,1,0:T(8,128)S(1)}, f32[1,64,256]{2,1,0:T(8,128)S(1)}, u32[]{:S(2)}, u32[]{:S(2)}) %collective-permute-start.26) | collective-permute-done | bytes 65568 | tf_op jit(solution)/shard_map/ppermute | solution.py:316
  89.3 0.7 finish.7
  (40 shorter events, 0.7 us)
Async XLA Ops:
  0.0 1.0 %copy-start = (bf16[128,1664]{1,0:T(8,128)(2,1)S(1)}, bf16[128,1664]{1,0:T(8,128)(2,1)}, u32[]{:S(2)}) copy-start(bf16[128,1664]{1,0:T(8,128)(2,1)} %activations.7) | copy-start | bytes 1277956
  1.0 0.7 copy-start.1
  2.9 20.2 %collective-permute-start.3 = (f32[128,384]{1,0:T(8,128)S(1)}, f32[128,384]{1,0:T(8,128)S(1)}, u32[]{:S(2)}, u32[]{:S(2)}) collective-permute-start(f32[128,384]{1,0:T(8,128)S(1)} %mix.4.refs_0_), channel_id=1, source_target_pairs={{0,8},{1,9},{2,10},{3,11},{4,12},{5,13},{6,14},{7,15},{8,0},{9,1},... | collective-permute-start | bytes 589832 | tf_op jit(solution)/shard_map/ppermute | solution.py:316
  8.2 5.7 %collective-permute-start = (f32[128,384]{1,0:T(8,128)S(1)}, f32[128,384]{1,0:T(8,128)S(1)}, u32[]{:S(2)}, u32[]{:S(2)}) collective-permute-start(f32[128,384]{1,0:T(8,128)S(1)} %mix.5.refs_0_), channel_id=1, source_target_pairs={{0,1},{1,0},{2,3},{3,2},{4,5},{5,4},{6,7},{7,6},{8,9},{9,8},{10,11... | collective-permute-start | bytes 589832 | tf_op jit(solution)/shard_map/ppermute | solution.py:316
  9.5 10.6 %collective-permute-start.4 = (f32[128,384]{1,0:T(8,128)S(1)}, f32[128,384]{1,0:T(8,128)S(1)}, u32[]{:S(2)}, u32[]{:S(2)}) collective-permute-start(f32[128,384]{1,0:T(8,128)S(1)} %mix.6.refs_0_), channel_id=1, source_target_pairs={{0,2},{1,3},{2,0},{3,1},{4,6},{5,7},{6,4},{7,5},{8,10},{9,11},{10,... | collective-permute-start | bytes 589832 | tf_op jit(solution)/shard_map/ppermute | solution.py:316
  12.3 12.7 %collective-permute-start.2 = (f32[128,512]{1,0:T(8,128)S(1)}, f32[128,512]{1,0:T(8,128)S(1)}, u32[]{:S(2)}, u32[]{:S(2)}) collective-permute-start(f32[128,512]{1,0:T(8,128)S(1)} %mix.7.refs_2_.refs_0_), channel_id=1, source_target_pairs={{0,4},{1,5},{2,6},{3,7},{4,0},{5,1},{6,2},{7,3},{8,12},{9,13},{10,... | collective-permute-start | bytes 786440 | tf_op jit(solution)/shard_map/ppermute | solution.py:316
  14.0 20.3 %collective-permute-start.1 = (f32[128,384]{1,0:T(8,128)S(1)}, f32[128,384]{1,0:T(8,128)S(1)}, u32[]{:S(2)}, u32[]{:S(2)}) collective-permute-start(f32[128,384]{1,0:T(8,128)S(1)} %fold.16.refs_0_), channel_id=1, source_target_pairs={{0,8},{1,9},{2,10},{3,11},{4,12},{5,13},{6,14},{7,15},{8,0},{9,1},... | collective-permute-start | bytes 589832 | tf_op jit(solution)/shard_map/ppermute | solution.py:316
  23.1 4.6 %collective-permute-start.6 = (f32[128,384]{1,0:T(8,128)S(1)}, f32[128,384]{1,0:T(8,128)S(1)}, u32[]{:S(2)}, u32[]{:S(2)}) collective-permute-start(f32[128,384]{1,0:T(8,128)S(1)} %get-tuple-element.43.refs_2_.refs_0_), channel_id=1, source_target_pairs={{0,1},{1,0},{2,3},{3,2},{4,5},{5,4},{6,7},{7,6},{8,9},{9,8},{10,11... | collective-permute-start | bytes 589832 | tf_op jit(solution)/shard_map/ppermute | solution.py:316
  23.2 11.2 %collective-permute-start.9 = (f32[128,384]{1,0:T(8,128)S(1)}, f32[128,384]{1,0:T(8,128)S(1)}, u32[]{:S(2)}, u32[]{:S(2)}) collective-permute-start(f32[128,384]{1,0:T(8,128)S(1)} %fold.18.refs_2_.refs_0_), channel_id=1, source_target_pairs={{0,4},{1,5},{2,6},{3,7},{4,0},{5,1},{6,2},{7,3},{8,12},{9,13},{10,... | collective-permute-start | bytes 589832 | tf_op jit(solution)/shard_map/ppermute | solution.py:316
  25.0 9.2 %collective-permute-start.5 = (f32[128,512]{1,0:T(8,128)S(1)}, f32[128,512]{1,0:T(8,128)S(1)}, u32[]{:S(2)}, u32[]{:S(2)}) collective-permute-start(f32[128,512]{1,0:T(8,128)S(1)} %fold.19.refs_2_.refs_0_), channel_id=1, source_target_pairs={{0,2},{1,3},{2,0},{3,1},{4,6},{5,7},{6,4},{7,5},{8,10},{9,11},{10,... | collective-permute-start | bytes 786440 | tf_op jit(solution)/shard_map/ppermute | solution.py:316
  27.8 14.2 %collective-permute-start.8 = (f32[128,384]{1,0:T(8,128)S(1)}, f32[128,384]{1,0:T(8,128)S(1)}, u32[]{:S(2)}, u32[]{:S(2)}) collective-permute-start(f32[128,384]{1,0:T(8,128)S(1)} %fold.20.refs_2_.refs_0_), channel_id=1, source_target_pairs={{0,8},{1,9},{2,10},{3,11},{4,12},{5,13},{6,14},{7,15},{8,0},{9,1},... | collective-permute-start | bytes 589832 | tf_op jit(solution)/shard_map/ppermute | solution.py:316
  34.2 2.1 %collective-permute-start.11 = (f32[128,512]{1,0:T(8,128)S(1)}, f32[128,512]{1,0:T(8,128)S(1)}, u32[]{:S(2)}, u32[]{:S(2)}) collective-permute-start(f32[128,512]{1,0:T(8,128)S(1)} %fold.21.refs_2_.refs_0_), channel_id=1, source_target_pairs={{0,1},{1,0},{2,3},{3,2},{4,5},{5,4},{6,7},{7,6},{8,9},{9,8},{10,11... | collective-permute-start | bytes 786440 | tf_op jit(solution)/shard_map/ppermute | solution.py:316
  34.3 12.1 %collective-permute-start.7 = (f32[128,384]{1,0:T(8,128)S(1)}, f32[128,384]{1,0:T(8,128)S(1)}, u32[]{:S(2)}, u32[]{:S(2)}) collective-permute-start(f32[128,384]{1,0:T(8,128)S(1)} %fold.22.refs_2_.refs_0_), channel_id=1, source_target_pairs={{0,4},{1,5},{2,6},{3,7},{4,0},{5,1},{6,2},{7,3},{8,12},{9,13},{10,... | collective-permute-start | bytes 589832 | tf_op jit(solution)/shard_map/ppermute | solution.py:316
  34.5 7.4 %collective-permute-start.10 = (f32[128,384]{1,0:T(8,128)S(1)}, f32[128,384]{1,0:T(8,128)S(1)}, u32[]{:S(2)}, u32[]{:S(2)}) collective-permute-start(f32[128,384]{1,0:T(8,128)S(1)} %fold.23.refs_2_.refs_0_), channel_id=1, source_target_pairs={{0,2},{1,3},{2,0},{3,1},{4,6},{5,7},{6,4},{7,5},{8,10},{9,11},{10,... | collective-permute-start | bytes 589832 | tf_op jit(solution)/shard_map/ppermute | solution.py:316
  36.3 18.5 %collective-permute-start.14 = (f32[128,512]{1,0:T(8,128)S(1)}, f32[128,512]{1,0:T(8,128)S(1)}, u32[]{:S(2)}, u32[]{:S(2)}) collective-permute-start(f32[128,512]{1,0:T(8,128)S(1)} %fold.24.refs_2_.refs_0_), channel_id=1, source_target_pairs={{0,8},{1,9},{2,10},{3,11},{4,12},{5,13},{6,14},{7,15},{8,0},{9,1},... | collective-permute-start | bytes 786440 | tf_op jit(solution)/shard_map/ppermute | solution.py:316
  41.8 5.6 %collective-permute-start.13 = (f32[128,384]{1,0:T(8,128)S(1)}, f32[128,384]{1,0:T(8,128)S(1)}, u32[]{:S(2)}, u32[]{:S(2)}) collective-permute-start(f32[128,384]{1,0:T(8,128)S(1)} %fold.25.refs_2_.refs_0_), channel_id=1, source_target_pairs={{0,1},{1,0},{2,3},{3,2},{4,5},{5,4},{6,7},{7,6},{8,9},{9,8},{10,11... | collective-permute-start | bytes 589832 | tf_op jit(solution)/shard_map/ppermute | solution.py:316
  42.0 12.8 %collective-permute-start.15 = (f32[128,384]{1,0:T(8,128)S(1)}, f32[128,384]{1,0:T(8,128)S(1)}, u32[]{:S(2)}, u32[]{:S(2)}) collective-permute-start(f32[128,384]{1,0:T(8,128)S(1)} %fold.26.refs_2_.refs_0_), channel_id=1, source_target_pairs={{0,4},{1,5},{2,6},{3,7},{4,0},{5,1},{6,2},{7,3},{8,12},{9,13},{10,... | collective-permute-start | bytes 589832 | tf_op jit(solution)/shard_map/ppermute | solution.py:316
  46.5 6.9 %collective-permute-start.12 = (f32[128,384]{1,0:T(8,128)S(1)}, f32[128,384]{1,0:T(8,128)S(1)}, u32[]{:S(2)}, u32[]{:S(2)}) collective-permute-start(f32[128,384]{1,0:T(8,128)S(1)} %fold.27.refs_2_.refs_0_), channel_id=1, source_target_pairs={{0,2},{1,3},{2,0},{3,1},{4,6},{5,7},{6,4},{7,5},{8,10},{9,11},{10,... | collective-permute-start | bytes 589832 | tf_op jit(solution)/shard_map/ppermute | solution.py:316
  56.2 2.7 %collective-permute-start.17 = (f32[8,128,256]{2,1,0:T(8,128)S(1)}, f32[8,128,256]{2,1,0:T(8,128)S(1)}, u32[]{:S(2)}, u32[]{:S(2)}) collective-permute-start(f32[8,128,256]{2,1,0:T(8,128)S(1)} %get-tuple-element.52), channel_id=1, source_target_pairs={{0,1},{1,0},{2,3},{3,2},{4,5},{5,4},{6,7},{7,6},{8,9},{9,8},{10,11... | collective-permute-start | bytes 3145736 | tf_op jit(solution)/shard_map/ppermute | solution.py:316
  56.2 4.1 %collective-permute-start.16 = (f32[8,128,256]{2,1,0:T(8,128)S(1)}, f32[8,128,256]{2,1,0:T(8,128)S(1)}, u32[]{:S(2)}, u32[]{:S(2)}) collective-permute-start(f32[8,128,256]{2,1,0:T(8,128)S(1)} %get-tuple-element.49.refs_4_), channel_id=1, source_target_pairs={{0,1},{1,0},{2,3},{3,2},{4,5},{5,4},{6,7},{7,6},{8,9},{9,8},{10,11... | collective-permute-start | bytes 3145736 | tf_op jit(solution)/shard_map/ppermute | solution.py:316
  59.0 9.2 %collective-permute-start.21 = (f32[4,64,256]{2,1,0:T(8,128)S(1)}, f32[4,64,256]{2,1,0:T(8,128)S(1)}, u32[]{:S(2)}, u32[]{:S(2)}) collective-permute-start(f32[4,64,256]{2,1,0:T(8,128)S(1)} %get-tuple-element.60), channel_id=1, source_target_pairs={{0,4},{1,5},{2,6},{3,7},{4,0},{5,1},{6,2},{7,3},{8,12},{9,13},{10,... | collective-permute-start | bytes 786440 | tf_op jit(solution)/shard_map/ppermute | solution.py:316
  59.1 10.2 %collective-permute-start.20 = (f32[4,64,256]{2,1,0:T(8,128)S(1)}, f32[4,64,256]{2,1,0:T(8,128)S(1)}, u32[]{:S(2)}, u32[]{:S(2)}) collective-permute-start(f32[4,64,256]{2,1,0:T(8,128)S(1)} %get-tuple-element.53.refs_0_), channel_id=1, source_target_pairs={{0,2},{1,3},{2,0},{3,1},{4,6},{5,7},{6,4},{7,5},{8,10},{9,11},{10,... | collective-permute-start | bytes 786440 | tf_op jit(solution)/shard_map/ppermute | solution.py:316
  60.5 14.3 %collective-permute-start.19 = (f32[4,64,256]{2,1,0:T(8,128)S(1)}, f32[4,64,256]{2,1,0:T(8,128)S(1)}, u32[]{:S(2)}, u32[]{:S(2)}) collective-permute-start(f32[4,64,256]{2,1,0:T(8,128)S(1)} %get-tuple-element.57.refs_0_), channel_id=1, source_target_pairs={{0,4},{1,5},{2,6},{3,7},{4,0},{5,1},{6,2},{7,3},{8,12},{9,13},{10,... | collective-permute-start | bytes 786440 | tf_op jit(solution)/shard_map/ppermute | solution.py:316
  62.2 13.7 %collective-permute-start.18 = (f32[4,64,256]{2,1,0:T(8,128)S(1)}, f32[4,64,256]{2,1,0:T(8,128)S(1)}, u32[]{:S(2)}, u32[]{:S(2)}) collective-permute-start(f32[4,64,256]{2,1,0:T(8,128)S(1)} %get-tuple-element.55), channel_id=1, source_target_pairs={{0,2},{1,3},{2,0},{3,1},{4,6},{5,7},{6,4},{7,5},{8,10},{9,11},{10,... | collective-permute-start | bytes 786440 | tf_op jit(solution)/shard_map/ppermute | solution.py:316
  68.2 7.8 %collective-permute-start.25 = (f32[2,64,256]{2,1,0:T(8,128)S(1)}, f32[2,64,256]{2,1,0:T(8,128)S(1)}, u32[]{:S(2)}, u32[]{:S(2)}) collective-permute-start(f32[2,64,256]{2,1,0:T(8,128)S(1)} %get-tuple-element.61.refs_0_), channel_id=1, source_target_pairs={{0,2},{1,3},{2,0},{3,1},{4,6},{5,7},{6,4},{7,5},{8,10},{9,11},{10,... | collective-permute-start | bytes 393224 | tf_op jit(solution)/shard_map/ppermute | solution.py:316
  69.3 10.9 %collective-permute-start.24 = (f32[2,64,256]{2,1,0:T(8,128)S(1)}, f32[2,64,256]{2,1,0:T(8,128)S(1)}, u32[]{:S(2)}, u32[]{:S(2)}) collective-permute-start(f32[2,64,256]{2,1,0:T(8,128)S(1)} %get-tuple-element.62.refs_0_), channel_id=1, source_target_pairs={{0,8},{1,9},{2,10},{3,11},{4,12},{5,13},{6,14},{7,15},{8,0},{9,1},... | collective-permute-start | bytes 393224 | tf_op jit(solution)/shard_map/ppermute | solution.py:316
  74.9 5.5 %collective-permute-start.23 = (f32[2,64,256]{2,1,0:T(8,128)S(1)}, f32[2,64,256]{2,1,0:T(8,128)S(1)}, u32[]{:S(2)}, u32[]{:S(2)}) collective-permute-start(f32[2,64,256]{2,1,0:T(8,128)S(1)} %get-tuple-element.63.refs_0_), channel_id=1, source_target_pairs={{0,2},{1,3},{2,0},{3,1},{4,6},{5,7},{6,4},{7,5},{8,10},{9,11},{10,... | collective-permute-start | bytes 393224 | tf_op jit(solution)/shard_map/ppermute | solution.py:316
  76.0 7.4 %collective-permute-start.22 = (f32[2,64,256]{2,1,0:T(8,128)S(1)}, f32[2,64,256]{2,1,0:T(8,128)S(1)}, u32[]{:S(2)}, u32[]{:S(2)}) collective-permute-start(f32[2,64,256]{2,1,0:T(8,128)S(1)} %get-tuple-element.65.refs_0_), channel_id=1, source_target_pairs={{0,4},{1,5},{2,6},{3,7},{4,0},{5,1},{6,2},{7,3},{8,12},{9,13},{10,... | collective-permute-start | bytes 393224 | tf_op jit(solution)/shard_map/ppermute | solution.py:316
  76.1 8.5 %collective-permute-start.27 = (f32[1,64,256]{2,1,0:T(8,128)S(1)}, f32[1,64,256]{2,1,0:T(8,128)S(1)}, u32[]{:S(2)}, u32[]{:S(2)}) collective-permute-start(f32[1,64,256]{2,1,0:T(8,128)S(1)} %get-tuple-element.69.refs_0_), channel_id=1, source_target_pairs={{0,8},{1,9},{2,10},{3,11},{4,12},{5,13},{6,14},{7,15},{8,0},{9,1},... | collective-permute-start | bytes 196616 | tf_op jit(solution)/shard_map/ppermute | solution.py:316
  80.2 4.4 %collective-permute-start.28 = (f32[1,64,256]{2,1,0:T(8,128)S(1)}, f32[1,64,256]{2,1,0:T(8,128)S(1)}, u32[]{:S(2)}, u32[]{:S(2)}) collective-permute-start(f32[1,64,256]{2,1,0:T(8,128)S(1)} %get-tuple-element.70.refs_0_), channel_id=1, source_target_pairs={{0,4},{1,5},{2,6},{3,7},{4,0},{5,1},{6,2},{7,3},{8,12},{9,13},{10,... | collective-permute-start | bytes 196616 | tf_op jit(solution)/shard_map/ppermute | solution.py:316
  80.3 7.5 %collective-permute-start.29 = (f32[1,64,256]{2,1,0:T(8,128)S(1)}, f32[1,64,256]{2,1,0:T(8,128)S(1)}, u32[]{:S(2)}, u32[]{:S(2)}) collective-permute-start(f32[1,64,256]{2,1,0:T(8,128)S(1)} %get-tuple-element.71.refs_0_), channel_id=1, source_target_pairs={{0,8},{1,9},{2,10},{3,11},{4,12},{5,13},{6,14},{7,15},{8,0},{9,1},... | collective-permute-start | bytes 196616 | tf_op jit(solution)/shard_map/ppermute | solution.py:316
  83.4 5.9 %collective-permute-start.26 = (f32[1,64,256]{2,1,0:T(8,128)S(1)}, f32[1,64,256]{2,1,0:T(8,128)S(1)}, u32[]{:S(2)}, u32[]{:S(2)}) collective-permute-start(f32[1,64,256]{2,1,0:T(8,128)S(1)} %get-tuple-element.73.refs_0_), channel_id=1, source_target_pairs={{0,8},{1,9},{2,10},{3,11},{4,12},{5,13},{6,14},{7,15},{8,0},{9,1},... | collective-permute-start | bytes 196616 | tf_op jit(solution)/shard_map/ppermute | solution.py:316

commit v15 on v14

--- a/solution.py
+++ b/solution.py
@@ -13,7 +13,7 @@
 BF16 = jnp.bfloat16
 
 
-TILES = (3, 3, 3, 4)
+TILES = (3, 4, 3, 3)
 DIRECT = 2
 PIECES = 4
 PERM = (0, 1, 3, 2)
@@ -79,7 +79,7 @@
 COST = pl.CostEstimate(flops=10**10, bytes_accessed=10**8, transcendentals=0)
 
 
-def call(name, kernel, operands, specs, shapes, after, scratch=(), limit=8):
+def call(name, kernel, operands, specs, shapes, after, scratch=(), limit=4):
     return pl.pallas_call(
         kernel,
         out_shape=shapes,

time: 90.2 us -> 93.1 us (1.032)
  waiting for transfers between devices: 27.2 us -> 33 us
  starting transfers between devices: 37.2 us -> 34.2 us
    ppermute x30, waiting for transfers between devices: 27.2 us -> 33 us  [swap(): return lax.ppermute(x, 'tensor', [(d, d ^ bit) for d in range(shards)])]
    ppermute x30, starting transfers between devices: 37.2 us -> 34.2 us  [swap(): return lax.ppermute(x, 'tensor', [(d, d ^ bit) for d in range(shards)])]
  transfers between devices with their start and end apart: 30 -> 30, of which waited for: 13 -> 14; matrix products, arithmetic and copies ran while one was open for 0% -> 0% of each run, Pallas kernels for 23% -> 22%
where the time goes in v15:
time: 93.1 us; the launch traced here: 92.9 us
  starting transfers between devices  34.2 us (37%)
  waiting for transfers between devices  33 us (35%)
  Pallas kernels  23.6 us (25%)
  local copies, waits for them, and re-layouts  1.75 us (2%)
    ppermute x30, starting transfers between devices, swap(): return lax.ppermute(x, 'tensor', [(d, d ^ bit) for d in range(shards)])  34.2 us
    ppermute x30, waiting for transfers between devices, swap(): return lax.ppermute(x, 'tensor', [(d, d ^ bit) for d in range(shards)])  33 us
    pallas_call x40, Pallas kernels, call(): pl.pallas_call(kernel, out_shape=shapes, in_specs=list(specs) + [UNREAD]...  23.6 us
  transfers between devices with their start and end apart: 30, of which 14 were waited for; matrix products, arithmetic and copies ran while one was open for 0% of the time, Pallas kernels for 22%

profile of v15, /device:TPU:0, one launch (start us, length us, event | category | flops | bytes accessed | tf_op | source)
XLA Modules:
  0.0 92.9 jit_solution(7675628172536958227)
XLA Ops:
  0.0 1.0 %copy-done = bf16[128,1664]{1,0:T(8,128)(2,1)S(1)} copy-done((bf16[128,1664]{1,0:T(8,128)(2,1)S(1)}, bf16[128,1664]{1,0:T(8,128)(2,1)}, u32[]{:S(2)}) %copy-start) | copy-done | bytes 426008
  1.0 0.7 copy-done.1
  1.8 1.2 %mix.4.refs_0_ = f32[128,384]{1,0:T(8,128)S(1)} custom-call(bf16[128,1664]{1,0:T(8,128)(2,1)S(1)} %copy-done, f32[52,52]{1,0:T(8,128)S(1)} %copy-done.1), custom_call_target="tpu_custom_call" | custom-call | flops 10000000000 | bytes 100000000 | tf_op jit(solution)/shard_map/mix/pallas_call | solution.py:83
  2.9 4.1 %collective-permute-start.3 = (f32[128,384]{1,0:T(8,128)S(1)}, f32[128,384]{1,0:T(8,128)S(1)}, u32[]{:S(2)}, u32[]{:S(2)}) collective-permute-start(f32[128,384]{1,0:T(8,128)S(1)} %mix.4.refs_0_), channel_id=1, source_target_pairs={{0,8},{1,9},{2,10},{3,11},{4,12},{5,13},{6,14},{7,15},{8,0},{9,1},... | collective-permute-start | bytes 589832 | tf_op jit(solution)/shard_map/ppermute | solution.py:316
  7.0 1.2 %mix.5.refs_0_ = f32[128,512]{1,0:T(8,128)S(1)} custom-call(bf16[128,1664]{1,0:T(8,128)(2,1)S(1)} %copy-done, f32[52,52]{1,0:T(8,128)S(1)} %copy-done.1, f32[128,384]{1,0:T(8,128)S(1)} %mix.4.refs_0_), custom_call_target="tpu_custom_call" | custom-call | flops 10000000000 | bytes 100000000 | tf_op jit(solution)/shard_map/mix/pallas_call | solution.py:83
  8.2 0.1 collective-permute-start
  8.3 1.2 %mix.6.refs_0_ = f32[128,384]{1,0:T(8,128)S(1)} custom-call(bf16[128,1664]{1,0:T(8,128)(2,1)S(1)} %copy-done, f32[52,52]{1,0:T(8,128)S(1)} %copy-done.1, f32[128,512]{1,0:T(8,128)S(1)} %mix.5.refs_0_), custom_call_target="tpu_custom_call" | custom-call | flops 10000000000 | bytes 100000000 | tf_op jit(solution)/shard_map/mix/pallas_call | solution.py:83
  9.5 1.6 %collective-permute-start.4 = (f32[128,384]{1,0:T(8,128)S(1)}, f32[128,384]{1,0:T(8,128)S(1)}, u32[]{:S(2)}, u32[]{:S(2)}) collective-permute-start(f32[128,384]{1,0:T(8,128)S(1)} %mix.6.refs_0_), channel_id=1, source_target_pairs={{0,2},{1,3},{2,0},{3,1},{4,6},{5,7},{6,4},{7,5},{8,10},{9,11},{10,... | collective-permute-start | bytes 589832 | tf_op jit(solution)/shard_map/ppermute | solution.py:316
  11.1 1.2 %mix.7.refs_2_.refs_0_ = f32[128,384]{1,0:T(8,128)S(1)} custom-call(bf16[128,1664]{1,0:T(8,128)(2,1)S(1)} %copy-done, f32[52,52]{1,0:T(8,128)S(1)} %copy-done.1, f32[128,384]{1,0:T(8,128)S(1)} %mix.6.refs_0_), custom_call_target="tpu_custom_call" | custom-call | flops 10000000000 | bytes 100000000 | tf_op jit(solution)/shard_map/mix/pallas_call | solution.py:83
  12.3 1.6 %collective-permute-start.2 = (f32[128,384]{1,0:T(8,128)S(1)}, f32[128,384]{1,0:T(8,128)S(1)}, u32[]{:S(2)}, u32[]{:S(2)}) collective-permute-start(f32[128,384]{1,0:T(8,128)S(1)} %mix.7.refs_2_.refs_0_), channel_id=1, source_target_pairs={{0,4},{1,5},{2,6},{3,7},{4,0},{5,1},{6,2},{7,3},{8,12},{9,13},{10,... | collective-permute-start | bytes 589832 | tf_op jit(solution)/shard_map/ppermute | solution.py:316
  14.0 0.4 collective-permute-start.1
  14.4 2.9 %load.2 = (bf16[384,8192]{1,0:T(8,128)(2,1)S(1)}, f32[8,128]{1,0:T(8,128)S(1)}) custom-call(s32[1]{0:T(128)} %bitcast.me_ref, bf16[1664,8192]{1,0:T(8,128)(2,1)} %weight_ref.7, f32[128,512]{1,0:T(8,128)S(1)} %fold.16.refs_0_), custom_call_target="tpu_custom_call" | custom-call | flops 10000000000 | bytes 100000000 | tf_op jit(solution)/shard_map/load/pallas_call | solution.py:83
  17.2 3.5 %load.3 = (bf16[512,8192]{1,0:T(8,128)(2,1)S(1)}, f32[8,128]{1,0:T(8,128)S(1)}) custom-call(s32[1]{0:T(128)} %bitcast.me_ref, bf16[1664,8192]{1,0:T(8,128)(2,1)} %weight_ref.7, f32[8,128]{1,0:T(8,128)S(1)} %get-tuple-element.41.refs_0_), custom_call_target="tpu_custom_call" | custom-call | flops 10000000000 | bytes 100000000 | tf_op jit(solution)/shard_map/load/pallas_call | solution.py:83
  20.8 0.0 collective-permute-done.4.refs_1_
  20.8 3.0 %fold.17 = (bf16[384,8192]{1,0:T(8,128)(2,1)S(1)}, f32[128,384]{1,0:T(8,128)S(1)}) custom-call(s32[1]{0:T(128)} %bitcast.me_ref, bf16[1664,8192]{1,0:T(8,128)(2,1)} %weight_ref.7, f32[128,384]{1,0:T(8,128)S(1)} %mix.6.refs_0_, f32[128,384]{1,0:T(8,128)S(1)} %collective-permute-done.4.refs_1_, f32[8,128]{1,0:T(8,128)S(1)} %get-tuple-element.42.refs_2_), custom_call_target="tpu_custom_call" | custom-call | flops 10000000000 | bytes 100000000 | tf_op jit(solution)/shard_map/fold/pallas_call | solution.py:83
  23.7 0.1 collective-permute-start.6
  23.9 0.5 collective-permute-start.9
  24.4 0.0 collective-permute-done.2.refs_1_
  24.4 0.3 collective-permute-start.5
  24.7 0.6 collective-permute-done.6.refs_1_
  25.3 2.6 %collective-permute-start.8 = (f32[128,384]{1,0:T(8,128)S(1)}, f32[128,384]{1,0:T(8,128)S(1)}, u32[]{:S(2)}, u32[]{:S(2)}) collective-permute-start(f32[128,384]{1,0:T(8,128)S(1)} %fold.20.refs_2_.refs_0_), channel_id=1, source_target_pairs={{0,8},{1,9},{2,10},{3,11},{4,12},{5,13},{6,14},{7,15},{8,0},{9,1},... | collective-permute-start | bytes 589832 | tf_op jit(solution)/shard_map/ppermute | solution.py:316
  27.9 3.6 %collective-permute-done.5.refs_1_ = f32[128,384]{1,0:T(8,128)S(1)} collective-permute-done((f32[128,384]{1,0:T(8,128)S(1)}, f32[128,384]{1,0:T(8,128)S(1)}, u32[]{:S(2)}, u32[]{:S(2)}) %collective-permute-start.5) | collective-permute-done | bytes 196640 | tf_op jit(solution)/shard_map/ppermute | solution.py:316
  31.5 0.1 collective-permute-start.11
  31.6 0.0 collective-permute-done.1.refs_1_
  31.6 1.6 %collective-permute-start.7 = (f32[128,512]{1,0:T(8,128)S(1)}, f32[128,512]{1,0:T(8,128)S(1)}, u32[]{:S(2)}, u32[]{:S(2)}) collective-permute-start(f32[128,512]{1,0:T(8,128)S(1)} %fold.22.refs_2_.refs_0_), channel_id=1, source_target_pairs={{0,4},{1,5},{2,6},{3,7},{4,0},{5,1},{6,2},{7,3},{8,12},{9,13},{10,... | collective-permute-start | bytes 786440 | tf_op jit(solution)/shard_map/ppermute | solution.py:316
  33.3 3.9 %collective-permute-done.9.refs_1_ = f32[128,384]{1,0:T(8,128)S(1)} collective-permute-done((f32[128,384]{1,0:T(8,128)S(1)}, f32[128,384]{1,0:T(8,128)S(1)}, u32[]{:S(2)}, u32[]{:S(2)}) %collective-permute-start.9) | collective-permute-done | bytes 196640 | tf_op jit(solution)/shard_map/ppermute | solution.py:316
  37.2 0.1 collective-permute-start.10
  37.3 0.0 collective-permute-done.11.refs_1_
  37.4 0.1 collective-permute-start.14
  37.4 6.7 %collective-permute-done.10.refs_1_ = f32[128,384]{1,0:T(8,128)S(1)} collective-permute-done((f32[128,384]{1,0:T(8,128)S(1)}, f32[128,384]{1,0:T(8,128)S(1)}, u32[]{:S(2)}, u32[]{:S(2)}) %collective-permute-start.10) | collective-permute-done | bytes 196640 | tf_op jit(solution)/shard_map/ppermute | solution.py:316
  44.1 0.1 collective-permute-start.13
  44.3 0.1 collective-permute-start.15
  44.3 0.6 collective-permute-done.7.refs_1_
  45.0 0.1 collective-permute-start.12
  45.1 0.6 collective-permute-done.13.refs_1_
  45.7 4.0 %step.2 = (bf16[384,8192]{1,0:T(8,128)(2,1)S(1)}, f32[16,128,512]{2,1,0:T(8,128)S(1)}) custom-call(s32[1]{0:T(128)} %bitcast.me_ref, bf16[1664,8192]{1,0:T(8,128)(2,1)} %weight_ref.7, bf16[128,384]{1,0:T(8,128)(2,1)S(1)} %fold.28.refs_0_.refs_2_, bf16[384,8192]{1,0:T(8,128)(2,1)S(1)} %get-tuple-element.44.refs_1_, bf16[128,384]{1,0:T(8,128)(2,1)S(1)} %fold.28.refs_0_.refs_2_), custom_call_target="tpu_custom_call" | custom-call | flops 10000000000 | bytes 100000000 | tf_op jit(solution)/shard_map/step/pallas_call | solution.py:83
  49.7 3.7 %collective-permute-done.12.refs_1_ = f32[128,512]{1,0:T(8,128)S(1)} collective-permute-done((f32[128,512]{1,0:T(8,128)S(1)}, f32[128,512]{1,0:T(8,128)S(1)}, u32[]{:S(2)}, u32[]{:S(2)}) %collective-permute-start.12) | collective-permute-done | bytes 262176 | tf_op jit(solution)/shard_map/ppermute | solution.py:316
  53.4 1.4 %step.3.refs_2_.total_ref = f32[16,128,512]{2,1,0:T(8,128)S(1)} custom-call(bf16[128,512]{1,0:T(8,128)(2,1)S(1)} %fold.29.refs_0_.refs_3_, bf16[512,8192]{1,0:T(8,128)(2,1)S(1)} %get-tuple-element.46.refs_1_, f32[16,128,512]{2,1,0:T(8,128)S(1)} %get-tuple-element.45.refs_2_, bf16[128,512]{1,0:T(8,128)(2,1)S(1)} %fold.29.refs_0_.refs_3_), custom_call_target="tpu_custom_call" | custom-call | flops 10000000000 | bytes 100000000 | tf_op jit(solution)/shard_map/step/pallas_call | solution.py:83
  54.9 1.3 %product.2 = (f32[8,128,256]{2,1,0:T(8,128)S(1)}, f32[8,128,256]{2,1,0:T(8,128)S(1)}) custom-call(s32[1]{0:T(128)} %bitcast.me_ref, f32[16,128,512]{2,1,0:T(8,128)S(1)} %step.3.refs_2_.total_ref, bf16[128,384]{1,0:T(8,128)(2,1)S(1)} %fold.30.refs_2_.refs_0_, bf16[128,384]{1,0:T(8,128)(2,1)S(1)} %fold.31.refs_1_.refs_4_, ...), custom_call_target="tpu_custom_call" | custom-call | flops 10000000000 | bytes 100000000 | tf_op jit(solution)/shard_map/product/pallas_call | solution.py:83
  56.2 0.1 collective-permute-start.17
  56.3 0.5 collective-permute-start.16
  56.8 1.3 %product.3 = (f32[8,128,256]{2,1,0:T(8,128)S(1)}, f32[8,128,256]{2,1,0:T(8,128)S(1)}) custom-call(s32[1]{0:T(128)} %bitcast.me_ref, f32[16,128,512]{2,1,0:T(8,128)S(1)} %step.3.refs_2_.total_ref, bf16[128,384]{1,0:T(8,128)(2,1)S(1)} %fold.30.refs_2_.refs_0_, bf16[128,384]{1,0:T(8,128)(2,1)S(1)} %fold.31.refs_1_.refs_4_, ...), custom_call_target="tpu_custom_call" | custom-call | flops 10000000000 | bytes 100000000 | tf_op jit(solution)/shard_map/product/pallas_call | solution.py:83
  58.1 0.9 collective-permute-done.17.got_ref
  59.0 0.1 halve.10
  59.1 1.6 %collective-permute-start.21 = (f32[4,64,256]{2,1,0:T(8,128)S(1)}, f32[4,64,256]{2,1,0:T(8,128)S(1)}, u32[]{:S(2)}, u32[]{:S(2)}) collective-permute-start(f32[4,64,256]{2,1,0:T(8,128)S(1)} %get-tuple-element.60), channel_id=1, source_target_pairs={{0,4},{1,5},{2,6},{3,7},{4,0},{5,1},{6,2},{7,3},{8,12},{9,13},{10,... | collective-permute-start | bytes 786440 | tf_op jit(solution)/shard_map/ppermute | solution.py:316
  60.7 0.3 collective-permute-start.20
  61.0 0.1 halve.11
  61.1 1.1 %collective-permute-start.19 = (f32[4,64,256]{2,1,0:T(8,128)S(1)}, f32[4,64,256]{2,1,0:T(8,128)S(1)}, u32[]{:S(2)}, u32[]{:S(2)}) collective-permute-start(f32[4,64,256]{2,1,0:T(8,128)S(1)} %get-tuple-element.57.refs_0_), channel_id=1, source_target_pairs={{0,4},{1,5},{2,6},{3,7},{4,0},{5,1},{6,2},{7,3},{8,12},{9,13},{10,... | collective-permute-start | bytes 786440 | tf_op jit(solution)/shard_map/ppermute | solution.py:316
  62.2 1.2 %collective-permute-start.18 = (f32[4,64,256]{2,1,0:T(8,128)S(1)}, f32[4,64,256]{2,1,0:T(8,128)S(1)}, u32[]{:S(2)}, u32[]{:S(2)}) collective-permute-start(f32[4,64,256]{2,1,0:T(8,128)S(1)} %get-tuple-element.55), channel_id=1, source_target_pairs={{0,2},{1,3},{2,0},{3,1},{4,6},{5,7},{6,4},{7,5},{8,10},{9,11},{10,... | collective-permute-start | bytes 786440 | tf_op jit(solution)/shard_map/ppermute | solution.py:316
  63.4 4.9 %collective-permute-done.21.got_ref = f32[4,64,256]{2,1,0:T(8,128)S(1)} collective-permute-done((f32[4,64,256]{2,1,0:T(8,128)S(1)}, f32[4,64,256]{2,1,0:T(8,128)S(1)}, u32[]{:S(2)}, u32[]{:S(2)}) %collective-permute-start.21) | collective-permute-done | bytes 262176 | tf_op jit(solution)/shard_map/ppermute | solution.py:316
  68.3 0.4 collective-permute-start.25
  68.7 1.2 %collective-permute-done.20.got_ref = f32[4,64,256]{2,1,0:T(8,128)S(1)} collective-permute-done((f32[4,64,256]{2,1,0:T(8,128)S(1)}, f32[4,64,256]{2,1,0:T(8,128)S(1)}, u32[]{:S(2)}, u32[]{:S(2)}) %collective-permute-start.20) | collective-permute-done | bytes 262176 | tf_op jit(solution)/shard_map/ppermute | solution.py:316
  69.9 4.5 %collective-permute-start.24 = (f32[2,64,256]{2,1,0:T(8,128)S(1)}, f32[2,64,256]{2,1,0:T(8,128)S(1)}, u32[]{:S(2)}, u32[]{:S(2)}) collective-permute-start(f32[2,64,256]{2,1,0:T(8,128)S(1)} %get-tuple-element.62.refs_0_), channel_id=1, source_target_pairs={{0,8},{1,9},{2,10},{3,11},{4,12},{5,13},{6,14},{7,15},{8,0},{9,1},... | collective-permute-start | bytes 393224 | tf_op jit(solution)/shard_map/ppermute | solution.py:316
  74.4 1.6 %collective-permute-start.23 = (f32[2,64,256]{2,1,0:T(8,128)S(1)}, f32[2,64,256]{2,1,0:T(8,128)S(1)}, u32[]{:S(2)}, u32[]{:S(2)}) collective-permute-start(f32[2,64,256]{2,1,0:T(8,128)S(1)} %get-tuple-element.63.refs_0_), channel_id=1, source_target_pairs={{0,2},{1,3},{2,0},{3,1},{4,6},{5,7},{6,4},{7,5},{8,10},{9,11},{10,... | collective-permute-start | bytes 393224 | tf_op jit(solution)/shard_map/ppermute | solution.py:316
  76.0 0.6 collective-permute-start.22
  76.7 1.6 %collective-permute-done.25.got_ref = f32[2,64,256]{2,1,0:T(8,128)S(1)} collective-permute-done((f32[2,64,256]{2,1,0:T(8,128)S(1)}, f32[2,64,256]{2,1,0:T(8,128)S(1)}, u32[]{:S(2)}, u32[]{:S(2)}) %collective-permute-start.25) | collective-permute-done | bytes 131104 | tf_op jit(solution)/shard_map/ppermute | solution.py:316
  78.3 5.2 %collective-permute-start.27 = (f32[1,64,256]{2,1,0:T(8,128)S(1)}, f32[1,64,256]{2,1,0:T(8,128)S(1)}, u32[]{:S(2)}, u32[]{:S(2)}) collective-permute-start(f32[1,64,256]{2,1,0:T(8,128)S(1)} %get-tuple-element.69.refs_0_), channel_id=1, source_target_pairs={{0,8},{1,9},{2,10},{3,11},{4,12},{5,13},{6,14},{7,15},{8,0},{9,1},... | collective-permute-start | bytes 196616 | tf_op jit(solution)/shard_map/ppermute | solution.py:316
  83.5 0.1 collective-permute-start.28
  83.6 0.9 collective-permute-start.29
  84.5 2.8 %collective-permute-start.26 = (f32[1,64,256]{2,1,0:T(8,128)S(1)}, f32[1,64,256]{2,1,0:T(8,128)S(1)}, u32[]{:S(2)}, u32[]{:S(2)}) collective-permute-start(f32[1,64,256]{2,1,0:T(8,128)S(1)} %get-tuple-element.73.refs_0_), channel_id=1, source_target_pairs={{0,8},{1,9},{2,10},{3,11},{4,12},{5,13},{6,14},{7,15},{8,0},{9,1},... | collective-permute-start | bytes 196616 | tf_op jit(solution)/shard_map/ppermute | solution.py:316
  87.3 0.6 collective-permute-done.28.got_ref
  87.9 2.9 %collective-permute-done.29.got_ref = f32[1,64,256]{2,1,0:T(8,128)S(1)} collective-permute-done((f32[1,64,256]{2,1,0:T(8,128)S(1)}, f32[1,64,256]{2,1,0:T(8,128)S(1)}, u32[]{:S(2)}, u32[]{:S(2)}) %collective-permute-start.29) | collective-permute-done | bytes 65568 | tf_op jit(solution)/shard_map/ppermute | solution.py:316
  90.8 1.4 %collective-permute-done.26.got_ref = f32[1,64,256]{2,1,0:T(8,128)S(1)} collective-permute-done((f32[1,64,256]{2,1,0:T(8,128)S(1)}, f32[1,64,256]{2,1,0:T(8,128)S(1)}, u32[]{:S(2)}, u32[]{:S(2)}) %collective-permute-start.26) | collective-permute-done | bytes 65568 | tf_op jit(solution)/shard_map/ppermute | solution.py:316
  92.2 0.7 finish.7
  (40 shorter events, 0.7 us)
Async XLA Ops:
  0.0 1.0 %copy-start = (bf16[128,1664]{1,0:T(8,128)(2,1)S(1)}, bf16[128,1664]{1,0:T(8,128)(2,1)}, u32[]{:S(2)}) copy-start(bf16[128,1664]{1,0:T(8,128)(2,1)} %activations.7) | copy-start | bytes 1277956
  1.0 0.7 copy-start.1
  2.9 20.9 %collective-permute-start.3 = (f32[128,384]{1,0:T(8,128)S(1)}, f32[128,384]{1,0:T(8,128)S(1)}, u32[]{:S(2)}, u32[]{:S(2)}) collective-permute-start(f32[128,384]{1,0:T(8,128)S(1)} %mix.4.refs_0_), channel_id=1, source_target_pairs={{0,8},{1,9},{2,10},{3,11},{4,12},{5,13},{6,14},{7,15},{8,0},{9,1},... | collective-permute-start | bytes 589832 | tf_op jit(solution)/shard_map/ppermute | solution.py:316
  8.2 5.7 %collective-permute-start = (f32[128,512]{1,0:T(8,128)S(1)}, f32[128,512]{1,0:T(8,128)S(1)}, u32[]{:S(2)}, u32[]{:S(2)}) collective-permute-start(f32[128,512]{1,0:T(8,128)S(1)} %mix.5.refs_0_), channel_id=1, source_target_pairs={{0,1},{1,0},{2,3},{3,2},{4,5},{5,4},{6,7},{7,6},{8,9},{9,8},{10,11... | collective-permute-start | bytes 786440 | tf_op jit(solution)/shard_map/ppermute | solution.py:316
  9.5 11.2 %collective-permute-start.4 = (f32[128,384]{1,0:T(8,128)S(1)}, f32[128,384]{1,0:T(8,128)S(1)}, u32[]{:S(2)}, u32[]{:S(2)}) collective-permute-start(f32[128,384]{1,0:T(8,128)S(1)} %mix.6.refs_0_), channel_id=1, source_target_pairs={{0,2},{1,3},{2,0},{3,1},{4,6},{5,7},{6,4},{7,5},{8,10},{9,11},{10,... | collective-permute-start | bytes 589832 | tf_op jit(solution)/shard_map/ppermute | solution.py:316
  12.3 12.1 %collective-permute-start.2 = (f32[128,384]{1,0:T(8,128)S(1)}, f32[128,384]{1,0:T(8,128)S(1)}, u32[]{:S(2)}, u32[]{:S(2)}) collective-permute-start(f32[128,384]{1,0:T(8,128)S(1)} %mix.7.refs_2_.refs_0_), channel_id=1, source_target_pairs={{0,4},{1,5},{2,6},{3,7},{4,0},{5,1},{6,2},{7,3},{8,12},{9,13},{10,... | collective-permute-start | bytes 589832 | tf_op jit(solution)/shard_map/ppermute | solution.py:316
  14.0 17.6 %collective-permute-start.1 = (f32[128,512]{1,0:T(8,128)S(1)}, f32[128,512]{1,0:T(8,128)S(1)}, u32[]{:S(2)}, u32[]{:S(2)}) collective-permute-start(f32[128,512]{1,0:T(8,128)S(1)} %fold.16.refs_0_), channel_id=1, source_target_pairs={{0,8},{1,9},{2,10},{3,11},{4,12},{5,13},{6,14},{7,15},{8,0},{9,1},... | collective-permute-start | bytes 786440 | tf_op jit(solution)/shard_map/ppermute | solution.py:316
  23.7 1.5 %collective-permute-start.6 = (f32[128,384]{1,0:T(8,128)S(1)}, f32[128,384]{1,0:T(8,128)S(1)}, u32[]{:S(2)}, u32[]{:S(2)}) collective-permute-start(f32[128,384]{1,0:T(8,128)S(1)} %get-tuple-element.43.refs_2_.refs_0_), channel_id=1, source_target_pairs={{0,1},{1,0},{2,3},{3,2},{4,5},{5,4},{6,7},{7,6},{8,9},{9,8},{10,11... | collective-permute-start | bytes 589832 | tf_op jit(solution)/shard_map/ppermute | solution.py:316
  23.9 13.3 %collective-permute-start.9 = (f32[128,384]{1,0:T(8,128)S(1)}, f32[128,384]{1,0:T(8,128)S(1)}, u32[]{:S(2)}, u32[]{:S(2)}) collective-permute-start(f32[128,384]{1,0:T(8,128)S(1)} %fold.18.refs_2_.refs_0_), channel_id=1, source_target_pairs={{0,4},{1,5},{2,6},{3,7},{4,0},{5,1},{6,2},{7,3},{8,12},{9,13},{10,... | collective-permute-start | bytes 589832 | tf_op jit(solution)/shard_map/ppermute | solution.py:316
  24.4 7.1 %collective-permute-start.5 = (f32[128,384]{1,0:T(8,128)S(1)}, f32[128,384]{1,0:T(8,128)S(1)}, u32[]{:S(2)}, u32[]{:S(2)}) collective-permute-start(f32[128,384]{1,0:T(8,128)S(1)} %fold.19.refs_2_.refs_0_), channel_id=1, source_target_pairs={{0,2},{1,3},{2,0},{3,1},{4,6},{5,7},{6,4},{7,5},{8,10},{9,11},{10,... | collective-permute-start | bytes 589832 | tf_op jit(solution)/shard_map/ppermute | solution.py:316
  25.3 18.9 %collective-permute-start.8 = (f32[128,384]{1,0:T(8,128)S(1)}, f32[128,384]{1,0:T(8,128)S(1)}, u32[]{:S(2)}, u32[]{:S(2)}) collective-permute-start(f32[128,384]{1,0:T(8,128)S(1)} %fold.20.refs_2_.refs_0_), channel_id=1, source_target_pairs={{0,8},{1,9},{2,10},{3,11},{4,12},{5,13},{6,14},{7,15},{8,0},{9,1},... | collective-permute-start | bytes 589832 | tf_op jit(solution)/shard_map/ppermute | solution.py:316
  31.5 5.8 %collective-permute-start.11 = (f32[128,384]{1,0:T(8,128)S(1)}, f32[128,384]{1,0:T(8,128)S(1)}, u32[]{:S(2)}, u32[]{:S(2)}) collective-permute-start(f32[128,384]{1,0:T(8,128)S(1)} %fold.21.refs_2_.refs_0_), channel_id=1, source_target_pairs={{0,1},{1,0},{2,3},{3,2},{4,5},{5,4},{6,7},{7,6},{8,9},{9,8},{10,11... | collective-permute-start | bytes 589832 | tf_op jit(solution)/shard_map/ppermute | solution.py:316
  31.6 13.3 %collective-permute-start.7 = (f32[128,512]{1,0:T(8,128)S(1)}, f32[128,512]{1,0:T(8,128)S(1)}, u32[]{:S(2)}, u32[]{:S(2)}) collective-permute-start(f32[128,512]{1,0:T(8,128)S(1)} %fold.22.refs_2_.refs_0_), channel_id=1, source_target_pairs={{0,4},{1,5},{2,6},{3,7},{4,0},{5,1},{6,2},{7,3},{8,12},{9,13},{10,... | collective-permute-start | bytes 786440 | tf_op jit(solution)/shard_map/ppermute | solution.py:316
  37.2 6.9 %collective-permute-start.10 = (f32[128,384]{1,0:T(8,128)S(1)}, f32[128,384]{1,0:T(8,128)S(1)}, u32[]{:S(2)}, u32[]{:S(2)}) collective-permute-start(f32[128,384]{1,0:T(8,128)S(1)} %fold.23.refs_2_.refs_0_), channel_id=1, source_target_pairs={{0,2},{1,3},{2,0},{3,1},{4,6},{5,7},{6,4},{7,5},{8,10},{9,11},{10,... | collective-permute-start | bytes 589832 | tf_op jit(solution)/shard_map/ppermute | solution.py:316
  37.4 17.5 %collective-permute-start.14 = (f32[128,384]{1,0:T(8,128)S(1)}, f32[128,384]{1,0:T(8,128)S(1)}, u32[]{:S(2)}, u32[]{:S(2)}) collective-permute-start(f32[128,384]{1,0:T(8,128)S(1)} %fold.24.refs_2_.refs_0_), channel_id=1, source_target_pairs={{0,8},{1,9},{2,10},{3,11},{4,12},{5,13},{6,14},{7,15},{8,0},{9,1},... | collective-permute-start | bytes 589832 | tf_op jit(solution)/shard_map/ppermute | solution.py:316
  44.1 1.5 %collective-permute-start.13 = (f32[128,384]{1,0:T(8,128)S(1)}, f32[128,384]{1,0:T(8,128)S(1)}, u32[]{:S(2)}, u32[]{:S(2)}) collective-permute-start(f32[128,384]{1,0:T(8,128)S(1)} %fold.25.refs_2_.refs_0_), channel_id=1, source_target_pairs={{0,1},{1,0},{2,3},{3,2},{4,5},{5,4},{6,7},{7,6},{8,9},{9,8},{10,11... | collective-permute-start | bytes 589832 | tf_op jit(solution)/shard_map/ppermute | solution.py:316
  44.3 10.6 %collective-permute-start.15 = (f32[128,384]{1,0:T(8,128)S(1)}, f32[128,384]{1,0:T(8,128)S(1)}, u32[]{:S(2)}, u32[]{:S(2)}) collective-permute-start(f32[128,384]{1,0:T(8,128)S(1)} %fold.26.refs_2_.refs_0_), channel_id=1, source_target_pairs={{0,4},{1,5},{2,6},{3,7},{4,0},{5,1},{6,2},{7,3},{8,12},{9,13},{10,... | collective-permute-start | bytes 589832 | tf_op jit(solution)/shard_map/ppermute | solution.py:316
  45.0 8.3 %collective-permute-start.12 = (f32[128,512]{1,0:T(8,128)S(1)}, f32[128,512]{1,0:T(8,128)S(1)}, u32[]{:S(2)}, u32[]{:S(2)}) collective-permute-start(f32[128,512]{1,0:T(8,128)S(1)} %fold.27.refs_2_.refs_0_), channel_id=1, source_target_pairs={{0,2},{1,3},{2,0},{3,1},{4,6},{5,7},{6,4},{7,5},{8,10},{9,11},{10,... | collective-permute-start | bytes 786440 | tf_op jit(solution)/shard_map/ppermute | solution.py:316
  56.2 2.7 %collective-permute-start.17 = (f32[8,128,256]{2,1,0:T(8,128)S(1)}, f32[8,128,256]{2,1,0:T(8,128)S(1)}, u32[]{:S(2)}, u32[]{:S(2)}) collective-permute-start(f32[8,128,256]{2,1,0:T(8,128)S(1)} %get-tuple-element.52), channel_id=1, source_target_pairs={{0,1},{1,0},{2,3},{3,2},{4,5},{5,4},{6,7},{7,6},{8,9},{9,8},{10,11... | collective-permute-start | bytes 3145736 | tf_op jit(solution)/shard_map/ppermute | solution.py:316
  56.3 4.7 %collective-permute-start.16 = (f32[8,128,256]{2,1,0:T(8,128)S(1)}, f32[8,128,256]{2,1,0:T(8,128)S(1)}, u32[]{:S(2)}, u32[]{:S(2)}) collective-permute-start(f32[8,128,256]{2,1,0:T(8,128)S(1)} %get-tuple-element.49.refs_4_), channel_id=1, source_target_pairs={{0,1},{1,0},{2,3},{3,2},{4,5},{5,4},{6,7},{7,6},{8,9},{9,8},{10,11... | collective-permute-start | bytes 3145736 | tf_op jit(solution)/shard_map/ppermute | solution.py:316
  59.1 9.2 %collective-permute-start.21 = (f32[4,64,256]{2,1,0:T(8,128)S(1)}, f32[4,64,256]{2,1,0:T(8,128)S(1)}, u32[]{:S(2)}, u32[]{:S(2)}) collective-permute-start(f32[4,64,256]{2,1,0:T(8,128)S(1)} %get-tuple-element.60), channel_id=1, source_target_pairs={{0,4},{1,5},{2,6},{3,7},{4,0},{5,1},{6,2},{7,3},{8,12},{9,13},{10,... | collective-permute-start | bytes 786440 | tf_op jit(solution)/shard_map/ppermute | solution.py:316
  60.7 9.2 %collective-permute-start.20 = (f32[4,64,256]{2,1,0:T(8,128)S(1)}, f32[4,64,256]{2,1,0:T(8,128)S(1)}, u32[]{:S(2)}, u32[]{:S(2)}) collective-permute-start(f32[4,64,256]{2,1,0:T(8,128)S(1)} %get-tuple-element.53.refs_0_), channel_id=1, source_target_pairs={{0,2},{1,3},{2,0},{3,1},{4,6},{5,7},{6,4},{7,5},{8,10},{9,11},{10,... | collective-permute-start | bytes 786440 | tf_op jit(solution)/shard_map/ppermute | solution.py:316
  61.1 13.3 %collective-permute-start.19 = (f32[4,64,256]{2,1,0:T(8,128)S(1)}, f32[4,64,256]{2,1,0:T(8,128)S(1)}, u32[]{:S(2)}, u32[]{:S(2)}) collective-permute-start(f32[4,64,256]{2,1,0:T(8,128)S(1)} %get-tuple-element.57.refs_0_), channel_id=1, source_target_pairs={{0,4},{1,5},{2,6},{3,7},{4,0},{5,1},{6,2},{7,3},{8,12},{9,13},{10,... | collective-permute-start | bytes 786440 | tf_op jit(solution)/shard_map/ppermute | solution.py:316
  62.2 13.8 %collective-permute-start.18 = (f32[4,64,256]{2,1,0:T(8,128)S(1)}, f32[4,64,256]{2,1,0:T(8,128)S(1)}, u32[]{:S(2)}, u32[]{:S(2)}) collective-permute-start(f32[4,64,256]{2,1,0:T(8,128)S(1)} %get-tuple-element.55), channel_id=1, source_target_pairs={{0,2},{1,3},{2,0},{3,1},{4,6},{5,7},{6,4},{7,5},{8,10},{9,11},{10,... | collective-permute-start | bytes 786440 | tf_op jit(solution)/shard_map/ppermute | solution.py:316
  68.3 10.0 %collective-permute-start.25 = (f32[2,64,256]{2,1,0:T(8,128)S(1)}, f32[2,64,256]{2,1,0:T(8,128)S(1)}, u32[]{:S(2)}, u32[]{:S(2)}) collective-permute-start(f32[2,64,256]{2,1,0:T(8,128)S(1)} %get-tuple-element.61.refs_0_), channel_id=1, source_target_pairs={{0,2},{1,3},{2,0},{3,1},{4,6},{5,7},{6,4},{7,5},{8,10},{9,11},{10,... | collective-permute-start | bytes 393224 | tf_op jit(solution)/shard_map/ppermute | solution.py:316
  69.9 13.6 %collective-permute-start.24 = (f32[2,64,256]{2,1,0:T(8,128)S(1)}, f32[2,64,256]{2,1,0:T(8,128)S(1)}, u32[]{:S(2)}, u32[]{:S(2)}) collective-permute-start(f32[2,64,256]{2,1,0:T(8,128)S(1)} %get-tuple-element.62.refs_0_), channel_id=1, source_target_pairs={{0,8},{1,9},{2,10},{3,11},{4,12},{5,13},{6,14},{7,15},{8,0},{9,1},... | collective-permute-start | bytes 393224 | tf_op jit(solution)/shard_map/ppermute | solution.py:316
  74.4 9.1 %collective-permute-start.23 = (f32[2,64,256]{2,1,0:T(8,128)S(1)}, f32[2,64,256]{2,1,0:T(8,128)S(1)}, u32[]{:S(2)}, u32[]{:S(2)}) collective-permute-start(f32[2,64,256]{2,1,0:T(8,128)S(1)} %get-tuple-element.63.refs_0_), channel_id=1, source_target_pairs={{0,2},{1,3},{2,0},{3,1},{4,6},{5,7},{6,4},{7,5},{8,10},{9,11},{10,... | collective-permute-start | bytes 393224 | tf_op jit(solution)/shard_map/ppermute | solution.py:316
  76.0 8.5 %collective-permute-start.22 = (f32[2,64,256]{2,1,0:T(8,128)S(1)}, f32[2,64,256]{2,1,0:T(8,128)S(1)}, u32[]{:S(2)}, u32[]{:S(2)}) collective-permute-start(f32[2,64,256]{2,1,0:T(8,128)S(1)} %get-tuple-element.65.refs_0_), channel_id=1, source_target_pairs={{0,4},{1,5},{2,6},{3,7},{4,0},{5,1},{6,2},{7,3},{8,12},{9,13},{10,... | collective-permute-start | bytes 393224 | tf_op jit(solution)/shard_map/ppermute | solution.py:316
  78.3 9.0 %collective-permute-start.27 = (f32[1,64,256]{2,1,0:T(8,128)S(1)}, f32[1,64,256]{2,1,0:T(8,128)S(1)}, u32[]{:S(2)}, u32[]{:S(2)}) collective-permute-start(f32[1,64,256]{2,1,0:T(8,128)S(1)} %get-tuple-element.69.refs_0_), channel_id=1, source_target_pairs={{0,8},{1,9},{2,10},{3,11},{4,12},{5,13},{6,14},{7,15},{8,0},{9,1},... | collective-permute-start | bytes 196616 | tf_op jit(solution)/shard_map/ppermute | solution.py:316
  83.5 4.4 %collective-permute-start.28 = (f32[1,64,256]{2,1,0:T(8,128)S(1)}, f32[1,64,256]{2,1,0:T(8,128)S(1)}, u32[]{:S(2)}, u32[]{:S(2)}) collective-permute-start(f32[1,64,256]{2,1,0:T(8,128)S(1)} %get-tuple-element.70.refs_0_), channel_id=1, source_target_pairs={{0,4},{1,5},{2,6},{3,7},{4,0},{5,1},{6,2},{7,3},{8,12},{9,13},{10,... | collective-permute-start | bytes 196616 | tf_op jit(solution)/shard_map/ppermute | solution.py:316
  83.6 7.2 %collective-permute-start.29 = (f32[1,64,256]{2,1,0:T(8,128)S(1)}, f32[1,64,256]{2,1,0:T(8,128)S(1)}, u32[]{:S(2)}, u32[]{:S(2)}) collective-permute-start(f32[1,64,256]{2,1,0:T(8,128)S(1)} %get-tuple-element.71.refs_0_), channel_id=1, source_target_pairs={{0,8},{1,9},{2,10},{3,11},{4,12},{5,13},{6,14},{7,15},{8,0},{9,1},... | collective-permute-start | bytes 196616 | tf_op jit(solution)/shard_map/ppermute | solution.py:316
  84.5 7.7 %collective-permute-start.26 = (f32[1,64,256]{2,1,0:T(8,128)S(1)}, f32[1,64,256]{2,1,0:T(8,128)S(1)}, u32[]{:S(2)}, u32[]{:S(2)}) collective-permute-start(f32[1,64,256]{2,1,0:T(8,128)S(1)} %get-tuple-element.73.refs_0_), channel_id=1, source_target_pairs={{0,8},{1,9},{2,10},{3,11},{4,12},{5,13},{6,14},{7,15},{8,0},{9,1},... | collective-permute-start | bytes 196616 | tf_op jit(solution)/shard_map/ppermute | solution.py:316
